TPU v7x, 32 devices: a whole 2x2x4 slice. The times are simulated.
32 devices in a mesh: seq: 8 (over z, core), tensor: 4 (over y, x).
Axes of the slice: x: 2, y: 2, z: 4, core: 2. Of those that a mesh axis runs over, the one named last changes fastest.
Arguments:
- activations: bfloat16 [1024, 131072], P('tensor', 'seq'), may hold values from -24 to 24
- first_factor: bfloat16 [512, 512], replicated, may hold values from -0.25 to 0.25
- spectral: float32 [1024, 131072], P('tensor', 'seq'), may hold values from -4 to 4
- second_factor: float32 [256, 256], replicated, may hold values from -0.375 to 0.375
- gate_scale: float32 [1024], replicated, may hold values from -4 to 4
- gate_shift: float32 [1024], replicated, may hold values from -4 to 4
- expand_weight: bfloat16 [1024, 6144], P(None, ('seq', 'tensor')), may hold values from -0.1875 to 0.1875
- reduce_weight: bfloat16 [6144, 1024], P(('seq', 'tensor')), may hold values from -0.15625 to 0.15625
Outputs:
- layer_out: bfloat16 [1024, 131072], P('tensor', 'seq')
All inputs are finite; a program needn't handle non-finite values.
Results may differ from a plain program's by a relative error of at most 0.0052.
Values may be sent and summed in bfloat16 or wider, within the bound.
No kernel may reach another device: no remote copies, remote signals or barrier semaphores. Data moves between devices by JAX's collectives and lax.ppermute only.
A program may use at most 192 MiB of HBM per device.

v0:
```python
import jax
import jax.numpy as jnp
from jax import lax
from jax.sharding import PartitionSpec as P

B = 512


epsilon = 1e-06


def normalize(block):
    values = block.astype(jnp.float32)
    scale = lax.rsqrt(jnp.mean(values * values, axis=0, keepdims=True) + epsilon)
    return (values * scale).astype(jnp.bfloat16)


def expand(normed, shard_rows):
    product = jnp.einsum("ch,cl->hl", shard_rows, normed, preferred_element_type=jnp.float32)
    return jax.nn.gelu(product).astype(jnp.bfloat16)


def on_device(
    activations,
    first_factor,
    spectral,
    second_factor,
    gate_scale,
    gate_shift,
    expand_weight,
    reduce_weight,
):
    channels = activations.shape[0]
    blocks = activations.shape[1] // B
    first_pass = jnp.einsum(
        "cai,ij->caj",
        activations.reshape(channels, blocks, B),
        first_factor,
        preferred_element_type=jnp.float32,
    )
    spectrum = first_pass * spectral.reshape(channels, blocks, B)
    mixed_part = jnp.einsum(
        "pa,caj->cpj",
        second_factor,
        lax.all_to_all(spectrum, "seq", split_axis=0, concat_axis=1, tiled=True),
        precision=lax.Precision.HIGHEST,
    )
    returned = lax.all_to_all(mixed_part, "seq", split_axis=1, concat_axis=0, tiled=True)
    offset = lax.axis_index("tensor") * channels
    scale_here = lax.dynamic_slice_in_dim(gate_scale, offset, channels)[:, None]
    shift_here = lax.dynamic_slice_in_dim(gate_shift, offset, channels)[:, None]
    inputs = activations.astype(jnp.float32)
    gating = jax.nn.sigmoid(inputs * scale_here + shift_here)
    residual_in = (inputs + gating * returned.reshape(channels, -1)).astype(jnp.bfloat16)
    token_block = lax.all_to_all(residual_in, "tensor", split_axis=1, concat_axis=0, tiled=True)
    normed = normalize(token_block)
    hidden = expand(normed, lax.all_gather(expand_weight, ("seq", "tensor"), axis=1, tiled=True))
    weight_full = lax.all_gather(reduce_weight, ("seq", "tensor"), axis=0, tiled=True)
    summed = jnp.einsum("hc,hl->cl", weight_full, hidden, preferred_element_type=jnp.float32)
    combined = (token_block.astype(jnp.float32) + summed).astype(jnp.bfloat16)
    return lax.all_to_all(combined, "tensor", split_axis=0, concat_axis=1, tiled=True)


def solution(mesh):
    return jax.shard_map(
        on_device,
        mesh=mesh,
        in_specs=(
            P("tensor", "seq"),
            P(),
            P("tensor", "seq"),
            P(),
            P(),
            P(),
            P(None, ("seq", "tensor")),
            P(("seq", "tensor"), None),
        ),
        out_specs=P("tensor", "seq"),
        check_vma=False,
    )
```

profile of v0, /device:TPU:0, one launch (start us, length us, event | category | flops | bytes accessed | tf_op | source)
XLA Modules:
  0.0 1387.4 jit_solution(12243936937271801510)
XLA Ops:
  6.5 0.0 copy-start
  6.5 17.5 %copy.42 = f32[256,16384]{0,1:T(8,128)} copy(f32[256,16384]{1,0:T(8,128)} %param.10) | data formatting | bytes 33554432 | tf_op args[2]
  24.0 17.5 %copy.43 = f32[256,32,512]{2,0,1:T(8,128)} copy(f32[256,32,512]{0,2,1:T(8,128)} %bitcast.69) | data formatting | bytes 33554432 | tf_op jit(solution)/shard_map/reshape | solution.py:41
  41.5 0.0 copy-done
  41.5 14.1 %convolution_multiply_fusion = f32[256,32,512]{2,0,1:T(8,128)} fusion(f32[256,32,512]{2,0,1:T(8,128)} %copy.43, bf16[32,32,8,512]{3,2,1,0:T(8,128)(2,1)} %bitcast.73, bf16[512,512]{1,0:T(8,128)(2,1)S(1)} %copy-done), kind=kOutput, calls=%fused_computation.25 | convolution fusion | flops 4299161600 | bytes 42467328 | tf_op jit(solution)/shard_map/cai,ij->caj/dot_general | solution.py:35
  55.6 15.2 %copy.44 = f32[256,32,512]{2,1,0:T(8,128)S(1)} copy(f32[256,32,512]{2,0,1:T(8,128)} %convolution_multiply_fusion) | data formatting | bytes 33554432 | tf_op jit(solution)/shard_map/mul | solution.py:41
  70.8 370.5 %all_to_all.65 = f32[256,32,512]{2,1,0:T(8,128)S(1)} all-to-all(f32[256,32,512]{2,1,0:T(8,128)S(1)} %copy.44), channel_id=1, replica_groups=mesh['seq'=8,'tensor'=4] {'seq'}, dimensions={0} | all-to-all | bytes 33554432 | tf_op jit(solution)/shard_map/all_to_all | solution.py:45
  441.3 0.0 copy-start.2
  441.3 6.2 copy.45
  447.5 0.0 copy-done.2
  447.6 33.6 %convolution_bitcast_fusion = f32[32,256,512]{1,2,0:T(8,128)} fusion(f32[32,256,512]{2,1,0:T(8,128)} %bitcast.67, f32[256,256]{1,0:T(8,128)S(1)} %copy-done.2), kind=kOutput, calls=%fused_computation.26 | convolution fusion | flops 12884901888 | bytes 33816576 | tf_op jit(solution)/shard_map/pa,caj->cpj/dot_general | solution.py:42
  481.2 20.2 %copy.47 = f32[32,256,512]{2,0,1:T(8,128)} copy(f32[32,256,512]{1,2,0:T(8,128)} %convolution_bitcast_fusion) | data formatting | bytes 33554432 | tf_op jit(solution)/shard_map/pa,caj->cpj/transpose | solution.py:42
  501.4 5.7 all-to-all-start.1
  507.1 0.0 all-gather.3.cloned.1.call-start
  507.2 0.7 all-gather.3.cloned.1.call-update
  507.9 0.8 dynamic_slice.6
  508.6 0.8 dynamic_slice.7
  509.4 420.4 %all-to-all-done.1 = f32[32,256,512]{2,0,1:T(8,128)} async-done(((f32[32,256,512]{2,0,1:T(8,128)}), f32[32,256,512]{2,0,1:T(8,128)}, u32[]{:S(2)}, u32[]{:S(2)}) %all-to-all-start.1) | async-done | bytes 16777248 | tf_op jit(solution)/shard_map/all_to_all | solution.py:48
  929.8 15.2 %copy.49 = f32[8,32,32,512]{3,2,1,0:T(8,128)S(1)} copy(f32[8,32,32,512]{3,1,2,0:T(8,128)} %bitcast.9) | data formatting | bytes 33554432 | tf_op jit(solution)/shard_map/all_to_all | solution.py:48
  945.0 10.3 copy.57
  955.3 9.8 fusion.18
  965.1 7.7 copy.63
  972.8 5.6 all-to-all-start.2
  978.4 0.0 all-gather.5.cloned.1.call-start
  978.5 0.7 all-gather.5.cloned.1.call-update
  979.2 108.5 %all-to-all-done.2 = bf16[256,4,4096]{2,0,1:T(8,128)(2,1)} async-done(((bf16[256,4,4096]{2,0,1:T(8,128)(2,1)}), bf16[256,4,4096]{2,0,1:T(8,128)(2,1)}, u32[]{:S(2)}, u32[]{:S(2)}) %all-to-all-start.2) | async-done | bytes 8388640 | tf_op jit(solution)/shard_map/all_to_all | solution.py:55
  1087.7 5.1 fusion.16
  1092.8 9.5 fusion.17
  1102.3 0.0 all-gather.3.cloned.1.call-done
  1102.3 86.7 %fusion.7.clone.6 = bf16[6144,4096]{0,1:T(8,128)(2,1)} fusion(bf16[1024,4096]{1,0:T(8,128)(2,1)} %fusion.17, bf16[1024,6144]{0,1:T(8,128)(2,1)} %all-gather.3.cloned.1.call-done), kind=kOutput, calls=%fused_computation.8.clone.clone.clone.clone.clone.1 | convolution fusion | flops 51766099968 | bytes 71303168 | tf_op jit(solution)/shard_map/ch,cl->hl/dot_general | solution.py:19
  1189.0 0.0 all-gather.5.cloned.1.call-done
  1189.1 86.4 %fusion.15 = bf16[1024,4096]{1,0:T(8,128)(2,1)} fusion(bf16[256,4,4096]{2,0,1:T(8,128)(2,1)} %all-to-all-done.2, bf16[6144,1024]{1,0:T(8,128)(2,1)} %all-gather.5.cloned.1.call-done, bf16[6144,4096]{0,1:T(8,128)(2,1)} %fusion.7.clone.6), kind=kOutput, calls=%fused_computation.19 | convolution fusion | flops 51552190464 | bytes 79691776 | tf_op jit(solution)/shard_map/hc,hl->cl/dot_general | solution.py:59
  1275.5 0.0 copy-start.1
  1275.5 97.0 %all_to_all.66 = bf16[4,256,4096]{2,1,0:T(8,128)(2,1)} all-to-all(bf16[4,256,4096]{2,1,0:T(8,128)(2,1)} %bitcast.74), channel_id=1, replica_groups=mesh['seq'=8,'tensor'=4] {'tensor'}, dimensions={0} | all-to-all | bytes 16777216 | tf_op jit(solution)/shard_map/all_to_all | solution.py:61
  1372.4 7.9 copy.56
  1380.3 0.0 copy-done.1
  (1 shorter events, 0.0 us)
Async XLA Ops:
  6.5 35.0 %copy-start = (bf16[512,512]{1,0:T(8,128)(2,1)S(1)}, bf16[512,512]{1,0:T(8,128)(2,1)}, u32[]{:S(2)}) copy-start(bf16[512,512]{1,0:T(8,128)(2,1)} %param.9) | copy-start | bytes 1572868
  441.3 6.3 copy-start.2
  501.4 428.4 %all-to-all-start.1 = ((f32[32,256,512]{2,0,1:T(8,128)}), f32[32,256,512]{2,0,1:T(8,128)}, u32[]{:S(2)}, u32[]{:S(2)}) async-start(f32[32,256,512]{2,0,1:T(8,128)} %copy.47), calls=%async_computation.1 | async-start | bytes 33554432 | tf_op jit(solution)/shard_map/all_to_all | solution.py:48
  507.1 595.2 %all-gather.3.cloned.1.call-start = ((), (), s32[]{:S(2)}) async-start(), calls=%async_computation.4 | async-start | bytes 12976128 | tf_op jit(solution)/shard_map/all_gather | solution.py:57
  972.8 114.9 %all-to-all-start.2 = ((bf16[256,4,4096]{2,0,1:T(8,128)(2,1)}), bf16[256,4,4096]{2,0,1:T(8,128)(2,1)}, u32[]{:S(2)}, u32[]{:S(2)}) async-start(bf16[256,4,4096]{2,0,1:T(8,128)(2,1)} %bitcast.70), calls=%async_computation.2 | async-start | bytes 16777216 | tf_op jit(solution)/shard_map/all_to_all | solution.py:55
  978.4 210.6 %all-gather.5.cloned.1.call-start = ((), (), s32[]{:S(2)}) async-start(), calls=%async_computation.5 | async-start | bytes 12976128 | tf_op jit(solution)/shard_map/all_gather | solution.py:58
  1275.5 104.9 %copy-start.1 = (bf16[512,512]{1,0:T(8,128)(2,1)S(1)}, bf16[512,512]{1,0:T(8,128)(2,1)}, u32[]{:S(2)}) copy-start(bf16[512,512]{1,0:T(8,128)(2,1)} %param.9) | copy-start | bytes 1572868
Sparse Core Ops, SparseCore 0:
  510.8 198.3 all-gather.2
  982.2 140.6 all-gather.4
where the time goes:
time: 1390 us
  waiting for transfers between devices  530 us (38%)
  blocking collectives  467 us (34%)
  matrix products  221 us (16%)
  local copies, waits for them, and re-layouts  119 us (9%)
  other arithmetic  24.4 us (2%)
    all_to_all x1, waiting for transfers between devices, on_device(): lax.all_to_all(mixed_part, 'seq', split_axis=1, concat_axis=0, tiled=True)  420 us
    all_to_all x1, blocking collectives, on_device(): lax.all_to_all(spectrum, 'seq', split_axis=0, concat_axis=1, tiled=True)  371 us
    all_to_all x1, waiting for transfers between devices, on_device(): lax.all_to_all(residual_in, 'tensor', split_axis=1, concat_axis=0, tiled=...  109 us
    all_to_all x1, blocking collectives, on_device(): lax.all_to_all(combined, 'tensor', split_axis=0, concat_axis=1, tiled=True)  97 us
    dot_general x1, matrix products, expand(): jnp.einsum('ch,cl->hl', shard_rows, normed, preferred_element_type=jnp.fl...  86.7 us
    dot_general x1, matrix products, on_device(): jnp.einsum('hc,hl->cl', weight_full, hidden, preferred_element_type=jnp.f...  86.4 us
    dot_general x1, matrix products, on_device(): jnp.einsum('pa,caj->cpj', second_factor, lax.all_to_all(spectrum, 'seq',...  33.6 us
    unnamed x8, local copies, waits for them, and re-layouts  27.8 us
  transfers between devices with their start and end apart: 4, of which 2 were waited for; matrix products, arithmetic and copies ran while one was open for 11% of the time, Pallas kernels for 0%

commit v1 on v0

v1 whole, which is shorter than its diff:
```python
import jax
import jax.numpy as jnp
from jax import lax
from jax.sharding import PartitionSpec as P

B = 512
COLUMNS = 128
epsilon = 1e-06


def normalize(block):
    values = block.astype(jnp.float32)
    scale = lax.rsqrt(jnp.mean(values * values, axis=0, keepdims=True) + epsilon)
    return (values * scale).astype(jnp.bfloat16)


def expand(normed, shard_rows):
    product = jnp.einsum("ch,cl->hl", shard_rows, normed, preferred_element_type=jnp.float32)
    return jax.nn.gelu(product).astype(jnp.bfloat16)


def on_device(
    activations,
    first_factor,
    spectral,
    second_factor,
    gate_scale,
    gate_shift,
    expand_weight,
    reduce_weight,
):
    channels = activations.shape[0]
    blocks = activations.shape[1] // B
    offset = lax.axis_index("tensor") * channels
    scale_here = lax.dynamic_slice_in_dim(gate_scale, offset, channels)[:, None, None]
    shift_here = lax.dynamic_slice_in_dim(gate_shift, offset, channels)[:, None, None]
    weight_in = lax.all_gather(expand_weight, ("seq", "tensor"), axis=1, tiled=True)
    weight_out = lax.all_gather(reduce_weight, ("seq", "tensor"), axis=0, tiled=True)
    act3 = activations.reshape(channels, blocks, B)
    spec3 = spectral.reshape(channels, blocks, B)
    high = lax.reduce_precision(second_factor, 8, 7)
    low = (second_factor - high).astype(jnp.bfloat16)
    high = high.astype(jnp.bfloat16)

    outs = []
    for start in range(0, B, COLUMNS):
        stop = start + COLUMNS
        first_pass = jnp.einsum(
            "cai,ij->caj", act3, first_factor[:, start:stop], preferred_element_type=jnp.float32
        )
        spectrum = (first_pass * spec3[:, :, start:stop]).astype(jnp.bfloat16)
        gathered = lax.all_to_all(spectrum, "seq", split_axis=0, concat_axis=1, tiled=True)
        mixed = jnp.einsum("pa,caj->cpj", high, gathered, preferred_element_type=jnp.float32)
        mixed += jnp.einsum("pa,caj->cpj", low, gathered, preferred_element_type=jnp.float32)
        returned = lax.all_to_all(
            mixed.astype(jnp.bfloat16), "seq", split_axis=1, concat_axis=0, tiled=True
        )
        inputs = act3[:, :, start:stop].astype(jnp.float32)
        gating = jax.nn.sigmoid(inputs * scale_here + shift_here)
        residual_in = (inputs + gating * returned.astype(jnp.float32)).astype(jnp.bfloat16)
        token_block = lax.all_to_all(residual_in, "tensor", split_axis=1, concat_axis=0, tiled=True)
        shape = token_block.shape
        token_block = token_block.reshape(shape[0], -1)
        hidden = expand(normalize(token_block), weight_in)
        summed = jnp.einsum("hc,hl->cl", weight_out, hidden, preferred_element_type=jnp.float32)
        combined = (token_block.astype(jnp.float32) + summed).astype(jnp.bfloat16).reshape(shape)
        outs.append(lax.all_to_all(combined, "tensor", split_axis=0, concat_axis=1, tiled=True))
    return jnp.concatenate(outs, axis=2).reshape(channels, -1)


def solution(mesh):
    return jax.shard_map(
        on_device,
        mesh=mesh,
        in_specs=(
            P("tensor", "seq"),
            P(),
            P("tensor", "seq"),
            P(),
            P(),
            P(),
            P(None, ("seq", "tensor")),
            P(("seq", "tensor"), None),
        ),
        out_specs=P("tensor", "seq"),
        check_vma=False,
    )
```

time: 1390 us -> 1030 us (0.74)
  blocking collectives: 467 us -> 0 us
  local copies, waits for them, and re-layouts: 119 us -> 224 us
  waiting for transfers between devices: 530 us -> 448 us
  starting transfers between devices: 11.4 us -> 70.5 us
  other arithmetic: 24.4 us -> 45.5 us
    all_to_all x2 -> x0, blocking collectives: 467 us -> none  [the longest x1 371 us: on_device(): lax.all_to_all(spectrum, 'seq', split_axis=0, concat_axis=1, tiled=True)]
    convert_element_type x0 -> x20, local copies, waits for them, and re-layouts: none -> 72 us  [the longest x4 21.3 us: on_device(): token_block.astype(jnp.float32) + summed]
    unnamed x8 -> x39, local copies, waits for them, and re-layouts: 27.8 us -> 96.8 us
    all_to_all x1 -> x12, starting transfers between devices: 5.74 us -> 53.2 us  [the longest x4 18.5 us: on_device(): lax.all_to_all(combined, 'tensor', split_axis=0, concat_axis=1, tiled=True)]
    all_to_all x1 -> x4, waiting for transfers between devices: 109 us -> 63 us  [on_device(): lax.all_to_all(residual_in, 'tensor', split_axis=1, concat_axis=0, tiled=...]
    all_to_all x1 -> x12, waiting for transfers between devices: 420 us -> 384 us  [the longest x4 195 us: on_device(): lax.all_to_all(mixed.astype(jnp.bfloat16), 'seq', split_axis=1, concat_ax...]
    transpose x1 -> x0, local copies, waits for them, and re-layouts: 20.2 us -> none  [on_device(): jnp.einsum('pa,caj->cpj', second_factor, lax.all_to_all(spectrum, 'seq',...]
    mul x1 -> x0, local copies, waits for them, and re-layouts: 15.2 us -> none  [on_device(): spectrum = first_pass * spectral.reshape(channels, blocks, B)]
  transfers between devices with their start and end apart: 4 -> 18, of which waited for: 2 -> 12; matrix products, arithmetic and copies ran while one was open for 11% -> 42% of each run, Pallas kernels for 0% -> 0%
where the time goes in v1:
time: 1030 us; the launch traced here: 1020 us
  waiting for transfers between devices  448 us (43%)
  local copies, waits for them, and re-layouts  224 us (22%)
  matrix products  217 us (21%)
  starting transfers between devices  70.5 us (7%)
  other arithmetic  45.5 us (4%)
  between operations  14.2 us (1%)
    all_to_all x4, waiting for transfers between devices, on_device(): lax.all_to_all(mixed.astype(jnp.bfloat16), 'seq', split_axis=1, concat_ax...  195 us
    all_to_all x4, waiting for transfers between devices, on_device(): lax.all_to_all(spectrum, 'seq', split_axis=0, concat_axis=1, tiled=True)  174 us
    unnamed x39, local copies, waits for them, and re-layouts  96.8 us
    dot_general x4, matrix products, expand(): jnp.einsum('ch,cl->hl', shard_rows, normed, preferred_element_type=jnp.fl...  96.2 us
    dot_general x4, matrix products, on_device(): jnp.einsum('hc,hl->cl', weight_out, hidden, preferred_element_type=jnp.fl...  81.4 us
    all_to_all x4, waiting for transfers between devices, on_device(): lax.all_to_all(residual_in, 'tensor', split_axis=1, concat_axis=0, tiled=...  63 us
    dot_general x4, matrix products, on_device(): jnp.einsum('cai,ij->caj', act3, first_factor[:, start:stop], preferred_el...  27.7 us
    convert_element_type x4, local copies, waits for them, and re-layouts, on_device(): token_block.astype(jnp.float32) + summed  21.3 us
  transfers between devices with their start and end apart: 18, of which 12 were waited for; matrix products, arithmetic and copies ran while one was open for 42% of the time, Pallas kernels for 0%

profile of v1, /device:TPU:0, one launch (start us, length us, event | category | flops | bytes accessed | tf_op | source)
XLA Modules:
  0.0 1019.4 jit_solution(9646753145286029156)
XLA Ops:
  7.3 17.6 %copy.218 = f32[256,16384]{0,1:T(8,128)} copy(f32[256,16384]{1,0:T(8,128)} %param.10) | data formatting | bytes 33554432 | tf_op args[2]
  24.8 12.4 %fusion.123 = (f32[256,32,128]{0,2,1:T(8,128)}, f32[256,32,128]{0,2,1:T(8,128)}, f32[256,32,128]{0,2,1:T(8,128)}, f32[256,32,128]{0,2,1:T(8,128)}) fusion(f32[256,32,512]{0,2,1:T(8,128)} %bitcast.254), kind=kLoop, calls=%fused_computation.170 | loop fusion | bytes 33554432 | tf_op jit(solution)/shard_map/slice | solution.py:51
  37.2 5.8 copy.283
  43.0 7.0 multiply_convert_fusion.5
  52.7 6.3 all-to-all-start.4
  59.0 5.6 copy.284
  64.6 6.9 multiply_convert_fusion.3
  74.3 67.1 %all-to-all-done.4 = bf16[256,32,128]{2,1,0:T(8,128)(2,1)S(1)} async-done(((bf16[256,32,128]{2,1,0:T(8,128)(2,1)}), bf16[256,32,128]{2,1,0:T(8,128)(2,1)S(1)}, u32[]{:S(2)}, u32[]{:S(2)}) %all-to-all-start.4) | async-done | bytes 2097184 | tf_op jit(solution)/shard_map/all_to_all | solution.py:52
  142.7 3.8 all-to-all-start.8
  146.5 5.7 copy.285
  152.2 6.9 multiply_convert_fusion.1
  161.8 33.7 %all-to-all-done.8 = bf16[256,32,128]{2,1,0:T(8,128)(2,1)S(1)} async-done(((bf16[256,32,128]{2,1,0:T(8,128)(2,1)}), bf16[256,32,128]{2,1,0:T(8,128)(2,1)S(1)}, u32[]{:S(2)}, u32[]{:S(2)}) %all-to-all-start.8) | async-done | bytes 2097184 | tf_op jit(solution)/shard_map/all_to_all | solution.py:52
  200.4 5.6 copy.282
  206.1 6.9 multiply_convert_fusion.7
  215.7 33.7 %all-to-all-done.12 = bf16[256,32,128]{2,1,0:T(8,128)(2,1)S(1)} async-done(((bf16[256,32,128]{2,1,0:T(8,128)(2,1)}), bf16[256,32,128]{2,1,0:T(8,128)(2,1)S(1)}, u32[]{:S(2)}, u32[]{:S(2)}) %all-to-all-start.12) | async-done | bytes 2097184 | tf_op jit(solution)/shard_map/all_to_all | solution.py:52
  259.4 4.6 copy.238
  264.0 39.4 %all-to-all-done = bf16[256,32,128]{2,1,0:T(8,128)(2,1)S(1)} async-done(((bf16[256,32,128]{2,1,0:T(8,128)(2,1)}), bf16[256,32,128]{2,1,0:T(8,128)(2,1)S(1)}, u32[]{:S(2)}, u32[]{:S(2)}) %all-to-all-start) | async-done | bytes 2097184 | tf_op jit(solution)/shard_map/all_to_all | solution.py:52
  304.6 4.0 all-to-all-start.5
  313.7 4.6 copy.252
  318.2 39.4 %all-to-all-done.5 = bf16[32,256,128]{2,0,1:T(8,128)(2,1)S(1)} async-done(((bf16[32,256,128]{2,0,1:T(8,128)(2,1)}), bf16[32,256,128]{2,0,1:T(8,128)(2,1)S(1)}, u32[]{:S(2)}, u32[]{:S(2)}) %all-to-all-start.5) | async-done | bytes 2097184 | tf_op jit(solution)/shard_map/all_to_all | solution.py:55
  357.6 4.4 all-to-all-start.9
  367.0 4.6 copy.266
  371.6 39.4 %all-to-all-done.9 = bf16[32,256,128]{2,0,1:T(8,128)(2,1)} async-done(((bf16[32,256,128]{2,0,1:T(8,128)(2,1)}), bf16[32,256,128]{2,0,1:T(8,128)(2,1)}, u32[]{:S(2)}, u32[]{:S(2)}) %all-to-all-start.9) | async-done | bytes 2097184 | tf_op jit(solution)/shard_map/all_to_all | solution.py:55
  411.1 4.4 all-to-all-start.13
  421.2 4.6 copy.224
  425.8 64.0 %all-to-all-done.13 = bf16[32,256,128]{2,0,1:T(8,128)(2,1)} async-done(((bf16[32,256,128]{2,0,1:T(8,128)(2,1)}), bf16[32,256,128]{2,0,1:T(8,128)(2,1)}, u32[]{:S(2)}, u32[]{:S(2)}) %all-to-all-start.13) | async-done | bytes 2097184 | tf_op jit(solution)/shard_map/all_to_all | solution.py:55
  489.8 4.6 all-to-all-start.1
  495.9 10.7 %copy.287 = bf16[32,8,32,512]{3,2,1,0:T(8,128)(2,1)} copy(bf16[32,8,32,512]{3,1,2,0:T(8,128)(2,1)} %bitcast.253) | data formatting | bytes 16777216
  521.7 51.7 %all-to-all-done.1 = bf16[32,256,128]{2,0,1:T(8,128)(2,1)} async-done(((bf16[32,256,128]{2,0,1:T(8,128)(2,1)}), bf16[32,256,128]{2,0,1:T(8,128)(2,1)}, u32[]{:S(2)}, u32[]{:S(2)}) %all-to-all-start.1) | async-done | bytes 2097184 | tf_op jit(solution)/shard_map/all_to_all | solution.py:55
  580.7 11.7 %fusion.76 = (bf16[256,32,128]{2,1,0:T(8,128)(2,1)S(1)}, bf16[256,32,128]{2,1,0:T(8,128)(2,1)}, bf16[256,32,128]{2,1,0:T(8,128)(2,1)}, bf16[256,32,128]{2,1,0:T(8,128)(2,1)}) fusion(f32[8,32,32,128]{3,2,1,0:T(8,128)S(1)} %copy.226, bf16[256,32,512]{2,1,0:T(8,128)(2,1)S(1)} %bitcast.258, f32[256]{0:T(256)S(1)} %dynamic_slice.7, f32[256]{0:T(256)S(1)} %dynamic_slice.6, ...), kind=kLoop, calls=%fused_computation.117 | loop fusion | flops 37748736 | bytes 33556480 | tf_op jit(solution)/shard_map/convert_element_type | solution.py:60
  601.9 21.6 %all-to-all-done.2 = bf16[256,32,128]{2,0,1:T(8,128)(2,1)S(1)} async-done(((bf16[256,32,128]{2,0,1:T(8,128)(2,1)}), bf16[256,32,128]{2,0,1:T(8,128)(2,1)S(1)}, u32[]{:S(2)}, u32[]{:S(2)}) %all-to-all-start.2) | async-done | bytes 2097184 | tf_op jit(solution)/shard_map/all_to_all | solution.py:61
  623.5 4.5 all-to-all-start.6
  631.7 20.8 %all-to-all-done.6 = bf16[256,32,128]{2,0,1:T(8,128)(2,1)} async-done(((bf16[256,32,128]{2,0,1:T(8,128)(2,1)}), bf16[256,32,128]{2,0,1:T(8,128)(2,1)}, u32[]{:S(2)}, u32[]{:S(2)}) %all-to-all-start.6) | async-done | bytes 2097184 | tf_op jit(solution)/shard_map/all_to_all | solution.py:61
  652.5 4.4 all-to-all-start.10
  660.7 20.6 %all-to-all-done.10 = bf16[256,32,128]{2,0,1:T(8,128)(2,1)} async-done(((bf16[256,32,128]{2,0,1:T(8,128)(2,1)}), bf16[256,32,128]{2,0,1:T(8,128)(2,1)}, u32[]{:S(2)}, u32[]{:S(2)}) %all-to-all-start.10) | async-done | bytes 2097184 | tf_op jit(solution)/shard_map/all_to_all | solution.py:61
  681.3 4.7 all-to-all-start.14
  689.3 5.2 copy.229
  694.5 5.2 copy.288
  699.7 4.8 convert_bitcast_fusion.2
  704.5 5.2 copy.243
  709.7 5.1 copy.289
  714.9 4.8 convert_bitcast_fusion.1
  719.7 5.2 copy.257
  724.9 5.2 copy.290
  730.0 4.8 convert_bitcast_fusion
  734.9 5.7 copy.271
  740.6 5.2 copy.291
  755.6 24.2 %fusion.7.clone.2 = bf16[6144,1024]{0,1:T(8,128)(2,1)} fusion(bf16[1024,6144]{0,1:T(8,128)(2,1)} %all-gather.3.cloned.1.call-done, f32[1024,1024]{0,1:T(8,128)} %bitcast.290, f32[1024]{0:T(1024)S(1)} %rsqrt_bitcast_fusion.3), kind=kOutput, calls=%fused_computation.11.clone.clone.clone | convolution fusion | flops 12943622144 | bytes 29364224 | tf_op jit(solution)/shard_map/ch,cl->hl/dot_general | solution.py:18
  779.8 19.9 %fusion.75 = bf16[1024,1024]{0,1:T(8,128)(2,1)S(1)} fusion(f32[1024,1024]{0,1:T(8,128)} %bitcast.291, bf16[6144,1024]{1,0:T(8,128)(2,1)} %all-gather.5.cloned.1.call-done, bf16[6144,1024]{0,1:T(8,128)(2,1)} %fusion.7.clone.2), kind=kOutput, calls=%fused_computation.104 | convolution fusion | flops 12886999040 | bytes 31457280 | tf_op jit(solution)/shard_map/hc,hl->cl/dot_general | solution.py:65
  802.6 4.9 all-to-all-start.3
  807.5 23.9 %fusion.15.clone.2 = bf16[6144,1024]{0,1:T(8,128)(2,1)} fusion(bf16[1024,6144]{0,1:T(8,128)(2,1)} %all-gather.3.cloned.1.call-done, f32[1024,1024]{0,1:T(8,128)} %bitcast.288, f32[1024]{0:T(1024)S(1)} %rsqrt_bitcast_fusion.2), kind=kOutput, calls=%fused_computation.19.clone.clone.clone | convolution fusion | flops 12943622144 | bytes 29364224 | tf_op jit(solution)/shard_map/ch,cl->hl/dot_general | solution.py:18
  831.5 23.9 %fusion.23.clone.2 = bf16[6144,1024]{0,1:T(8,128)(2,1)} fusion(bf16[1024,6144]{0,1:T(8,128)(2,1)} %all-gather.3.cloned.1.call-done, f32[1024,1024]{0,1:T(8,128)} %bitcast.286, f32[1024]{0:T(1024)S(1)} %rsqrt_bitcast_fusion.1), kind=kOutput, calls=%fused_computation.27.clone.clone.clone | convolution fusion | flops 12943622144 | bytes 29364224 | tf_op jit(solution)/shard_map/ch,cl->hl/dot_general | solution.py:18
  855.4 24.1 %fusion.31.clone.4 = bf16[6144,1024]{0,1:T(8,128)(2,1)} fusion(bf16[1024,6144]{0,1:T(8,128)(2,1)} %all-gather.3.cloned.1.call-done, f32[1024,1024]{0,1:T(8,128)} %bitcast.284, f32[1024]{0:T(1024)S(1)} %copy-done.11), kind=kOutput, calls=%fused_computation.35.clone.clone.clone.1 | convolution fusion | flops 12943622144 | bytes 29364224 | tf_op jit(solution)/shard_map/ch,cl->hl/dot_general | solution.py:18
  879.6 19.9 %fusion.74 = bf16[1024,1024]{0,1:T(8,128)(2,1)S(1)} fusion(f32[1024,1024]{0,1:T(8,128)} %bitcast.289, bf16[6144,1024]{1,0:T(8,128)(2,1)} %all-gather.5.cloned.1.call-done, bf16[6144,1024]{0,1:T(8,128)(2,1)} %fusion.15.clone.2), kind=kOutput, calls=%fused_computation.102 | convolution fusion | flops 12886999040 | bytes 31457280 | tf_op jit(solution)/shard_map/hc,hl->cl/dot_general | solution.py:65
  902.4 4.4 all-to-all-start.7
  906.8 20.8 %fusion.73 = bf16[1024,1024]{0,1:T(8,128)(2,1)} fusion(f32[1024,1024]{0,1:T(8,128)} %bitcast.287, bf16[6144,1024]{1,0:T(8,128)(2,1)} %all-gather.5.cloned.1.call-done, bf16[6144,1024]{0,1:T(8,128)(2,1)} %fusion.23.clone.2), kind=kOutput, calls=%fused_computation.100 | convolution fusion | flops 12886999040 | bytes 31457280 | tf_op jit(solution)/shard_map/hc,hl->cl/dot_general | solution.py:65
  927.6 4.2 copy.258
  931.8 4.5 all-to-all-start.11
  936.3 20.8 %fusion.72 = bf16[1024,1024]{0,1:T(8,128)(2,1)} fusion(f32[1024,1024]{0,1:T(8,128)} %bitcast.285, bf16[6144,1024]{1,0:T(8,128)(2,1)} %all-gather.5.cloned.1.call-done, bf16[6144,1024]{0,1:T(8,128)(2,1)} %fusion.31.clone.4), kind=kOutput, calls=%fused_computation.98 | convolution fusion | flops 12886999040 | bytes 31457280 | tf_op jit(solution)/shard_map/hc,hl->cl/dot_general | solution.py:65
  957.1 4.1 copy.272
  961.3 4.7 all-to-all-start.15
  974.4 15.3 %all-to-all-done.15 = bf16[1024,8,128]{2,1,0:T(8,128)(2,1)} async-done(((bf16[1024,8,128]{2,1,0:T(8,128)(2,1)}), bf16[1024,8,128]{2,1,0:T(8,128)(2,1)}, u32[]{:S(2)}, u32[]{:S(2)}) %all-to-all-start.15) | async-done | bytes 2097184 | tf_op jit(solution)/shard_map/all_to_all | solution.py:67
  992.6 4.0 pad_maximum_fusion
  996.6 15.5 %copy.292 = bf16[32,8,32,512]{3,1,2,0:T(8,128)(2,1)} copy(bf16[32,8,32,512]{3,2,1,0:T(8,128)(2,1)} %bitcast.255) | data formatting | bytes 16777216
  (96 shorter events, 115.8 us)
Async XLA Ops:
  6.5 749.1 %all-gather.3.cloned.1.call-start = ((), (), s32[]{:S(2)}) async-start(), calls=%async_computation.16 | async-start | bytes 12976128 | tf_op jit(solution)/shard_map/all_gather | solution.py:37
  37.2 5.8 copy-start.9
  52.7 88.7 %all-to-all-start.4 = ((bf16[256,32,128]{2,1,0:T(8,128)(2,1)}), bf16[256,32,128]{2,1,0:T(8,128)(2,1)S(1)}, u32[]{:S(2)}, u32[]{:S(2)}) async-start(bf16[256,32,128]{2,1,0:T(8,128)(2,1)} %copy.234), calls=%async_computation.4 | async-start | bytes 4194304 | tf_op jit(solution)/shard_map/all_to_all | solution.py:52
  141.3 1.4 copy-start.5
  142.7 52.8 %all-to-all-start.8 = ((bf16[256,32,128]{2,1,0:T(8,128)(2,1)}), bf16[256,32,128]{2,1,0:T(8,128)(2,1)S(1)}, u32[]{:S(2)}, u32[]{:S(2)}) async-start(bf16[256,32,128]{2,1,0:T(8,128)(2,1)} %copy.248), calls=%async_computation.8 | async-start | bytes 4194304 | tf_op jit(solution)/shard_map/all_to_all | solution.py:52
  195.5 1.3 copy-start.4
  196.8 52.6 %all-to-all-start.12 = ((bf16[256,32,128]{2,1,0:T(8,128)(2,1)}), bf16[256,32,128]{2,1,0:T(8,128)(2,1)S(1)}, u32[]{:S(2)}, u32[]{:S(2)}) async-start(bf16[256,32,128]{2,1,0:T(8,128)(2,1)} %copy.262), calls=%async_computation.12 | async-start | bytes 4194304 | tf_op jit(solution)/shard_map/all_to_all | solution.py:52
  213.0 41.4 %copy-start.10 = (f32[256,256]{1,0:T(8,128)S(1)}, f32[256,256]{1,0:T(8,128)}, u32[]{:S(2)}) copy-start(f32[256,256]{1,0:T(8,128)} %param.11) | copy-start | bytes 786436
  249.4 1.3 copy-start.3
  250.7 52.6 %all-to-all-start = ((bf16[256,32,128]{2,1,0:T(8,128)(2,1)}), bf16[256,32,128]{2,1,0:T(8,128)(2,1)S(1)}, u32[]{:S(2)}, u32[]{:S(2)}) async-start(bf16[256,32,128]{2,1,0:T(8,128)(2,1)} %copy.220), calls=%async_computation | async-start | bytes 4194304 | tf_op jit(solution)/shard_map/all_to_all | solution.py:52
  303.3 1.3 copy-start.2
  304.6 53.0 %all-to-all-start.5 = ((bf16[32,256,128]{2,0,1:T(8,128)(2,1)}), bf16[32,256,128]{2,0,1:T(8,128)(2,1)S(1)}, u32[]{:S(2)}, u32[]{:S(2)}) async-start(bf16[32,256,128]{2,0,1:T(8,128)(2,1)} %copy.238), calls=%async_computation.5 | async-start | bytes 4194304 | tf_op jit(solution)/shard_map/all_to_all | solution.py:55
  357.6 53.4 %all-to-all-start.9 = ((bf16[32,256,128]{2,0,1:T(8,128)(2,1)}), bf16[32,256,128]{2,0,1:T(8,128)(2,1)}, u32[]{:S(2)}, u32[]{:S(2)}) async-start(bf16[32,256,128]{2,0,1:T(8,128)(2,1)} %copy.252), calls=%async_computation.9 | async-start | bytes 4194304 | tf_op jit(solution)/shard_map/all_to_all | solution.py:55
  411.1 78.7 %all-to-all-start.13 = ((bf16[32,256,128]{2,0,1:T(8,128)(2,1)}), bf16[32,256,128]{2,0,1:T(8,128)(2,1)}, u32[]{:S(2)}, u32[]{:S(2)}) async-start(bf16[32,256,128]{2,0,1:T(8,128)(2,1)} %copy.266), calls=%async_computation.13 | async-start | bytes 4194304 | tf_op jit(solution)/shard_map/all_to_all | solution.py:55
  415.4 364.4 %all-gather.5.cloned.1.call-start = ((), (), s32[]{:S(2)}) async-start(), calls=%async_computation.17 | async-start | bytes 12976128 | tf_op jit(solution)/shard_map/all_gather | solution.py:38
  489.8 83.6 %all-to-all-start.1 = ((bf16[32,256,128]{2,0,1:T(8,128)(2,1)}), bf16[32,256,128]{2,0,1:T(8,128)(2,1)}, u32[]{:S(2)}, u32[]{:S(2)}) async-start(bf16[32,256,128]{2,0,1:T(8,128)(2,1)} %copy.224), calls=%async_computation.1 | async-start | bytes 4194304 | tf_op jit(solution)/shard_map/all_to_all | solution.py:55
  573.4 3.6 slice-start
  576.0 2.3 slice-start.1
  576.5 2.9 copy-start
  576.5 4.1 copy-start.1
  594.5 29.0 %all-to-all-start.2 = ((bf16[256,32,128]{2,0,1:T(8,128)(2,1)}), bf16[256,32,128]{2,0,1:T(8,128)(2,1)S(1)}, u32[]{:S(2)}, u32[]{:S(2)}) async-start(bf16[256,32,128]{2,0,1:T(8,128)(2,1)} %copy.227), calls=%async_computation.2 | async-start | bytes 4194304 | tf_op jit(solution)/shard_map/all_to_all | solution.py:61
  623.5 29.0 %all-to-all-start.6 = ((bf16[256,32,128]{2,0,1:T(8,128)(2,1)}), bf16[256,32,128]{2,0,1:T(8,128)(2,1)}, u32[]{:S(2)}, u32[]{:S(2)}) async-start(bf16[256,32,128]{2,0,1:T(8,128)(2,1)} %copy.241), calls=%async_computation.6 | async-start | bytes 4194304 | tf_op jit(solution)/shard_map/all_to_all | solution.py:61
  652.5 28.8 %all-to-all-start.10 = ((bf16[256,32,128]{2,0,1:T(8,128)(2,1)}), bf16[256,32,128]{2,0,1:T(8,128)(2,1)}, u32[]{:S(2)}, u32[]{:S(2)}) async-start(bf16[256,32,128]{2,0,1:T(8,128)(2,1)} %copy.255), calls=%async_computation.10 | async-start | bytes 4194304 | tf_op jit(solution)/shard_map/all_to_all | solution.py:61
  681.3 48.7 %all-to-all-start.14 = ((bf16[256,32,128]{2,0,1:T(8,128)(2,1)}), bf16[256,32,128]{2,0,1:T(8,128)(2,1)}, u32[]{:S(2)}, u32[]{:S(2)}) async-start(bf16[256,32,128]{2,0,1:T(8,128)(2,1)} %copy.269), calls=%async_computation.14 | async-start | bytes 4194304 | tf_op jit(solution)/shard_map/all_to_all | solution.py:61
  802.6 99.8 %all-to-all-start.3 = ((bf16[1024,8,128]{2,1,0:T(8,128)(2,1)}), bf16[1024,8,128]{2,1,0:T(8,128)(2,1)}, u32[]{:S(2)}, u32[]{:S(2)}) async-start(bf16[1024,8,128]{2,1,0:T(8,128)(2,1)} %copy.230), calls=%async_computation.3 | async-start | bytes 4194304 | tf_op jit(solution)/shard_map/all_to_all | solution.py:67
  831.5 24.0 %copy-start.11 = (f32[1024]{0:T(1024)S(1)}, f32[1024]{0:T(1024)}, u32[]{:S(2)}) copy-start(f32[1024]{0:T(1024)} %rsqrt_bitcast_fusion) | copy-start | bytes 12292
  902.4 29.4 %all-to-all-start.7 = ((bf16[1024,8,128]{2,1,0:T(8,128)(2,1)}), bf16[1024,8,128]{2,1,0:T(8,128)(2,1)S(1)}, u32[]{:S(2)}, u32[]{:S(2)}) async-start(bf16[1024,8,128]{2,1,0:T(8,128)(2,1)} %copy.244), calls=%async_computation.7 | async-start | bytes 4194304 | tf_op jit(solution)/shard_map/all_to_all | solution.py:67
  931.8 29.5 %all-to-all-start.11 = ((bf16[1024,8,128]{2,1,0:T(8,128)(2,1)}), bf16[1024,8,128]{2,1,0:T(8,128)(2,1)}, u32[]{:S(2)}, u32[]{:S(2)}) async-start(bf16[1024,8,128]{2,1,0:T(8,128)(2,1)} %copy.258), calls=%async_computation.11 | async-start | bytes 4194304 | tf_op jit(solution)/shard_map/all_to_all | solution.py:67
  961.3 28.5 %all-to-all-start.15 = ((bf16[1024,8,128]{2,1,0:T(8,128)(2,1)}), bf16[1024,8,128]{2,1,0:T(8,128)(2,1)}, u32[]{:S(2)}, u32[]{:S(2)}) async-start(bf16[1024,8,128]{2,1,0:T(8,128)(2,1)} %copy.272), calls=%async_computation.15 | async-start | bytes 4194304 | tf_op jit(solution)/shard_map/all_to_all | solution.py:67
  971.0 20.9 %copy-start.6 = (bf16[256,4,8,128]{3,2,1,0:T(8,128)(2,1)S(1)}, bf16[256,4,8,128]{3,2,1,0:T(8,128)(2,1)}, u32[]{:S(2)}) copy-start(bf16[256,4,8,128]{3,2,1,0:T(8,128)(2,1)} %copy.332) | copy-start | bytes 6291460
  989.8 2.2 copy-start.7
  989.8 2.9 copy-start.8
Sparse Core Ops, SparseCore 0:
  10.2 134.1 all-gather.2
  419.2 148.7 all-gather.4

commit v2 on v0

v2 whole, which is shorter than its diff:
```python
import functools

import jax
import jax.numpy as jnp
from jax import lax
from jax.experimental import pallas as pl
from jax.experimental.pallas import tpu as pltpu
from jax.sharding import PartitionSpec as P

B = 512
J = 128
epsilon = 1e-06
f32 = jnp.float32
bf16 = jnp.bfloat16
ANY = pl.BlockSpec(memory_space=pl.ANY)


def params(mib):
    return pltpu.CompilerParams(vmem_limit_bytes=mib * 2**20)


def first_pass(k, activations, first_factor, spectral, ns, dep):
    c, tokens = activations.shape
    blocks = tokens // B
    step = min(4, blocks)
    per = B // J
    deps = [] if dep is None else [dep]

    def kernel(act, factor, *rest):
        specs, out = rest[:step], rest[-1]
        for q in range(step):
            product = jnp.dot(act[:, q * B : (q + 1) * B], factor[...], preferred_element_type=f32)
            value = (product * specs[q][...]).astype(bf16)
            out[:, q] = value.reshape(ns, c // ns, J)

    def spec_at(q):
        return pl.BlockSpec((c, J), lambda i: (0, (i * step + q) * per + k))

    return pl.pallas_call(
        kernel,
        grid=(blocks // step,),
        in_specs=[
            pl.BlockSpec((c, step * B), lambda i: (0, i)),
            pl.BlockSpec((B, J), lambda i: (0, k)),
        ]
        + [spec_at(q) for q in range(step)]
        + [ANY] * len(deps),
        out_specs=pl.BlockSpec((ns, step, c // ns, J), lambda i: (0, i, 0, 0)),
        out_shape=jax.ShapeDtypeStruct((ns, blocks, c // ns, J), bf16),
        compiler_params=params(32),
        cost_estimate=pl.CostEstimate(
            flops=4 * c * blocks * B * J,
            bytes_accessed=2 * c * tokens + 6 * c * blocks * J,
            transcendentals=0,
        ),
    )(activations, first_factor, *[spectral] * step, *deps)


def second_pass(gathered, second_factor, deps):
    a, c, _ = gathered.shape
    cb = min(16, c)

    def kernel(x_ref, s_ref, *rest):
        out, x_wide, y_wide = rest[-3:]
        x_wide[...] = x_ref[...].astype(f32).reshape(a * cb, J)
        factor = s_ref[...]
        high = factor.astype(bf16)
        low = (factor - high.astype(f32)).astype(bf16)
        for i in range(0, cb, 2):
            x = jnp.concatenate(
                [x_wide[pl.ds(i + n, a, stride=cb), :] for n in range(2)], axis=1
            ).astype(bf16)
            y = jnp.dot(high, x, preferred_element_type=f32)
            y += jnp.dot(low, x, preferred_element_type=f32)
            for n in range(2):
                y_wide[pl.ds(i + n, a, stride=cb), :] = y[:, n * J : (n + 1) * J]
        out[...] = y_wide[...].reshape(a, cb, J).astype(bf16)

    return pl.pallas_call(
        kernel,
        grid=(c // cb,),
        in_specs=[
            pl.BlockSpec((a, cb, J), lambda i: (0, i, 0)),
            pl.BlockSpec((a, a), lambda i: (0, 0)),
        ]
        + [ANY] * len(deps),
        out_specs=pl.BlockSpec((a, cb, J), lambda i: (0, i, 0)),
        out_shape=jax.ShapeDtypeStruct((a, c, J), bf16),
        scratch_shapes=[pltpu.VMEM((a * cb, J), f32), pltpu.VMEM((a * cb, J), f32)],
        compiler_params=params(32),
        cost_estimate=pl.CostEstimate(
            flops=8 * a * a * c * J, bytes_accessed=4 * a * c * J, transcendentals=0
        ),
    )(gathered, second_factor, *deps)


def gate(k, me, activations, returned, scale, shift, nt, deps):
    c, tokens = activations.shape
    ns, blocks, ci, _ = returned.shape
    mine = blocks // nt
    step = min(2, mine)
    steps = mine // step

    def kernel(me_ref, *rest):
        acts, rets = rest[:nt], rest[nt : 2 * nt]
        scale_ref, shift_ref = rest[2 * nt : 2 * nt + 2]
        outs = rest[-nt:]
        for s in range(nt):
            for q in range(step):
                x = acts[s][:, q * B + k * J : q * B + (k + 1) * J].astype(f32)
                mixed = rets[s][:, q].reshape(c, J).astype(f32)
                gating = jax.nn.sigmoid(x * scale_ref[...] + shift_ref[...])
                outs[s][:, q * J : (q + 1) * J] = (x + gating * mixed).astype(bf16)

    def act_at(s):
        return pl.BlockSpec((c, step * B), lambda i, me: (0, (me[0] ^ s) * steps + i))

    def ret_at(s):
        return pl.BlockSpec(
            (ns, step, ci, J), lambda i, me: (0, (me[0] ^ s) * steps + i, 0, 0)
        )

    column = pl.BlockSpec((c, 1), lambda i, me: (0, 0))
    return pl.pallas_call(
        kernel,
        grid_spec=pltpu.PrefetchScalarGridSpec(
            num_scalar_prefetch=1,
            grid=(steps,),
            in_specs=[act_at(s) for s in range(nt)]
            + [ret_at(s) for s in range(nt)]
            + [column, column]
            + [ANY] * len(deps),
            out_specs=[pl.BlockSpec((c, step * J), lambda i, me: (0, i))] * nt,
        ),
        out_shape=[jax.ShapeDtypeStruct((c, mine * J), bf16)] * nt,
        compiler_params=params(32),
        cost_estimate=pl.CostEstimate(
            flops=8 * c * blocks * J,
            bytes_accessed=2 * c * tokens + 4 * c * blocks * J,
            transcendentals=c * blocks * J,
        ),
    )(me, *[activations] * nt, *[returned] * nt, scale, shift, *deps)


def mlp(me, slots, weight_in, weight_out, deps):
    nt = len(slots)
    c, tokens = slots[0].shape
    hidden, full = weight_in.shape
    hb = hidden // 8
    tile = min(256, tokens)

    def kernel(me_ref, *rest):
        xs, (w1, w2) = rest[:nt], rest[nt : nt + 2]
        outs = rest[-nt - 2 : -2]
        normed, total = rest[-2:]
        step = pl.program_id(0)

        @pl.when(step == 0)
        def _():
            squares = jnp.zeros((1, tokens), f32)
            for s in range(nt):
                x = xs[s][...].astype(f32)
                squares += jnp.sum(x * x, axis=0, keepdims=True)
            scale = lax.rsqrt(squares / full + epsilon)
            for s in range(nt):
                at = pl.multiple_of((me_ref[0] ^ s) * c, c)
                normed[pl.ds(at, c), :] = (xs[s][...].astype(f32) * scale).astype(bf16)
            total[...] = jnp.zeros_like(total)

        for t in range(0, tokens, tile):
            x = jnp.dot(w1[...], normed[:, t : t + tile], preferred_element_type=f32)
            h = jax.nn.gelu(x).astype(bf16)
            total[:, t : t + tile] += jnp.dot(w2[...], h, preferred_element_type=f32)

        @pl.when(step == pl.num_programs(0) - 1)
        def _():
            for s in range(nt):
                at = pl.multiple_of((me_ref[0] ^ s) * c, c)
                outs[s][...] = (xs[s][...].astype(f32) + total[pl.ds(at, c), :]).astype(bf16)

    whole = pl.BlockSpec((c, tokens), lambda i, me: (0, 0))
    return pl.pallas_call(
        kernel,
        grid_spec=pltpu.PrefetchScalarGridSpec(
            num_scalar_prefetch=1,
            grid=(hidden // hb,),
            in_specs=[whole] * nt
            + [
                pl.BlockSpec((hb, full), lambda i, me: (i, 0)),
                pl.BlockSpec((full, hb), lambda i, me: (0, i)),
            ]
            + [ANY] * len(deps),
            out_specs=[whole] * nt,
            scratch_shapes=[pltpu.VMEM((full, tokens), bf16), pltpu.VMEM((full, tokens), f32)],
        ),
        out_shape=[jax.ShapeDtypeStruct((c, tokens), bf16)] * nt,
        compiler_params=params(40),
        cost_estimate=pl.CostEstimate(
            flops=4 * full * hidden * tokens,
            bytes_accessed=4 * full * hidden + 4 * full * tokens,
            transcendentals=hidden * tokens,
        ),
    )(me, *slots, weight_in, weight_out, *deps)


def place(k, me, slots, result, shape):
    nt = len(slots)
    c, tokens = slots[0].shape
    mine = tokens // J
    given = [] if result is None else [result]

    def kernel(me_ref, *rest):
        ys, out, sems = rest[:nt], rest[-2], rest[-1]
        copies = []
        for s in range(nt):
            for q in range(mine):
                at = pl.multiple_of(((me_ref[0] ^ s) * mine + q) * B + k * J, J)
                copies.append(
                    pltpu.make_async_copy(
                        ys[s].at[:, q * J : (q + 1) * J],
                        out.at[:, pl.ds(at, J)],
                        sems.at[s * mine + q],
                    )
                )
        for copy in copies:
            copy.start()
        for copy in copies:
            copy.wait()

    return pl.pallas_call(
        kernel,
        in_specs=[pl.BlockSpec(memory_space=pltpu.SMEM)] + [ANY] * (nt + len(given)),
        out_specs=ANY,
        out_shape=jax.ShapeDtypeStruct(shape, bf16),
        scratch_shapes=[pltpu.SemaphoreType.DMA((nt * mine,))],
        input_output_aliases={1 + nt: 0} if given else {},
        cost_estimate=pl.CostEstimate(
            flops=0, bytes_accessed=4 * c * tokens * nt, transcendentals=0
        ),
    )(me, *slots, *given)


def swap(slots):
    n = len(slots)
    return [slots[0]] + [
        lax.ppermute(slots[s], "tensor", [(i, i ^ s) for i in range(n)]) for s in range(1, n)
    ]


def on_device(
    ns,
    nt,
    activations,
    first_factor,
    spectral,
    second_factor,
    gate_scale,
    gate_shift,
    expand_weight,
    reduce_weight,
):
    c = activations.shape[0]
    full = expand_weight.shape[0]
    at = lax.axis_index("tensor")
    me = at.astype(jnp.int32).reshape(1)
    scale = lax.dynamic_slice_in_dim(gate_scale, at * c, c)[:, None]
    shift = lax.dynamic_slice_in_dim(gate_shift, at * c, c)[:, None]
    weight_in = lax.all_gather(expand_weight.T, ("seq", "tensor"), axis=0, tiled=True)
    weight_out = lax.all_gather(reduce_weight, ("seq", "tensor"), axis=0, tiled=True).T

    exchange = functools.partial(
        lax.all_to_all, axis_name="seq", split_axis=0, concat_axis=0, tiled=True
    )
    chunks = B // J
    front, back, done = {}, {}, {}
    mixed, ins, outs = {}, {}, {}
    result = None

    def do_front(k, dep=None):
        front[k] = exchange(first_pass(k, activations, first_factor, spectral, ns, dep))

    def do_second(k, deps=()):
        blocks = front[k].shape[1]
        x = front[k].reshape(ns * blocks, c // ns, J)
        mixed[k] = second_pass(x, second_factor, list(deps)).reshape(ns, blocks, c // ns, J)
        back[k] = exchange(mixed[k])

    def do_gate(k, deps=()):
        ins[k] = swap(gate(k, me, activations, back[k], scale, shift, nt, list(deps)))

    def do_mlp(k, deps=()):
        outs[k] = mlp(me, ins[k], weight_in, weight_out, list(deps))
        done[k] = swap(outs[k])

    do_front(0)
    do_front(1)
    do_second(0)
    do_front(2, front[1])
    do_second(1)
    do_front(3, back[0])
    do_gate(0)
    do_second(2)
    do_mlp(0)
    do_gate(1)
    do_second(3, [outs[0][0]])
    do_mlp(1)
    do_gate(2, [outs[0][0]])
    do_mlp(2)
    do_gate(3, [outs[1][0]])
    do_mlp(3)
    for k in range(chunks):
        result = place(k, me, done[k], result, activations.shape)
    return result


def solution(mesh):
    return jax.shard_map(
        functools.partial(on_device, mesh.shape["seq"], mesh.shape["tensor"]),
        mesh=mesh,
        in_specs=(
            P("tensor", "seq"),
            P(),
            P("tensor", "seq"),
            P(),
            P(),
            P(),
            P(None, ("seq", "tensor")),
            P(("seq", "tensor"), None),
        ),
        out_specs=P("tensor", "seq"),
        check_vma=False,
    )
```

time: 1390 us -> 1000 us (0.72)
  Pallas kernels: 0 us -> 482 us
  blocking collectives: 467 us -> 0 us
  matrix products: 221 us -> 0 us
  waiting for transfers between devices: 530 us -> 362 us
  starting transfers between devices: 11.4 us -> 64.7 us
  local copies, waits for them, and re-layouts: 119 us -> 67.6 us
  other arithmetic: 24.4 us -> 0 us
    pallas_call x0 -> x20, Pallas kernels: none -> 482 us  [the longest x4 260 us: place(): pl.pallas_call(kernel, in_specs=[pl.BlockSpec(memory_space=pltpu.SMEM)] +...]
    all_to_all x2 -> x0, blocking collectives: 467 us -> none  [the longest x1 371 us: on_device(): lax.all_to_all(spectrum, 'seq', split_axis=0, concat_axis=1, tiled=True)]
    dot_general x4 -> x0, matrix products: 221 us -> none  [the longest x1 86.7 us: expand(): jnp.einsum('ch,cl->hl', shard_rows, normed, preferred_element_type=jnp.fl...]
    all_to_all x2 -> x8, waiting for transfers between devices: 529 us -> 340 us  [the longest x4 208 us: do_front(): exchange(first_pass(k, activations, first_factor, spectral, ns, dep))]
    all_to_all x4 -> x0, local copies, waits for them, and re-layouts: 37 us -> none  [the longest x1 15.2 us: on_device(): lax.all_to_all(mixed_part, 'seq', split_axis=1, concat_axis=0, tiled=True)]
    ppermute x0 -> x24, starting transfers between devices: none -> 28.1 us  [swap(): lax.ppermute(slots[s], 'tensor', [(i, i ^ s) for i in range(n)])]
    all_to_all x2 -> x8, starting transfers between devices: 11.4 us -> 36.6 us  [the longest x4 18.8 us: do_front(): exchange(first_pass(k, activations, first_factor, spectral, ns, dep))]
    unnamed x8 -> x88, local copies, waits for them, and re-layouts: 27.8 us -> 49.1 us
  transfers between devices with their start and end apart: 4 -> 34, of which waited for: 2 -> 10; matrix products, arithmetic and copies ran while one was open for 11% -> 2% of each run, Pallas kernels for 0% -> 42%
where the time goes in v2:
time: 1000 us; the launch traced here: 991 us
  Pallas kernels  482 us (48%)
  waiting for transfers between devices  362 us (36%)
  local copies, waits for them, and re-layouts  67.6 us (7%)
  starting transfers between devices  64.7 us (6%)
  between operations  14.1 us (1%)
    pallas_call x4, Pallas kernels, place(): pl.pallas_call(kernel, in_specs=[pl.BlockSpec(memory_space=pltpu.SMEM)] +...  260 us
    all_to_all x4, waiting for transfers between devices, do_front(): exchange(first_pass(k, activations, first_factor, spectral, ns, dep))  208 us
    pallas_call x4, Pallas kernels, mlp(): pl.pallas_call(kernel, grid_spec=pltpu.PrefetchScalarGridSpec(num_scalar_...  157 us
    all_to_all x4, waiting for transfers between devices, do_second(): back[k] = exchange(mixed[k])  132 us
    unnamed x88, local copies, waits for them, and re-layouts  49.1 us
    pallas_call x4, Pallas kernels, first_pass(): pl.pallas_call(kernel, grid=(blocks // step,), in_specs=[pl.BlockSpec((c,...  29.3 us
    ppermute x24, starting transfers between devices, swap(): lax.ppermute(slots[s], 'tensor', [(i, i ^ s) for i in range(n)])  28.1 us
    ppermute x24, waiting for transfers between devices, swap(): lax.ppermute(slots[s], 'tensor', [(i, i ^ s) for i in range(n)])  20.5 us
  transfers between devices with their start and end apart: 34, of which 10 were waited for; matrix products, arithmetic and copies ran while one was open for 2% of the time, Pallas kernels for 42%

profile of v2, /device:TPU:0, one launch (start us, length us, event | category | flops | bytes accessed | tf_op | source)
XLA Modules:
  0.0 991.1 jit_solution(5995233725356421592)
XLA Ops:
  8.0 3.4 copy-done
  12.4 7.8 shard_map.82
  20.3 6.5 all-to-all-start
  26.7 3.4 copy-done.1
  30.2 7.2 shard_map.88
  38.6 58.2 %all-to-all-done = bf16[8,32,32,128]{3,2,1,0:T(8,128)(2,1)S(1)} async-done(((bf16[8,32,32,128]{3,2,1,0:T(8,128)(2,1)}), bf16[8,32,32,128]{3,2,1,0:T(8,128)(2,1)S(1)}, u32[]{:S(2)}, u32[]{:S(2)}) %all-to-all-start) | async-done | bytes 2097184 | tf_op jit(solution)/shard_map/all_to_all | solution.py:280
  98.2 3.6 all-to-all-start.4
  101.8 1.6 copy-done.20
  103.4 3.7 shard_map.83
  108.5 69.7 %all-to-all-done.4.rest_4_ = bf16[8,32,32,128]{3,2,1,0:T(8,128)(2,1)S(1)} async-done(((bf16[8,32,32,128]{3,2,1,0:T(8,128)(2,1)}), bf16[8,32,32,128]{3,2,1,0:T(8,128)(2,1)S(1)}, u32[]{:S(2)}, u32[]{:S(2)}) %all-to-all-start.4) | async-done | bytes 2097184 | tf_op jit(solution)/shard_map/all_to_all | solution.py:280
  179.5 3.6 all-to-all-start.1
  183.1 1.7 copy-done.10
  184.8 3.8 shard_map.89
  189.9 67.0 %all-to-all-done.1.rest_4_.rest_5_.rest_6_.rest_7_ = bf16[8,32,32,128]{3,2,1,0:T(8,128)(2,1)S(1)} async-done(((bf16[8,32,32,128]{3,2,1,0:T(8,128)(2,1)}), bf16[8,32,32,128]{3,2,1,0:T(8,128)(2,1)S(1)}, u32[]{:S(2)}, u32[]{:S(2)}) %all-to-all-start.1) | async-done | bytes 2097184 | tf_op jit(solution)/shard_map/all_to_all | solution.py:286
  256.9 4.4 all-to-all-start.5
  261.3 3.4 copy-done.2
  264.7 1.6 copy-done.11
  266.3 7.2 shard_map.94
  274.8 65.4 %all-to-all-done.5.rest_4_.rest_5_.rest_6_.rest_7_ = bf16[8,32,32,128]{3,2,1,0:T(8,128)(2,1)} async-done(((bf16[8,32,32,128]{3,2,1,0:T(8,128)(2,1)}), bf16[8,32,32,128]{3,2,1,0:T(8,128)(2,1)}, u32[]{:S(2)}, u32[]{:S(2)}) %all-to-all-start.5) | async-done | bytes 2097184 | tf_op jit(solution)/shard_map/all_to_all | solution.py:286
  340.2 4.3 all-to-all-start.6
  344.6 3.4 copy-done.3
  347.9 7.1 shard_map.84
  356.4 37.2 %all-to-all-done.6 = bf16[8,32,32,128]{3,2,1,0:T(8,128)(2,1)} async-done(((bf16[8,32,32,128]{3,2,1,0:T(8,128)(2,1)}), bf16[8,32,32,128]{3,2,1,0:T(8,128)(2,1)}, u32[]{:S(2)}, u32[]{:S(2)}) %all-to-all-start.6) | async-done | bytes 2097184 | tf_op jit(solution)/shard_map/all_to_all | solution.py:280
  393.6 4.4 all-to-all-start.2
  398.0 4.8 shard_map.95
  404.2 42.8 %all-to-all-done.2 = bf16[8,32,32,128]{3,2,1,0:T(8,128)(2,1)} async-done(((bf16[8,32,32,128]{3,2,1,0:T(8,128)(2,1)}), bf16[8,32,32,128]{3,2,1,0:T(8,128)(2,1)}, u32[]{:S(2)}, u32[]{:S(2)}) %all-to-all-start.2) | async-done | bytes 2097184 | tf_op jit(solution)/shard_map/all_to_all | solution.py:280
  447.0 4.8 all-to-all-start.7
  453.7 3.4 copy-done.4
  457.1 4.4 shard_map.85
  462.3 1.5 collective-permute-start
  463.8 1.5 collective-permute-start.1
  465.8 16.8 %copy.24 = bf16[6144,1024]{0,1:T(8,128)(2,1)} copy(bf16[6144,1024]{1,0:T(8,128)(2,1)} %all-gather.5.cloned.1.call-done) | data formatting | bytes 25165824 | tf_op jit(solution)/shard_map/all_gather | solution.py:269
  482.6 5.4 collective-permute-done.1.rest_2_
  489.0 39.6 %shard_map.86 = (bf16[256,1024]{1,0:T(8,128)(2,1)S(1)}, bf16[256,1024]{1,0:T(8,128)(2,1)}, bf16[256,1024]{1,0:T(8,128)(2,1)}, bf16[256,1024]{1,0:T(8,128)(2,1)S(1)}) custom-call(s32[1]{0:T(128)} %bitcast.me_ref, bf16[256,1024]{1,0:T(8,128)(2,1)S(1)} %copy-done.34, bf16[256,1024]{1,0:T(8,128)(2,1)S(1)} %collective-permute-done.rest_1_, ...), custom_call_target="tpu_custom_call" | custom-call | flops 25769803776 | bytes 29360128 | tf_op jit(solution)/shard_map/pallas_call | solution.py:182
  528.6 5.0 shard_map.87
  534.9 5.0 all-to-all-start.3
  539.9 3.4 copy-done.5
  543.3 5.0 shard_map.90
  548.3 1.5 collective-permute-start.3
  550.4 1.5 collective-permute-start.5
  551.9 1.4 collective-permute-start.21
  553.9 5.6 shard_map.96
  560.3 2.8 collective-permute-done.3.rest_1_
  563.1 1.4 collective-permute-start.12
  564.5 11.3 %collective-permute-done.4.rest_2_ = bf16[256,1024]{1,0:T(8,128)(2,1)S(1)} collective-permute-done((bf16[256,1024]{1,0:T(8,128)(2,1)S(1)}, bf16[256,1024]{1,0:T(8,128)(2,1)S(1)}, u32[]{:S(2)}, u32[]{:S(2)}) %collective-permute-start.4) | collective-permute-done | bytes 524320 | tf_op jit(solution)/shard_map/ppermute | solution.py:246
  576.4 1.5 collective-permute-start.14
  577.9 38.8 %shard_map.91 = (bf16[256,1024]{1,0:T(8,128)(2,1)S(1)}, bf16[256,1024]{1,0:T(8,128)(2,1)S(1)}, bf16[256,1024]{1,0:T(8,128)(2,1)S(1)}, bf16[256,1024]{1,0:T(8,128)(2,1)S(1)}) custom-call(s32[1]{0:T(128)} %bitcast.me_ref, bf16[256,1024]{1,0:T(8,128)(2,1)S(1)} %get-tuple-element.42.rest_0_, bf16[256,1024]{1,0:T(8,128)(2,1)S(1)} %collective-permute-done.3.rest_1_, ...), custom_call_target="tpu_custom_call" | custom-call | flops 25769803776 | bytes 29360128 | tf_op jit(solution)/shard_map/pallas_call | solution.py:182
  619.0 3.6 copy-done.6
  622.6 3.9 shard_map.92
  626.5 1.5 collective-permute-start.6
  628.6 1.5 collective-permute-start.8
  630.1 39.3 %shard_map.97 = (bf16[256,1024]{1,0:T(8,128)(2,1)S(1)}, bf16[256,1024]{1,0:T(8,128)(2,1)S(1)}, bf16[256,1024]{1,0:T(8,128)(2,1)S(1)}, bf16[256,1024]{1,0:T(8,128)(2,1)S(1)}) custom-call(s32[1]{0:T(128)} %bitcast.me_ref, bf16[256,1024]{1,0:T(8,128)(2,1)S(1)} %copy-done.32, bf16[256,1024]{1,0:T(8,128)(2,1)} %collective-permute-done.12.rest_1_, ...), custom_call_target="tpu_custom_call" | custom-call | flops 25769803776 | bytes 29360128 | tf_op jit(solution)/shard_map/pallas_call | solution.py:182
  670.2 1.5 collective-permute-start.23
  671.7 1.5 collective-permute-start.18
  673.7 1.5 collective-permute-start.20
  675.2 1.5 collective-permute-start.15
  676.7 39.5 %shard_map.93 = (bf16[256,1024]{1,0:T(8,128)(2,1)S(1)}, bf16[256,1024]{1,0:T(8,128)(2,1)}, bf16[256,1024]{1,0:T(8,128)(2,1)S(1)}, bf16[256,1024]{1,0:T(8,128)(2,1)S(1)}) custom-call(s32[1]{0:T(128)} %bitcast.me_ref, bf16[256,1024]{1,0:T(8,128)(2,1)S(1)} %get-tuple-element.47.rest_0_, bf16[256,1024]{1,0:T(8,128)(2,1)S(1)} %collective-permute-done.6.rest_1_, ...), custom_call_target="tpu_custom_call" | custom-call | flops 25769803776 | bytes 29360128 | tf_op jit(solution)/shard_map/pallas_call | solution.py:182
  717.5 1.5 collective-permute-start.17
  719.0 1.5 collective-permute-start.9
  721.8 1.5 collective-permute-start.11
  723.3 64.9 %shard_map.98.rest_4_ = bf16[256,16384]{1,0:T(8,128)(2,1)} custom-call(s32[1]{0:T(128)} %bitcast.me_ref, bf16[256,1024]{1,0:T(8,128)(2,1)} %copy-done.16, bf16[256,1024]{1,0:T(8,128)(2,1)} %collective-permute-done.21.rest_1_, bf16[256,1024]{1,0:T(8,128)(2,1)} %collective-permute-done.22.rest_2_, bf16[256,1024]{1,0:T(8,128)(2,1)} %copy-done.43), custom_call_target="tpu_custom_call" | custom-call | bytes 4194304 | tf_op jit(solution)/shard_map/pallas_call | solution.py:230
  788.2 64.9 %shard_map.99.rest_4_ = bf16[256,16384]{1,0:T(8,128)(2,1)} custom-call(s32[1]{0:T(128)} %bitcast.me_ref, bf16[256,1024]{1,0:T(8,128)(2,1)} %copy-done.15, bf16[256,1024]{1,0:T(8,128)(2,1)} %copy-done.37, bf16[256,1024]{1,0:T(8,128)(2,1)} %copy-done.38, bf16[256,1024]{1,0:T(8,128)(2,1)} %copy-done.40, ...), custom_call_target="tpu_custom_call", output_to_operand_aliasing={{}: (5, {})} | custom-call | bytes 4194304 | tf_op jit(solution)/shard_map/pallas_call | solution.py:230
  853.2 64.9 %shard_map.100.rest_4_ = bf16[256,16384]{1,0:T(8,128)(2,1)} custom-call(s32[1]{0:T(128)} %bitcast.me_ref, bf16[256,1024]{1,0:T(8,128)(2,1)} %copy-done.23, bf16[256,1024]{1,0:T(8,128)(2,1)} %copy-done.39, bf16[256,1024]{1,0:T(8,128)(2,1)} %collective-permute-done.16.rest_2_, ...), custom_call_target="tpu_custom_call", output_to_operand_aliasing={{}: (5, {})} | custom-call | bytes 4194304 | tf_op jit(solution)/shard_map/pallas_call | solution.py:230
  919.1 64.9 %shard_map.101 = bf16[256,16384]{1,0:T(8,128)(2,1)} custom-call(s32[1]{0:T(128)} %bitcast.me_ref, bf16[256,1024]{1,0:T(8,128)(2,1)} %copy-done.24, bf16[256,1024]{1,0:T(8,128)(2,1)} %copy-done.41, bf16[256,1024]{1,0:T(8,128)(2,1)} %collective-permute-done.10.rest_2_, bf16[256,1024]{1,0:T(8,128)(2,1)} %copy-done.42, ...), custom_call_target="tpu_custom_call", output_to_operand_aliasing={{}: (5, {})} | custom-call | bytes 4194304 | tf_op jit(solution)/shard_map/pallas_call | solution.py:230
  (119 shorter events, 29.3 us)
Async XLA Ops:
  6.5 459.3 %all-gather.5.cloned.1.call-start = ((), (), s32[]{:S(2)}) async-start(), calls=%async_computation.9 | async-start | bytes 12976128 | tf_op jit(solution)/shard_map/all_gather | solution.py:269
  7.3 481.7 %all-gather.3.cloned.1.call-start = ((), (), s32[]{:S(2)}) async-start(), calls=%async_computation.8 | async-start | bytes 12976128 | tf_op jit(solution)/shard_map/all_gather | solution.py:268
  8.0 3.4 copy-start
  20.3 6.5 copy-start.8
  20.3 76.6 %all-to-all-start = ((bf16[8,32,32,128]{3,2,1,0:T(8,128)(2,1)}), bf16[8,32,32,128]{3,2,1,0:T(8,128)(2,1)S(1)}, u32[]{:S(2)}, u32[]{:S(2)}) async-start(bf16[8,32,32,128]{3,2,1,0:T(8,128)(2,1)} %shard_map.82), calls=%async_computation | async-start | bytes 4194304 | tf_op jit(solution)/shard_map/all_to_all | solution.py:280
  26.7 3.4 copy-start.1
  37.3 1.3 copy-start.12
  38.6 63.1 %copy-start.35 = (f32[256,256]{1,0:T(8,128)S(1)}, f32[256,256]{1,0:T(8,128)}, u32[]{:S(2)}) copy-start(f32[256,256]{1,0:T(8,128)} %s_ref.7) | copy-start | bytes 786436
  98.2 80.0 %all-to-all-start.4 = ((bf16[8,32,32,128]{3,2,1,0:T(8,128)(2,1)}), bf16[8,32,32,128]{3,2,1,0:T(8,128)(2,1)S(1)}, u32[]{:S(2)}, u32[]{:S(2)}) async-start(bf16[8,32,32,128]{3,2,1,0:T(8,128)(2,1)} %copy-done.12), calls=%async_computation.4 | async-start | bytes 4194304 | tf_op jit(solution)/shard_map/all_to_all | solution.py:280
  101.8 1.6 copy-start.20
  107.1 1.3 copy-start.21
  178.2 1.3 copy-start.9
  179.5 77.4 %all-to-all-start.1 = ((bf16[8,32,32,128]{3,2,1,0:T(8,128)(2,1)}), bf16[8,32,32,128]{3,2,1,0:T(8,128)(2,1)S(1)}, u32[]{:S(2)}, u32[]{:S(2)}) async-start(bf16[8,32,32,128]{3,2,1,0:T(8,128)(2,1)} %bitcast.17), calls=%async_computation.1 | async-start | bytes 4194304 | tf_op jit(solution)/shard_map/all_to_all | solution.py:286
  183.1 1.7 copy-start.10
  188.5 1.3 copy-start.22
  256.9 83.3 %all-to-all-start.5 = ((bf16[8,32,32,128]{3,2,1,0:T(8,128)(2,1)}), bf16[8,32,32,128]{3,2,1,0:T(8,128)(2,1)}, u32[]{:S(2)}, u32[]{:S(2)}) async-start(bf16[8,32,32,128]{3,2,1,0:T(8,128)(2,1)} %bitcast.18), calls=%async_computation.5 | async-start | bytes 4194304 | tf_op jit(solution)/shard_map/all_to_all | solution.py:286
  261.3 3.4 copy-start.2
  264.7 1.6 copy-start.11
  273.5 1.3 copy-start.13
  340.2 53.4 %all-to-all-start.6 = ((bf16[8,32,32,128]{3,2,1,0:T(8,128)(2,1)}), bf16[8,32,32,128]{3,2,1,0:T(8,128)(2,1)}, u32[]{:S(2)}, u32[]{:S(2)}) async-start(bf16[8,32,32,128]{3,2,1,0:T(8,128)(2,1)} %copy-done.13), calls=%async_computation.6 | async-start | bytes 4194304 | tf_op jit(solution)/shard_map/all_to_all | solution.py:280
  344.6 3.4 copy-start.3
  355.1 1.3 copy-start.14
  393.6 53.4 %all-to-all-start.2 = ((bf16[8,32,32,128]{3,2,1,0:T(8,128)(2,1)}), bf16[8,32,32,128]{3,2,1,0:T(8,128)(2,1)}, u32[]{:S(2)}, u32[]{:S(2)}) async-start(bf16[8,32,32,128]{3,2,1,0:T(8,128)(2,1)} %copy-done.14), calls=%async_computation.2 | async-start | bytes 4194304 | tf_op jit(solution)/shard_map/all_to_all | solution.py:280
  402.8 1.4 copy-start.17
  447.0 87.9 %all-to-all-start.7 = ((bf16[8,32,32,128]{3,2,1,0:T(8,128)(2,1)}), bf16[8,32,32,128]{3,2,1,0:T(8,128)(2,1)}, u32[]{:S(2)}, u32[]{:S(2)}) async-start(bf16[8,32,32,128]{3,2,1,0:T(8,128)(2,1)} %bitcast.14), calls=%async_computation.7 | async-start | bytes 4194304 | tf_op jit(solution)/shard_map/all_to_all | solution.py:286
  453.7 3.4 copy-start.4
  462.3 20.3 %collective-permute-start = (bf16[256,1024]{1,0:T(8,128)(2,1)}, bf16[256,1024]{1,0:T(8,128)(2,1)S(1)}, u32[]{:S(2)}, u32[]{:S(2)}) collective-permute-start(bf16[256,1024]{1,0:T(8,128)(2,1)} %get-tuple-element.38), channel_id=1, source_target_pairs={{0,1},{1,0},{2,3},{3,2},{4,5},{5,4},{6,7},{7,6},{8,9},{9,8},{10,11... | collective-permute-start | bytes 1572872 | tf_op jit(solution)/shard_map/ppermute | solution.py:246
  463.8 24.2 %collective-permute-start.1 = (bf16[256,1024]{1,0:T(8,128)(2,1)S(1)}, bf16[256,1024]{1,0:T(8,128)(2,1)S(1)}, u32[]{:S(2)}, u32[]{:S(2)}) collective-permute-start(bf16[256,1024]{1,0:T(8,128)(2,1)S(1)} %get-tuple-element.39), channel_id=1, source_target_pairs={{0,2},{1,3},{2,0},{3,1},{4,6},{5,7},{6,4},{7,5},{8,10},{9,11},{10,... | collective-permute-start | bytes 1572872 | tf_op jit(solution)/shard_map/ppermute | solution.py:246
  465.3 23.8 %copy-start.34 = (bf16[256,1024]{1,0:T(8,128)(2,1)S(1)}, bf16[256,1024]{1,0:T(8,128)(2,1)}, u32[]{:S(2)}) copy-start(bf16[256,1024]{1,0:T(8,128)(2,1)} %copy-done.33) | copy-start | bytes 1572868
  465.3 23.7 %collective-permute-start.2 = (bf16[256,1024]{1,0:T(8,128)(2,1)S(1)}, bf16[256,1024]{1,0:T(8,128)(2,1)S(1)}, u32[]{:S(2)}, u32[]{:S(2)}) collective-permute-start(bf16[256,1024]{1,0:T(8,128)(2,1)S(1)} %get-tuple-element.40), channel_id=1, source_target_pairs={{0,3},{1,2},{2,1},{3,0},{4,7},{5,6},{6,5},{7,4},{8,11},{9,10},{10,... | collective-permute-start | bytes 1572872 | tf_op jit(solution)/shard_map/ppermute | solution.py:246
  489.0 39.6 %copy-start.36 = (f32[256,256]{1,0:T(8,128)S(1)}, f32[256,256]{1,0:T(8,128)}, u32[]{:S(2)}) copy-start(f32[256,256]{1,0:T(8,128)} %s_ref.7) | copy-start | bytes 786436
  528.6 25.3 %copy-start.16 = (bf16[256,1024]{1,0:T(8,128)(2,1)}, bf16[256,1024]{1,0:T(8,128)(2,1)S(1)}, u32[]{:S(2)}) copy-start(bf16[256,1024]{1,0:T(8,128)(2,1)S(1)} %get-tuple-element.41.rest_0_.rest_10_) | copy-start | bytes 1572868
  534.9 84.1 %all-to-all-start.3 = ((bf16[8,32,32,128]{3,2,1,0:T(8,128)(2,1)}), bf16[8,32,32,128]{3,2,1,0:T(8,128)(2,1)S(1)}, u32[]{:S(2)}, u32[]{:S(2)}) async-start(bf16[8,32,32,128]{3,2,1,0:T(8,128)(2,1)} %bitcast.15), calls=%async_computation.3 | async-start | bytes 4194304 | tf_op jit(solution)/shard_map/all_to_all | solution.py:286
  539.9 3.4 copy-start.5
  548.3 14.8 %collective-permute-start.3 = (bf16[256,1024]{1,0:T(8,128)(2,1)S(1)}, bf16[256,1024]{1,0:T(8,128)(2,1)S(1)}, u32[]{:S(2)}, u32[]{:S(2)}) collective-permute-start(bf16[256,1024]{1,0:T(8,128)(2,1)S(1)} %get-tuple-element.43), channel_id=1, source_target_pairs={{0,1},{1,0},{2,3},{3,2},{4,5},{5,4},{6,7},{7,6},{8,9},{9,8},{10,11... | collective-permute-start | bytes 1572872 | tf_op jit(solution)/shard_map/ppermute | solution.py:246
  549.8 26.0 %collective-permute-start.4 = (bf16[256,1024]{1,0:T(8,128)(2,1)S(1)}, bf16[256,1024]{1,0:T(8,128)(2,1)S(1)}, u32[]{:S(2)}, u32[]{:S(2)}) collective-permute-start(bf16[256,1024]{1,0:T(8,128)(2,1)S(1)} %get-tuple-element.44), channel_id=1, source_target_pairs={{0,2},{1,3},{2,0},{3,1},{4,6},{5,7},{6,4},{7,5},{8,10},{9,11},{10,... | collective-permute-start | bytes 1572872 | tf_op jit(solution)/shard_map/ppermute | solution.py:246
  550.4 26.0 %collective-permute-start.5 = (bf16[256,1024]{1,0:T(8,128)(2,1)S(1)}, bf16[256,1024]{1,0:T(8,128)(2,1)S(1)}, u32[]{:S(2)}, u32[]{:S(2)}) collective-permute-start(bf16[256,1024]{1,0:T(8,128)(2,1)S(1)} %get-tuple-element.45), channel_id=1, source_target_pairs={{0,3},{1,2},{2,1},{3,0},{4,7},{5,6},{6,5},{7,4},{8,11},{9,10},{10,... | collective-permute-start | bytes 1572872 | tf_op jit(solution)/shard_map/ppermute | solution.py:246
  551.9 118.4 %collective-permute-start.21 = (bf16[256,1024]{1,0:T(8,128)(2,1)}, bf16[256,1024]{1,0:T(8,128)(2,1)}, u32[]{:S(2)}, u32[]{:S(2)}) collective-permute-start(bf16[256,1024]{1,0:T(8,128)(2,1)} %get-tuple-element.66), channel_id=1, source_target_pairs={{0,1},{1,0},{2,3},{3,2},{4,5},{5,4},{6,7},{7,6},{8,9},{9,8},{10,11... | collective-permute-start | bytes 1572872 | tf_op jit(solution)/shard_map/ppermute | solution.py:246
  553.3 118.4 %collective-permute-start.22 = (bf16[256,1024]{1,0:T(8,128)(2,1)}, bf16[256,1024]{1,0:T(8,128)(2,1)}, u32[]{:S(2)}, u32[]{:S(2)}) collective-permute-start(bf16[256,1024]{1,0:T(8,128)(2,1)} %get-tuple-element.67), channel_id=1, source_target_pairs={{0,2},{1,3},{2,0},{3,1},{4,6},{5,7},{6,4},{7,5},{8,10},{9,11},{10,... | collective-permute-start | bytes 1572872 | tf_op jit(solution)/shard_map/ppermute | solution.py:246
  563.1 63.4 %collective-permute-start.12 = (bf16[256,1024]{1,0:T(8,128)(2,1)}, bf16[256,1024]{1,0:T(8,128)(2,1)}, u32[]{:S(2)}, u32[]{:S(2)}) collective-permute-start(bf16[256,1024]{1,0:T(8,128)(2,1)} %get-tuple-element.56), channel_id=1, source_target_pairs={{0,1},{1,0},{2,3},{3,2},{4,5},{5,4},{6,7},{7,6},{8,9},{9,8},{10,11... | collective-permute-start | bytes 1572872 | tf_op jit(solution)/shard_map/ppermute | solution.py:246
  575.8 52.2 %collective-permute-start.13 = (bf16[256,1024]{1,0:T(8,128)(2,1)}, bf16[256,1024]{1,0:T(8,128)(2,1)}, u32[]{:S(2)}, u32[]{:S(2)}) collective-permute-start(bf16[256,1024]{1,0:T(8,128)(2,1)} %get-tuple-element.57), channel_id=1, source_target_pairs={{0,2},{1,3},{2,0},{3,1},{4,6},{5,7},{6,4},{7,5},{8,10},{9,11},{10,... | collective-permute-start | bytes 1572872 | tf_op jit(solution)/shard_map/ppermute | solution.py:246
  576.4 52.2 %collective-permute-start.14 = (bf16[256,1024]{1,0:T(8,128)(2,1)}, bf16[256,1024]{1,0:T(8,128)(2,1)}, u32[]{:S(2)}, u32[]{:S(2)}) collective-permute-start(bf16[256,1024]{1,0:T(8,128)(2,1)} %get-tuple-element.58), channel_id=1, source_target_pairs={{0,3},{1,2},{2,1},{3,0},{4,7},{5,6},{6,5},{7,4},{8,11},{9,10},{10,... | collective-permute-start | bytes 1572872 | tf_op jit(solution)/shard_map/ppermute | solution.py:246
  619.0 7.5 copy-start.15
  619.0 3.6 copy-start.6
  622.6 7.5 copy-start.32
  626.5 46.7 %collective-permute-start.6 = (bf16[256,1024]{1,0:T(8,128)(2,1)S(1)}, bf16[256,1024]{1,0:T(8,128)(2,1)S(1)}, u32[]{:S(2)}, u32[]{:S(2)}) collective-permute-start(bf16[256,1024]{1,0:T(8,128)(2,1)S(1)} %get-tuple-element.48), channel_id=1, source_target_pairs={{0,1},{1,0},{2,3},{3,2},{4,5},{5,4},{6,7},{7,6},{8,9},{9,8},{10,11... | collective-permute-start | bytes 1572872 | tf_op jit(solution)/shard_map/ppermute | solution.py:246
  628.0 45.8 %collective-permute-start.7 = (bf16[256,1024]{1,0:T(8,128)(2,1)S(1)}, bf16[256,1024]{1,0:T(8,128)(2,1)S(1)}, u32[]{:S(2)}, u32[]{:S(2)}) collective-permute-start(bf16[256,1024]{1,0:T(8,128)(2,1)S(1)} %get-tuple-element.49), channel_id=1, source_target_pairs={{0,2},{1,3},{2,0},{3,1},{4,6},{5,7},{6,4},{7,5},{8,10},{9,11},{10,... | collective-permute-start | bytes 1572872 | tf_op jit(solution)/shard_map/ppermute | solution.py:246
  628.6 46.6 %collective-permute-start.8 = (bf16[256,1024]{1,0:T(8,128)(2,1)S(1)}, bf16[256,1024]{1,0:T(8,128)(2,1)S(1)}, u32[]{:S(2)}, u32[]{:S(2)}) collective-permute-start(bf16[256,1024]{1,0:T(8,128)(2,1)S(1)} %get-tuple-element.50), channel_id=1, source_target_pairs={{0,3},{1,2},{2,1},{3,0},{4,7},{5,6},{6,5},{7,4},{8,11},{9,10},{10,... | collective-permute-start | bytes 1572872 | tf_op jit(solution)/shard_map/ppermute | solution.py:246
  630.1 41.6 %copy-start.30 = (bf16[256,1024]{1,0:T(8,128)(2,1)S(1)}, bf16[256,1024]{1,0:T(8,128)(2,1)}, u32[]{:S(2)}) copy-start(bf16[256,1024]{1,0:T(8,128)(2,1)} %copy-done.29) | copy-start | bytes 1572868
  630.1 43.1 %copy-start.28 = (bf16[256,1024]{1,0:T(8,128)(2,1)S(1)}, bf16[256,1024]{1,0:T(8,128)(2,1)}, u32[]{:S(2)}) copy-start(bf16[256,1024]{1,0:T(8,128)(2,1)} %copy-done.27) | copy-start | bytes 1572868
  630.1 43.7 %copy-start.26 = (bf16[256,1024]{1,0:T(8,128)(2,1)S(1)}, bf16[256,1024]{1,0:T(8,128)(2,1)}, u32[]{:S(2)}) copy-start(bf16[256,1024]{1,0:T(8,128)(2,1)} %copy-done.25) | copy-start | bytes 1572868
  670.2 46.8 %collective-permute-start.23 = (bf16[256,1024]{1,0:T(8,128)(2,1)S(1)}, bf16[256,1024]{1,0:T(8,128)(2,1)S(1)}, u32[]{:S(2)}, u32[]{:S(2)}) collective-permute-start(bf16[256,1024]{1,0:T(8,128)(2,1)S(1)} %get-tuple-element.68), channel_id=1, source_target_pairs={{0,3},{1,2},{2,1},{3,0},{4,7},{5,6},{6,5},{7,4},{8,11},{9,10},{10,... | collective-permute-start | bytes 1572872 | tf_op jit(solution)/shard_map/ppermute | solution.py:246
  671.7 45.8 %collective-permute-start.18 = (bf16[256,1024]{1,0:T(8,128)(2,1)S(1)}, bf16[256,1024]{1,0:T(8,128)(2,1)S(1)}, u32[]{:S(2)}, u32[]{:S(2)}) collective-permute-start(bf16[256,1024]{1,0:T(8,128)(2,1)S(1)} %copy-done.30), channel_id=1, source_target_pairs={{0,1},{1,0},{2,3},{3,2},{4,5},{5,4},{6,7},{7,6},{8,9},{9,8},{10,11... | collective-permute-start | bytes 1572872 | tf_op jit(solution)/shard_map/ppermute | solution.py:246
  673.2 45.8 %collective-permute-start.19 = (bf16[256,1024]{1,0:T(8,128)(2,1)S(1)}, bf16[256,1024]{1,0:T(8,128)(2,1)S(1)}, u32[]{:S(2)}, u32[]{:S(2)}) collective-permute-start(bf16[256,1024]{1,0:T(8,128)(2,1)S(1)} %copy-done.28), channel_id=1, source_target_pairs={{0,2},{1,3},{2,0},{3,1},{4,6},{5,7},{6,4},{7,5},{8,10},{9,11},{10,... | collective-permute-start | bytes 1572872 | tf_op jit(solution)/shard_map/ppermute | solution.py:246
  673.7 46.7 %collective-permute-start.20 = (bf16[256,1024]{1,0:T(8,128)(2,1)S(1)}, bf16[256,1024]{1,0:T(8,128)(2,1)S(1)}, u32[]{:S(2)}, u32[]{:S(2)}) collective-permute-start(bf16[256,1024]{1,0:T(8,128)(2,1)S(1)} %copy-done.26), channel_id=1, source_target_pairs={{0,3},{1,2},{2,1},{3,0},{4,7},{5,6},{6,5},{7,4},{8,11},{9,10},{10,... | collective-permute-start | bytes 1572872 | tf_op jit(solution)/shard_map/ppermute | solution.py:246
  675.2 45.8 %collective-permute-start.15 = (bf16[256,1024]{1,0:T(8,128)(2,1)S(1)}, bf16[256,1024]{1,0:T(8,128)(2,1)S(1)}, u32[]{:S(2)}, u32[]{:S(2)}) collective-permute-start(bf16[256,1024]{1,0:T(8,128)(2,1)S(1)} %get-tuple-element.60), channel_id=1, source_target_pairs={{0,1},{1,0},{2,3},{3,2},{4,5},{5,4},{6,7},{7,6},{8,9},{9,8},{10,11... | collective-permute-start | bytes 1572872 | tf_op jit(solution)/shard_map/ppermute | solution.py:246
  717.0 4.1 copy-start.43
  717.0 136.2 %collective-permute-start.16 = (bf16[256,1024]{1,0:T(8,128)(2,1)S(1)}, bf16[256,1024]{1,0:T(8,128)(2,1)}, u32[]{:S(2)}, u32[]{:S(2)}) collective-permute-start(bf16[256,1024]{1,0:T(8,128)(2,1)S(1)} %get-tuple-element.61), channel_id=1, source_target_pairs={{0,2},{1,3},{2,0},{3,1},{4,6},{5,7},{6,4},{7,5},{8,10},{9,11},{10,... | collective-permute-start | bytes 1572872 | tf_op jit(solution)/shard_map/ppermute | solution.py:246
  717.5 3.5 copy-start.37
  717.5 135.6 %collective-permute-start.17 = (bf16[256,1024]{1,0:T(8,128)(2,1)S(1)}, bf16[256,1024]{1,0:T(8,128)(2,1)}, u32[]{:S(2)}, u32[]{:S(2)}) collective-permute-start(bf16[256,1024]{1,0:T(8,128)(2,1)S(1)} %get-tuple-element.62), channel_id=1, source_target_pairs={{0,3},{1,2},{2,1},{3,0},{4,7},{5,6},{6,5},{7,4},{8,11},{9,10},{10,... | collective-permute-start | bytes 1572872 | tf_op jit(solution)/shard_map/ppermute | solution.py:246
  719.0 2.0 copy-start.38
  719.0 199.1 %collective-permute-start.9 = (bf16[256,1024]{1,0:T(8,128)(2,1)}, bf16[256,1024]{1,0:T(8,128)(2,1)S(1)}, u32[]{:S(2)}, u32[]{:S(2)}) collective-permute-start(bf16[256,1024]{1,0:T(8,128)(2,1)} %get-tuple-element.52), channel_id=1, source_target_pairs={{0,1},{1,0},{2,3},{3,2},{4,5},{5,4},{6,7},{7,6},{8,9},{9,8},{10,11... | collective-permute-start | bytes 1572872 | tf_op jit(solution)/shard_map/ppermute | solution.py:246
  720.5 197.6 %collective-permute-start.10 = (bf16[256,1024]{1,0:T(8,128)(2,1)S(1)}, bf16[256,1024]{1,0:T(8,128)(2,1)}, u32[]{:S(2)}, u32[]{:S(2)}) collective-permute-start(bf16[256,1024]{1,0:T(8,128)(2,1)S(1)} %get-tuple-element.53), channel_id=1, source_target_pairs={{0,2},{1,3},{2,0},{3,1},{4,6},{5,7},{6,4},{7,5},{8,10},{9,11},{10,... | collective-permute-start | bytes 1572872 | tf_op jit(solution)/shard_map/ppermute | solution.py:246
  721.8 196.3 %collective-permute-start.11 = (bf16[256,1024]{1,0:T(8,128)(2,1)S(1)}, bf16[256,1024]{1,0:T(8,128)(2,1)S(1)}, u32[]{:S(2)}, u32[]{:S(2)}) collective-permute-start(bf16[256,1024]{1,0:T(8,128)(2,1)S(1)} %get-tuple-element.54), channel_id=1, source_target_pairs={{0,3},{1,2},{2,1},{3,0},{4,7},{5,6},{6,5},{7,4},{8,11},{9,10},{10,... | collective-permute-start | bytes 1572872 | tf_op jit(solution)/shard_map/ppermute | solution.py:246
  (14 other events, 12.6 us)
Sparse Core Ops, SparseCore 0:
  10.2 161.2 all-gather.4
  174.4 160.2 all-gather.2

commit v3 on v2

--- a/solution.py
+++ b/solution.py
@@ -142,21 +142,32 @@
     )(me, *[activations] * nt, *[returned] * nt, scale, shift, *deps)
 
 
-def mlp(me, slots, weight_in, weight_out, deps):
+def mlp(me, slots, pieces_in, pieces_out, deps):
     nt = len(slots)
     c, tokens = slots[0].shape
-    hidden, full = weight_in.shape
-    hb = hidden // 8
+    hb, full = pieces_in[0].shape
+    n = len(pieces_in)
     tile = min(256, tokens)
 
     def kernel(me_ref, *rest):
-        xs, (w1, w2) = rest[:nt], rest[nt : nt + 2]
-        outs = rest[-nt - 2 : -2]
-        normed, total = rest[-2:]
+        xs, w1s, w2s = rest[:nt], rest[nt : nt + n], rest[nt + n : nt + 2 * n]
+        outs = rest[-nt - 5 : -5]
+        normed, total, w1, w2, sems = rest[-5:]
         step = pl.program_id(0)
+
+        def fetch(piece, slot):
+            return (
+                pltpu.make_async_copy(w1s[piece], w1.at[slot], sems.at[0, slot]),
+                pltpu.make_async_copy(w2s[piece], w2.at[slot], sems.at[1, slot]),
+            )
+
+        def start(piece):
+            for copy in fetch(piece, piece % 2):
+                copy.start()
 
         @pl.when(step == 0)
         def _():
+            start(0)
             squares = jnp.zeros((1, tokens), f32)
             for s in range(nt):
                 x = xs[s][...].astype(f32)
@@ -167,12 +178,18 @@
                 normed[pl.ds(at, c), :] = (xs[s][...].astype(f32) * scale).astype(bf16)
             total[...] = jnp.zeros_like(total)
 
+        for piece in range(1, n):
+            pl.when(step == piece - 1)(functools.partial(start, piece))
+        slot = lax.rem(step, 2)
+        for copy in fetch(0, slot):
+            copy.wait()
+
         for t in range(0, tokens, tile):
-            x = jnp.dot(w1[...], normed[:, t : t + tile], preferred_element_type=f32)
+            x = jnp.dot(w1[slot], normed[:, t : t + tile], preferred_element_type=f32)
             h = jax.nn.gelu(x).astype(bf16)
-            total[:, t : t + tile] += jnp.dot(w2[...], h, preferred_element_type=f32)
-
-        @pl.when(step == pl.num_programs(0) - 1)
+            total[:, t : t + tile] += jnp.dot(w2[slot], h, preferred_element_type=f32)
+
+        @pl.when(step == n - 1)
         def _():
             for s in range(nt):
                 at = pl.multiple_of((me_ref[0] ^ s) * c, c)
@@ -183,24 +200,25 @@
         kernel,
         grid_spec=pltpu.PrefetchScalarGridSpec(
             num_scalar_prefetch=1,
-            grid=(hidden // hb,),
-            in_specs=[whole] * nt
-            + [
-                pl.BlockSpec((hb, full), lambda i, me: (i, 0)),
-                pl.BlockSpec((full, hb), lambda i, me: (0, i)),
-            ]
-            + [ANY] * len(deps),
+            grid=(n,),
+            in_specs=[whole] * nt + [ANY] * (2 * n + len(deps)),
             out_specs=[whole] * nt,
-            scratch_shapes=[pltpu.VMEM((full, tokens), bf16), pltpu.VMEM((full, tokens), f32)],
+            scratch_shapes=[
+                pltpu.VMEM((full, tokens), bf16),
+                pltpu.VMEM((full, tokens), f32),
+                pltpu.VMEM((2, hb, full), bf16),
+                pltpu.VMEM((2, full, hb), bf16),
+                pltpu.SemaphoreType.DMA((2, 2)),
+            ],
         ),
         out_shape=[jax.ShapeDtypeStruct((c, tokens), bf16)] * nt,
         compiler_params=params(40),
         cost_estimate=pl.CostEstimate(
-            flops=4 * full * hidden * tokens,
-            bytes_accessed=4 * full * hidden + 4 * full * tokens,
-            transcendentals=hidden * tokens,
-        ),
-    )(me, *slots, weight_in, weight_out, *deps)
+            flops=4 * full * hb * n * tokens,
+            bytes_accessed=4 * full * hb * n + 4 * full * tokens,
+            transcendentals=hb * n * tokens,
+        ),
+    )(me, *slots, *pieces_in, *pieces_out, *deps)
 
 
 def place(k, me, slots, result, shape):
@@ -229,10 +247,13 @@
 
     return pl.pallas_call(
         kernel,
-        in_specs=[pl.BlockSpec(memory_space=pltpu.SMEM)] + [ANY] * (nt + len(given)),
+        in_specs=[pl.BlockSpec(memory_space=pltpu.SMEM)]
+        + [pl.BlockSpec(memory_space=pltpu.VMEM)] * nt
+        + [ANY] * len(given),
         out_specs=ANY,
         out_shape=jax.ShapeDtypeStruct(shape, bf16),
         scratch_shapes=[pltpu.SemaphoreType.DMA((nt * mine,))],
+        compiler_params=params(16),
         input_output_aliases={1 + nt: 0} if given else {},
         cost_estimate=pl.CostEstimate(
             flops=0, bytes_accessed=4 * c * tokens * nt, transcendentals=0
@@ -245,6 +266,39 @@
     return [slots[0]] + [
         lax.ppermute(slots[s], "tensor", [(i, i ^ s) for i in range(n)]) for s in range(1, n)
     ]
+
+
+def after(x, *deps):
+    return pl.pallas_call(
+        lambda *refs: None,
+        in_specs=[ANY] * (1 + len(deps)),
+        out_specs=ANY,
+        out_shape=jax.ShapeDtypeStruct(x.shape, x.dtype),
+        input_output_aliases={0: 0},
+    )(x, *deps)
+
+
+def gather_weights(ns, nt, expand_weight, reduce_weight):
+    def flip(x, axis, bit):
+        n = ns if axis == "seq" else nt
+        return lax.ppermute(x, axis, [(i, i ^ bit) for i in range(n)])
+
+    rows, full = reduce_weight.shape
+    both = jnp.stack([expand_weight.T, reduce_weight])[None]
+    bit = 2
+    while bit < ns:
+        both = jnp.concatenate([both, flip(both, "seq", bit)])
+        bit *= 2
+    bits = [1 << i for i in range(nt.bit_length() - 1)]
+    column = [both[:, 0].reshape(-1, full), both[:, 1].reshape(-1, full).T]
+    found = []
+    for start, order in zip(column, (bits, bits[::-1])):
+        pieces = {0: start}
+        for bit in order:
+            pieces |= {s ^ bit: flip(x, "tensor", bit) for s, x in pieces.items()}
+        found.append([pieces[s] for s in range(nt)])
+    other = [[flip(x, "seq", 1) for x in pieces] for pieces in found]
+    return both, found[0], found[1], found[0] + other[0], found[1] + other[1]
 
 
 def on_device(
@@ -260,56 +314,58 @@
     reduce_weight,
 ):
     c = activations.shape[0]
-    full = expand_weight.shape[0]
     at = lax.axis_index("tensor")
     me = at.astype(jnp.int32).reshape(1)
     scale = lax.dynamic_slice_in_dim(gate_scale, at * c, c)[:, None]
     shift = lax.dynamic_slice_in_dim(gate_shift, at * c, c)[:, None]
-    weight_in = lax.all_gather(expand_weight.T, ("seq", "tensor"), axis=0, tiled=True)
-    weight_out = lax.all_gather(reduce_weight, ("seq", "tensor"), axis=0, tiled=True).T
-
-    exchange = functools.partial(
-        lax.all_to_all, axis_name="seq", split_axis=0, concat_axis=0, tiled=True
+    both, near_in, near_out, pieces_in, pieces_out = gather_weights(
+        ns, nt, expand_weight, reduce_weight
     )
-    chunks = B // J
-    front, back, done = {}, {}, {}
-    mixed, ins, outs = {}, {}, {}
+
+    def exchange(x):
+        return lax.all_to_all(x, "seq", split_axis=0, concat_axis=0, tiled=True)
+
+    def first(k, dep=None):
+        return first_pass(k, activations, first_factor, spectral, ns, dep)
+
+    def second(front, deps=()):
+        blocks = front.shape[1]
+        x = front.reshape(ns * blocks, c // ns, J)
+        return second_pass(x, second_factor, list(deps)).reshape(ns, blocks, c // ns, J)
+
+    def gated(k, back, deps=()):
+        return gate(k, me, activations, back, scale, shift, nt, list(deps))
+
+    def layer(slots, deps=()):
+        return mlp(me, slots, pieces_in, pieces_out, list(deps))
+
+    front0 = exchange(first(0))
+    front1 = exchange(first(1))
+    back0 = exchange(second(front0))
+    front2 = exchange(first(2, both))
+    back1 = exchange(second(front1))
+    sent3 = first(3, front1)
+    in0 = swap(gated(0, back0, near_in + near_out))
+    mixed2 = second(front2)
+    out0 = layer(in0, [front2])
+    front3 = exchange(after(sent3, out0[0], mixed2))
+    in1 = swap(gated(1, back1, [out0[0]]))
+    back2 = exchange(mixed2)
+    mixed3 = second(front3)
+    out1 = layer(in1, [front3])
+    back3 = exchange(after(mixed3, out1[0]))
+    done0 = swap(out0)
+    in2 = swap(gated(2, back2, [out1[0]]))
+    done1 = swap(out1)
+    gate3 = gated(3, back3)
+    in3 = swap(gate3)
+    out2 = layer(in2, [gate3[0]])
+    done2 = swap(out2)
+    out3 = layer(in3)
+    done3 = swap(out3)
     result = None
-
-    def do_front(k, dep=None):
-        front[k] = exchange(first_pass(k, activations, first_factor, spectral, ns, dep))
-
-    def do_second(k, deps=()):
-        blocks = front[k].shape[1]
-        x = front[k].reshape(ns * blocks, c // ns, J)
-        mixed[k] = second_pass(x, second_factor, list(deps)).reshape(ns, blocks, c // ns, J)
-        back[k] = exchange(mixed[k])
-
-    def do_gate(k, deps=()):
-        ins[k] = swap(gate(k, me, activations, back[k], scale, shift, nt, list(deps)))
-
-    def do_mlp(k, deps=()):
-        outs[k] = mlp(me, ins[k], weight_in, weight_out, list(deps))
-        done[k] = swap(outs[k])
-
-    do_front(0)
-    do_front(1)
-    do_second(0)
-    do_front(2, front[1])
-    do_second(1)
-    do_front(3, back[0])
-    do_gate(0)
-    do_second(2)
-    do_mlp(0)
-    do_gate(1)
-    do_second(3, [outs[0][0]])
-    do_mlp(1)
-    do_gate(2, [outs[0][0]])
-    do_mlp(2)
-    do_gate(3, [outs[1][0]])
-    do_mlp(3)
-    for k in range(chunks):
-        result = place(k, me, done[k], result, activations.shape)
+    for k, done in enumerate((done0, done1, done2, done3)):
+        result = place(k, me, done, result, activations.shape)
     return result
 
 

time: 1000 us -> 775 us (0.78)
  Pallas kernels: 482 us -> 229 us
  blocking collectives: 0 us -> 53.9 us
  local copies, waits for them, and re-layouts: 67.6 us -> 51.4 us
  between operations: 14.1 us -> 0.91 us
  starting transfers between devices: 64.7 us -> 75.9 us
    pallas_call x4, Pallas kernels: 260 us -> 6.28 us  [place(): pl.pallas_call(kernel, in_specs=[pl.BlockSpec(memory_space=pltpu.SMEM)] +...]
    all_to_all x8 -> x7, waiting for transfers between devices: 340 us -> 110 us  [exchange(): return lax.all_to_all(x, 'seq', split_axis=0, concat_axis=0, tiled=True)]
    ppermute x0 -> x16, waiting for transfers between devices: none -> 186 us  [flip(): return lax.ppermute(x, axis, [(i, i ^ bit) for i in range(n)])]
    all_to_all x0 -> x1, blocking collectives: none -> 53.9 us  [exchange(): return lax.all_to_all(x, 'seq', split_axis=0, concat_axis=0, tiled=True)]
    ppermute x24, waiting for transfers between devices: 20.5 us -> 60.7 us  [swap(): lax.ppermute(slots[s], 'tensor', [(i, i ^ s) for i in range(n)])]
    all_gather x1 -> x0, local copies, waits for them, and re-layouts: 16.8 us -> none  [on_device(): lax.all_gather(reduce_weight, ('seq', 'tensor'), axis=0, tiled=True)]
    ppermute x0 -> x16, starting transfers between devices: none -> 14.1 us  [flip(): return lax.ppermute(x, axis, [(i, i ^ bit) for i in range(n)])]
    unnamed x88 -> x110, local copies, waits for them, and re-layouts: 49.1 us -> 44.9 us
  transfers between devices with their start and end apart: 34 -> 47, of which waited for: 10 -> 14; matrix products, arithmetic and copies ran while one was open for 2% -> 1% of each run, Pallas kernels for 42% -> 29%
where the time goes in v3:
time: 775 us; the launch traced here: 767 us
  waiting for transfers between devices  356 us (46%)
  Pallas kernels  229 us (30%)
  starting transfers between devices  75.9 us (10%)
  blocking collectives  53.9 us (7%)
  local copies, waits for them, and re-layouts  51.4 us (7%)
    ppermute x16, waiting for transfers between devices, flip(): return lax.ppermute(x, axis, [(i, i ^ bit) for i in range(n)])  186 us
    pallas_call x4, Pallas kernels, mlp(): pl.pallas_call(kernel, grid_spec=pltpu.PrefetchScalarGridSpec(num_scalar_...  155 us
    all_to_all x7, waiting for transfers between devices, exchange(): return lax.all_to_all(x, 'seq', split_axis=0, concat_axis=0, tiled=True)  110 us
    ppermute x24, waiting for transfers between devices, swap(): lax.ppermute(slots[s], 'tensor', [(i, i ^ s) for i in range(n)])  60.7 us
    all_to_all x1, blocking collectives, exchange(): return lax.all_to_all(x, 'seq', split_axis=0, concat_axis=0, tiled=True)  53.9 us
    unnamed x110, local copies, waits for them, and re-layouts  44.9 us
    all_to_all x7, starting transfers between devices, exchange(): return lax.all_to_all(x, 'seq', split_axis=0, concat_axis=0, tiled=True)  32.9 us
    ppermute x24, starting transfers between devices, swap(): lax.ppermute(slots[s], 'tensor', [(i, i ^ s) for i in range(n)])  28.9 us
  transfers between devices with their start and end apart: 47, of which 14 were waited for; matrix products, arithmetic and copies ran while one was open for 1% of the time, Pallas kernels for 29%

profile of v3, /device:TPU:0, one launch (start us, length us, event | category | flops | bytes accessed | tf_op | source)
XLA Modules:
  0.0 767.4 jit_solution(11356975905903814819)
XLA Ops:
  0.0 3.4 copy-done
  4.4 7.1 shard_map.82
  12.9 6.5 all-to-all-start
  19.4 3.4 copy-done.1
  22.8 7.1 shard_map.84
  31.2 37.2 %all-to-all-done.rest_4_ = bf16[8,32,32,128]{3,2,1,0:T(8,128)(2,1)S(1)} async-done(((bf16[8,32,32,128]{3,2,1,0:T(8,128)(2,1)}), bf16[8,32,32,128]{3,2,1,0:T(8,128)(2,1)S(1)}, u32[]{:S(2)}, u32[]{:S(2)}) %all-to-all-start) | async-done | bytes 2097184 | tf_op jit(solution)/shard_map/all_to_all | solution.py:326
  69.7 4.4 all-to-all-start.1
  74.2 2.0 collective-permute-start
  76.2 51.6 %collective-permute-done = bf16[1,2,192,1024]{3,2,1,0:T(8,128)(2,1)S(1)} collective-permute-done((bf16[1,2,192,1024]{3,2,1,0:T(8,128)(2,1)S(1)}, bf16[1,2,192,1024]{3,2,1,0:T(8,128)(2,1)S(1)}, u32[]{:S(2)}, u32[]{:S(2)}) %collective-permute-start) | collective-permute-done | bytes 786464 | tf_op jit(solution)/shard_map/ppermute | solution.py:284
  127.9 2.5 collective-permute-start.1
  130.5 68.1 %collective-permute-done.1 = bf16[2,2,192,1024]{3,2,1,0:T(8,128)(2,1)S(1)} collective-permute-done((bf16[2,2,192,1024]{3,2,1,0:T(8,128)(2,1)S(1)}, bf16[2,2,192,1024]{3,2,1,0:T(8,128)(2,1)S(1)}, u32[]{:S(2)}, u32[]{:S(2)}) %collective-permute-start.1) | collective-permute-done | bytes 1572896 | tf_op jit(solution)/shard_map/ppermute | solution.py:284
  198.9 3.4 copy-done.2
  202.2 7.1 shard_map.87
  210.8 4.4 all-to-all-start.3
  215.2 2.1 fusion
  218.8 1.5 collective-permute-start.3
  220.3 4.8 shard_map.85
  226.5 37.8 %all-to-all-done.3.rest_20_ = bf16[8,32,32,128]{3,2,1,0:T(8,128)(2,1)} async-done(((bf16[8,32,32,128]{3,2,1,0:T(8,128)(2,1)}), bf16[8,32,32,128]{3,2,1,0:T(8,128)(2,1)}, u32[]{:S(2)}, u32[]{:S(2)}) %all-to-all-start.3) | async-done | bytes 2097184 | tf_op jit(solution)/shard_map/all_to_all | solution.py:326
  264.2 3.6 all-to-all-start.2
  267.8 2.6 copy.15
  270.4 1.5 collective-permute-start.6
  274.4 33.5 %collective-permute-done.6.rest_16_.rest_14_ = bf16[1024,768]{1,0:T(8,128)(2,1)} collective-permute-done((bf16[1024,768]{1,0:T(8,128)(2,1)}, bf16[1024,768]{1,0:T(8,128)(2,1)}, u32[]{:S(2)}, u32[]{:S(2)}) %collective-permute-start.6) | collective-permute-done | bytes 1572896 | tf_op jit(solution)/shard_map/ppermute | solution.py:284
  311.2 29.9 %collective-permute-done.4.rest_13_.rest_7_ = bf16[768,1024]{1,0:T(8,128)(2,1)} collective-permute-done((bf16[768,1024]{1,0:T(8,128)(2,1)}, bf16[768,1024]{1,0:T(8,128)(2,1)}, u32[]{:S(2)}, u32[]{:S(2)}) %collective-permute-start.4) | collective-permute-done | bytes 1572896 | tf_op jit(solution)/shard_map/ppermute | solution.py:284
  341.2 2.5 collective-permute-done.7.rest_17_.rest_15_
  345.4 1.6 copy-done.12
  347.0 3.7 shard_map.92
  352.1 5.0 all-to-all-start.5
  359.0 1.5 copy-done.19
  360.5 6.4 shard_map.86
  367.0 1.6 collective-permute-start.8
  368.5 1.5 collective-permute-start.9
  370.6 7.2 shard_map.83.refs_0_
  377.8 5.6 shard_map.89
  384.7 9.1 %collective-permute-done.9.rest_2_ = bf16[256,1024]{1,0:T(8,128)(2,1)S(1)} collective-permute-done((bf16[256,1024]{1,0:T(8,128)(2,1)S(1)}, bf16[256,1024]{1,0:T(8,128)(2,1)S(1)}, u32[]{:S(2)}, u32[]{:S(2)}) %collective-permute-start.9) | collective-permute-done | bytes 524320 | tf_op jit(solution)/shard_map/ppermute | solution.py:267
  393.8 39.3 %shard_map.88 = (bf16[256,1024]{1,0:T(8,128)(2,1)S(1)}, bf16[256,1024]{1,0:T(8,128)(2,1)}, bf16[256,1024]{1,0:T(8,128)(2,1)}, bf16[256,1024]{1,0:T(8,128)(2,1)S(1)}) custom-call(s32[1]{0:T(128)} %bitcast.me_ref, bf16[256,1024]{1,0:T(8,128)(2,1)S(1)} %get-tuple-element.37.rest_0_, bf16[256,1024]{1,0:T(8,128)(2,1)S(1)} %collective-permute-done.8.rest_1_, ...), custom_call_target="tpu_custom_call" | custom-call | flops 25769803776 | bytes 29360128 | tf_op jit(solution)/shard_map/pallas_call | solution.py:199
  434.7 53.9 %all_to_all.40.rest_20_ = bf16[8,32,32,128]{3,2,1,0:T(8,128)(2,1)} all-to-all(bf16[8,32,32,128]{3,2,1,0:T(8,128)(2,1)} %shard_map.90), channel_id=1, replica_groups=mesh['seq'=8,'tensor'=4] {'seq'}, dimensions={0} | all-to-all | bytes 4194304 | tf_op jit(solution)/shard_map/all_to_all | solution.py:326
  488.6 3.9 all-to-all-start.7
  492.5 3.4 copy-done.3
  495.9 5.1 shard_map.93
  504.6 3.8 shard_map.91
  509.7 6.1 collective-permute-done.19.rest_1_
  515.8 10.1 %collective-permute-done.20.rest_2_ = bf16[256,1024]{1,0:T(8,128)(2,1)S(1)} collective-permute-done((bf16[256,1024]{1,0:T(8,128)(2,1)S(1)}, bf16[256,1024]{1,0:T(8,128)(2,1)S(1)}, u32[]{:S(2)}, u32[]{:S(2)}) %collective-permute-start.20) | collective-permute-done | bytes 524320 | tf_op jit(solution)/shard_map/ppermute | solution.py:267
  525.9 1.6 collective-permute-done.21.rest_3_
  527.6 38.2 %shard_map.94 = (bf16[256,1024]{1,0:T(8,128)(2,1)S(1)}, bf16[256,1024]{1,0:T(8,128)(2,1)S(1)}, bf16[256,1024]{1,0:T(8,128)(2,1)S(1)}, bf16[256,1024]{1,0:T(8,128)(2,1)S(1)}) custom-call(s32[1]{0:T(128)} %bitcast.me_ref, bf16[256,1024]{1,0:T(8,128)(2,1)S(1)} %get-tuple-element.42.rest_0_, bf16[256,1024]{1,0:T(8,128)(2,1)S(1)} %collective-permute-done.19.rest_1_, ...), custom_call_target="tpu_custom_call" | custom-call | flops 25769803776 | bytes 29360128 | tf_op jit(solution)/shard_map/pallas_call | solution.py:199
  569.1 5.2 all-to-all-start.6
  574.3 3.4 copy-done.4
  577.6 4.5 shard_map.98
  583.7 1.5 collective-permute-start.29
  587.2 1.5 collective-permute-start.38
  588.7 34.6 %all-to-all-done.6.rest_4_.rest_5_.rest_6_.rest_7_ = bf16[8,32,32,128]{3,2,1,0:T(8,128)(2,1)} async-done(((bf16[8,32,32,128]{3,2,1,0:T(8,128)(2,1)}), bf16[8,32,32,128]{3,2,1,0:T(8,128)(2,1)}, u32[]{:S(2)}, u32[]{:S(2)}) %all-to-all-start.6) | async-done | bytes 2097184 | tf_op jit(solution)/shard_map/all_to_all | solution.py:326
  623.4 3.4 copy-done.5
  626.7 5.2 shard_map.96
  637.4 39.1 %shard_map.99 = (bf16[256,1024]{1,0:T(8,128)(2,1)S(1)}, bf16[256,1024]{1,0:T(8,128)(2,1)S(1)}, bf16[256,1024]{1,0:T(8,128)(2,1)S(1)}, bf16[256,1024]{1,0:T(8,128)(2,1)S(1)}) custom-call(s32[1]{0:T(128)} %bitcast.me_ref, bf16[256,1024]{1,0:T(8,128)(2,1)S(1)} %copy-done.44, bf16[256,1024]{1,0:T(8,128)(2,1)S(1)} %collective-permute-done.28.rest_1_, ...), custom_call_target="tpu_custom_call" | custom-call | flops 25769803776 | bytes 29360128 | tf_op jit(solution)/shard_map/pallas_call | solution.py:199
  676.5 1.9 collective-permute-start.39
  680.1 1.8 collective-permute-start.36
  682.4 38.0 %shard_map.97 = (bf16[256,1024]{1,0:T(8,128)(2,1)S(1)}, bf16[256,1024]{1,0:T(8,128)(2,1)S(1)}, bf16[256,1024]{1,0:T(8,128)(2,1)S(1)}, bf16[256,1024]{1,0:T(8,128)(2,1)S(1)}) custom-call(s32[1]{0:T(128)} %bitcast.me_ref, bf16[256,1024]{1,0:T(8,128)(2,1)S(1)} %get-tuple-element.47.rest_0_.rest_20_, bf16[256,1024]{1,0:T(8,128)(2,1)S(1)} %collective-permute-done.22.rest_1_, ...), custom_call_target="tpu_custom_call" | custom-call | flops 25769803776 | bytes 29360128 | tf_op jit(solution)/shard_map/pallas_call | solution.py:199
  721.7 1.8 collective-permute-start.33
  725.2 1.8 collective-permute-start.27
  727.0 1.6 shard_map.100.rest_4_
  728.6 1.6 shard_map.101.rest_4_
  730.2 17.4 %collective-permute-done.32.rest_2_ = bf16[256,1024]{1,0:T(8,128)(2,1)S(1)} collective-permute-done((bf16[256,1024]{1,0:T(8,128)(2,1)S(1)}, bf16[256,1024]{1,0:T(8,128)(2,1)S(1)}, u32[]{:S(2)}, u32[]{:S(2)}) %collective-permute-start.32) | collective-permute-done | bytes 524320 | tf_op jit(solution)/shard_map/ppermute | solution.py:267
  747.6 1.6 shard_map.102.rest_4_
  749.2 16.3 %collective-permute-done.26.rest_2_ = bf16[256,1024]{1,0:T(8,128)(2,1)S(1)} collective-permute-done((bf16[256,1024]{1,0:T(8,128)(2,1)S(1)}, bf16[256,1024]{1,0:T(8,128)(2,1)S(1)}, u32[]{:S(2)}, u32[]{:S(2)}) %collective-permute-start.26) | collective-permute-done | bytes 524320 | tf_op jit(solution)/shard_map/ppermute | solution.py:267
  765.5 1.6 shard_map.103
  (173 shorter events, 46.1 us)
Async XLA Ops:
  12.9 55.5 %all-to-all-start = ((bf16[8,32,32,128]{3,2,1,0:T(8,128)(2,1)}), bf16[8,32,32,128]{3,2,1,0:T(8,128)(2,1)S(1)}, u32[]{:S(2)}, u32[]{:S(2)}) async-start(bf16[8,32,32,128]{3,2,1,0:T(8,128)(2,1)} %copy-done.16), calls=%async_computation | async-start | bytes 4194304 | tf_op jit(solution)/shard_map/all_to_all | solution.py:326
  31.2 42.9 %copy-start.50 = (bf16[192,1024]{1,0:T(8,128)(2,1)S(1)}, bf16[192,1024]{1,0:T(8,128)(2,1)}, u32[]{:S(2)}) copy-start(bf16[192,1024]{1,0:T(8,128)(2,1)} %param.15) | copy-start | bytes 1179652
  31.2 42.9 %copy-start.51 = (bf16[1024,192]{0,1:T(8,128)(2,1)S(1)}, bf16[1024,192]{0,1:T(8,128)(2,1)}, u32[]{:S(2)}) copy-start(bf16[1024,192]{0,1:T(8,128)(2,1)} %param.14) | copy-start | bytes 1179652
  69.7 141.0 %all-to-all-start.1 = ((bf16[8,32,32,128]{3,2,1,0:T(8,128)(2,1)}), bf16[8,32,32,128]{3,2,1,0:T(8,128)(2,1)}, u32[]{:S(2)}, u32[]{:S(2)}) async-start(bf16[8,32,32,128]{3,2,1,0:T(8,128)(2,1)} %copy-done.14), calls=%async_computation.1 | async-start | bytes 4194304 | tf_op jit(solution)/shard_map/all_to_all | solution.py:326
  74.2 53.6 %collective-permute-start = (bf16[1,2,192,1024]{3,2,1,0:T(8,128)(2,1)S(1)}, bf16[1,2,192,1024]{3,2,1,0:T(8,128)(2,1)S(1)}, u32[]{:S(2)}, u32[]{:S(2)}) collective-permute-start(bf16[1,2,192,1024]{3,2,1,0:T(8,128)(2,1)S(1)} %maximum_bitcast_fusion), channel_id=1, source_target_pairs={{0,8},{4,12},{8,0},{12,4},{16,24},{20,28},{24,16},{28,20},{1,9},{5... | collective-permute-start | bytes 2359304 | tf_op jit(solution)/shard_map/ppermute | solution.py:284
  127.9 70.9 %copy-start.9 = (bf16[512,512]{1,0:T(8,128)(2,1)S(1)}, bf16[512,512]{1,0:T(8,128)(2,1)}, u32[]{:S(2)}) copy-start(bf16[512,512]{1,0:T(8,128)(2,1)} %factor.7) | copy-start | bytes 1572868
  127.9 70.6 %collective-permute-start.1 = (bf16[2,2,192,1024]{3,2,1,0:T(8,128)(2,1)S(1)}, bf16[2,2,192,1024]{3,2,1,0:T(8,128)(2,1)S(1)}, u32[]{:S(2)}, u32[]{:S(2)}) collective-permute-start(bf16[2,2,192,1024]{3,2,1,0:T(8,128)(2,1)S(1)} %pad_maximum_fusion.1), channel_id=1, source_target_pairs={{0,16},{4,20},{8,24},{12,28},{16,0},{20,4},{24,8},{28,12},{1,17},{... | collective-permute-start | bytes 4718600 | tf_op jit(solution)/shard_map/ppermute | solution.py:284
  210.8 53.4 %all-to-all-start.3 = ((bf16[8,32,32,128]{3,2,1,0:T(8,128)(2,1)}), bf16[8,32,32,128]{3,2,1,0:T(8,128)(2,1)}, u32[]{:S(2)}, u32[]{:S(2)}) async-start(bf16[8,32,32,128]{3,2,1,0:T(8,128)(2,1)} %copy-done.15), calls=%async_computation.3 | async-start | bytes 4194304 | tf_op jit(solution)/shard_map/all_to_all | solution.py:326
  217.3 56.1 %collective-permute-start.2 = (bf16[768,1024]{1,0:T(8,128)(2,1)}, bf16[768,1024]{1,0:T(8,128)(2,1)}, u32[]{:S(2)}, u32[]{:S(2)}) collective-permute-start(bf16[768,1024]{1,0:T(8,128)(2,1)} %bitcast.9.rest_10_.rest_4_), channel_id=1, source_target_pairs={{0,1},{1,0},{2,3},{3,2},{4,5},{5,4},{6,7},{7,6},{8,9},{9,8},{10,11... | collective-permute-start | bytes 4718600 | tf_op jit(solution)/shard_map/ppermute | solution.py:284
  218.8 55.1 %collective-permute-start.3 = (bf16[768,1024]{1,0:T(8,128)(2,1)}, bf16[768,1024]{1,0:T(8,128)(2,1)}, u32[]{:S(2)}, u32[]{:S(2)}) collective-permute-start(bf16[768,1024]{1,0:T(8,128)(2,1)} %bitcast.9.rest_10_.rest_4_), channel_id=1, source_target_pairs={{0,2},{1,3},{2,0},{3,1},{4,6},{5,7},{6,4},{7,5},{8,10},{9,11},{10,... | collective-permute-start | bytes 4718600 | tf_op jit(solution)/shard_map/ppermute | solution.py:284
  264.2 87.9 %all-to-all-start.2 = ((bf16[8,32,32,128]{3,2,1,0:T(8,128)(2,1)}), bf16[8,32,32,128]{3,2,1,0:T(8,128)(2,1)S(1)}, u32[]{:S(2)}, u32[]{:S(2)}) async-start(bf16[8,32,32,128]{3,2,1,0:T(8,128)(2,1)} %bitcast.35), calls=%async_computation.2 | async-start | bytes 4194304 | tf_op jit(solution)/shard_map/all_to_all | solution.py:326
  270.4 37.5 %collective-permute-start.6 = (bf16[1024,768]{1,0:T(8,128)(2,1)}, bf16[1024,768]{1,0:T(8,128)(2,1)}, u32[]{:S(2)}, u32[]{:S(2)}) collective-permute-start(bf16[1024,768]{1,0:T(8,128)(2,1)} %bitcast.26), channel_id=1, source_target_pairs={{0,2},{1,3},{2,0},{3,1},{4,6},{5,7},{6,4},{7,5},{8,10},{9,11},{10,... | collective-permute-start | bytes 4718600 | tf_op jit(solution)/shard_map/ppermute | solution.py:284
  271.9 37.5 %collective-permute-start.5 = (bf16[1024,768]{1,0:T(8,128)(2,1)}, bf16[1024,768]{1,0:T(8,128)(2,1)}, u32[]{:S(2)}, u32[]{:S(2)}) collective-permute-start(bf16[1024,768]{1,0:T(8,128)(2,1)} %bitcast.27), channel_id=1, source_target_pairs={{0,1},{1,0},{2,3},{3,2},{4,5},{5,4},{6,7},{7,6},{8,9},{9,8},{10,11... | collective-permute-start | bytes 4718600 | tf_op jit(solution)/shard_map/ppermute | solution.py:284
  273.4 36.0 %collective-permute-start.11 = (bf16[768,1024]{1,0:T(8,128)(2,1)}, bf16[768,1024]{1,0:T(8,128)(2,1)S(1)}, u32[]{:S(2)}, u32[]{:S(2)}) collective-permute-start(bf16[768,1024]{1,0:T(8,128)(2,1)} %bitcast.9.rest_10_.rest_4_), channel_id=1, source_target_pairs={{0,4},{4,0},{8,12},{12,8},{16,20},{20,16},{24,28},{28,24},{1,5},{5... | collective-permute-start | bytes 4718600 | tf_op jit(solution)/shard_map/ppermute | solution.py:284
  273.4 37.7 %collective-permute-start.15 = (bf16[1024,768]{1,0:T(8,128)(2,1)}, bf16[1024,768]{1,0:T(8,128)(2,1)S(1)}, u32[]{:S(2)}, u32[]{:S(2)}) collective-permute-start(bf16[1024,768]{1,0:T(8,128)(2,1)} %bitcast.28), channel_id=1, source_target_pairs={{0,4},{4,0},{8,12},{12,8},{16,20},{20,16},{24,28},{28,24},{1,5},{5... | collective-permute-start | bytes 4718600 | tf_op jit(solution)/shard_map/ppermute | solution.py:284
  273.9 67.2 %collective-permute-start.4 = (bf16[768,1024]{1,0:T(8,128)(2,1)}, bf16[768,1024]{1,0:T(8,128)(2,1)}, u32[]{:S(2)}, u32[]{:S(2)}) collective-permute-start(bf16[768,1024]{1,0:T(8,128)(2,1)} %collective-permute-done.2.rest_11_.rest_5_), channel_id=1, source_target_pairs={{0,2},{1,3},{2,0},{3,1},{4,6},{5,7},{6,4},{7,5},{8,10},{9,11},{10,... | collective-permute-start | bytes 4718600 | tf_op jit(solution)/shard_map/ppermute | solution.py:284
  307.9 35.8 %collective-permute-start.7 = (bf16[1024,768]{1,0:T(8,128)(2,1)}, bf16[1024,768]{1,0:T(8,128)(2,1)}, u32[]{:S(2)}, u32[]{:S(2)}) collective-permute-start(bf16[1024,768]{1,0:T(8,128)(2,1)} %collective-permute-done.6.rest_16_.rest_14_), channel_id=1, source_target_pairs={{0,1},{1,0},{2,3},{3,2},{4,5},{5,4},{6,7},{7,6},{8,9},{9,8},{10,11... | collective-permute-start | bytes 4718600 | tf_op jit(solution)/shard_map/ppermute | solution.py:284
  309.4 34.3 %collective-permute-start.12 = (bf16[768,1024]{1,0:T(8,128)(2,1)}, bf16[768,1024]{1,0:T(8,128)(2,1)S(1)}, u32[]{:S(2)}, u32[]{:S(2)}) collective-permute-start(bf16[768,1024]{1,0:T(8,128)(2,1)} %collective-permute-done.2.rest_11_.rest_5_), channel_id=1, source_target_pairs={{0,4},{4,0},{8,12},{12,8},{16,20},{20,16},{24,28},{28,24},{1,5},{5... | collective-permute-start | bytes 4718600 | tf_op jit(solution)/shard_map/ppermute | solution.py:284
  310.6 56.3 %collective-permute-start.13 = (bf16[768,1024]{1,0:T(8,128)(2,1)}, bf16[768,1024]{1,0:T(8,128)(2,1)}, u32[]{:S(2)}, u32[]{:S(2)}) collective-permute-start(bf16[768,1024]{1,0:T(8,128)(2,1)} %collective-permute-done.3.rest_12_.rest_6_), channel_id=1, source_target_pairs={{0,4},{4,0},{8,12},{12,8},{16,20},{20,16},{24,28},{28,24},{1,5},{5... | collective-permute-start | bytes 4718600 | tf_op jit(solution)/shard_map/ppermute | solution.py:284
  311.2 34.3 %copy-start.52 = (bf16[1024,768]{1,0:T(8,128)(2,1)}, bf16[1024,768]{1,0:T(8,128)(2,1)S(1)}, u32[]{:S(2)}) copy-start(bf16[1024,768]{1,0:T(8,128)(2,1)S(1)} %collective-permute-done.15.rest_16_) | copy-start | bytes 4718596
  311.2 57.4 %collective-permute-start.16 = (bf16[1024,768]{1,0:T(8,128)(2,1)}, bf16[1024,768]{1,0:T(8,128)(2,1)}, u32[]{:S(2)}, u32[]{:S(2)}) collective-permute-start(bf16[1024,768]{1,0:T(8,128)(2,1)} %collective-permute-done.5.rest_15_.rest_13_), channel_id=1, source_target_pairs={{0,4},{4,0},{8,12},{12,8},{16,20},{20,16},{24,28},{28,24},{1,5},{5... | collective-permute-start | bytes 4718600 | tf_op jit(solution)/shard_map/ppermute | solution.py:284
  341.2 28.9 %collective-permute-start.17 = (bf16[1024,768]{1,0:T(8,128)(2,1)}, bf16[1024,768]{1,0:T(8,128)(2,1)}, u32[]{:S(2)}, u32[]{:S(2)}) collective-permute-start(bf16[1024,768]{1,0:T(8,128)(2,1)} %collective-permute-done.6.rest_16_.rest_14_), channel_id=1, source_target_pairs={{0,4},{4,0},{8,12},{12,8},{16,20},{20,16},{24,28},{28,24},{1,5},{5... | collective-permute-start | bytes 4718600 | tf_op jit(solution)/shard_map/ppermute | solution.py:284
  343.7 41.0 %collective-permute-start.14 = (bf16[768,1024]{1,0:T(8,128)(2,1)}, bf16[768,1024]{1,0:T(8,128)(2,1)}, u32[]{:S(2)}, u32[]{:S(2)}) collective-permute-start(bf16[768,1024]{1,0:T(8,128)(2,1)} %collective-permute-done.4.rest_13_.rest_7_), channel_id=1, source_target_pairs={{0,4},{4,0},{8,12},{12,8},{16,20},{20,16},{24,28},{28,24},{1,5},{5... | collective-permute-start | bytes 4718600 | tf_op jit(solution)/shard_map/ppermute | solution.py:284
  344.9 39.8 %collective-permute-start.18 = (bf16[1024,768]{1,0:T(8,128)(2,1)}, bf16[1024,768]{1,0:T(8,128)(2,1)}, u32[]{:S(2)}, u32[]{:S(2)}) collective-permute-start(bf16[1024,768]{1,0:T(8,128)(2,1)} %collective-permute-done.7.rest_17_.rest_15_), channel_id=1, source_target_pairs={{0,4},{4,0},{8,12},{12,8},{16,20},{20,16},{24,28},{28,24},{1,5},{5... | collective-permute-start | bytes 4718600 | tf_op jit(solution)/shard_map/ppermute | solution.py:284
  352.1 82.6 %all-to-all-start.5 = ((bf16[8,32,32,128]{3,2,1,0:T(8,128)(2,1)}), bf16[8,32,32,128]{3,2,1,0:T(8,128)(2,1)}, u32[]{:S(2)}, u32[]{:S(2)}) async-start(bf16[8,32,32,128]{3,2,1,0:T(8,128)(2,1)} %bitcast.34), calls=%async_computation.5 | async-start | bytes 4194304 | tf_op jit(solution)/shard_map/all_to_all | solution.py:326
  358.9 11.6 %slice-start = ((s8[8388608]{0:T(1024)(128)(4,1)}), s8[4194304]{0:T(1024)(128)(4,1)S(1)}, s32[]{:S(2)}) async-start(s8[8388608]{0:T(1024)(128)(4,1)} %bitcast.20), calls=%async_computation.8 | async-start | bytes 8388608
  360.5 10.0 %slice-start.1 = ((s8[8388608]{0:T(1024)(128)(4,1)}), s8[4194304]{0:T(1024)(128)(4,1)S(1)}, s32[]{:S(2)}) async-start(s8[8388608]{0:T(1024)(128)(4,1)} %bitcast.20), calls=%async_computation.9 | async-start | bytes 8388608
  360.5 10.0 %copy-start.10 = (bf16[512,512]{1,0:T(8,128)(2,1)S(1)}, bf16[512,512]{1,0:T(8,128)(2,1)}, u32[]{:S(2)}) copy-start(bf16[512,512]{1,0:T(8,128)(2,1)} %factor.7) | copy-start | bytes 1572868
  360.5 10.0 %copy-start.13 = (bf16[8,32,32,128]{3,2,1,0:T(8,128)(2,1)S(1)}, bf16[8,32,32,128]{3,2,1,0:T(8,128)(2,1)}, u32[]{:S(2)}) copy-start(bf16[8,32,32,128]{3,2,1,0:T(8,128)(2,1)} %copy-done.11) | copy-start | bytes 6291460
  367.0 17.8 %collective-permute-start.8 = (bf16[256,1024]{1,0:T(8,128)(2,1)S(1)}, bf16[256,1024]{1,0:T(8,128)(2,1)S(1)}, u32[]{:S(2)}, u32[]{:S(2)}) collective-permute-start(bf16[256,1024]{1,0:T(8,128)(2,1)S(1)} %get-tuple-element.38), channel_id=1, source_target_pairs={{0,1},{1,0},{2,3},{3,2},{4,5},{5,4},{6,7},{7,6},{8,9},{9,8},{10,11... | collective-permute-start | bytes 1572872 | tf_op jit(solution)/shard_map/ppermute | solution.py:267
  368.5 25.3 %collective-permute-start.9 = (bf16[256,1024]{1,0:T(8,128)(2,1)S(1)}, bf16[256,1024]{1,0:T(8,128)(2,1)S(1)}, u32[]{:S(2)}, u32[]{:S(2)}) collective-permute-start(bf16[256,1024]{1,0:T(8,128)(2,1)S(1)} %get-tuple-element.39), channel_id=1, source_target_pairs={{0,2},{1,3},{2,0},{3,1},{4,6},{5,7},{6,4},{7,5},{8,10},{9,11},{10,... | collective-permute-start | bytes 1572872 | tf_op jit(solution)/shard_map/ppermute | solution.py:267
  370.1 23.8 %collective-permute-start.10 = (bf16[256,1024]{1,0:T(8,128)(2,1)S(1)}, bf16[256,1024]{1,0:T(8,128)(2,1)S(1)}, u32[]{:S(2)}, u32[]{:S(2)}) collective-permute-start(bf16[256,1024]{1,0:T(8,128)(2,1)S(1)} %get-tuple-element.40), channel_id=1, source_target_pairs={{0,3},{1,2},{2,1},{3,0},{4,7},{5,6},{6,5},{7,4},{8,11},{9,10},{10,... | collective-permute-start | bytes 1572872 | tf_op jit(solution)/shard_map/ppermute | solution.py:267
  377.8 16.0 %copy-start.28 = (bf16[768,1024]{1,0:T(8,128)(2,1)S(1)}, bf16[768,1024]{1,0:T(8,128)(2,1)}, u32[]{:S(2)}) copy-start(bf16[768,1024]{1,0:T(8,128)(2,1)} %copy-done.27) | copy-start | bytes 4718596
  377.8 16.0 %copy-start.32 = (bf16[768,1024]{1,0:T(8,128)(2,1)S(1)}, bf16[768,1024]{1,0:T(8,128)(2,1)}, u32[]{:S(2)}) copy-start(bf16[768,1024]{1,0:T(8,128)(2,1)} %copy-done.31) | copy-start | bytes 4718596
  488.6 80.5 %all-to-all-start.7 = ((bf16[8,32,32,128]{3,2,1,0:T(8,128)(2,1)}), bf16[8,32,32,128]{3,2,1,0:T(8,128)(2,1)S(1)}, u32[]{:S(2)}, u32[]{:S(2)}) async-start(bf16[8,32,32,128]{3,2,1,0:T(8,128)(2,1)} %bitcast.24), calls=%async_computation.7 | async-start | bytes 4194304 | tf_op jit(solution)/shard_map/all_to_all | solution.py:326
  501.1 14.8 %collective-permute-start.19 = (bf16[256,1024]{1,0:T(8,128)(2,1)S(1)}, bf16[256,1024]{1,0:T(8,128)(2,1)S(1)}, u32[]{:S(2)}, u32[]{:S(2)}) collective-permute-start(bf16[256,1024]{1,0:T(8,128)(2,1)S(1)} %get-tuple-element.43), channel_id=1, source_target_pairs={{0,1},{1,0},{2,3},{3,2},{4,5},{5,4},{6,7},{7,6},{8,9},{9,8},{10,11... | collective-permute-start | bytes 1572872 | tf_op jit(solution)/shard_map/ppermute | solution.py:267
  502.3 23.6 %collective-permute-start.20 = (bf16[256,1024]{1,0:T(8,128)(2,1)S(1)}, bf16[256,1024]{1,0:T(8,128)(2,1)S(1)}, u32[]{:S(2)}, u32[]{:S(2)}) collective-permute-start(bf16[256,1024]{1,0:T(8,128)(2,1)S(1)} %get-tuple-element.44), channel_id=1, source_target_pairs={{0,2},{1,3},{2,0},{3,1},{4,6},{5,7},{6,4},{7,5},{8,10},{9,11},{10,... | collective-permute-start | bytes 1572872 | tf_op jit(solution)/shard_map/ppermute | solution.py:267
  503.2 24.4 %collective-permute-start.21 = (bf16[256,1024]{1,0:T(8,128)(2,1)S(1)}, bf16[256,1024]{1,0:T(8,128)(2,1)S(1)}, u32[]{:S(2)}, u32[]{:S(2)}) collective-permute-start(bf16[256,1024]{1,0:T(8,128)(2,1)S(1)} %get-tuple-element.45), channel_id=1, source_target_pairs={{0,3},{1,2},{2,1},{3,0},{4,7},{5,6},{6,5},{7,4},{8,11},{9,10},{10,... | collective-permute-start | bytes 1572872 | tf_op jit(solution)/shard_map/ppermute | solution.py:267
  504.6 23.0 %copy-start.29 = (bf16[768,1024]{1,0:T(8,128)(2,1)S(1)}, bf16[768,1024]{1,0:T(8,128)(2,1)}, u32[]{:S(2)}) copy-start(bf16[768,1024]{1,0:T(8,128)(2,1)} %copy-done.27) | copy-start | bytes 4718596
  504.6 23.0 %copy-start.33 = (bf16[768,1024]{1,0:T(8,128)(2,1)S(1)}, bf16[768,1024]{1,0:T(8,128)(2,1)}, u32[]{:S(2)}) copy-start(bf16[768,1024]{1,0:T(8,128)(2,1)} %copy-done.31) | copy-start | bytes 4718596
  569.1 54.3 %all-to-all-start.6 = ((bf16[8,32,32,128]{3,2,1,0:T(8,128)(2,1)}), bf16[8,32,32,128]{3,2,1,0:T(8,128)(2,1)}, u32[]{:S(2)}, u32[]{:S(2)}) async-start(bf16[8,32,32,128]{3,2,1,0:T(8,128)(2,1)} %shard_map.95), calls=%async_computation.6 | async-start | bytes 4194304 | tf_op jit(solution)/shard_map/all_to_all | solution.py:326
  582.9 49.1 %collective-permute-start.28 = (bf16[256,1024]{1,0:T(8,128)(2,1)}, bf16[256,1024]{1,0:T(8,128)(2,1)S(1)}, u32[]{:S(2)}, u32[]{:S(2)}) collective-permute-start(bf16[256,1024]{1,0:T(8,128)(2,1)} %get-tuple-element.56), channel_id=1, source_target_pairs={{0,1},{1,0},{2,3},{3,2},{4,5},{5,4},{6,7},{7,6},{8,9},{9,8},{10,11... | collective-permute-start | bytes 1572872 | tf_op jit(solution)/shard_map/ppermute | solution.py:267
  583.7 49.1 %collective-permute-start.29 = (bf16[256,1024]{1,0:T(8,128)(2,1)}, bf16[256,1024]{1,0:T(8,128)(2,1)S(1)}, u32[]{:S(2)}, u32[]{:S(2)}) collective-permute-start(bf16[256,1024]{1,0:T(8,128)(2,1)} %get-tuple-element.57), channel_id=1, source_target_pairs={{0,2},{1,3},{2,0},{3,1},{4,6},{5,7},{6,4},{7,5},{8,10},{9,11},{10,... | collective-permute-start | bytes 1572872 | tf_op jit(solution)/shard_map/ppermute | solution.py:267
  585.3 49.9 %collective-permute-start.30 = (bf16[256,1024]{1,0:T(8,128)(2,1)}, bf16[256,1024]{1,0:T(8,128)(2,1)}, u32[]{:S(2)}, u32[]{:S(2)}) collective-permute-start(bf16[256,1024]{1,0:T(8,128)(2,1)} %get-tuple-element.58), channel_id=1, source_target_pairs={{0,3},{1,2},{2,1},{3,0},{4,7},{5,6},{6,5},{7,4},{8,11},{9,10},{10,... | collective-permute-start | bytes 1572872 | tf_op jit(solution)/shard_map/ppermute | solution.py:267
  586.4 90.1 %collective-permute-start.37 = (bf16[256,1024]{1,0:T(8,128)(2,1)}, bf16[256,1024]{1,0:T(8,128)(2,1)S(1)}, u32[]{:S(2)}, u32[]{:S(2)}) collective-permute-start(bf16[256,1024]{1,0:T(8,128)(2,1)} %get-tuple-element.66), channel_id=1, source_target_pairs={{0,1},{1,0},{2,3},{3,2},{4,5},{5,4},{6,7},{7,6},{8,9},{9,8},{10,11... | collective-permute-start | bytes 1572872 | tf_op jit(solution)/shard_map/ppermute | solution.py:267
  587.2 91.1 %collective-permute-start.38 = (bf16[256,1024]{1,0:T(8,128)(2,1)}, bf16[256,1024]{1,0:T(8,128)(2,1)S(1)}, u32[]{:S(2)}, u32[]{:S(2)}) collective-permute-start(bf16[256,1024]{1,0:T(8,128)(2,1)} %get-tuple-element.67), channel_id=1, source_target_pairs={{0,2},{1,3},{2,0},{3,1},{4,6},{5,7},{6,4},{7,5},{8,10},{9,11},{10,... | collective-permute-start | bytes 1572872 | tf_op jit(solution)/shard_map/ppermute | solution.py:267
  626.7 9.6 %copy-start.44 = (bf16[256,1024]{1,0:T(8,128)(2,1)S(1)}, bf16[256,1024]{1,0:T(8,128)(2,1)}, u32[]{:S(2)}) copy-start(bf16[256,1024]{1,0:T(8,128)(2,1)} %copy-done.43) | copy-start | bytes 1572868
  632.0 46.9 %collective-permute-start.22 = (bf16[256,1024]{1,0:T(8,128)(2,1)S(1)}, bf16[256,1024]{1,0:T(8,128)(2,1)S(1)}, u32[]{:S(2)}, u32[]{:S(2)}) collective-permute-start(bf16[256,1024]{1,0:T(8,128)(2,1)S(1)} %get-tuple-element.48), channel_id=1, source_target_pairs={{0,1},{1,0},{2,3},{3,2},{4,5},{5,4},{6,7},{7,6},{8,9},{9,8},{10,11... | collective-permute-start | bytes 1572872 | tf_op jit(solution)/shard_map/ppermute | solution.py:267
  633.7 46.4 %collective-permute-start.23 = (bf16[256,1024]{1,0:T(8,128)(2,1)S(1)}, bf16[256,1024]{1,0:T(8,128)(2,1)S(1)}, u32[]{:S(2)}, u32[]{:S(2)}) collective-permute-start(bf16[256,1024]{1,0:T(8,128)(2,1)S(1)} %get-tuple-element.49), channel_id=1, source_target_pairs={{0,2},{1,3},{2,0},{3,1},{4,6},{5,7},{6,4},{7,5},{8,10},{9,11},{10,... | collective-permute-start | bytes 1572872 | tf_op jit(solution)/shard_map/ppermute | solution.py:267
  635.2 46.7 %collective-permute-start.24 = (bf16[256,1024]{1,0:T(8,128)(2,1)S(1)}, bf16[256,1024]{1,0:T(8,128)(2,1)S(1)}, u32[]{:S(2)}, u32[]{:S(2)}) collective-permute-start(bf16[256,1024]{1,0:T(8,128)(2,1)S(1)} %get-tuple-element.50), channel_id=1, source_target_pairs={{0,3},{1,2},{2,1},{3,0},{4,7},{5,6},{6,5},{7,4},{8,11},{9,10},{10,... | collective-permute-start | bytes 1572872 | tf_op jit(solution)/shard_map/ppermute | solution.py:267
  637.4 39.1 %copy-start.36 = (bf16[256,1024]{1,0:T(8,128)(2,1)S(1)}, bf16[256,1024]{1,0:T(8,128)(2,1)}, u32[]{:S(2)}) copy-start(bf16[256,1024]{1,0:T(8,128)(2,1)} %copy-done.35) | copy-start | bytes 1572868
  637.4 41.0 %copy-start.42 = (bf16[256,1024]{1,0:T(8,128)(2,1)S(1)}, bf16[256,1024]{1,0:T(8,128)(2,1)}, u32[]{:S(2)}) copy-start(bf16[256,1024]{1,0:T(8,128)(2,1)} %copy-done.41) | copy-start | bytes 1572868
  637.4 41.5 %copy-start.40 = (bf16[256,1024]{1,0:T(8,128)(2,1)S(1)}, bf16[256,1024]{1,0:T(8,128)(2,1)}, u32[]{:S(2)}) copy-start(bf16[256,1024]{1,0:T(8,128)(2,1)} %copy-done.39) | copy-start | bytes 1572868
  637.4 42.7 %copy-start.38 = (bf16[256,1024]{1,0:T(8,128)(2,1)S(1)}, bf16[256,1024]{1,0:T(8,128)(2,1)}, u32[]{:S(2)}) copy-start(bf16[256,1024]{1,0:T(8,128)(2,1)} %copy-done.37) | copy-start | bytes 1572868
  676.5 44.0 %collective-permute-start.39 = (bf16[256,1024]{1,0:T(8,128)(2,1)S(1)}, bf16[256,1024]{1,0:T(8,128)(2,1)S(1)}, u32[]{:S(2)}, u32[]{:S(2)}) collective-permute-start(bf16[256,1024]{1,0:T(8,128)(2,1)S(1)} %copy-done.36), channel_id=1, source_target_pairs={{0,3},{1,2},{2,1},{3,0},{4,7},{5,6},{6,5},{7,4},{8,11},{9,10},{10,... | collective-permute-start | bytes 1572872 | tf_op jit(solution)/shard_map/ppermute | solution.py:267
  678.4 43.3 %collective-permute-start.34 = (bf16[256,1024]{1,0:T(8,128)(2,1)S(1)}, bf16[256,1024]{1,0:T(8,128)(2,1)S(1)}, u32[]{:S(2)}, u32[]{:S(2)}) collective-permute-start(bf16[256,1024]{1,0:T(8,128)(2,1)S(1)} %copy-done.42), channel_id=1, source_target_pairs={{0,1},{1,0},{2,3},{3,2},{4,5},{5,4},{6,7},{7,6},{8,9},{9,8},{10,11... | collective-permute-start | bytes 1572872 | tf_op jit(solution)/shard_map/ppermute | solution.py:267
  678.9 44.6 %collective-permute-start.35 = (bf16[256,1024]{1,0:T(8,128)(2,1)S(1)}, bf16[256,1024]{1,0:T(8,128)(2,1)S(1)}, u32[]{:S(2)}, u32[]{:S(2)}) collective-permute-start(bf16[256,1024]{1,0:T(8,128)(2,1)S(1)} %copy-done.40), channel_id=1, source_target_pairs={{0,2},{1,3},{2,0},{3,1},{4,6},{5,7},{6,4},{7,5},{8,10},{9,11},{10,... | collective-permute-start | bytes 1572872 | tf_op jit(solution)/shard_map/ppermute | solution.py:267
  680.1 44.0 %collective-permute-start.36 = (bf16[256,1024]{1,0:T(8,128)(2,1)S(1)}, bf16[256,1024]{1,0:T(8,128)(2,1)S(1)}, u32[]{:S(2)}, u32[]{:S(2)}) collective-permute-start(bf16[256,1024]{1,0:T(8,128)(2,1)S(1)} %copy-done.38), channel_id=1, source_target_pairs={{0,3},{1,2},{2,1},{3,0},{4,7},{5,6},{6,5},{7,4},{8,11},{9,10},{10,... | collective-permute-start | bytes 1572872 | tf_op jit(solution)/shard_map/ppermute | solution.py:267
  681.9 43.3 %collective-permute-start.31 = (bf16[256,1024]{1,0:T(8,128)(2,1)S(1)}, bf16[256,1024]{1,0:T(8,128)(2,1)S(1)}, u32[]{:S(2)}, u32[]{:S(2)}) collective-permute-start(bf16[256,1024]{1,0:T(8,128)(2,1)S(1)} %get-tuple-element.60), channel_id=1, source_target_pairs={{0,1},{1,0},{2,3},{3,2},{4,5},{5,4},{6,7},{7,6},{8,9},{9,8},{10,11... | collective-permute-start | bytes 1572872 | tf_op jit(solution)/shard_map/ppermute | solution.py:267
  720.5 27.1 %collective-permute-start.32 = (bf16[256,1024]{1,0:T(8,128)(2,1)S(1)}, bf16[256,1024]{1,0:T(8,128)(2,1)S(1)}, u32[]{:S(2)}, u32[]{:S(2)}) collective-permute-start(bf16[256,1024]{1,0:T(8,128)(2,1)S(1)} %get-tuple-element.61), channel_id=1, source_target_pairs={{0,2},{1,3},{2,0},{3,1},{4,6},{5,7},{6,4},{7,5},{8,10},{9,11},{10,... | collective-permute-start | bytes 1572872 | tf_op jit(solution)/shard_map/ppermute | solution.py:267
  721.7 25.9 %collective-permute-start.33 = (bf16[256,1024]{1,0:T(8,128)(2,1)S(1)}, bf16[256,1024]{1,0:T(8,128)(2,1)S(1)}, u32[]{:S(2)}, u32[]{:S(2)}) collective-permute-start(bf16[256,1024]{1,0:T(8,128)(2,1)S(1)} %get-tuple-element.62), channel_id=1, source_target_pairs={{0,3},{1,2},{2,1},{3,0},{4,7},{5,6},{6,5},{7,4},{8,11},{9,10},{10,... | collective-permute-start | bytes 1572872 | tf_op jit(solution)/shard_map/ppermute | solution.py:267
  723.5 25.7 %collective-permute-start.25 = (bf16[256,1024]{1,0:T(8,128)(2,1)S(1)}, bf16[256,1024]{1,0:T(8,128)(2,1)S(1)}, u32[]{:S(2)}, u32[]{:S(2)}) collective-permute-start(bf16[256,1024]{1,0:T(8,128)(2,1)S(1)} %get-tuple-element.52), channel_id=1, source_target_pairs={{0,1},{1,0},{2,3},{3,2},{4,5},{5,4},{6,7},{7,6},{8,9},{9,8},{10,11... | collective-permute-start | bytes 1572872 | tf_op jit(solution)/shard_map/ppermute | solution.py:267
  724.0 41.4 %collective-permute-start.26 = (bf16[256,1024]{1,0:T(8,128)(2,1)S(1)}, bf16[256,1024]{1,0:T(8,128)(2,1)S(1)}, u32[]{:S(2)}, u32[]{:S(2)}) collective-permute-start(bf16[256,1024]{1,0:T(8,128)(2,1)S(1)} %get-tuple-element.53), channel_id=1, source_target_pairs={{0,2},{1,3},{2,0},{3,1},{4,6},{5,7},{6,4},{7,5},{8,10},{9,11},{10,... | collective-permute-start | bytes 1572872 | tf_op jit(solution)/shard_map/ppermute | solution.py:267
  725.2 40.3 %collective-permute-start.27 = (bf16[256,1024]{1,0:T(8,128)(2,1)S(1)}, bf16[256,1024]{1,0:T(8,128)(2,1)S(1)}, u32[]{:S(2)}, u32[]{:S(2)}) collective-permute-start(bf16[256,1024]{1,0:T(8,128)(2,1)S(1)} %get-tuple-element.54), channel_id=1, source_target_pairs={{0,3},{1,2},{2,1},{3,0},{4,7},{5,6},{6,5},{7,4},{8,11},{9,10},{10,... | collective-permute-start | bytes 1572872 | tf_op jit(solution)/shard_map/ppermute | solution.py:267
  (38 other events, 115.6 us)

commit v4 on v3

--- a/solution.py
+++ b/solution.py
@@ -19,45 +19,47 @@
     return pltpu.CompilerParams(vmem_limit_bytes=mib * 2**20)
 
 
-def first_pass(k, activations, first_factor, spectral, ns, dep):
+def first_pass(at, n, activations, first_factor, spectral, ns, deps=()):
     c, tokens = activations.shape
     blocks = tokens // B
     step = min(4, blocks)
-    per = B // J
-    deps = [] if dep is None else [dep]
+    wide = n * J
+    per = B // wide
 
     def kernel(act, factor, *rest):
         specs, out = rest[:step], rest[-1]
         for q in range(step):
             product = jnp.dot(act[:, q * B : (q + 1) * B], factor[...], preferred_element_type=f32)
             value = (product * specs[q][...]).astype(bf16)
-            out[:, q] = value.reshape(ns, c // ns, J)
+            for m in range(n):
+                out[:, m, q] = value[:, m * J : (m + 1) * J].reshape(ns, c // ns, J)
 
     def spec_at(q):
-        return pl.BlockSpec((c, J), lambda i: (0, (i * step + q) * per + k))
+        return pl.BlockSpec((c, wide), lambda i: (0, (i * step + q) * per + at))
 
     return pl.pallas_call(
         kernel,
         grid=(blocks // step,),
         in_specs=[
             pl.BlockSpec((c, step * B), lambda i: (0, i)),
-            pl.BlockSpec((B, J), lambda i: (0, k)),
+            pl.BlockSpec((B, wide), lambda i: (0, at)),
         ]
         + [spec_at(q) for q in range(step)]
         + [ANY] * len(deps),
-        out_specs=pl.BlockSpec((ns, step, c // ns, J), lambda i: (0, i, 0, 0)),
-        out_shape=jax.ShapeDtypeStruct((ns, blocks, c // ns, J), bf16),
+        out_specs=pl.BlockSpec((ns, n, step, c // ns, J), lambda i: (0, 0, i, 0, 0)),
+        out_shape=jax.ShapeDtypeStruct((ns, n, blocks, c // ns, J), bf16),
         compiler_params=params(32),
         cost_estimate=pl.CostEstimate(
-            flops=4 * c * blocks * B * J,
-            bytes_accessed=2 * c * tokens + 6 * c * blocks * J,
+            flops=2 * c * blocks * B * wide,
+            bytes_accessed=2 * c * tokens + 6 * c * blocks * wide,
             transcendentals=0,
         ),
     )(activations, first_factor, *[spectral] * step, *deps)
 
 
-def second_pass(gathered, second_factor, deps):
-    a, c, _ = gathered.shape
+def second_pass(gathered, m, second_factor, deps=()):
+    ns, _, blocks, c, _ = gathered.shape
+    a = ns * blocks
     cb = min(16, c)
 
     def kernel(x_ref, s_ref, *rest):
@@ -68,24 +70,24 @@
         low = (factor - high.astype(f32)).astype(bf16)
         for i in range(0, cb, 2):
             x = jnp.concatenate(
-                [x_wide[pl.ds(i + n, a, stride=cb), :] for n in range(2)], axis=1
+                [x_wide[pl.ds(i + h, a, stride=cb), :] for h in range(2)], axis=1
             ).astype(bf16)
             y = jnp.dot(high, x, preferred_element_type=f32)
             y += jnp.dot(low, x, preferred_element_type=f32)
-            for n in range(2):
-                y_wide[pl.ds(i + n, a, stride=cb), :] = y[:, n * J : (n + 1) * J]
-        out[...] = y_wide[...].reshape(a, cb, J).astype(bf16)
+            for h in range(2):
+                y_wide[pl.ds(i + h, a, stride=cb), :] = y[:, h * J : (h + 1) * J]
+        out[...] = y_wide[...].reshape(ns, blocks, cb, J).astype(bf16)
 
     return pl.pallas_call(
         kernel,
         grid=(c // cb,),
         in_specs=[
-            pl.BlockSpec((a, cb, J), lambda i: (0, i, 0)),
+            pl.BlockSpec((ns, 1, blocks, cb, J), lambda i: (0, m, 0, i, 0)),
             pl.BlockSpec((a, a), lambda i: (0, 0)),
         ]
         + [ANY] * len(deps),
-        out_specs=pl.BlockSpec((a, cb, J), lambda i: (0, i, 0)),
-        out_shape=jax.ShapeDtypeStruct((a, c, J), bf16),
+        out_specs=pl.BlockSpec((ns, blocks, cb, J), lambda i: (0, 0, i, 0)),
+        out_shape=jax.ShapeDtypeStruct((ns, blocks, c, J), bf16),
         scratch_shapes=[pltpu.VMEM((a * cb, J), f32), pltpu.VMEM((a * cb, J), f32)],
         compiler_params=params(32),
         cost_estimate=pl.CostEstimate(
@@ -142,23 +144,27 @@
     )(me, *[activations] * nt, *[returned] * nt, scale, shift, *deps)
 
 
-def mlp(me, slots, pieces_in, pieces_out, deps):
+def mlp(me, slots, halves_in, halves_out, deps):
     nt = len(slots)
     c, tokens = slots[0].shape
-    hb, full = pieces_in[0].shape
-    n = len(pieces_in)
+    half, hb, full = halves_in[0].shape
+    n = 2 * half
     tile = min(256, tokens)
 
     def kernel(me_ref, *rest):
-        xs, w1s, w2s = rest[:nt], rest[nt : nt + n], rest[nt + n : nt + 2 * n]
+        xs, w1s, w2s = rest[:nt], rest[nt : nt + 2], rest[nt + 2 : nt + 4]
         outs = rest[-nt - 5 : -5]
         normed, total, w1, w2, sems = rest[-5:]
         step = pl.program_id(0)
 
         def fetch(piece, slot):
             return (
-                pltpu.make_async_copy(w1s[piece], w1.at[slot], sems.at[0, slot]),
-                pltpu.make_async_copy(w2s[piece], w2.at[slot], sems.at[1, slot]),
+                pltpu.make_async_copy(
+                    w1s[piece // half].at[piece % half], w1.at[slot], sems.at[0, slot]
+                ),
+                pltpu.make_async_copy(
+                    w2s[piece // half].at[piece % half], w2.at[slot], sems.at[1, slot]
+                ),
             )
 
         def start(piece):
@@ -184,8 +190,14 @@
         for copy in fetch(0, slot):
             copy.wait()
 
+        def expand(t):
+            return jnp.dot(w1[slot], normed[:, t : t + tile], preferred_element_type=f32)
+
+        ahead = expand(0)
         for t in range(0, tokens, tile):
-            x = jnp.dot(w1[slot], normed[:, t : t + tile], preferred_element_type=f32)
+            x = ahead
+            if t + tile < tokens:
+                ahead = expand(t + tile)
             h = jax.nn.gelu(x).astype(bf16)
             total[:, t : t + tile] += jnp.dot(w2[slot], h, preferred_element_type=f32)
 
@@ -201,7 +213,7 @@
         grid_spec=pltpu.PrefetchScalarGridSpec(
             num_scalar_prefetch=1,
             grid=(n,),
-            in_specs=[whole] * nt + [ANY] * (2 * n + len(deps)),
+            in_specs=[whole] * nt + [ANY] * (4 + len(deps)),
             out_specs=[whole] * nt,
             scratch_shapes=[
                 pltpu.VMEM((full, tokens), bf16),
@@ -218,7 +230,7 @@
             bytes_accessed=4 * full * hb * n + 4 * full * tokens,
             transcendentals=hb * n * tokens,
         ),
-    )(me, *slots, *pieces_in, *pieces_out, *deps)
+    )(me, *slots, *halves_in, *halves_out, *deps)
 
 
 def place(k, me, slots, result, shape):
@@ -278,27 +290,32 @@
     )(x, *deps)
 
 
-def gather_weights(ns, nt, expand_weight, reduce_weight):
-    def flip(x, axis, bit):
-        n = ns if axis == "seq" else nt
-        return lax.ppermute(x, axis, [(i, i ^ bit) for i in range(n)])
-
-    rows, full = reduce_weight.shape
-    both = jnp.stack([expand_weight.T, reduce_weight])[None]
-    bit = 2
+def flip(x, axis, n, bit):
+    return lax.ppermute(x, axis, [(i, i ^ bit) for i in range(n)])
+
+
+def gather_along(ns, both):
+    got = [flip(both, "seq", ns, 2)]
+    both = jnp.concatenate([both, got[0]])
+    bit = 4
+    if ns % 8 == 0:
+        middle = [i for i in range(ns) if ((i >> 1) ^ (i >> 2)) & 1]
+        got.append(lax.ppermute(both, "seq", [(i, i ^ 6) for i in middle]))
+        got.append(lax.ppermute(got[1], "seq", [(i, i ^ 2) for i in middle]))
+        both = jnp.concatenate([both, got[1] + got[2]])
+        bit = 8
     while bit < ns:
-        both = jnp.concatenate([both, flip(both, "seq", bit)])
+        got.append(flip(both, "seq", ns, bit))
+        both = jnp.concatenate([both, got[-1]])
         bit *= 2
-    bits = [1 << i for i in range(nt.bit_length() - 1)]
-    column = [both[:, 0].reshape(-1, full), both[:, 1].reshape(-1, full).T]
-    found = []
-    for start, order in zip(column, (bits, bits[::-1])):
-        pieces = {0: start}
-        for bit in order:
-            pieces |= {s ^ bit: flip(x, "tensor", bit) for s, x in pieces.items()}
-        found.append([pieces[s] for s in range(nt)])
-    other = [[flip(x, "seq", 1) for x in pieces] for pieces in found]
-    return both, found[0], found[1], found[0] + other[0], found[1] + other[1]
+    return both, got
+
+
+def gather_across(nt, start, order):
+    pieces = {0: start}
+    for bit in order:
+        pieces |= {s ^ bit: flip(x, "tensor", nt, bit) for s, x in pieces.items()}
+    return pieces
 
 
 def on_device(
@@ -314,59 +331,65 @@
     reduce_weight,
 ):
     c = activations.shape[0]
+    full = reduce_weight.shape[1]
     at = lax.axis_index("tensor")
     me = at.astype(jnp.int32).reshape(1)
     scale = lax.dynamic_slice_in_dim(gate_scale, at * c, c)[:, None]
     shift = lax.dynamic_slice_in_dim(gate_shift, at * c, c)[:, None]
-    both, near_in, near_out, pieces_in, pieces_out = gather_weights(
-        ns, nt, expand_weight, reduce_weight
-    )
+    both, got = gather_along(ns, jnp.stack([expand_weight.T, reduce_weight])[None])
+    bits = [1 << i for i in range(nt.bit_length() - 1)]
+    near_in = gather_across(nt, both[:, 0].reshape(-1, full), bits)
+    near_out = gather_across(nt, both[:, 1].reshape(-1, full).T, bits[::-1])
+    halves_in = [jnp.stack([near_in[s] for s in range(nt)])]
+    halves_in.append(flip(halves_in[0], "seq", ns, 1))
+    halves_out = [jnp.stack([near_out[s] for s in range(nt)])]
+    halves_out.append(flip(halves_out[0], "seq", ns, 1))
 
     def exchange(x):
         return lax.all_to_all(x, "seq", split_axis=0, concat_axis=0, tiled=True)
 
-    def first(k, dep=None):
-        return first_pass(k, activations, first_factor, spectral, ns, dep)
-
-    def second(front, deps=()):
-        blocks = front.shape[1]
-        x = front.reshape(ns * blocks, c // ns, J)
-        return second_pass(x, second_factor, list(deps)).reshape(ns, blocks, c // ns, J)
+    def first(at, n, deps=()):
+        return first_pass(at, n, activations, first_factor, spectral, ns, deps)
+
+    def second(front, m, deps=()):
+        return second_pass(front, m, second_factor, deps)
 
     def gated(k, back, deps=()):
         return gate(k, me, activations, back, scale, shift, nt, list(deps))
 
     def layer(slots, deps=()):
-        return mlp(me, slots, pieces_in, pieces_out, list(deps))
-
-    front0 = exchange(first(0))
-    front1 = exchange(first(1))
-    back0 = exchange(second(front0))
-    front2 = exchange(first(2, both))
-    back1 = exchange(second(front1))
-    sent3 = first(3, front1)
-    in0 = swap(gated(0, back0, near_in + near_out))
-    mixed2 = second(front2)
-    out0 = layer(in0, [front2])
-    front3 = exchange(after(sent3, out0[0], mixed2))
-    in1 = swap(gated(1, back1, [out0[0]]))
-    back2 = exchange(mixed2)
-    mixed3 = second(front3)
-    out1 = layer(in1, [front3])
-    back3 = exchange(after(mixed3, out1[0]))
+        return mlp(me, slots, halves_in, halves_out, list(deps))
+
+    front01 = exchange(after(first(0, 2), got[0]))
+    front23 = exchange(after(first(1, 2, [got[1]]), got[-1]))
+    mixed0 = second(front01, 0, [near_in[bits[0]], near_out[bits[-1]]])
+    mixed1 = second(front01, 1)
+    back0 = exchange(mixed0)
+    mixed2 = second(front23, 0, [halves_in[0], halves_out[0]])
+    back1 = exchange(mixed1)
+    mixed3 = second(front23, 1, [halves_in[1], halves_out[1]])
+    gate0 = gated(0, back0)
+    in0 = swap(gate0)
+    back2 = exchange(after(mixed2, gate0[0]))
+    gate1 = gated(1, back1)
+    in1 = swap(gate1)
+    out0 = layer(in0, [gate1[0]])
     done0 = swap(out0)
-    in2 = swap(gated(2, back2, [out1[0]]))
+    back3 = exchange(after(mixed3, out0[0]))
+    gate2 = gated(2, back2)
+    in2 = swap(gate2)
+    out1 = layer(in1, [gate2[0]])
     done1 = swap(out1)
-    gate3 = gated(3, back3)
+    result = place(0, me, done0, None, activations.shape)
+    gate3 = gated(3, back3, [out1[0], result])
     in3 = swap(gate3)
     out2 = layer(in2, [gate3[0]])
     done2 = swap(out2)
-    out3 = layer(in3)
+    result = place(1, me, done1, result, activations.shape)
+    out3 = layer(in3, [out2[0], result])
     done3 = swap(out3)
-    result = None
-    for k, done in enumerate((done0, done1, done2, done3)):
-        result = place(k, me, done, result, activations.shape)
-    return result
+    result = place(2, me, done2, result, activations.shape)
+    return place(3, me, done3, result, activations.shape)
 
 
 def solution(mesh):

time: 775 us -> 645 us (0.83)
  blocking collectives: 53.9 us -> 0 us
  Pallas kernels: 229 us -> 186 us
  waiting for transfers between devices: 356 us -> 326 us
  other arithmetic: 0.53 us -> 16.9 us
  starting transfers between devices: 75.9 us -> 67.7 us
    ppermute x0 -> x2, waiting for transfers between devices: none -> 148 us  [the longest x1 148 us: gather_along(): got.append(lax.ppermute(got[1], 'seq', [(i, i ^ 2) for i in middle]))]
    ppermute x16 -> x9, waiting for transfers between devices: 186 us -> 49.2 us  [flip(): return lax.ppermute(x, axis, [(i, i ^ bit) for i in range(n)])]
    all_to_all x1 -> x0, blocking collectives: 53.9 us -> none  [exchange(): return lax.all_to_all(x, 'seq', split_axis=0, concat_axis=0, tiled=True)]
    pallas_call x4, Pallas kernels: 155 us -> 125 us  [mlp(): pl.pallas_call(kernel, grid_spec=pltpu.PrefetchScalarGridSpec(num_scalar_...]
    ppermute x24, waiting for transfers between devices: 60.7 us -> 37.3 us  [swap(): lax.ppermute(slots[s], 'tensor', [(i, i ^ s) for i in range(n)])]
    all_to_all x7 -> x6, waiting for transfers between devices: 110 us -> 91.3 us  [exchange(): return lax.all_to_all(x, 'seq', split_axis=0, concat_axis=0, tiled=True)]
    another operation x0 -> x2, other arithmetic: none -> 13.2 us  [the longest x1 6.69 us: on_device(): halves_out = [jnp.stack([near_out[s] for s in range(nt)])]]
    pallas_call x4 -> x2, Pallas kernels: 28.6 us -> 15.9 us  [first_pass(): pl.pallas_call(kernel, grid=(blocks // step,), in_specs=[pl.BlockSpec((c,...]
  transfers between devices with their start and end apart: 47 -> 41, of which waited for: 14 -> 13; matrix products, arithmetic and copies ran while one was open for 1% -> 3% of each run, Pallas kernels for 29% -> 29%
where the time goes in v4:
time: 645 us; the launch traced here: 644 us
  waiting for transfers between devices  326 us (51%)
  Pallas kernels  186 us (29%)
  starting transfers between devices  67.7 us (10%)
  local copies, waits for them, and re-layouts  47 us (7%)
  other arithmetic  16.9 us (3%)
    ppermute x1, waiting for transfers between devices, gather_along(): got.append(lax.ppermute(got[1], 'seq', [(i, i ^ 2) for i in middle]))  148 us
    pallas_call x4, Pallas kernels, mlp(): pl.pallas_call(kernel, grid_spec=pltpu.PrefetchScalarGridSpec(num_scalar_...  125 us
    all_to_all x6, waiting for transfers between devices, exchange(): return lax.all_to_all(x, 'seq', split_axis=0, concat_axis=0, tiled=True)  91.3 us
    ppermute x9, waiting for transfers between devices, flip(): return lax.ppermute(x, axis, [(i, i ^ bit) for i in range(n)])  49.2 us
    unnamed x66, local copies, waits for them, and re-layouts  42.1 us
    ppermute x24, waiting for transfers between devices, swap(): lax.ppermute(slots[s], 'tensor', [(i, i ^ s) for i in range(n)])  37.3 us
    ppermute x24, starting transfers between devices, swap(): lax.ppermute(slots[s], 'tensor', [(i, i ^ s) for i in range(n)])  28.7 us
    all_to_all x6, starting transfers between devices, exchange(): return lax.all_to_all(x, 'seq', split_axis=0, concat_axis=0, tiled=True)  26.3 us
  transfers between devices with their start and end apart: 41, of which 13 were waited for; matrix products, arithmetic and copies ran while one was open for 3% of the time, Pallas kernels for 29%

profile of v4, /device:TPU:0, one launch (start us, length us, event | category | flops | bytes accessed | tf_op | source)
XLA Modules:
  0.0 643.8 jit_solution(4821914427579926782)
XLA Ops:
  1.2 3.1 collective-permute-start
  4.3 3.4 copy-done
  8.7 7.9 %shard_map.85.refs_0_ = bf16[8,2,32,32,128]{4,3,2,1,0:T(8,128)(2,1)S(1)} custom-call(bf16[256,16384]{1,0:T(8,128)(2,1)S(1)} %copy-done, bf16[512,512]{1,0:T(8,128)(2,1)S(1)} %copy-done.15, f32[256,16384]{1,0:T(8,128)} %rest_3_.7, f32[256,16384]{1,0:T(8,128)} %rest_3_.7, f32[256,16384]{1,0:T(8,128)} %rest_3_.7, f32[256,16384]{1,0:T(8,128)} %rest_3_.7), custom_call_target="tpu_custom_call" | custom-call | flops 2147483648 | bytes 20971520 | tf_op jit(solution)/shard_map/pallas_call | solution.py:40
  16.7 2.0 copy-done.9
  18.7 3.1 collective-permute-done.refs_1_
  22.7 5.2 all-to-all-start.1
  30.2 3.4 copy-done.1
  33.5 8.0 %shard_map.82.refs_0_ = bf16[8,2,32,32,128]{4,3,2,1,0:T(8,128)(2,1)S(1)} custom-call(bf16[256,16384]{1,0:T(8,128)(2,1)S(1)} %copy-done.1, bf16[512,512]{1,0:T(8,128)(2,1)S(1)} %copy-done.16, f32[256,16384]{1,0:T(8,128)} %rest_3_.7, f32[256,16384]{1,0:T(8,128)} %rest_3_.7, f32[256,16384]{1,0:T(8,128)} %rest_3_.7, f32[256,16384]{1,0:T(8,128)} %rest_3_.7, ...), custom_call_target="tpu_custom_call" | custom-call | flops 2147483648 | bytes 20971520 | tf_op jit(solution)/shard_map/pallas_call | solution.py:40
  41.5 2.0 copy-done.10
  43.5 148.2 %collective-permute-done.2.refs_1_ = bf16[2,2,192,1024]{3,2,1,0:T(8,128)(2,1)} collective-permute-done((bf16[2,2,192,1024]{3,2,1,0:T(8,128)(2,1)S(1)}, bf16[2,2,192,1024]{3,2,1,0:T(8,128)(2,1)}, u32[]{:S(2)}, u32[]{:S(2)}) %collective-permute-start.2) | collective-permute-done | bytes 1572896 | tf_op jit(solution)/shard_map/ppermute | solution.py:304
  191.7 4.6 all-to-all-start
  196.3 2.1 add.7
  198.7 1.6 fusion
  200.3 1.5 collective-permute-start.3
  201.8 1.6 copy.17
  203.3 1.5 collective-permute-start.8
  205.4 31.9 %collective-permute-done.3.rest_0_ = bf16[768,1024]{1,0:T(8,128)(2,1)} collective-permute-done((bf16[768,1024]{1,0:T(8,128)(2,1)}, bf16[768,1024]{1,0:T(8,128)(2,1)}, u32[]{:S(2)}, u32[]{:S(2)}) %collective-permute-start.3) | collective-permute-done | bytes 1572896 | tf_op jit(solution)/shard_map/ppermute | solution.py:294
  237.2 1.5 collective-permute-start.5
  241.4 4.8 shard_map.87
  247.6 42.7 %all-to-all-done.x_ref = bf16[8,2,32,32,128]{4,3,2,1,0:T(8,128)(2,1)} async-done(((bf16[8,2,32,32,128]{4,3,2,1,0:T(8,128)(2,1)}), bf16[8,2,32,32,128]{4,3,2,1,0:T(8,128)(2,1)}, u32[]{:S(2)}, u32[]{:S(2)}) %all-to-all-start) | async-done | bytes 4194336 | tf_op jit(solution)/shard_map/all_to_all | solution.py:349
  290.3 3.6 all-to-all-start.2
  293.9 13.5 %collective-permute-done.5 = bf16[768,1024]{1,0:T(8,128)(2,1)} collective-permute-done((bf16[768,1024]{1,0:T(8,128)(2,1)}, bf16[768,1024]{1,0:T(8,128)(2,1)}, u32[]{:S(2)}, u32[]{:S(2)}) %collective-permute-start.5) | collective-permute-done | bytes 1572896 | tf_op jit(solution)/shard_map/ppermute | solution.py:294
  307.4 6.5 %pad_maximum_fusion.rest_4_.rest_0_ = bf16[4,768,1024]{2,1,0:T(8,128)(2,1)} fusion(bf16[1,768,1024]{2,1,0:T(8,128)(2,1)} %bitcast.9, bf16[1,768,1024]{2,1,0:T(8,128)(2,1)} %bitcast.8, bf16[1,768,1024]{2,1,0:T(8,128)(2,1)} %bitcast.7, bf16[1,768,1024]{2,1,0:T(8,128)(2,1)} %bitcast.5), kind=kLoop, calls=%fused_computation | loop fusion | flops 9437184 | bytes 12582912 | tf_op jit(solution)/shard_map/stack | solution.py:343
  313.9 6.7 %pad_maximum_fusion.1.rest_6_.rest_1_ = bf16[4,1024,768]{2,1,0:T(8,128)(2,1)} fusion(bf16[1,1024,768]{2,1,0:T(8,128)(2,1)} %bitcast.15, bf16[1,1024,768]{2,1,0:T(8,128)(2,1)} %bitcast.14, bf16[1,1024,768]{2,1,0:T(8,128)(2,1)} %bitcast.13, bf16[1,1024,768]{2,1,0:T(8,128)(2,1)} %bitcast.12), kind=kLoop, calls=%fused_computation.1 | loop fusion | flops 9437184 | bytes 12582912 | tf_op jit(solution)/shard_map/stack | solution.py:345
  321.1 4.8 shard_map.89
  327.3 15.6 %all-to-all-done.2.rest_4_.rest_5_.rest_6_.rest_7_ = bf16[8,32,32,128]{3,2,1,0:T(8,128)(2,1)S(1)} async-done(((bf16[8,32,32,128]{3,2,1,0:T(8,128)(2,1)}), bf16[8,32,32,128]{3,2,1,0:T(8,128)(2,1)S(1)}, u32[]{:S(2)}, u32[]{:S(2)}) %all-to-all-start.2) | async-done | bytes 2097184 | tf_op jit(solution)/shard_map/all_to_all | solution.py:349
  342.9 4.4 all-to-all-start.3
  349.1 4.8 shard_map.93.refs_0_
  353.9 4.1 copy-done.2
  358.1 4.5 shard_map.88
  363.4 33.0 %all-to-all-done.3.rest_4_.rest_5_.rest_6_.rest_7_ = bf16[8,32,32,128]{3,2,1,0:T(8,128)(2,1)} async-done(((bf16[8,32,32,128]{3,2,1,0:T(8,128)(2,1)}), bf16[8,32,32,128]{3,2,1,0:T(8,128)(2,1)}, u32[]{:S(2)}, u32[]{:S(2)}) %all-to-all-start.3) | async-done | bytes 2097184 | tf_op jit(solution)/shard_map/all_to_all | solution.py:349
  396.3 3.8 all-to-all-start.5
  400.1 1.6 collective-permute-start.11
  401.7 1.5 collective-permute-start.12
  403.7 3.4 copy-done.3
  407.1 5.0 shard_map.90
  414.5 4.9 shard_map.84.refs_0_
  420.7 6.1 collective-permute-done.12.rest_2_
  426.8 31.5 %shard_map.91 = (bf16[256,1024]{1,0:T(8,128)(2,1)S(1)}, bf16[256,1024]{1,0:T(8,128)(2,1)S(1)}, bf16[256,1024]{1,0:T(8,128)(2,1)}, bf16[256,1024]{1,0:T(8,128)(2,1)}) custom-call(s32[1]{0:T(128)} %bitcast.me_ref, bf16[256,1024]{1,0:T(8,128)(2,1)S(1)} %copy-done.21, bf16[256,1024]{1,0:T(8,128)(2,1)S(1)} %collective-permute-done.11.rest_1_, ...), custom_call_target="tpu_custom_call" | custom-call | flops 25769803776 | bytes 29360128 | tf_op jit(solution)/shard_map/pallas_call | solution.py:211
  461.3 4.8 all-to-all-start.4
  471.6 3.4 copy-done.4
  475.0 1.6 copy-done.8
  476.6 4.5 shard_map.95
  482.5 11.0 %collective-permute-done.15.rest_2_ = bf16[256,1024]{1,0:T(8,128)(2,1)S(1)} collective-permute-done((bf16[256,1024]{1,0:T(8,128)(2,1)}, bf16[256,1024]{1,0:T(8,128)(2,1)S(1)}, u32[]{:S(2)}, u32[]{:S(2)}) %collective-permute-start.15) | collective-permute-done | bytes 524320 | tf_op jit(solution)/shard_map/ppermute | solution.py:279
  494.3 1.5 collective-permute-start.24
  495.8 31.3 %shard_map.96 = (bf16[256,1024]{1,0:T(8,128)(2,1)S(1)}, bf16[256,1024]{1,0:T(8,128)(2,1)}, bf16[256,1024]{1,0:T(8,128)(2,1)}, bf16[256,1024]{1,0:T(8,128)(2,1)S(1)}) custom-call(s32[1]{0:T(128)} %bitcast.me_ref, bf16[256,1024]{1,0:T(8,128)(2,1)S(1)} %get-tuple-element.41.rest_8_.rest_0_, bf16[256,1024]{1,0:T(8,128)(2,1)S(1)} %collective-permute-done.14.rest_1_, ...), custom_call_target="tpu_custom_call" | custom-call | flops 25769803776 | bytes 29360128 | tf_op jit(solution)/shard_map/pallas_call | solution.py:211
  529.2 1.6 shard_map.97.rest_11_.rest_4_
  530.8 1.6 collective-permute-start.27
  532.4 3.4 copy-done.5
  535.8 3.4 copy-done.6
  539.2 3.9 shard_map.98
  545.1 1.5 collective-permute-start.21
  546.6 6.9 %collective-permute-done.26.rest_1_ = bf16[256,1024]{1,0:T(8,128)(2,1)S(1)} collective-permute-done((bf16[256,1024]{1,0:T(8,128)(2,1)}, bf16[256,1024]{1,0:T(8,128)(2,1)S(1)}, u32[]{:S(2)}, u32[]{:S(2)}) %collective-permute-start.26) | collective-permute-done | bytes 524320 | tf_op jit(solution)/shard_map/ppermute | solution.py:279
  555.0 31.9 %shard_map.99 = (bf16[256,1024]{1,0:T(8,128)(2,1)S(1)}, bf16[256,1024]{1,0:T(8,128)(2,1)S(1)}, bf16[256,1024]{1,0:T(8,128)(2,1)S(1)}, bf16[256,1024]{1,0:T(8,128)(2,1)S(1)}) custom-call(s32[1]{0:T(128)} %bitcast.me_ref, bf16[256,1024]{1,0:T(8,128)(2,1)S(1)} %copy-done.23, bf16[256,1024]{1,0:T(8,128)(2,1)} %collective-permute-done.23.rest_1_, ...), custom_call_target="tpu_custom_call" | custom-call | flops 25769803776 | bytes 29360128 | tf_op jit(solution)/shard_map/pallas_call | solution.py:211
  587.0 1.6 collective-permute-start.32
  589.0 2.6 shard_map.100.rest_9_.rest_4_
  591.6 1.6 collective-permute-start.34
  593.2 30.4 %shard_map.101 = (bf16[256,1024]{1,0:T(8,128)(2,1)S(1)}, bf16[256,1024]{1,0:T(8,128)(2,1)S(1)}, bf16[256,1024]{1,0:T(8,128)(2,1)S(1)}, bf16[256,1024]{1,0:T(8,128)(2,1)S(1)}) custom-call(s32[1]{0:T(128)} %bitcast.me_ref, bf16[256,1024]{1,0:T(8,128)(2,1)S(1)} %get-tuple-element.51.rest_8_.rest_0_, bf16[256,1024]{1,0:T(8,128)(2,1)S(1)} %collective-permute-done.20.rest_1_, ...), custom_call_target="tpu_custom_call" | custom-call | flops 25769803776 | bytes 29360128 | tf_op jit(solution)/shard_map/pallas_call | solution.py:211
  623.7 1.6 collective-permute-start.29
  625.7 1.5 collective-permute-start.31
  627.2 1.6 shard_map.102.rest_4_
  628.8 6.8 %collective-permute-done.29.rest_1_ = bf16[256,1024]{1,0:T(8,128)(2,1)S(1)} collective-permute-done((bf16[256,1024]{1,0:T(8,128)(2,1)S(1)}, bf16[256,1024]{1,0:T(8,128)(2,1)S(1)}, u32[]{:S(2)}, u32[]{:S(2)}) %collective-permute-start.29) | collective-permute-done | bytes 524320 | tf_op jit(solution)/shard_map/ppermute | solution.py:279
  635.6 6.4 collective-permute-done.30.rest_2_
  642.1 1.6 shard_map.103
  (118 shorter events, 36.2 us)
Async XLA Ops:
  1.2 20.6 %collective-permute-start = (bf16[1,2,192,1024]{3,2,1,0:T(8,128)(2,1)S(1)}, bf16[1,2,192,1024]{3,2,1,0:T(8,128)(2,1)S(1)}, u32[]{:S(2)}, u32[]{:S(2)}) collective-permute-start(bf16[1,2,192,1024]{3,2,1,0:T(8,128)(2,1)S(1)} %maximum_bitcast_fusion), channel_id=1, source_target_pairs={{0,8},{4,12},{8,0},{12,4},{16,24},{20,28},{24,16},{28,20},{1,9},{5... | collective-permute-start | bytes 2359304 | tf_op jit(solution)/shard_map/ppermute | solution.py:294
  4.3 3.4 copy-start
  16.7 2.0 copy-start.9
  22.7 5.2 copy-start.32
  22.7 169.0 %all-to-all-start.1 = ((bf16[8,2,32,32,128]{4,3,2,1,0:T(8,128)(2,1)}), bf16[8,2,32,32,128]{4,3,2,1,0:T(8,128)(2,1)}, u32[]{:S(2)}, u32[]{:S(2)}) async-start(bf16[8,2,32,32,128]{4,3,2,1,0:T(8,128)(2,1)} %shard_map.86), calls=%async_computation.1 | async-start | bytes 8388608 | tf_op jit(solution)/shard_map/all_to_all | solution.py:349
  27.9 2.2 copy-start.16
  28.1 0.8 collective-permute-start.1
  28.8 162.9 %collective-permute-start.2 = (bf16[2,2,192,1024]{3,2,1,0:T(8,128)(2,1)S(1)}, bf16[2,2,192,1024]{3,2,1,0:T(8,128)(2,1)}, u32[]{:S(2)}, u32[]{:S(2)}) collective-permute-start(bf16[2,2,192,1024]{3,2,1,0:T(8,128)(2,1)S(1)} %collective-permute-done.1.rest_4_), channel_id=1, source_target_pairs={{8,0},{12,4},{16,24},{20,28},{9,1},{13,5},{17,25},{21,29},{10,2},{... | collective-permute-start | bytes 4718600 | tf_op jit(solution)/shard_map/ppermute | solution.py:304
  30.1 3.4 copy-start.1
  41.5 2.0 copy-start.10
  191.7 98.6 %all-to-all-start = ((bf16[8,2,32,32,128]{4,3,2,1,0:T(8,128)(2,1)}), bf16[8,2,32,32,128]{4,3,2,1,0:T(8,128)(2,1)}, u32[]{:S(2)}, u32[]{:S(2)}) async-start(bf16[8,2,32,32,128]{4,3,2,1,0:T(8,128)(2,1)} %shard_map.83), calls=%async_computation | async-start | bytes 8388608 | tf_op jit(solution)/shard_map/all_to_all | solution.py:349
  200.3 41.2 %copy-start.14 = (f32[256,256]{1,0:T(8,128)S(1)}, f32[256,256]{1,0:T(8,128)}, u32[]{:S(2)}) copy-start(f32[256,256]{1,0:T(8,128)} %s_ref.7) | copy-start | bytes 786436
  200.3 37.0 %collective-permute-start.3 = (bf16[768,1024]{1,0:T(8,128)(2,1)}, bf16[768,1024]{1,0:T(8,128)(2,1)}, u32[]{:S(2)}, u32[]{:S(2)}) collective-permute-start(bf16[768,1024]{1,0:T(8,128)(2,1)} %bitcast.6), channel_id=1, source_target_pairs={{0,1},{1,0},{2,3},{3,2},{4,5},{5,4},{6,7},{7,6},{8,9},{9,8},{10,11... | collective-permute-start | bytes 4718600 | tf_op jit(solution)/shard_map/ppermute | solution.py:294
  203.3 37.6 %collective-permute-start.8 = (bf16[1024,768]{1,0:T(8,128)(2,1)}, bf16[1024,768]{1,0:T(8,128)(2,1)}, u32[]{:S(2)}, u32[]{:S(2)}) collective-permute-start(bf16[1024,768]{1,0:T(8,128)(2,1)} %bitcast.11), channel_id=1, source_target_pairs={{0,2},{1,3},{2,0},{3,1},{4,6},{5,7},{6,4},{7,5},{8,10},{9,11},{10,... | collective-permute-start | bytes 4718600 | tf_op jit(solution)/shard_map/ppermute | solution.py:294
  204.9 89.0 %collective-permute-start.4 = (bf16[768,1024]{1,0:T(8,128)(2,1)}, bf16[768,1024]{1,0:T(8,128)(2,1)}, u32[]{:S(2)}, u32[]{:S(2)}) collective-permute-start(bf16[768,1024]{1,0:T(8,128)(2,1)} %bitcast.6), channel_id=1, source_target_pairs={{0,2},{1,3},{2,0},{3,1},{4,6},{5,7},{6,4},{7,5},{8,10},{9,11},{10,... | collective-permute-start | bytes 4718600 | tf_op jit(solution)/shard_map/ppermute | solution.py:294
  237.2 70.2 %collective-permute-start.5 = (bf16[768,1024]{1,0:T(8,128)(2,1)}, bf16[768,1024]{1,0:T(8,128)(2,1)}, u32[]{:S(2)}, u32[]{:S(2)}) collective-permute-start(bf16[768,1024]{1,0:T(8,128)(2,1)} %collective-permute-done.3.rest_0_), channel_id=1, source_target_pairs={{0,2},{1,3},{2,0},{3,1},{4,6},{5,7},{6,4},{7,5},{8,10},{9,11},{10,... | collective-permute-start | bytes 4718600 | tf_op jit(solution)/shard_map/ppermute | solution.py:294
  238.8 75.2 %collective-permute-start.7 = (bf16[1024,768]{1,0:T(8,128)(2,1)}, bf16[1024,768]{1,0:T(8,128)(2,1)}, u32[]{:S(2)}, u32[]{:S(2)}) collective-permute-start(bf16[1024,768]{1,0:T(8,128)(2,1)} %bitcast.11), channel_id=1, source_target_pairs={{0,1},{1,0},{2,3},{3,2},{4,5},{5,4},{6,7},{7,6},{8,9},{9,8},{10,11... | collective-permute-start | bytes 4718600 | tf_op jit(solution)/shard_map/ppermute | solution.py:294
  240.9 73.0 %collective-permute-start.9 = (bf16[1024,768]{1,0:T(8,128)(2,1)}, bf16[1024,768]{1,0:T(8,128)(2,1)}, u32[]{:S(2)}, u32[]{:S(2)}) collective-permute-start(bf16[1024,768]{1,0:T(8,128)(2,1)} %collective-permute-done.8.rest_1_), channel_id=1, source_target_pairs={{0,1},{1,0},{2,3},{3,2},{4,5},{5,4},{6,7},{7,6},{8,9},{9,8},{10,11... | collective-permute-start | bytes 4718600 | tf_op jit(solution)/shard_map/ppermute | solution.py:294
  290.3 52.6 %all-to-all-start.2 = ((bf16[8,32,32,128]{3,2,1,0:T(8,128)(2,1)}), bf16[8,32,32,128]{3,2,1,0:T(8,128)(2,1)S(1)}, u32[]{:S(2)}, u32[]{:S(2)}) async-start(bf16[8,32,32,128]{3,2,1,0:T(8,128)(2,1)} %copy-done.13), calls=%async_computation.2 | async-start | bytes 4194304 | tf_op jit(solution)/shard_map/all_to_all | solution.py:349
  313.9 100.6 %collective-permute-start.6 = (bf16[4,768,1024]{2,1,0:T(8,128)(2,1)}, bf16[4,768,1024]{2,1,0:T(8,128)(2,1)}, u32[]{:S(2)}, u32[]{:S(2)}) collective-permute-start(bf16[4,768,1024]{2,1,0:T(8,128)(2,1)} %pad_maximum_fusion.rest_4_.rest_0_), channel_id=1, source_target_pairs={{0,4},{4,0},{8,12},{12,8},{16,20},{20,16},{24,28},{28,24},{1,5},{5... | collective-permute-start | bytes 18874376 | tf_op jit(solution)/shard_map/ppermute | solution.py:294
  320.6 93.9 %collective-permute-start.10 = (bf16[4,1024,768]{2,1,0:T(8,128)(2,1)}, bf16[4,1024,768]{2,1,0:T(8,128)(2,1)}, u32[]{:S(2)}, u32[]{:S(2)}) collective-permute-start(bf16[4,1024,768]{2,1,0:T(8,128)(2,1)} %pad_maximum_fusion.1.rest_6_.rest_1_), channel_id=1, source_target_pairs={{0,4},{4,0},{8,12},{12,8},{16,20},{20,16},{24,28},{28,24},{1,5},{5... | collective-permute-start | bytes 18874376 | tf_op jit(solution)/shard_map/ppermute | solution.py:294
  325.9 1.3 copy-start.17
  342.9 53.4 %all-to-all-start.3 = ((bf16[8,32,32,128]{3,2,1,0:T(8,128)(2,1)}), bf16[8,32,32,128]{3,2,1,0:T(8,128)(2,1)}, u32[]{:S(2)}, u32[]{:S(2)}) async-start(bf16[8,32,32,128]{3,2,1,0:T(8,128)(2,1)} %copy-done.17), calls=%async_computation.3 | async-start | bytes 4194304 | tf_op jit(solution)/shard_map/all_to_all | solution.py:349
  353.9 8.6 %copy-start.12 = (bf16[8,32,32,128]{3,2,1,0:T(8,128)(2,1)}, bf16[8,32,32,128]{3,2,1,0:T(8,128)(2,1)S(1)}, u32[]{:S(2)}) copy-start(bf16[8,32,32,128]{3,2,1,0:T(8,128)(2,1)S(1)} %shard_map.93.refs_0_) | copy-start | bytes 6291460
  353.9 4.1 copy-start.2
  396.3 63.7 %all-to-all-start.5 = ((bf16[8,32,32,128]{3,2,1,0:T(8,128)(2,1)}), bf16[8,32,32,128]{3,2,1,0:T(8,128)(2,1)S(1)}, u32[]{:S(2)}, u32[]{:S(2)}) async-start(bf16[8,32,32,128]{3,2,1,0:T(8,128)(2,1)} %shard_map.94), calls=%async_computation.5 | async-start | bytes 4194304 | tf_op jit(solution)/shard_map/all_to_all | solution.py:349
  400.1 20.6 %collective-permute-start.11 = (bf16[256,1024]{1,0:T(8,128)(2,1)}, bf16[256,1024]{1,0:T(8,128)(2,1)S(1)}, u32[]{:S(2)}, u32[]{:S(2)}) collective-permute-start(bf16[256,1024]{1,0:T(8,128)(2,1)} %get-tuple-element.38), channel_id=1, source_target_pairs={{0,1},{1,0},{2,3},{3,2},{4,5},{5,4},{6,7},{7,6},{8,9},{9,8},{10,11... | collective-permute-start | bytes 1572872 | tf_op jit(solution)/shard_map/ppermute | solution.py:279
  401.7 25.2 %collective-permute-start.12 = (bf16[256,1024]{1,0:T(8,128)(2,1)}, bf16[256,1024]{1,0:T(8,128)(2,1)S(1)}, u32[]{:S(2)}, u32[]{:S(2)}) collective-permute-start(bf16[256,1024]{1,0:T(8,128)(2,1)} %get-tuple-element.39), channel_id=1, source_target_pairs={{0,2},{1,3},{2,0},{3,1},{4,6},{5,7},{6,4},{7,5},{8,10},{9,11},{10,... | collective-permute-start | bytes 1572872 | tf_op jit(solution)/shard_map/ppermute | solution.py:279
  403.2 23.6 %collective-permute-start.13 = (bf16[256,1024]{1,0:T(8,128)(2,1)}, bf16[256,1024]{1,0:T(8,128)(2,1)S(1)}, u32[]{:S(2)}, u32[]{:S(2)}) collective-permute-start(bf16[256,1024]{1,0:T(8,128)(2,1)} %get-tuple-element.40), channel_id=1, source_target_pairs={{0,3},{1,2},{2,1},{3,0},{4,7},{5,6},{6,5},{7,4},{8,11},{9,10},{10,... | collective-permute-start | bytes 1572872 | tf_op jit(solution)/shard_map/ppermute | solution.py:279
  403.7 3.4 copy-start.3
  414.5 12.4 %copy-start.21 = (bf16[256,1024]{1,0:T(8,128)(2,1)S(1)}, bf16[256,1024]{1,0:T(8,128)(2,1)}, u32[]{:S(2)}) copy-start(bf16[256,1024]{1,0:T(8,128)(2,1)} %copy-done.20) | copy-start | bytes 1572868
  460.0 8.2 %copy-start.27 = (bf16[256,1024]{1,0:T(8,128)(2,1)S(1)}, bf16[256,1024]{1,0:T(8,128)(2,1)}, u32[]{:S(2)}) copy-start(bf16[256,1024]{1,0:T(8,128)(2,1)} %copy-done.26) | copy-start | bytes 1572868
  460.0 1.3 copy-start.7
  461.3 71.1 %all-to-all-start.4 = ((bf16[8,32,32,128]{3,2,1,0:T(8,128)(2,1)}), bf16[8,32,32,128]{3,2,1,0:T(8,128)(2,1)S(1)}, u32[]{:S(2)}, u32[]{:S(2)}) async-start(bf16[8,32,32,128]{3,2,1,0:T(8,128)(2,1)} %shard_map.92), calls=%async_computation.4 | async-start | bytes 4194304 | tf_op jit(solution)/shard_map/all_to_all | solution.py:349
  466.1 15.0 %collective-permute-start.14 = (bf16[256,1024]{1,0:T(8,128)(2,1)}, bf16[256,1024]{1,0:T(8,128)(2,1)S(1)}, u32[]{:S(2)}, u32[]{:S(2)}) collective-permute-start(bf16[256,1024]{1,0:T(8,128)(2,1)} %copy-done.30), channel_id=1, source_target_pairs={{0,1},{1,0},{2,3},{3,2},{4,5},{5,4},{6,7},{7,6},{8,9},{9,8},{10,11... | collective-permute-start | bytes 1572872 | tf_op jit(solution)/shard_map/ppermute | solution.py:279
  467.3 26.2 %collective-permute-start.15 = (bf16[256,1024]{1,0:T(8,128)(2,1)}, bf16[256,1024]{1,0:T(8,128)(2,1)S(1)}, u32[]{:S(2)}, u32[]{:S(2)}) collective-permute-start(bf16[256,1024]{1,0:T(8,128)(2,1)} %copy-done.28), channel_id=1, source_target_pairs={{0,2},{1,3},{2,0},{3,1},{4,6},{5,7},{6,4},{7,5},{8,10},{9,11},{10,... | collective-permute-start | bytes 1572872 | tf_op jit(solution)/shard_map/ppermute | solution.py:279
  468.1 26.2 %collective-permute-start.16 = (bf16[256,1024]{1,0:T(8,128)(2,1)S(1)}, bf16[256,1024]{1,0:T(8,128)(2,1)S(1)}, u32[]{:S(2)}, u32[]{:S(2)}) collective-permute-start(bf16[256,1024]{1,0:T(8,128)(2,1)S(1)} %copy-done.27), channel_id=1, source_target_pairs={{0,3},{1,2},{2,1},{3,0},{4,7},{5,6},{6,5},{7,4},{8,11},{9,10},{10,... | collective-permute-start | bytes 1572872 | tf_op jit(solution)/shard_map/ppermute | solution.py:279
  469.6 57.6 %collective-permute-start.17 = (bf16[256,1024]{1,0:T(8,128)(2,1)}, bf16[256,1024]{1,0:T(8,128)(2,1)S(1)}, u32[]{:S(2)}, u32[]{:S(2)}) collective-permute-start(bf16[256,1024]{1,0:T(8,128)(2,1)} %copy-done.29), channel_id=1, source_target_pairs={{0,1},{1,0},{2,3},{3,2},{4,5},{5,4},{6,7},{7,6},{8,9},{9,8},{10,11... | collective-permute-start | bytes 1572872 | tf_op jit(solution)/shard_map/ppermute | solution.py:279
  470.8 57.6 %collective-permute-start.18 = (bf16[256,1024]{1,0:T(8,128)(2,1)}, bf16[256,1024]{1,0:T(8,128)(2,1)S(1)}, u32[]{:S(2)}, u32[]{:S(2)}) collective-permute-start(bf16[256,1024]{1,0:T(8,128)(2,1)} %get-tuple-element.49), channel_id=1, source_target_pairs={{0,2},{1,3},{2,0},{3,1},{4,6},{5,7},{6,4},{7,5},{8,10},{9,11},{10,... | collective-permute-start | bytes 1572872 | tf_op jit(solution)/shard_map/ppermute | solution.py:279
  471.6 3.4 copy-start.4
  475.0 1.6 copy-start.8
  481.1 46.1 %copy-start.22 = (bf16[256,1024]{1,0:T(8,128)(2,1)}, bf16[256,1024]{1,0:T(8,128)(2,1)S(1)}, u32[]{:S(2)}) copy-start(bf16[256,1024]{1,0:T(8,128)(2,1)S(1)} %get-tuple-element.46.rest_8_.rest_0_) | copy-start | bytes 1572868
  481.1 48.1 %collective-permute-start.19 = (bf16[256,1024]{1,0:T(8,128)(2,1)}, bf16[256,1024]{1,0:T(8,128)(2,1)S(1)}, u32[]{:S(2)}, u32[]{:S(2)}) collective-permute-start(bf16[256,1024]{1,0:T(8,128)(2,1)} %get-tuple-element.50), channel_id=1, source_target_pairs={{0,3},{1,2},{2,1},{3,0},{4,7},{5,6},{6,5},{7,4},{8,11},{9,10},{10,... | collective-permute-start | bytes 1572872 | tf_op jit(solution)/shard_map/ppermute | solution.py:279
  493.5 49.5 %collective-permute-start.23 = (bf16[256,1024]{1,0:T(8,128)(2,1)}, bf16[256,1024]{1,0:T(8,128)(2,1)}, u32[]{:S(2)}, u32[]{:S(2)}) collective-permute-start(bf16[256,1024]{1,0:T(8,128)(2,1)} %get-tuple-element.55), channel_id=1, source_target_pairs={{0,1},{1,0},{2,3},{3,2},{4,5},{5,4},{6,7},{7,6},{8,9},{9,8},{10,11... | collective-permute-start | bytes 1572872 | tf_op jit(solution)/shard_map/ppermute | solution.py:279
  494.3 50.0 %collective-permute-start.24 = (bf16[256,1024]{1,0:T(8,128)(2,1)}, bf16[256,1024]{1,0:T(8,128)(2,1)}, u32[]{:S(2)}, u32[]{:S(2)}) collective-permute-start(bf16[256,1024]{1,0:T(8,128)(2,1)} %get-tuple-element.56), channel_id=1, source_target_pairs={{0,2},{1,3},{2,0},{3,1},{4,6},{5,7},{6,4},{7,5},{8,10},{9,11},{10,... | collective-permute-start | bytes 1572872 | tf_op jit(solution)/shard_map/ppermute | solution.py:279
  495.8 33.4 %copy-start.19 = (bf16[256,1024]{1,0:T(8,128)(2,1)S(1)}, bf16[256,1024]{1,0:T(8,128)(2,1)}, u32[]{:S(2)}) copy-start(bf16[256,1024]{1,0:T(8,128)(2,1)} %copy-done.18) | copy-start | bytes 1572868
  527.1 3.6 copy-start.24
  527.2 18.0 %collective-permute-start.25 = (bf16[256,1024]{1,0:T(8,128)(2,1)}, bf16[256,1024]{1,0:T(8,128)(2,1)}, u32[]{:S(2)}, u32[]{:S(2)}) collective-permute-start(bf16[256,1024]{1,0:T(8,128)(2,1)} %get-tuple-element.57), channel_id=1, source_target_pairs={{0,3},{1,2},{2,1},{3,0},{4,7},{5,6},{6,5},{7,4},{8,11},{9,10},{10,... | collective-permute-start | bytes 1572872 | tf_op jit(solution)/shard_map/ppermute | solution.py:279
  528.4 25.1 %collective-permute-start.26 = (bf16[256,1024]{1,0:T(8,128)(2,1)}, bf16[256,1024]{1,0:T(8,128)(2,1)S(1)}, u32[]{:S(2)}, u32[]{:S(2)}) collective-permute-start(bf16[256,1024]{1,0:T(8,128)(2,1)} %get-tuple-element.59), channel_id=1, source_target_pairs={{0,1},{1,0},{2,3},{3,2},{4,5},{5,4},{6,7},{7,6},{8,9},{9,8},{10,11... | collective-permute-start | bytes 1572872 | tf_op jit(solution)/shard_map/ppermute | solution.py:279
  530.8 56.2 %collective-permute-start.27 = (bf16[256,1024]{1,0:T(8,128)(2,1)}, bf16[256,1024]{1,0:T(8,128)(2,1)}, u32[]{:S(2)}, u32[]{:S(2)}) collective-permute-start(bf16[256,1024]{1,0:T(8,128)(2,1)} %get-tuple-element.60), channel_id=1, source_target_pairs={{0,2},{1,3},{2,0},{3,1},{4,6},{5,7},{6,4},{7,5},{8,10},{9,11},{10,... | collective-permute-start | bytes 1572872 | tf_op jit(solution)/shard_map/ppermute | solution.py:279
  532.4 3.4 copy-start.5
  535.8 3.4 copy-start.6
  539.1 3.9 copy-start.25
  539.1 15.9 %copy-start.23 = (bf16[256,1024]{1,0:T(8,128)(2,1)S(1)}, bf16[256,1024]{1,0:T(8,128)(2,1)}, u32[]{:S(2)}) copy-start(bf16[256,1024]{1,0:T(8,128)(2,1)} %copy-done.22) | copy-start | bytes 1572868
  543.1 45.4 %collective-permute-start.28 = (bf16[256,1024]{1,0:T(8,128)(2,1)S(1)}, bf16[256,1024]{1,0:T(8,128)(2,1)S(1)}, u32[]{:S(2)}, u32[]{:S(2)}) collective-permute-start(bf16[256,1024]{1,0:T(8,128)(2,1)S(1)} %copy-done.25), channel_id=1, source_target_pairs={{0,3},{1,2},{2,1},{3,0},{4,7},{5,6},{6,5},{7,4},{8,11},{9,10},{10,... | collective-permute-start | bytes 1572872 | tf_op jit(solution)/shard_map/ppermute | solution.py:279
  544.3 47.3 %collective-permute-start.20 = (bf16[256,1024]{1,0:T(8,128)(2,1)S(1)}, bf16[256,1024]{1,0:T(8,128)(2,1)S(1)}, u32[]{:S(2)}, u32[]{:S(2)}) collective-permute-start(bf16[256,1024]{1,0:T(8,128)(2,1)S(1)} %get-tuple-element.52), channel_id=1, source_target_pairs={{0,1},{1,0},{2,3},{3,2},{4,5},{5,4},{6,7},{7,6},{8,9},{9,8},{10,11... | collective-permute-start | bytes 1572872 | tf_op jit(solution)/shard_map/ppermute | solution.py:279
  545.1 48.1 %collective-permute-start.21 = (bf16[256,1024]{1,0:T(8,128)(2,1)S(1)}, bf16[256,1024]{1,0:T(8,128)(2,1)S(1)}, u32[]{:S(2)}, u32[]{:S(2)}) collective-permute-start(bf16[256,1024]{1,0:T(8,128)(2,1)S(1)} %get-tuple-element.53), channel_id=1, source_target_pairs={{0,2},{1,3},{2,0},{3,1},{4,6},{5,7},{6,4},{7,5},{8,10},{9,11},{10,... | collective-permute-start | bytes 1572872 | tf_op jit(solution)/shard_map/ppermute | solution.py:279
  553.5 39.7 %collective-permute-start.22 = (bf16[256,1024]{1,0:T(8,128)(2,1)S(1)}, bf16[256,1024]{1,0:T(8,128)(2,1)S(1)}, u32[]{:S(2)}, u32[]{:S(2)}) collective-permute-start(bf16[256,1024]{1,0:T(8,128)(2,1)S(1)} %get-tuple-element.54), channel_id=1, source_target_pairs={{0,3},{1,2},{2,1},{3,0},{4,7},{5,6},{6,5},{7,4},{8,11},{9,10},{10,... | collective-permute-start | bytes 1572872 | tf_op jit(solution)/shard_map/ppermute | solution.py:279
  587.0 38.8 %collective-permute-start.32 = (bf16[256,1024]{1,0:T(8,128)(2,1)S(1)}, bf16[256,1024]{1,0:T(8,128)(2,1)S(1)}, u32[]{:S(2)}, u32[]{:S(2)}) collective-permute-start(bf16[256,1024]{1,0:T(8,128)(2,1)S(1)} %get-tuple-element.66), channel_id=1, source_target_pairs={{0,1},{1,0},{2,3},{3,2},{4,5},{5,4},{6,7},{7,6},{8,9},{9,8},{10,11... | collective-permute-start | bytes 1572872 | tf_op jit(solution)/shard_map/ppermute | solution.py:279
  588.5 38.7 %collective-permute-start.33 = (bf16[256,1024]{1,0:T(8,128)(2,1)S(1)}, bf16[256,1024]{1,0:T(8,128)(2,1)S(1)}, u32[]{:S(2)}, u32[]{:S(2)}) collective-permute-start(bf16[256,1024]{1,0:T(8,128)(2,1)S(1)} %get-tuple-element.67), channel_id=1, source_target_pairs={{0,2},{1,3},{2,0},{3,1},{4,6},{5,7},{6,4},{7,5},{8,10},{9,11},{10,... | collective-permute-start | bytes 1572872 | tf_op jit(solution)/shard_map/ppermute | solution.py:279
  591.6 35.6 %collective-permute-start.34 = (bf16[256,1024]{1,0:T(8,128)(2,1)S(1)}, bf16[256,1024]{1,0:T(8,128)(2,1)S(1)}, u32[]{:S(2)}, u32[]{:S(2)}) collective-permute-start(bf16[256,1024]{1,0:T(8,128)(2,1)S(1)} %get-tuple-element.68), channel_id=1, source_target_pairs={{0,3},{1,2},{2,1},{3,0},{4,7},{5,6},{6,5},{7,4},{8,11},{9,10},{10,... | collective-permute-start | bytes 1572872 | tf_op jit(solution)/shard_map/ppermute | solution.py:279
  623.7 12.0 %collective-permute-start.29 = (bf16[256,1024]{1,0:T(8,128)(2,1)S(1)}, bf16[256,1024]{1,0:T(8,128)(2,1)S(1)}, u32[]{:S(2)}, u32[]{:S(2)}) collective-permute-start(bf16[256,1024]{1,0:T(8,128)(2,1)S(1)} %get-tuple-element.63), channel_id=1, source_target_pairs={{0,1},{1,0},{2,3},{3,2},{4,5},{5,4},{6,7},{7,6},{8,9},{9,8},{10,11... | collective-permute-start | bytes 1572872 | tf_op jit(solution)/shard_map/ppermute | solution.py:279
  625.2 16.8 %collective-permute-start.30 = (bf16[256,1024]{1,0:T(8,128)(2,1)S(1)}, bf16[256,1024]{1,0:T(8,128)(2,1)S(1)}, u32[]{:S(2)}, u32[]{:S(2)}) collective-permute-start(bf16[256,1024]{1,0:T(8,128)(2,1)S(1)} %get-tuple-element.64), channel_id=1, source_target_pairs={{0,2},{1,3},{2,0},{3,1},{4,6},{5,7},{6,4},{7,5},{8,10},{9,11},{10,... | collective-permute-start | bytes 1572872 | tf_op jit(solution)/shard_map/ppermute | solution.py:279
  625.7 16.3 %collective-permute-start.31 = (bf16[256,1024]{1,0:T(8,128)(2,1)S(1)}, bf16[256,1024]{1,0:T(8,128)(2,1)S(1)}, u32[]{:S(2)}, u32[]{:S(2)}) collective-permute-start(bf16[256,1024]{1,0:T(8,128)(2,1)S(1)} %get-tuple-element.65), channel_id=1, source_target_pairs={{0,3},{1,2},{2,1},{3,0},{4,7},{5,6},{6,5},{7,4},{8,11},{9,10},{10,... | collective-permute-start | bytes 1572872 | tf_op jit(solution)/shard_map/ppermute | solution.py:279
  (10 other events, 9.4 us)

commit v5 on v4

--- a/solution.py
+++ b/solution.py
@@ -57,13 +57,14 @@
     )(activations, first_factor, *[spectral] * step, *deps)
 
 
-def second_pass(gathered, m, second_factor, deps=()):
+def second_pass(gathered, m, second_factor, groups, deps=()):
     ns, _, blocks, c, _ = gathered.shape
     a = ns * blocks
     cb = min(16, c)
+    part = blocks // groups
 
     def kernel(x_ref, s_ref, *rest):
-        out, x_wide, y_wide = rest[-3:]
+        outs, (x_wide, y_wide) = rest[-groups - 2 : -2], rest[-2:]
         x_wide[...] = x_ref[...].astype(f32).reshape(a * cb, J)
         factor = s_ref[...]
         high = factor.astype(bf16)
@@ -76,7 +77,9 @@
             y += jnp.dot(low, x, preferred_element_type=f32)
             for h in range(2):
                 y_wide[pl.ds(i + h, a, stride=cb), :] = y[:, h * J : (h + 1) * J]
-        out[...] = y_wide[...].reshape(ns, blocks, cb, J).astype(bf16)
+        y = y_wide[...].reshape(ns, blocks, cb, J)
+        for g in range(groups):
+            outs[g][...] = y[:, g * part : (g + 1) * part].astype(bf16)
 
     return pl.pallas_call(
         kernel,
@@ -86,8 +89,8 @@
             pl.BlockSpec((a, a), lambda i: (0, 0)),
         ]
         + [ANY] * len(deps),
-        out_specs=pl.BlockSpec((ns, blocks, cb, J), lambda i: (0, 0, i, 0)),
-        out_shape=jax.ShapeDtypeStruct((ns, blocks, c, J), bf16),
+        out_specs=[pl.BlockSpec((ns, part, cb, J), lambda i: (0, 0, i, 0))] * groups,
+        out_shape=[jax.ShapeDtypeStruct((ns, part, c, J), bf16)] * groups,
         scratch_shapes=[pltpu.VMEM((a * cb, J), f32), pltpu.VMEM((a * cb, J), f32)],
         compiler_params=params(32),
         cost_estimate=pl.CostEstimate(
@@ -96,12 +99,13 @@
     )(gathered, second_factor, *deps)
 
 
-def gate(k, me, activations, returned, scale, shift, nt, deps):
+def gate(k, group, me, activations, returned, scale, shift, nt, deps):
     c, tokens = activations.shape
     ns, blocks, ci, _ = returned.shape
     mine = blocks // nt
     step = min(2, mine)
     steps = mine // step
+    begin = group * blocks // step
 
     def kernel(me_ref, *rest):
         acts, rets = rest[:nt], rest[nt : 2 * nt]
@@ -115,7 +119,7 @@
                 outs[s][:, q * J : (q + 1) * J] = (x + gating * mixed).astype(bf16)
 
     def act_at(s):
-        return pl.BlockSpec((c, step * B), lambda i, me: (0, (me[0] ^ s) * steps + i))
+        return pl.BlockSpec((c, step * B), lambda i, me: (0, begin + (me[0] ^ s) * steps + i))
 
     def ret_at(s):
         return pl.BlockSpec(
@@ -233,7 +237,7 @@
     )(me, *slots, *halves_in, *halves_out, *deps)
 
 
-def place(k, me, slots, result, shape):
+def place(k, group, me, slots, result, shape):
     nt = len(slots)
     c, tokens = slots[0].shape
     mine = tokens // J
@@ -244,7 +248,8 @@
         copies = []
         for s in range(nt):
             for q in range(mine):
-                at = pl.multiple_of(((me_ref[0] ^ s) * mine + q) * B + k * J, J)
+                block = group * nt * mine + (me_ref[0] ^ s) * mine + q
+                at = pl.multiple_of(block * B + k * J, J)
                 copies.append(
                     pltpu.make_async_copy(
                         ys[s].at[:, q * J : (q + 1) * J],
@@ -351,45 +356,51 @@
     def first(at, n, deps=()):
         return first_pass(at, n, activations, first_factor, spectral, ns, deps)
 
-    def second(front, m, deps=()):
-        return second_pass(front, m, second_factor, deps)
-
-    def gated(k, back, deps=()):
-        return gate(k, me, activations, back, scale, shift, nt, list(deps))
+    def second(front, m, deps=(), groups=1):
+        return second_pass(front, m, second_factor, groups, deps)
+
+    def gated(k, back, deps=(), group=0):
+        return gate(k, group, me, activations, back, scale, shift, nt, list(deps))
 
     def layer(slots, deps=()):
         return mlp(me, slots, halves_in, halves_out, list(deps))
 
+    def put(k, done, result, group=0):
+        return place(k, group, me, done, result, activations.shape)
+
     front01 = exchange(after(first(0, 2), got[0]))
-    front23 = exchange(after(first(1, 2, [got[1]]), got[-1]))
-    mixed0 = second(front01, 0, [near_in[bits[0]], near_out[bits[-1]]])
-    mixed1 = second(front01, 1)
+    front23 = exchange(after(first(1, 2), got[1]))
+    (mixed0,) = second(front01, 0, [near_in[bits[0]], near_out[bits[-1]]])
+    (mixed1,) = second(front01, 1)
     back0 = exchange(mixed0)
-    mixed2 = second(front23, 0, [halves_in[0], halves_out[0]])
+    (mixed2,) = second(front23, 0, [halves_in[0], halves_out[0]])
     back1 = exchange(mixed1)
-    mixed3 = second(front23, 1, [halves_in[1], halves_out[1]])
-    gate0 = gated(0, back0)
-    in0 = swap(gate0)
-    back2 = exchange(after(mixed2, gate0[0]))
-    gate1 = gated(1, back1)
-    in1 = swap(gate1)
-    out0 = layer(in0, [gate1[0]])
+    mixed3 = second(front23, 1, [halves_in[1], halves_out[1]], 2)
+    in0 = swap(gated(0, back0))
+    out0 = layer(in0)
+    back2 = exchange(after(mixed2, out0[0]))
     done0 = swap(out0)
-    back3 = exchange(after(mixed3, out0[0]))
-    gate2 = gated(2, back2)
-    in2 = swap(gate2)
-    out1 = layer(in1, [gate2[0]])
+    in1 = swap(gated(1, back1))
+    out1 = layer(in1)
+    back3a = exchange(after(mixed3[0], out1[0]))
     done1 = swap(out1)
-    result = place(0, me, done0, None, activations.shape)
-    gate3 = gated(3, back3, [out1[0], result])
-    in3 = swap(gate3)
-    out2 = layer(in2, [gate3[0]])
+    result = put(0, done0, None)
+    in2 = swap(gated(2, back2, [result]))
+    back3b = exchange(after(mixed3[1], *in2[1:]))
+    gate3a = gated(3, back3a)
+    in3a = swap(gate3a)
+    out2 = layer(in2, [gate3a[0]])
     done2 = swap(out2)
-    result = place(1, me, done1, result, activations.shape)
-    out3 = layer(in3, [out2[0], result])
-    done3 = swap(out3)
-    result = place(2, me, done2, result, activations.shape)
-    return place(3, me, done3, result, activations.shape)
+    result = put(1, done1, result)
+    gate3b = gated(3, back3b, [out2[0], result], 1)
+    in3b = swap(gate3b)
+    out3a = layer(in3a, [gate3b[0]])
+    done3a = swap(out3a)
+    result = put(2, done2, result)
+    out3b = layer(in3b, [out3a[0], result])
+    done3b = swap(out3b)
+    result = put(3, done3a, result)
+    return put(3, done3b, result, 1)
 
 
 def solution(mesh):

time: 645 us -> 757 us (1.17)
  starting transfers between devices: 67.7 us -> 141 us
  local copies, waits for them, and re-layouts: 47 us -> 66.4 us
  waiting for transfers between devices: 326 us -> 338 us
    ppermute x1, waiting for transfers between devices: 148 us -> 36.8 us  [gather_along(): got.append(lax.ppermute(got[1], 'seq', [(i, i ^ 2) for i in middle]))]
    all_to_all x6 -> x7, starting transfers between devices: 26.3 us -> 89.9 us  [exchange(): return lax.all_to_all(x, 'seq', split_axis=0, concat_axis=0, tiled=True)]
    ppermute x24 -> x30, waiting for transfers between devices: 37.3 us -> 84.4 us  [swap(): lax.ppermute(slots[s], 'tensor', [(i, i ^ s) for i in range(n)])]
    ppermute x9, waiting for transfers between devices: 49.2 us -> 95.9 us  [flip(): return lax.ppermute(x, axis, [(i, i ^ bit) for i in range(n)])]
    all_to_all x6 -> x7, waiting for transfers between devices: 91.3 us -> 121 us  [exchange(): return lax.all_to_all(x, 'seq', split_axis=0, concat_axis=0, tiled=True)]
    unnamed x66 -> x88, local copies, waits for them, and re-layouts: 42.1 us -> 60.8 us
    ppermute x24 -> x30, starting transfers between devices: 28.7 us -> 36 us  [swap(): lax.ppermute(slots[s], 'tensor', [(i, i ^ s) for i in range(n)])]
    pallas_call x4 -> x5, Pallas kernels: 125 us -> 130 us  [mlp(): pl.pallas_call(kernel, grid_spec=pltpu.PrefetchScalarGridSpec(num_scalar_...]
  transfers between devices with their start and end apart: 41 -> 48, of which waited for: 13 -> 22; matrix products, arithmetic and copies ran while one was open for 3% -> 2% of each run, Pallas kernels for 29% -> 25%
where the time goes in v5:
time: 757 us; the launch traced here: 749 us
  waiting for transfers between devices  338 us (45%)
  Pallas kernels  190 us (25%)
  starting transfers between devices  141 us (19%)
  local copies, waits for them, and re-layouts  66.4 us (9%)
  other arithmetic  12.6 us (2%)
    pallas_call x5, Pallas kernels, mlp(): pl.pallas_call(kernel, grid_spec=pltpu.PrefetchScalarGridSpec(num_scalar_...  130 us
    all_to_all x7, waiting for transfers between devices, exchange(): return lax.all_to_all(x, 'seq', split_axis=0, concat_axis=0, tiled=True)  121 us
    ppermute x9, waiting for transfers between devices, flip(): return lax.ppermute(x, axis, [(i, i ^ bit) for i in range(n)])  95.9 us
    all_to_all x7, starting transfers between devices, exchange(): return lax.all_to_all(x, 'seq', split_axis=0, concat_axis=0, tiled=True)  89.9 us
    ppermute x30, waiting for transfers between devices, swap(): lax.ppermute(slots[s], 'tensor', [(i, i ^ s) for i in range(n)])  84.4 us
    unnamed x88, local copies, waits for them, and re-layouts  60.8 us
    ppermute x1, waiting for transfers between devices, gather_along(): got.append(lax.ppermute(got[1], 'seq', [(i, i ^ 2) for i in middle]))  36.8 us
    ppermute x30, starting transfers between devices, swap(): lax.ppermute(slots[s], 'tensor', [(i, i ^ s) for i in range(n)])  36 us
  transfers between devices with their start and end apart: 48, of which 22 were waited for; matrix products, arithmetic and copies ran while one was open for 2% of the time, Pallas kernels for 25%

profile of v5, /device:TPU:0, one launch (start us, length us, event | category | flops | bytes accessed | tf_op | source)
XLA Modules:
  0.0 748.8 jit_solution(9950738974267495977)
XLA Ops:
  1.2 3.1 collective-permute-start
  4.3 3.4 copy-done
  8.7 7.9 %shard_map.86.refs_0_ = bf16[8,2,32,32,128]{4,3,2,1,0:T(8,128)(2,1)S(1)} custom-call(bf16[256,16384]{1,0:T(8,128)(2,1)S(1)} %copy-done, bf16[512,512]{1,0:T(8,128)(2,1)S(1)} %copy-done.20, f32[256,16384]{1,0:T(8,128)} %rest_3_.8, f32[256,16384]{1,0:T(8,128)} %rest_3_.8, f32[256,16384]{1,0:T(8,128)} %rest_3_.8, f32[256,16384]{1,0:T(8,128)} %rest_3_.8), custom_call_target="tpu_custom_call" | custom-call | flops 2147483648 | bytes 20971520 | tf_op jit(solution)/shard_map/pallas_call | solution.py:40
  16.7 2.0 copy-done.13
  18.7 3.1 collective-permute-done.refs_1_
  22.7 5.2 all-to-all-start.1
  28.1 1.8 collective-permute-start.1
  31.2 3.4 copy-done.1
  34.6 8.0 %shard_map.82.refs_0_ = bf16[8,2,32,32,128]{4,3,2,1,0:T(8,128)(2,1)S(1)} custom-call(bf16[256,16384]{1,0:T(8,128)(2,1)S(1)} %copy-done.1, bf16[512,512]{1,0:T(8,128)(2,1)S(1)} %copy-done.21, f32[256,16384]{1,0:T(8,128)} %rest_3_.8, f32[256,16384]{1,0:T(8,128)} %rest_3_.8, f32[256,16384]{1,0:T(8,128)} %rest_3_.8, f32[256,16384]{1,0:T(8,128)} %rest_3_.8), custom_call_target="tpu_custom_call" | custom-call | flops 2147483648 | bytes 20971520 | tf_op jit(solution)/shard_map/pallas_call | solution.py:40
  42.6 2.0 copy-done.14
  44.6 77.9 %all-to-all-done.1.x_ref = bf16[8,2,32,32,128]{4,3,2,1,0:T(8,128)(2,1)} async-done(((bf16[8,2,32,32,128]{4,3,2,1,0:T(8,128)(2,1)}), bf16[8,2,32,32,128]{4,3,2,1,0:T(8,128)(2,1)}, u32[]{:S(2)}, u32[]{:S(2)}) %all-to-all-start.1) | async-done | bytes 4194336 | tf_op jit(solution)/shard_map/all_to_all | solution.py:354
  122.5 49.8 %all-to-all-start = ((bf16[8,2,32,32,128]{4,3,2,1,0:T(8,128)(2,1)}), bf16[8,2,32,32,128]{4,3,2,1,0:T(8,128)(2,1)}, u32[]{:S(2)}, u32[]{:S(2)}) async-start(bf16[8,2,32,32,128]{4,3,2,1,0:T(8,128)(2,1)} %shard_map.83), calls=%async_computation | async-start | bytes 8388608 | tf_op jit(solution)/shard_map/all_to_all | solution.py:354
  172.3 36.8 %collective-permute-done.2 = bf16[2,2,192,1024]{3,2,1,0:T(8,128)(2,1)S(1)} collective-permute-done((bf16[2,2,192,1024]{3,2,1,0:T(8,128)(2,1)}, bf16[2,2,192,1024]{3,2,1,0:T(8,128)(2,1)S(1)}, u32[]{:S(2)}, u32[]{:S(2)}) %collective-permute-start.2) | collective-permute-done | bytes 1572896 | tf_op jit(solution)/shard_map/ppermute | solution.py:309
  209.1 2.1 add.7
  211.5 2.1 fusion
  215.0 1.7 copy.19
  218.8 28.1 %collective-permute-done.3.rest_0_ = bf16[768,1024]{1,0:T(8,128)(2,1)S(1)} collective-permute-done((bf16[768,1024]{1,0:T(8,128)(2,1)}, bf16[768,1024]{1,0:T(8,128)(2,1)S(1)}, u32[]{:S(2)}, u32[]{:S(2)}) %collective-permute-start.3) | collective-permute-done | bytes 1572896 | tf_op jit(solution)/shard_map/ppermute | solution.py:299
  247.0 2.5 collective-permute-start.5
  251.0 3.2 collective-permute-done.8.rest_1_
  254.7 33.2 %collective-permute-done.4 = bf16[768,1024]{1,0:T(8,128)(2,1)S(1)} collective-permute-done((bf16[768,1024]{1,0:T(8,128)(2,1)}, bf16[768,1024]{1,0:T(8,128)(2,1)S(1)}, u32[]{:S(2)}, u32[]{:S(2)}) %collective-permute-start.4) | collective-permute-done | bytes 1572896 | tf_op jit(solution)/shard_map/ppermute | solution.py:299
  287.9 28.3 %collective-permute-done.5 = bf16[768,1024]{1,0:T(8,128)(2,1)S(1)} collective-permute-done((bf16[768,1024]{1,0:T(8,128)(2,1)S(1)}, bf16[768,1024]{1,0:T(8,128)(2,1)S(1)}, u32[]{:S(2)}, u32[]{:S(2)}) %collective-permute-start.5) | collective-permute-done | bytes 1572896 | tf_op jit(solution)/shard_map/ppermute | solution.py:299
  316.1 4.3 pad_maximum_fusion.rest_0_.rest_4_
  320.5 4.5 pad_maximum_fusion.1.rest_1_.rest_6_
  325.5 4.8 shard_map.88
  331.7 16.3 %all-to-all-start.2 = ((bf16[8,32,32,128]{3,2,1,0:T(8,128)(2,1)}), bf16[8,32,32,128]{3,2,1,0:T(8,128)(2,1)S(1)}, u32[]{:S(2)}, u32[]{:S(2)}) async-start(bf16[8,32,32,128]{3,2,1,0:T(8,128)(2,1)} %copy-done.16), calls=%async_computation.2 | async-start | bytes 4194304 | tf_op jit(solution)/shard_map/all_to_all | solution.py:354
  348.0 4.8 shard_map.95
  354.2 42.9 %all-to-all-done.2.rest_4_.rest_5_.rest_6_.rest_7_ = bf16[8,32,32,128]{3,2,1,0:T(8,128)(2,1)S(1)} async-done(((bf16[8,32,32,128]{3,2,1,0:T(8,128)(2,1)}), bf16[8,32,32,128]{3,2,1,0:T(8,128)(2,1)S(1)}, u32[]{:S(2)}, u32[]{:S(2)}) %all-to-all-start.2) | async-done | bytes 2097184 | tf_op jit(solution)/shard_map/all_to_all | solution.py:354
  398.4 3.8 all-to-all-start.5
  404.0 3.4 copy-done.2
  409.0 3.9 shard_map.89
  416.4 4.8 shard_map.85.refs_0_
  422.6 5.1 collective-permute-done.11.rest_1_
  427.7 10.1 %collective-permute-done.12.rest_2_ = bf16[256,1024]{1,0:T(8,128)(2,1)S(1)} collective-permute-done((bf16[256,1024]{1,0:T(8,128)(2,1)S(1)}, bf16[256,1024]{1,0:T(8,128)(2,1)S(1)}, u32[]{:S(2)}, u32[]{:S(2)}) %collective-permute-start.12) | collective-permute-done | bytes 524320 | tf_op jit(solution)/shard_map/ppermute | solution.py:284
  439.4 30.4 %shard_map.90 = (bf16[256,1024]{1,0:T(8,128)(2,1)S(1)}, bf16[256,1024]{1,0:T(8,128)(2,1)S(1)}, bf16[256,1024]{1,0:T(8,128)(2,1)S(1)}, bf16[256,1024]{1,0:T(8,128)(2,1)S(1)}) custom-call(s32[1]{0:T(128)} %bitcast.me_ref, bf16[256,1024]{1,0:T(8,128)(2,1)S(1)} %get-tuple-element.48.rest_0_, bf16[256,1024]{1,0:T(8,128)(2,1)S(1)} %collective-permute-done.11.rest_1_, ...), custom_call_target="tpu_custom_call" | custom-call | flops 25769803776 | bytes 29360128 | tf_op jit(solution)/shard_map/pallas_call | solution.py:215
  474.4 5.0 all-to-all-start.3
  479.4 3.4 copy-done.3
  484.4 3.9 shard_map.96
  491.9 4.8 shard_map.84
  498.6 4.5 collective-permute-done.20.rest_1_
  503.1 11.4 %collective-permute-done.21.rest_2_ = bf16[256,1024]{1,0:T(8,128)(2,1)S(1)} collective-permute-done((bf16[256,1024]{1,0:T(8,128)(2,1)S(1)}, bf16[256,1024]{1,0:T(8,128)(2,1)S(1)}, u32[]{:S(2)}, u32[]{:S(2)}) %collective-permute-start.21) | collective-permute-done | bytes 524320 | tf_op jit(solution)/shard_map/ppermute | solution.py:284
  514.5 31.6 %shard_map.97 = (bf16[256,1024]{1,0:T(8,128)(2,1)S(1)}, bf16[256,1024]{1,0:T(8,128)(2,1)}, bf16[256,1024]{1,0:T(8,128)(2,1)}, bf16[256,1024]{1,0:T(8,128)(2,1)}) custom-call(s32[1]{0:T(128)} %bitcast.me_ref, bf16[256,1024]{1,0:T(8,128)(2,1)S(1)} %get-tuple-element.61.rest_0_, bf16[256,1024]{1,0:T(8,128)(2,1)S(1)} %collective-permute-done.20.rest_1_, ...), custom_call_target="tpu_custom_call" | custom-call | flops 25769803776 | bytes 29360128 | tf_op jit(solution)/shard_map/pallas_call | solution.py:215
  546.9 4.7 all-to-all-start.6
  555.2 11.4 %collective-permute-done.14.rest_1_ = bf16[256,1024]{1,0:T(8,128)(2,1)S(1)} collective-permute-done((bf16[256,1024]{1,0:T(8,128)(2,1)}, bf16[256,1024]{1,0:T(8,128)(2,1)S(1)}, u32[]{:S(2)}, u32[]{:S(2)}) %collective-permute-start.14) | collective-permute-done | bytes 524320 | tf_op jit(solution)/shard_map/ppermute | solution.py:284
  566.6 10.3 %collective-permute-done.15.rest_2_ = bf16[256,1024]{1,0:T(8,128)(2,1)S(1)} collective-permute-done((bf16[256,1024]{1,0:T(8,128)(2,1)}, bf16[256,1024]{1,0:T(8,128)(2,1)S(1)}, u32[]{:S(2)}, u32[]{:S(2)}) %collective-permute-start.15) | collective-permute-done | bytes 524320 | tf_op jit(solution)/shard_map/ppermute | solution.py:284
  581.0 3.4 copy-done.4
  584.4 3.4 copy-done.7
  587.8 4.5 shard_map.93
  598.9 3.4 copy-done.5
  602.3 2.6 shard_map.99
  605.6 2.5 collective-permute-done.17.refs_1_.rest_1_
  608.1 1.8 collective-permute-start.25
  609.9 10.3 %collective-permute-done.18.refs_2_.rest_2_ = bf16[256,1024]{1,0:T(8,128)(2,1)S(1)} collective-permute-done((bf16[256,1024]{1,0:T(8,128)(2,1)}, bf16[256,1024]{1,0:T(8,128)(2,1)S(1)}, u32[]{:S(2)}, u32[]{:S(2)}) %collective-permute-start.18) | collective-permute-done | bytes 524320 | tf_op jit(solution)/shard_map/ppermute | solution.py:284
  621.2 5.0 all-to-all-start.4
  631.3 31.3 %shard_map.100 = (bf16[256,1024]{1,0:T(8,128)(2,1)S(1)}, bf16[256,1024]{1,0:T(8,128)(2,1)}, bf16[256,1024]{1,0:T(8,128)(2,1)}, bf16[256,1024]{1,0:T(8,128)(2,1)S(1)}) custom-call(s32[1]{0:T(128)} %bitcast.me_ref, bf16[256,1024]{1,0:T(8,128)(2,1)S(1)} %copy-done.37, bf16[256,1024]{1,0:T(8,128)(2,1)S(1)} %copy-done.28, bf16[256,1024]{1,0:T(8,128)(2,1)S(1)} %copy-done.30, ...), custom_call_target="tpu_custom_call" | custom-call | flops 25769803776 | bytes 29360128 | tf_op jit(solution)/shard_map/pallas_call | solution.py:215
  667.4 2.8 shard_map.101.rest_11_.rest_4_
  671.1 3.4 copy-done.6
  674.5 3.4 copy-done.8
  677.9 2.0 shard_map.102
  679.8 3.5 collective-permute-done.29.rest_1_
  686.3 3.7 collective-permute-done.31.rest_3_
  692.0 19.0 %shard_map.103 = (bf16[256,512]{1,0:T(8,128)(2,1)S(1)}, bf16[256,512]{1,0:T(8,128)(2,1)S(1)}, bf16[256,512]{1,0:T(8,128)(2,1)S(1)}, bf16[256,512]{1,0:T(8,128)(2,1)S(1)}) custom-call(s32[1]{0:T(128)} %bitcast.me_ref, bf16[256,512]{1,0:T(8,128)(2,1)S(1)} %copy-done.40, bf16[256,512]{1,0:T(8,128)(2,1)} %collective-permute-done.29.rest_1_, ...), custom_call_target="tpu_custom_call" | custom-call | flops 12884901888 | bytes 27262976 | tf_op jit(solution)/shard_map/pallas_call | solution.py:215
  716.3 17.9 %shard_map.105 = (bf16[256,512]{1,0:T(8,128)(2,1)S(1)}, bf16[256,512]{1,0:T(8,128)(2,1)S(1)}, bf16[256,512]{1,0:T(8,128)(2,1)S(1)}, bf16[256,512]{1,0:T(8,128)(2,1)S(1)}) custom-call(s32[1]{0:T(128)} %bitcast.me_ref, bf16[256,512]{1,0:T(8,128)(2,1)S(1)} %get-tuple-element.71.rest_8_.rest_0_, bf16[256,512]{1,0:T(8,128)(2,1)S(1)} %collective-permute-done.26.rest_1_, ...), custom_call_target="tpu_custom_call" | custom-call | flops 12884901888 | bytes 27262976 | tf_op jit(solution)/shard_map/pallas_call | solution.py:215
  738.9 4.4 collective-permute-done.35.rest_1_
  743.2 4.0 collective-permute-done.36.rest_2_
  (158 shorter events, 80.0 us)
Async XLA Ops:
  1.2 20.6 %collective-permute-start = (bf16[1,2,192,1024]{3,2,1,0:T(8,128)(2,1)S(1)}, bf16[1,2,192,1024]{3,2,1,0:T(8,128)(2,1)S(1)}, u32[]{:S(2)}, u32[]{:S(2)}) collective-permute-start(bf16[1,2,192,1024]{3,2,1,0:T(8,128)(2,1)S(1)} %maximum_bitcast_fusion), channel_id=1, source_target_pairs={{0,8},{4,12},{8,0},{12,4},{16,24},{20,28},{24,16},{28,20},{1,9},{5... | collective-permute-start | bytes 2359304 | tf_op jit(solution)/shard_map/ppermute | solution.py:299
  4.3 3.4 copy-start
  22.7 5.2 copy-start.42
  22.7 99.8 %all-to-all-start.1 = ((bf16[8,2,32,32,128]{4,3,2,1,0:T(8,128)(2,1)}), bf16[8,2,32,32,128]{4,3,2,1,0:T(8,128)(2,1)}, u32[]{:S(2)}, u32[]{:S(2)}) async-start(bf16[8,2,32,32,128]{4,3,2,1,0:T(8,128)(2,1)} %shard_map.87), calls=%async_computation.1 | async-start | bytes 8388608 | tf_op jit(solution)/shard_map/all_to_all | solution.py:354
  27.9 3.3 copy-start.21
  28.1 1.8 collective-permute-start.1
  29.9 179.2 %collective-permute-start.2 = (bf16[2,2,192,1024]{3,2,1,0:T(8,128)(2,1)}, bf16[2,2,192,1024]{3,2,1,0:T(8,128)(2,1)S(1)}, u32[]{:S(2)}, u32[]{:S(2)}) collective-permute-start(bf16[2,2,192,1024]{3,2,1,0:T(8,128)(2,1)} %collective-permute-done.1.refs_1_), channel_id=1, source_target_pairs={{8,0},{12,4},{16,24},{20,28},{9,1},{13,5},{17,25},{21,29},{10,2},{... | collective-permute-start | bytes 4718600 | tf_op jit(solution)/shard_map/ppermute | solution.py:309
  31.2 3.4 copy-start.1
  122.5 209.2 %all-to-all-start = ((bf16[8,2,32,32,128]{4,3,2,1,0:T(8,128)(2,1)}), bf16[8,2,32,32,128]{4,3,2,1,0:T(8,128)(2,1)}, u32[]{:S(2)}, u32[]{:S(2)}) async-start(bf16[8,2,32,32,128]{4,3,2,1,0:T(8,128)(2,1)} %shard_map.83), calls=%async_computation | async-start | bytes 8388608 | tf_op jit(solution)/shard_map/all_to_all | solution.py:354
  213.5 33.4 %collective-permute-start.3 = (bf16[768,1024]{1,0:T(8,128)(2,1)}, bf16[768,1024]{1,0:T(8,128)(2,1)S(1)}, u32[]{:S(2)}, u32[]{:S(2)}) collective-permute-start(bf16[768,1024]{1,0:T(8,128)(2,1)} %bitcast.6), channel_id=1, source_target_pairs={{0,1},{1,0},{2,3},{3,2},{4,5},{5,4},{6,7},{7,6},{8,9},{9,8},{10,11... | collective-permute-start | bytes 4718600 | tf_op jit(solution)/shard_map/ppermute | solution.py:299
  216.7 103.7 %copy-start.43 = (bf16[768,1024]{0,1:T(8,128)(2,1)}, bf16[768,1024]{0,1:T(8,128)(2,1)S(1)}, u32[]{:S(2)}) copy-start(bf16[768,1024]{0,1:T(8,128)(2,1)S(1)} %copy.19) | copy-start | bytes 4718596
  216.8 37.4 %collective-permute-start.8 = (bf16[1024,768]{1,0:T(8,128)(2,1)S(1)}, bf16[1024,768]{1,0:T(8,128)(2,1)S(1)}, u32[]{:S(2)}, u32[]{:S(2)}) collective-permute-start(bf16[1024,768]{1,0:T(8,128)(2,1)S(1)} %bitcast.23), channel_id=1, source_target_pairs={{0,2},{1,3},{2,0},{3,1},{4,6},{5,7},{6,4},{7,5},{8,10},{9,11},{10,... | collective-permute-start | bytes 4718600 | tf_op jit(solution)/shard_map/ppermute | solution.py:299
  218.3 69.5 %collective-permute-start.4 = (bf16[768,1024]{1,0:T(8,128)(2,1)}, bf16[768,1024]{1,0:T(8,128)(2,1)S(1)}, u32[]{:S(2)}, u32[]{:S(2)}) collective-permute-start(bf16[768,1024]{1,0:T(8,128)(2,1)} %bitcast.6), channel_id=1, source_target_pairs={{0,2},{1,3},{2,0},{3,1},{4,6},{5,7},{6,4},{7,5},{8,10},{9,11},{10,... | collective-permute-start | bytes 4718600 | tf_op jit(solution)/shard_map/ppermute | solution.py:299
  247.0 69.2 %collective-permute-start.5 = (bf16[768,1024]{1,0:T(8,128)(2,1)S(1)}, bf16[768,1024]{1,0:T(8,128)(2,1)S(1)}, u32[]{:S(2)}, u32[]{:S(2)}) collective-permute-start(bf16[768,1024]{1,0:T(8,128)(2,1)S(1)} %collective-permute-done.3.rest_0_), channel_id=1, source_target_pairs={{0,2},{1,3},{2,0},{3,1},{4,6},{5,7},{6,4},{7,5},{8,10},{9,11},{10,... | collective-permute-start | bytes 4718600 | tf_op jit(solution)/shard_map/ppermute | solution.py:299
  249.5 71.0 %collective-permute-start.7 = (bf16[1024,768]{1,0:T(8,128)(2,1)S(1)}, bf16[1024,768]{1,0:T(8,128)(2,1)S(1)}, u32[]{:S(2)}, u32[]{:S(2)}) collective-permute-start(bf16[1024,768]{1,0:T(8,128)(2,1)S(1)} %bitcast.24), channel_id=1, source_target_pairs={{0,1},{1,0},{2,3},{3,2},{4,5},{5,4},{6,7},{7,6},{8,9},{9,8},{10,11... | collective-permute-start | bytes 4718600 | tf_op jit(solution)/shard_map/ppermute | solution.py:299
  254.1 66.3 %collective-permute-start.9 = (bf16[1024,768]{1,0:T(8,128)(2,1)S(1)}, bf16[1024,768]{1,0:T(8,128)(2,1)S(1)}, u32[]{:S(2)}, u32[]{:S(2)}) collective-permute-start(bf16[1024,768]{1,0:T(8,128)(2,1)S(1)} %collective-permute-done.8.rest_1_), channel_id=1, source_target_pairs={{0,1},{1,0},{2,3},{3,2},{4,5},{5,4},{6,7},{7,6},{8,9},{9,8},{10,11... | collective-permute-start | bytes 4718600 | tf_op jit(solution)/shard_map/ppermute | solution.py:299
  320.5 119.0 %collective-permute-start.6 = (bf16[4,768,1024]{2,1,0:T(8,128)(2,1)}, bf16[4,768,1024]{2,1,0:T(8,128)(2,1)}, u32[]{:S(2)}, u32[]{:S(2)}) collective-permute-start(bf16[4,768,1024]{2,1,0:T(8,128)(2,1)} %pad_maximum_fusion.rest_0_.rest_4_), channel_id=1, source_target_pairs={{0,4},{4,0},{8,12},{12,8},{16,20},{20,16},{24,28},{28,24},{1,5},{5... | collective-permute-start | bytes 18874376 | tf_op jit(solution)/shard_map/ppermute | solution.py:299
  320.5 5.1 copy-start.19
  325.0 114.4 %collective-permute-start.10 = (bf16[4,1024,768]{2,1,0:T(8,128)(2,1)}, bf16[4,1024,768]{2,1,0:T(8,128)(2,1)}, u32[]{:S(2)}, u32[]{:S(2)}) collective-permute-start(bf16[4,1024,768]{2,1,0:T(8,128)(2,1)} %pad_maximum_fusion.1.rest_1_.rest_6_), channel_id=1, source_target_pairs={{0,4},{4,0},{8,12},{12,8},{16,20},{20,16},{24,28},{28,24},{1,5},{5... | collective-permute-start | bytes 18874376 | tf_op jit(solution)/shard_map/ppermute | solution.py:299
  331.7 65.4 %all-to-all-start.2 = ((bf16[8,32,32,128]{3,2,1,0:T(8,128)(2,1)}), bf16[8,32,32,128]{3,2,1,0:T(8,128)(2,1)S(1)}, u32[]{:S(2)}, u32[]{:S(2)}) async-start(bf16[8,32,32,128]{3,2,1,0:T(8,128)(2,1)} %copy-done.16), calls=%async_computation.2 | async-start | bytes 4194304 | tf_op jit(solution)/shard_map/all_to_all | solution.py:354
  398.4 74.7 %all-to-all-start.5 = ((bf16[8,32,32,128]{3,2,1,0:T(8,128)(2,1)}), bf16[8,32,32,128]{3,2,1,0:T(8,128)(2,1)S(1)}, u32[]{:S(2)}, u32[]{:S(2)}) async-start(bf16[8,32,32,128]{3,2,1,0:T(8,128)(2,1)} %copy-done.24), calls=%async_computation.5 | async-start | bytes 4194304 | tf_op jit(solution)/shard_map/all_to_all | solution.py:354
  404.0 3.4 copy-start.2
  412.9 14.8 %collective-permute-start.11 = (bf16[256,1024]{1,0:T(8,128)(2,1)S(1)}, bf16[256,1024]{1,0:T(8,128)(2,1)S(1)}, u32[]{:S(2)}, u32[]{:S(2)}) collective-permute-start(bf16[256,1024]{1,0:T(8,128)(2,1)S(1)} %get-tuple-element.49), channel_id=1, source_target_pairs={{0,1},{1,0},{2,3},{3,2},{4,5},{5,4},{6,7},{7,6},{8,9},{9,8},{10,11... | collective-permute-start | bytes 1572872 | tf_op jit(solution)/shard_map/ppermute | solution.py:284
  413.5 24.3 %collective-permute-start.12 = (bf16[256,1024]{1,0:T(8,128)(2,1)S(1)}, bf16[256,1024]{1,0:T(8,128)(2,1)S(1)}, u32[]{:S(2)}, u32[]{:S(2)}) collective-permute-start(bf16[256,1024]{1,0:T(8,128)(2,1)S(1)} %get-tuple-element.50), channel_id=1, source_target_pairs={{0,2},{1,3},{2,0},{3,1},{4,6},{5,7},{6,4},{7,5},{8,10},{9,11},{10,... | collective-permute-start | bytes 1572872 | tf_op jit(solution)/shard_map/ppermute | solution.py:284
  415.0 24.4 %collective-permute-start.13 = (bf16[256,1024]{1,0:T(8,128)(2,1)S(1)}, bf16[256,1024]{1,0:T(8,128)(2,1)S(1)}, u32[]{:S(2)}, u32[]{:S(2)}) collective-permute-start(bf16[256,1024]{1,0:T(8,128)(2,1)S(1)} %get-tuple-element.51), channel_id=1, source_target_pairs={{0,3},{1,2},{2,1},{3,0},{4,7},{5,6},{6,5},{7,4},{8,11},{9,10},{10,... | collective-permute-start | bytes 1572872 | tf_op jit(solution)/shard_map/ppermute | solution.py:284
  474.4 72.5 %all-to-all-start.3 = ((bf16[8,32,32,128]{3,2,1,0:T(8,128)(2,1)}), bf16[8,32,32,128]{3,2,1,0:T(8,128)(2,1)S(1)}, u32[]{:S(2)}, u32[]{:S(2)}) async-start(bf16[8,32,32,128]{3,2,1,0:T(8,128)(2,1)} %shard_map.91), calls=%async_computation.3 | async-start | bytes 4194304 | tf_op jit(solution)/shard_map/all_to_all | solution.py:354
  479.4 3.4 copy-start.3
  488.3 14.8 %collective-permute-start.20 = (bf16[256,1024]{1,0:T(8,128)(2,1)S(1)}, bf16[256,1024]{1,0:T(8,128)(2,1)S(1)}, u32[]{:S(2)}, u32[]{:S(2)}) collective-permute-start(bf16[256,1024]{1,0:T(8,128)(2,1)S(1)} %get-tuple-element.62), channel_id=1, source_target_pairs={{0,1},{1,0},{2,3},{3,2},{4,5},{5,4},{6,7},{7,6},{8,9},{9,8},{10,11... | collective-permute-start | bytes 1572872 | tf_op jit(solution)/shard_map/ppermute | solution.py:284
  489.2 25.3 %collective-permute-start.21 = (bf16[256,1024]{1,0:T(8,128)(2,1)S(1)}, bf16[256,1024]{1,0:T(8,128)(2,1)S(1)}, u32[]{:S(2)}, u32[]{:S(2)}) collective-permute-start(bf16[256,1024]{1,0:T(8,128)(2,1)S(1)} %get-tuple-element.63), channel_id=1, source_target_pairs={{0,2},{1,3},{2,0},{3,1},{4,6},{5,7},{6,4},{7,5},{8,10},{9,11},{10,... | collective-permute-start | bytes 1572872 | tf_op jit(solution)/shard_map/ppermute | solution.py:284
  490.7 23.8 %collective-permute-start.22 = (bf16[256,1024]{1,0:T(8,128)(2,1)S(1)}, bf16[256,1024]{1,0:T(8,128)(2,1)S(1)}, u32[]{:S(2)}, u32[]{:S(2)}) collective-permute-start(bf16[256,1024]{1,0:T(8,128)(2,1)S(1)} %get-tuple-element.64), channel_id=1, source_target_pairs={{0,3},{1,2},{2,1},{3,0},{4,7},{5,6},{6,5},{7,4},{8,11},{9,10},{10,... | collective-permute-start | bytes 1572872 | tf_op jit(solution)/shard_map/ppermute | solution.py:284
  546.9 51.9 %all-to-all-start.6 = ((bf16[8,16,32,128]{3,2,1,0:T(8,128)(2,1)}), bf16[8,16,32,128]{3,2,1,0:T(8,128)(2,1)S(1)}, u32[]{:S(2)}, u32[]{:S(2)}) async-start(bf16[8,16,32,128]{3,2,1,0:T(8,128)(2,1)} %shard_map.98), calls=%async_computation.6 | async-start | bytes 2097152 | tf_op jit(solution)/shard_map/all_to_all | solution.py:354
  551.7 14.9 %collective-permute-start.14 = (bf16[256,1024]{1,0:T(8,128)(2,1)}, bf16[256,1024]{1,0:T(8,128)(2,1)S(1)}, u32[]{:S(2)}, u32[]{:S(2)}) collective-permute-start(bf16[256,1024]{1,0:T(8,128)(2,1)} %copy-done.35), channel_id=1, source_target_pairs={{0,1},{1,0},{2,3},{3,2},{4,5},{5,4},{6,7},{7,6},{8,9},{9,8},{10,11... | collective-permute-start | bytes 1572872 | tf_op jit(solution)/shard_map/ppermute | solution.py:284
  552.9 24.0 %collective-permute-start.15 = (bf16[256,1024]{1,0:T(8,128)(2,1)}, bf16[256,1024]{1,0:T(8,128)(2,1)S(1)}, u32[]{:S(2)}, u32[]{:S(2)}) collective-permute-start(bf16[256,1024]{1,0:T(8,128)(2,1)} %copy-done.34), channel_id=1, source_target_pairs={{0,2},{1,3},{2,0},{3,1},{4,6},{5,7},{6,4},{7,5},{8,10},{9,11},{10,... | collective-permute-start | bytes 1572872 | tf_op jit(solution)/shard_map/ppermute | solution.py:284
  553.7 24.7 %collective-permute-start.16 = (bf16[256,1024]{1,0:T(8,128)(2,1)}, bf16[256,1024]{1,0:T(8,128)(2,1)S(1)}, u32[]{:S(2)}, u32[]{:S(2)}) collective-permute-start(bf16[256,1024]{1,0:T(8,128)(2,1)} %copy-done.33), channel_id=1, source_target_pairs={{0,3},{1,2},{2,1},{3,0},{4,7},{5,6},{6,5},{7,4},{8,11},{9,10},{10,... | collective-permute-start | bytes 1572872 | tf_op jit(solution)/shard_map/ppermute | solution.py:284
  581.0 3.4 copy-start.4
  584.4 3.4 copy-start.7
  593.1 15.0 %collective-permute-start.17 = (bf16[256,1024]{1,0:T(8,128)(2,1)}, bf16[256,1024]{1,0:T(8,128)(2,1)S(1)}, u32[]{:S(2)}, u32[]{:S(2)}) collective-permute-start(bf16[256,1024]{1,0:T(8,128)(2,1)} %get-tuple-element.56), channel_id=1, source_target_pairs={{0,1},{1,0},{2,3},{3,2},{4,5},{5,4},{6,7},{7,6},{8,9},{9,8},{10,11... | collective-permute-start | bytes 1572872 | tf_op jit(solution)/shard_map/ppermute | solution.py:284
  593.9 26.3 %collective-permute-start.18 = (bf16[256,1024]{1,0:T(8,128)(2,1)}, bf16[256,1024]{1,0:T(8,128)(2,1)S(1)}, u32[]{:S(2)}, u32[]{:S(2)}) collective-permute-start(bf16[256,1024]{1,0:T(8,128)(2,1)} %get-tuple-element.57), channel_id=1, source_target_pairs={{0,2},{1,3},{2,0},{3,1},{4,6},{5,7},{6,4},{7,5},{8,10},{9,11},{10,... | collective-permute-start | bytes 1572872 | tf_op jit(solution)/shard_map/ppermute | solution.py:284
  595.4 24.8 %collective-permute-start.19 = (bf16[256,1024]{1,0:T(8,128)(2,1)}, bf16[256,1024]{1,0:T(8,128)(2,1)S(1)}, u32[]{:S(2)}, u32[]{:S(2)}) collective-permute-start(bf16[256,1024]{1,0:T(8,128)(2,1)} %get-tuple-element.58), channel_id=1, source_target_pairs={{0,3},{1,2},{2,1},{3,0},{4,7},{5,6},{6,5},{7,4},{8,11},{9,10},{10,... | collective-permute-start | bytes 1572872 | tf_op jit(solution)/shard_map/ppermute | solution.py:284
  596.6 68.1 %collective-permute-start.23 = (bf16[256,1024]{1,0:T(8,128)(2,1)}, bf16[256,1024]{1,0:T(8,128)(2,1)}, u32[]{:S(2)}, u32[]{:S(2)}) collective-permute-start(bf16[256,1024]{1,0:T(8,128)(2,1)} %get-tuple-element.68), channel_id=1, source_target_pairs={{0,1},{1,0},{2,3},{3,2},{4,5},{5,4},{6,7},{7,6},{8,9},{9,8},{10,11... | collective-permute-start | bytes 1572872 | tf_op jit(solution)/shard_map/ppermute | solution.py:284
  597.4 68.9 %collective-permute-start.24 = (bf16[256,1024]{1,0:T(8,128)(2,1)}, bf16[256,1024]{1,0:T(8,128)(2,1)}, u32[]{:S(2)}, u32[]{:S(2)}) collective-permute-start(bf16[256,1024]{1,0:T(8,128)(2,1)} %get-tuple-element.69), channel_id=1, source_target_pairs={{0,2},{1,3},{2,0},{3,1},{4,6},{5,7},{6,4},{7,5},{8,10},{9,11},{10,... | collective-permute-start | bytes 1572872 | tf_op jit(solution)/shard_map/ppermute | solution.py:284
  598.9 3.4 copy-start.5
  608.1 12.1 %copy-start.27 = (bf16[256,1024]{1,0:T(8,128)(2,1)}, bf16[256,1024]{1,0:T(8,128)(2,1)S(1)}, u32[]{:S(2)}) copy-start(bf16[256,1024]{1,0:T(8,128)(2,1)S(1)} %collective-permute-done.17.refs_1_.rest_1_) | copy-start | bytes 1572868
  608.1 59.3 %collective-permute-start.25 = (bf16[256,1024]{1,0:T(8,128)(2,1)}, bf16[256,1024]{1,0:T(8,128)(2,1)S(1)}, u32[]{:S(2)}, u32[]{:S(2)}) collective-permute-start(bf16[256,1024]{1,0:T(8,128)(2,1)} %get-tuple-element.70), channel_id=1, source_target_pairs={{0,3},{1,2},{2,1},{3,0},{4,7},{5,6},{6,5},{7,4},{8,11},{9,10},{10,... | collective-permute-start | bytes 1572872 | tf_op jit(solution)/shard_map/ppermute | solution.py:284
  621.2 49.9 %all-to-all-start.4 = ((bf16[8,16,32,128]{3,2,1,0:T(8,128)(2,1)}), bf16[8,16,32,128]{3,2,1,0:T(8,128)(2,1)S(1)}, u32[]{:S(2)}, u32[]{:S(2)}) async-start(bf16[8,16,32,128]{3,2,1,0:T(8,128)(2,1)} %shard_map.94), calls=%async_computation.4 | async-start | bytes 2097152 | tf_op jit(solution)/shard_map/all_to_all | solution.py:354
  631.3 36.1 %copy-start.23 = (bf16[256,1024]{1,0:T(8,128)(2,1)S(1)}, bf16[256,1024]{1,0:T(8,128)(2,1)}, u32[]{:S(2)}) copy-start(bf16[256,1024]{1,0:T(8,128)(2,1)} %copy-done.22) | copy-start | bytes 1572868
  662.6 27.9 %collective-permute-start.32 = (bf16[256,1024]{1,0:T(8,128)(2,1)}, bf16[256,1024]{1,0:T(8,128)(2,1)S(1)}, u32[]{:S(2)}, u32[]{:S(2)}) collective-permute-start(bf16[256,1024]{1,0:T(8,128)(2,1)} %get-tuple-element.79), channel_id=1, source_target_pairs={{0,1},{1,0},{2,3},{3,2},{4,5},{5,4},{6,7},{7,6},{8,9},{9,8},{10,11... | collective-permute-start | bytes 1572872 | tf_op jit(solution)/shard_map/ppermute | solution.py:284
  663.9 19.4 %collective-permute-start.29 = (bf16[256,512]{1,0:T(8,128)(2,1)}, bf16[256,512]{1,0:T(8,128)(2,1)}, u32[]{:S(2)}, u32[]{:S(2)}) collective-permute-start(bf16[256,512]{1,0:T(8,128)(2,1)} %get-tuple-element.75), channel_id=1, source_target_pairs={{0,1},{1,0},{2,3},{3,2},{4,5},{5,4},{6,7},{7,6},{8,9},{9,8},{10,11... | collective-permute-start | bytes 786440 | tf_op jit(solution)/shard_map/ppermute | solution.py:284
  664.7 20.1 %collective-permute-start.30 = (bf16[256,512]{1,0:T(8,128)(2,1)}, bf16[256,512]{1,0:T(8,128)(2,1)}, u32[]{:S(2)}, u32[]{:S(2)}) collective-permute-start(bf16[256,512]{1,0:T(8,128)(2,1)} %get-tuple-element.76), channel_id=1, source_target_pairs={{0,2},{1,3},{2,0},{3,1},{4,6},{5,7},{6,4},{7,5},{8,10},{9,11},{10,... | collective-permute-start | bytes 786440 | tf_op jit(solution)/shard_map/ppermute | solution.py:284
  666.2 23.8 %collective-permute-start.31 = (bf16[256,512]{1,0:T(8,128)(2,1)}, bf16[256,512]{1,0:T(8,128)(2,1)}, u32[]{:S(2)}, u32[]{:S(2)}) collective-permute-start(bf16[256,512]{1,0:T(8,128)(2,1)} %get-tuple-element.77), channel_id=1, source_target_pairs={{0,3},{1,2},{2,1},{3,0},{4,7},{5,6},{6,5},{7,4},{8,11},{9,10},{10,... | collective-permute-start | bytes 786440 | tf_op jit(solution)/shard_map/ppermute | solution.py:284
  670.2 40.8 %collective-permute-start.33 = (bf16[256,1024]{1,0:T(8,128)(2,1)}, bf16[256,1024]{1,0:T(8,128)(2,1)S(1)}, u32[]{:S(2)}, u32[]{:S(2)}) collective-permute-start(bf16[256,1024]{1,0:T(8,128)(2,1)} %get-tuple-element.80), channel_id=1, source_target_pairs={{0,2},{1,3},{2,0},{3,1},{4,6},{5,7},{6,4},{7,5},{8,10},{9,11},{10,... | collective-permute-start | bytes 1572872 | tf_op jit(solution)/shard_map/ppermute | solution.py:284
  671.1 3.4 copy-start.6
  674.5 3.4 copy-start.8
  677.9 14.2 %copy-start.40 = (bf16[256,512]{1,0:T(8,128)(2,1)S(1)}, bf16[256,512]{1,0:T(8,128)(2,1)}, u32[]{:S(2)}) copy-start(bf16[256,512]{1,0:T(8,128)(2,1)} %copy-done.38) | copy-start | bytes 786436
  683.3 29.2 %collective-permute-start.34 = (bf16[256,1024]{1,0:T(8,128)(2,1)S(1)}, bf16[256,1024]{1,0:T(8,128)(2,1)S(1)}, u32[]{:S(2)}, u32[]{:S(2)}) collective-permute-start(bf16[256,1024]{1,0:T(8,128)(2,1)S(1)} %get-tuple-element.81), channel_id=1, source_target_pairs={{0,3},{1,2},{2,1},{3,0},{4,7},{5,6},{6,5},{7,4},{8,11},{9,10},{10,... | collective-permute-start | bytes 1572872 | tf_op jit(solution)/shard_map/ppermute | solution.py:284
  684.8 29.8 %collective-permute-start.26 = (bf16[256,512]{1,0:T(8,128)(2,1)S(1)}, bf16[256,512]{1,0:T(8,128)(2,1)S(1)}, u32[]{:S(2)}, u32[]{:S(2)}) collective-permute-start(bf16[256,512]{1,0:T(8,128)(2,1)S(1)} %get-tuple-element.72), channel_id=1, source_target_pairs={{0,1},{1,0},{2,3},{3,2},{4,5},{5,4},{6,7},{7,6},{8,9},{9,8},{10,11... | collective-permute-start | bytes 786440 | tf_op jit(solution)/shard_map/ppermute | solution.py:284
  690.0 26.2 %collective-permute-start.27 = (bf16[256,512]{1,0:T(8,128)(2,1)S(1)}, bf16[256,512]{1,0:T(8,128)(2,1)S(1)}, u32[]{:S(2)}, u32[]{:S(2)}) collective-permute-start(bf16[256,512]{1,0:T(8,128)(2,1)S(1)} %get-tuple-element.73), channel_id=1, source_target_pairs={{0,2},{1,3},{2,0},{3,1},{4,6},{5,7},{6,4},{7,5},{8,10},{9,11},{10,... | collective-permute-start | bytes 786440 | tf_op jit(solution)/shard_map/ppermute | solution.py:284
  690.5 25.7 %collective-permute-start.28 = (bf16[256,512]{1,0:T(8,128)(2,1)S(1)}, bf16[256,512]{1,0:T(8,128)(2,1)S(1)}, u32[]{:S(2)}, u32[]{:S(2)}) collective-permute-start(bf16[256,512]{1,0:T(8,128)(2,1)S(1)} %get-tuple-element.74), channel_id=1, source_target_pairs={{0,3},{1,2},{2,1},{3,0},{4,7},{5,6},{6,5},{7,4},{8,11},{9,10},{10,... | collective-permute-start | bytes 786440 | tf_op jit(solution)/shard_map/ppermute | solution.py:284
  711.0 25.2 %collective-permute-start.38 = (bf16[256,512]{1,0:T(8,128)(2,1)S(1)}, bf16[256,512]{1,0:T(8,128)(2,1)S(1)}, u32[]{:S(2)}, u32[]{:S(2)}) collective-permute-start(bf16[256,512]{1,0:T(8,128)(2,1)S(1)} %get-tuple-element.86), channel_id=1, source_target_pairs={{0,1},{1,0},{2,3},{3,2},{4,5},{5,4},{6,7},{7,6},{8,9},{9,8},{10,11... | collective-permute-start | bytes 786440 | tf_op jit(solution)/shard_map/ppermute | solution.py:284
  712.6 25.2 %collective-permute-start.39 = (bf16[256,512]{1,0:T(8,128)(2,1)S(1)}, bf16[256,512]{1,0:T(8,128)(2,1)S(1)}, u32[]{:S(2)}, u32[]{:S(2)}) collective-permute-start(bf16[256,512]{1,0:T(8,128)(2,1)S(1)} %get-tuple-element.87), channel_id=1, source_target_pairs={{0,2},{1,3},{2,0},{3,1},{4,6},{5,7},{6,4},{7,5},{8,10},{9,11},{10,... | collective-permute-start | bytes 786440 | tf_op jit(solution)/shard_map/ppermute | solution.py:284
  714.7 23.1 %collective-permute-start.40 = (bf16[256,512]{1,0:T(8,128)(2,1)S(1)}, bf16[256,512]{1,0:T(8,128)(2,1)S(1)}, u32[]{:S(2)}, u32[]{:S(2)}) collective-permute-start(bf16[256,512]{1,0:T(8,128)(2,1)S(1)} %get-tuple-element.88), channel_id=1, source_target_pairs={{0,3},{1,2},{2,1},{3,0},{4,7},{5,6},{6,5},{7,4},{8,11},{9,10},{10,... | collective-permute-start | bytes 786440 | tf_op jit(solution)/shard_map/ppermute | solution.py:284
  734.2 9.0 %collective-permute-start.35 = (bf16[256,512]{1,0:T(8,128)(2,1)S(1)}, bf16[256,512]{1,0:T(8,128)(2,1)S(1)}, u32[]{:S(2)}, u32[]{:S(2)}) collective-permute-start(bf16[256,512]{1,0:T(8,128)(2,1)S(1)} %get-tuple-element.83), channel_id=1, source_target_pairs={{0,1},{1,0},{2,3},{3,2},{4,5},{5,4},{6,7},{7,6},{8,9},{9,8},{10,11... | collective-permute-start | bytes 786440 | tf_op jit(solution)/shard_map/ppermute | solution.py:284
  735.8 11.4 %collective-permute-start.36 = (bf16[256,512]{1,0:T(8,128)(2,1)S(1)}, bf16[256,512]{1,0:T(8,128)(2,1)S(1)}, u32[]{:S(2)}, u32[]{:S(2)}) collective-permute-start(bf16[256,512]{1,0:T(8,128)(2,1)S(1)} %get-tuple-element.84), channel_id=1, source_target_pairs={{0,2},{1,3},{2,0},{3,1},{4,6},{5,7},{6,4},{7,5},{8,10},{9,11},{10,... | collective-permute-start | bytes 786440 | tf_op jit(solution)/shard_map/ppermute | solution.py:284
  736.3 11.0 %collective-permute-start.37 = (bf16[256,512]{1,0:T(8,128)(2,1)S(1)}, bf16[256,512]{1,0:T(8,128)(2,1)S(1)}, u32[]{:S(2)}, u32[]{:S(2)}) collective-permute-start(bf16[256,512]{1,0:T(8,128)(2,1)S(1)} %get-tuple-element.85), channel_id=1, source_target_pairs={{0,3},{1,2},{2,1},{3,0},{4,7},{5,6},{6,5},{7,4},{8,11},{9,10},{10,... | collective-permute-start | bytes 786440 | tf_op jit(solution)/shard_map/ppermute | solution.py:284
  (28 other events, 31.3 us)

commit v6 on v5

--- a/solution.py
+++ b/solution.py
@@ -368,39 +368,35 @@
     def put(k, done, result, group=0):
         return place(k, group, me, done, result, activations.shape)
 
-    front01 = exchange(after(first(0, 2), got[0]))
-    front23 = exchange(after(first(1, 2), got[1]))
+    front01 = exchange(after(first(0, 2), got[1]))
+    front23 = exchange(after(first(1, 2), got[-1]))
     (mixed0,) = second(front01, 0, [near_in[bits[0]], near_out[bits[-1]]])
     (mixed1,) = second(front01, 1)
     back0 = exchange(mixed0)
     (mixed2,) = second(front23, 0, [halves_in[0], halves_out[0]])
     back1 = exchange(mixed1)
-    mixed3 = second(front23, 1, [halves_in[1], halves_out[1]], 2)
+    (mixed3,) = second(front23, 1, [halves_in[1], halves_out[1]])
     in0 = swap(gated(0, back0))
-    out0 = layer(in0)
-    back2 = exchange(after(mixed2, out0[0]))
+    back2 = exchange(after(mixed2, *in0[1:]))
+    gate1 = gated(1, back1)
+    in1 = swap(gate1)
+    out0 = layer(in0, [gate1[0]])
+    back3 = exchange(after(mixed3, out0[0], *in1[1:]))
     done0 = swap(out0)
-    in1 = swap(gated(1, back1))
-    out1 = layer(in1)
-    back3a = exchange(after(mixed3[0], out1[0]))
+    gate2 = gated(2, back2)
+    in2 = swap(gate2)
+    out1 = layer(in1, [gate2[0]])
     done1 = swap(out1)
     result = put(0, done0, None)
-    in2 = swap(gated(2, back2, [result]))
-    back3b = exchange(after(mixed3[1], *in2[1:]))
-    gate3a = gated(3, back3a)
-    in3a = swap(gate3a)
-    out2 = layer(in2, [gate3a[0]])
+    gate3 = gated(3, back3, [out1[0], in2[1], result])
+    in3 = swap(gate3)
+    out2 = layer(in2, [gate3[0]])
     done2 = swap(out2)
     result = put(1, done1, result)
-    gate3b = gated(3, back3b, [out2[0], result], 1)
-    in3b = swap(gate3b)
-    out3a = layer(in3a, [gate3b[0]])
-    done3a = swap(out3a)
+    out3 = layer(in3, [out2[0], result])
+    done3 = swap(out3)
     result = put(2, done2, result)
-    out3b = layer(in3b, [out3a[0], result])
-    done3b = swap(out3b)
-    result = put(3, done3a, result)
-    return put(3, done3b, result, 1)
+    return put(3, done3, result)
 
 
 def solution(mesh):

time: 757 us -> 605 us (0.80)
  waiting for transfers between devices: 338 us -> 262 us
  starting transfers between devices: 141 us -> 89.8 us
  local copies, waits for them, and re-layouts: 66.4 us -> 48.1 us
    ppermute x1, waiting for transfers between devices: 36.8 us -> 89.8 us  [gather_along(): got.append(lax.ppermute(got[1], 'seq', [(i, i ^ 2) for i in middle]))]
    all_to_all x7 -> x6, waiting for transfers between devices: 121 us -> 68.9 us  [exchange(): return lax.all_to_all(x, 'seq', split_axis=0, concat_axis=0, tiled=True)]
    ppermute x30 -> x24, waiting for transfers between devices: 84.4 us -> 39.3 us  [swap(): lax.ppermute(slots[s], 'tensor', [(i, i ^ s) for i in range(n)])]
    all_to_all x7 -> x6, starting transfers between devices: 89.9 us -> 47.7 us  [exchange(): return lax.all_to_all(x, 'seq', split_axis=0, concat_axis=0, tiled=True)]
    ppermute x9, waiting for transfers between devices: 95.9 us -> 63.7 us  [flip(): return lax.ppermute(x, axis, [(i, i ^ bit) for i in range(n)])]
    unnamed x88 -> x66, local copies, waits for them, and re-layouts: 60.8 us -> 43.2 us
    ppermute x30 -> x24, starting transfers between devices: 36 us -> 29.4 us  [swap(): lax.ppermute(slots[s], 'tensor', [(i, i ^ s) for i in range(n)])]
    pallas_call x5 -> x4, Pallas kernels: 130 us -> 127 us  [mlp(): pl.pallas_call(kernel, grid_spec=pltpu.PrefetchScalarGridSpec(num_scalar_...]
  transfers between devices with their start and end apart: 48 -> 41, of which waited for: 22 -> 13; matrix products, arithmetic and copies ran while one was open for 2% -> 3% of each run, Pallas kernels for 25% -> 31%
where the time goes in v6:
time: 605 us; the launch traced here: 603 us
  waiting for transfers between devices  262 us (43%)
  Pallas kernels  186 us (31%)
  starting transfers between devices  89.8 us (15%)
  local copies, waits for them, and re-layouts  48.1 us (8%)
  other arithmetic  17 us (3%)
    pallas_call x4, Pallas kernels, mlp(): pl.pallas_call(kernel, grid_spec=pltpu.PrefetchScalarGridSpec(num_scalar_...  127 us
    ppermute x1, waiting for transfers between devices, gather_along(): got.append(lax.ppermute(got[1], 'seq', [(i, i ^ 2) for i in middle]))  89.8 us
    all_to_all x6, waiting for transfers between devices, exchange(): return lax.all_to_all(x, 'seq', split_axis=0, concat_axis=0, tiled=True)  68.9 us
    ppermute x9, waiting for transfers between devices, flip(): return lax.ppermute(x, axis, [(i, i ^ bit) for i in range(n)])  63.7 us
    all_to_all x6, starting transfers between devices, exchange(): return lax.all_to_all(x, 'seq', split_axis=0, concat_axis=0, tiled=True)  47.7 us
    unnamed x66, local copies, waits for them, and re-layouts  43.2 us
    ppermute x24, waiting for transfers between devices, swap(): lax.ppermute(slots[s], 'tensor', [(i, i ^ s) for i in range(n)])  39.3 us
    ppermute x24, starting transfers between devices, swap(): lax.ppermute(slots[s], 'tensor', [(i, i ^ s) for i in range(n)])  29.4 us
  transfers between devices with their start and end apart: 41, of which 13 were waited for; matrix products, arithmetic and copies ran while one was open for 3% of the time, Pallas kernels for 31%

profile of v6, /device:TPU:0, one launch (start us, length us, event | category | flops | bytes accessed | tf_op | source)
XLA Modules:
  0.0 603.5 jit_solution(3872330522178506286)
XLA Ops:
  1.3 3.1 collective-permute-start
  4.3 17.5 %collective-permute-done = bf16[1,2,192,1024]{3,2,1,0:T(8,128)(2,1)S(1)} collective-permute-done((bf16[1,2,192,1024]{3,2,1,0:T(8,128)(2,1)S(1)}, bf16[1,2,192,1024]{3,2,1,0:T(8,128)(2,1)S(1)}, u32[]{:S(2)}, u32[]{:S(2)}) %collective-permute-start) | collective-permute-done | bytes 786464 | tf_op jit(solution)/shard_map/ppermute | solution.py:299
  23.5 3.4 copy-done
  26.9 7.9 %shard_map.85.refs_0_ = bf16[8,2,32,32,128]{4,3,2,1,0:T(8,128)(2,1)S(1)} custom-call(bf16[256,16384]{1,0:T(8,128)(2,1)S(1)} %copy-done, bf16[512,512]{1,0:T(8,128)(2,1)S(1)} %copy-done.17, f32[256,16384]{1,0:T(8,128)} %rest_3_.7, f32[256,16384]{1,0:T(8,128)} %rest_3_.7, f32[256,16384]{1,0:T(8,128)} %rest_3_.7, f32[256,16384]{1,0:T(8,128)} %rest_3_.7), custom_call_target="tpu_custom_call" | custom-call | flops 2147483648 | bytes 20971520 | tf_op jit(solution)/shard_map/pallas_call | solution.py:40
  34.9 2.0 copy-done.11
  38.1 27.2 %all-to-all-start.1 = ((bf16[8,2,32,32,128]{4,3,2,1,0:T(8,128)(2,1)}), bf16[8,2,32,32,128]{4,3,2,1,0:T(8,128)(2,1)}, u32[]{:S(2)}, u32[]{:S(2)}) async-start(bf16[8,2,32,32,128]{4,3,2,1,0:T(8,128)(2,1)} %shard_map.86), calls=%async_computation.1 | async-start | bytes 8388608 | tf_op jit(solution)/shard_map/all_to_all | solution.py:354
  66.5 3.4 copy-done.1
  69.9 8.0 %shard_map.82.refs_0_ = bf16[8,2,32,32,128]{4,3,2,1,0:T(8,128)(2,1)S(1)} custom-call(bf16[256,16384]{1,0:T(8,128)(2,1)S(1)} %copy-done.1, bf16[512,512]{1,0:T(8,128)(2,1)S(1)} %copy-done.17, f32[256,16384]{1,0:T(8,128)} %rest_3_.7, f32[256,16384]{1,0:T(8,128)} %rest_3_.7, f32[256,16384]{1,0:T(8,128)} %rest_3_.7, f32[256,16384]{1,0:T(8,128)} %rest_3_.7), custom_call_target="tpu_custom_call" | custom-call | flops 2147483648 | bytes 20971520 | tf_op jit(solution)/shard_map/pallas_call | solution.py:40
  77.9 2.0 copy-done.12
  79.9 89.8 %collective-permute-done.2.refs_1_ = bf16[2,2,192,1024]{3,2,1,0:T(8,128)(2,1)} collective-permute-done((bf16[2,2,192,1024]{3,2,1,0:T(8,128)(2,1)S(1)}, bf16[2,2,192,1024]{3,2,1,0:T(8,128)(2,1)}, u32[]{:S(2)}, u32[]{:S(2)}) %collective-permute-start.2) | collective-permute-done | bytes 1572896 | tf_op jit(solution)/shard_map/ppermute | solution.py:309
  169.7 4.6 all-to-all-start
  174.2 2.1 add.7
  176.7 1.6 fusion
  179.8 1.6 copy.17
  181.4 1.5 collective-permute-start.8
  183.4 31.9 %collective-permute-done.3.rest_0_ = bf16[768,1024]{1,0:T(8,128)(2,1)} collective-permute-done((bf16[768,1024]{1,0:T(8,128)(2,1)}, bf16[768,1024]{1,0:T(8,128)(2,1)}, u32[]{:S(2)}, u32[]{:S(2)}) %collective-permute-start.3) | collective-permute-done | bytes 1572896 | tf_op jit(solution)/shard_map/ppermute | solution.py:299
  215.3 1.5 collective-permute-start.5
  219.5 4.8 shard_map.87
  225.6 42.6 %all-to-all-done.x_ref = bf16[8,2,32,32,128]{4,3,2,1,0:T(8,128)(2,1)} async-done(((bf16[8,2,32,32,128]{4,3,2,1,0:T(8,128)(2,1)}), bf16[8,2,32,32,128]{4,3,2,1,0:T(8,128)(2,1)}, u32[]{:S(2)}, u32[]{:S(2)}) %all-to-all-start) | async-done | bytes 4194336 | tf_op jit(solution)/shard_map/all_to_all | solution.py:354
  268.2 3.6 all-to-all-start.2
  271.9 13.6 %collective-permute-done.5 = bf16[768,1024]{1,0:T(8,128)(2,1)} collective-permute-done((bf16[768,1024]{1,0:T(8,128)(2,1)}, bf16[768,1024]{1,0:T(8,128)(2,1)}, u32[]{:S(2)}, u32[]{:S(2)}) %collective-permute-start.5) | collective-permute-done | bytes 1572896 | tf_op jit(solution)/shard_map/ppermute | solution.py:299
  285.5 6.5 %pad_maximum_fusion.rest_4_.rest_0_ = bf16[4,768,1024]{2,1,0:T(8,128)(2,1)} fusion(bf16[1,768,1024]{2,1,0:T(8,128)(2,1)} %bitcast.9, bf16[1,768,1024]{2,1,0:T(8,128)(2,1)} %bitcast.8, bf16[1,768,1024]{2,1,0:T(8,128)(2,1)} %bitcast.7, bf16[1,768,1024]{2,1,0:T(8,128)(2,1)} %bitcast.5), kind=kLoop, calls=%fused_computation | loop fusion | flops 9437184 | bytes 12582912 | tf_op jit(solution)/shard_map/stack | solution.py:348
  292.0 6.7 %pad_maximum_fusion.1.rest_6_.rest_1_ = bf16[4,1024,768]{2,1,0:T(8,128)(2,1)} fusion(bf16[1,1024,768]{2,1,0:T(8,128)(2,1)} %bitcast.15, bf16[1,1024,768]{2,1,0:T(8,128)(2,1)} %bitcast.14, bf16[1,1024,768]{2,1,0:T(8,128)(2,1)} %bitcast.13, bf16[1,1024,768]{2,1,0:T(8,128)(2,1)} %bitcast.12), kind=kLoop, calls=%fused_computation.1 | loop fusion | flops 9437184 | bytes 12582912 | tf_op jit(solution)/shard_map/stack | solution.py:350
  299.1 4.8 shard_map.89
  305.3 15.5 %all-to-all-done.2.rest_4_.rest_5_.rest_6_.rest_7_ = bf16[8,32,32,128]{3,2,1,0:T(8,128)(2,1)S(1)} async-done(((bf16[8,32,32,128]{3,2,1,0:T(8,128)(2,1)}), bf16[8,32,32,128]{3,2,1,0:T(8,128)(2,1)S(1)}, u32[]{:S(2)}, u32[]{:S(2)}) %all-to-all-start.2) | async-done | bytes 2097184 | tf_op jit(solution)/shard_map/all_to_all | solution.py:354
  322.1 3.6 all-to-all-start.3
  327.6 3.4 copy-done.2
  331.0 1.6 copy-done.10
  332.6 3.9 shard_map.88
  337.3 1.5 collective-permute-start.11
  338.8 1.5 collective-permute-start.12
  340.8 4.8 shard_map.93.refs_0_
  346.9 5.1 collective-permute-done.11.rest_1_.refs_1_
  352.0 12.0 %collective-permute-done.12.rest_2_.refs_2_ = bf16[256,1024]{1,0:T(8,128)(2,1)} collective-permute-done((bf16[256,1024]{1,0:T(8,128)(2,1)S(1)}, bf16[256,1024]{1,0:T(8,128)(2,1)}, u32[]{:S(2)}, u32[]{:S(2)}) %collective-permute-start.12) | collective-permute-done | bytes 524320 | tf_op jit(solution)/shard_map/ppermute | solution.py:284
  364.1 10.7 %all-to-all-done.3.rest_4_.rest_5_.rest_6_.rest_7_ = bf16[8,32,32,128]{3,2,1,0:T(8,128)(2,1)S(1)} async-done(((bf16[8,32,32,128]{3,2,1,0:T(8,128)(2,1)}), bf16[8,32,32,128]{3,2,1,0:T(8,128)(2,1)S(1)}, u32[]{:S(2)}, u32[]{:S(2)}) %all-to-all-start.3) | async-done | bytes 2097184 | tf_op jit(solution)/shard_map/all_to_all | solution.py:354
  376.1 3.8 all-to-all-start.5
  379.9 3.4 copy-done.3
  383.2 1.6 copy-done.8
  384.8 3.9 shard_map.90
  388.8 1.6 collective-permute-start.14
  390.3 1.5 collective-permute-start.15
  392.3 4.8 shard_map.84.refs_0_
  398.6 32.8 %shard_map.91 = (bf16[256,1024]{1,0:T(8,128)(2,1)S(1)}, bf16[256,1024]{1,0:T(8,128)(2,1)}, bf16[256,1024]{1,0:T(8,128)(2,1)}, bf16[256,1024]{1,0:T(8,128)(2,1)}) custom-call(s32[1]{0:T(128)} %bitcast.me_ref, bf16[256,1024]{1,0:T(8,128)(2,1)S(1)} %copy-done.28, bf16[256,1024]{1,0:T(8,128)(2,1)S(1)} %copy-done.24, ...), custom_call_target="tpu_custom_call" | custom-call | flops 25769803776 | bytes 29360128 | tf_op jit(solution)/shard_map/pallas_call | solution.py:215
  433.0 5.0 all-to-all-start.4
  441.6 3.4 copy-done.4
  444.9 4.5 shard_map.95
  452.4 32.8 %shard_map.96 = (bf16[256,1024]{1,0:T(8,128)(2,1)S(1)}, bf16[256,1024]{1,0:T(8,128)(2,1)}, bf16[256,1024]{1,0:T(8,128)(2,1)}, bf16[256,1024]{1,0:T(8,128)(2,1)}) custom-call(s32[1]{0:T(128)} %bitcast.me_ref, bf16[256,1024]{1,0:T(8,128)(2,1)S(1)} %copy-done.26, bf16[256,1024]{1,0:T(8,128)(2,1)S(1)} %copy-done.22, ...), custom_call_target="tpu_custom_call" | custom-call | flops 25769803776 | bytes 29360128 | tf_op jit(solution)/shard_map/pallas_call | solution.py:215
  487.3 1.6 shard_map.97.rest_12_.rest_4_
  488.8 1.6 collective-permute-start.27
  490.9 3.4 copy-done.5
  494.3 3.4 copy-done.6
  497.7 5.0 shard_map.98
  502.7 1.6 collective-permute-start.21
  505.8 5.8 collective-permute-done.26.rest_1_
  513.1 31.5 %shard_map.99 = (bf16[256,1024]{1,0:T(8,128)(2,1)S(1)}, bf16[256,1024]{1,0:T(8,128)(2,1)S(1)}, bf16[256,1024]{1,0:T(8,128)(2,1)S(1)}, bf16[256,1024]{1,0:T(8,128)(2,1)S(1)}) custom-call(s32[1]{0:T(128)} %bitcast.me_ref, bf16[256,1024]{1,0:T(8,128)(2,1)S(1)} %get-tuple-element.46.rest_8_.rest_0_, ...), custom_call_target="tpu_custom_call" | custom-call | flops 25769803776 | bytes 29360128 | tf_op jit(solution)/shard_map/pallas_call | solution.py:215
  544.6 1.6 collective-permute-start.32
  546.6 1.6 shard_map.100.rest_9_.rest_4_
  548.2 1.6 collective-permute-start.34
  549.8 30.4 %shard_map.101 = (bf16[256,1024]{1,0:T(8,128)(2,1)S(1)}, bf16[256,1024]{1,0:T(8,128)(2,1)S(1)}, bf16[256,1024]{1,0:T(8,128)(2,1)S(1)}, bf16[256,1024]{1,0:T(8,128)(2,1)S(1)}) custom-call(s32[1]{0:T(128)} %bitcast.me_ref, bf16[256,1024]{1,0:T(8,128)(2,1)S(1)} %get-tuple-element.52.rest_8_.rest_0_, bf16[256,1024]{1,0:T(8,128)(2,1)S(1)} %collective-permute-done.21.rest_1_, ...), custom_call_target="tpu_custom_call" | custom-call | flops 25769803776 | bytes 29360128 | tf_op jit(solution)/shard_map/pallas_call | solution.py:215
  580.2 1.6 collective-permute-start.29
  583.8 1.6 shard_map.102.rest_4_
  585.4 9.5 %collective-permute-done.29.rest_1_ = bf16[256,1024]{1,0:T(8,128)(2,1)S(1)} collective-permute-done((bf16[256,1024]{1,0:T(8,128)(2,1)S(1)}, bf16[256,1024]{1,0:T(8,128)(2,1)S(1)}, u32[]{:S(2)}, u32[]{:S(2)}) %collective-permute-start.29) | collective-permute-done | bytes 524320 | tf_op jit(solution)/shard_map/ppermute | solution.py:284
  594.9 6.8 %collective-permute-done.30.rest_2_ = bf16[256,1024]{1,0:T(8,128)(2,1)S(1)} collective-permute-done((bf16[256,1024]{1,0:T(8,128)(2,1)S(1)}, bf16[256,1024]{1,0:T(8,128)(2,1)S(1)}, u32[]{:S(2)}, u32[]{:S(2)}) %collective-permute-start.30) | collective-permute-done | bytes 524320 | tf_op jit(solution)/shard_map/ppermute | solution.py:284
  601.7 1.6 shard_map.103
  (118 shorter events, 38.6 us)
Async XLA Ops:
  0.0 23.5 %copy-start.17 = (bf16[512,512]{1,0:T(8,128)(2,1)S(1)}, bf16[512,512]{1,0:T(8,128)(2,1)}, u32[]{:S(2)}) copy-start(bf16[512,512]{1,0:T(8,128)(2,1)} %factor.3) | copy-start | bytes 1572868
  1.3 20.6 %collective-permute-start = (bf16[1,2,192,1024]{3,2,1,0:T(8,128)(2,1)S(1)}, bf16[1,2,192,1024]{3,2,1,0:T(8,128)(2,1)S(1)}, u32[]{:S(2)}, u32[]{:S(2)}) collective-permute-start(bf16[1,2,192,1024]{3,2,1,0:T(8,128)(2,1)S(1)} %maximum_bitcast_fusion), channel_id=1, source_target_pairs={{0,8},{4,12},{8,0},{12,4},{16,24},{20,28},{24,16},{28,20},{1,9},{5... | collective-permute-start | bytes 2359304 | tf_op jit(solution)/shard_map/ppermute | solution.py:299
  22.8 14.1 %collective-permute-start.1 = (bf16[2,2,192,1024]{3,2,1,0:T(8,128)(2,1)S(1)}, bf16[2,2,192,1024]{3,2,1,0:T(8,128)(2,1)S(1)}, u32[]{:S(2)}, u32[]{:S(2)}) collective-permute-start(bf16[2,2,192,1024]{3,2,1,0:T(8,128)(2,1)S(1)} %pad_maximum_fusion.3), channel_id=1, source_target_pairs={{8,16},{12,20},{16,8},{20,12},{9,17},{13,21},{17,9},{21,13},{10,18... | collective-permute-start | bytes 4718600 | tf_op jit(solution)/shard_map/ppermute | solution.py:308
  23.5 3.4 copy-start
  34.9 2.0 copy-start.11
  38.1 27.2 %copy-start.30 = (bf16[2,2,192,1024]{3,2,1,0:T(8,128)(2,1)S(1)}, bf16[2,2,192,1024]{3,2,1,0:T(8,128)(2,1)}, u32[]{:S(2)}) copy-start(bf16[2,2,192,1024]{3,2,1,0:T(8,128)(2,1)} %copy-done.29) | copy-start | bytes 4718596
  38.1 131.6 %all-to-all-start.1 = ((bf16[8,2,32,32,128]{4,3,2,1,0:T(8,128)(2,1)}), bf16[8,2,32,32,128]{4,3,2,1,0:T(8,128)(2,1)}, u32[]{:S(2)}, u32[]{:S(2)}) async-start(bf16[8,2,32,32,128]{4,3,2,1,0:T(8,128)(2,1)} %shard_map.86), calls=%async_computation.1 | async-start | bytes 8388608 | tf_op jit(solution)/shard_map/all_to_all | solution.py:354
  65.2 104.4 %collective-permute-start.2 = (bf16[2,2,192,1024]{3,2,1,0:T(8,128)(2,1)S(1)}, bf16[2,2,192,1024]{3,2,1,0:T(8,128)(2,1)}, u32[]{:S(2)}, u32[]{:S(2)}) collective-permute-start(bf16[2,2,192,1024]{3,2,1,0:T(8,128)(2,1)S(1)} %copy-done.30), channel_id=1, source_target_pairs={{8,0},{12,4},{16,24},{20,28},{9,1},{13,5},{17,25},{21,29},{10,2},{... | collective-permute-start | bytes 4718600 | tf_op jit(solution)/shard_map/ppermute | solution.py:309
  66.5 3.4 copy-start.1
  77.9 2.0 copy-start.12
  169.7 98.6 %all-to-all-start = ((bf16[8,2,32,32,128]{4,3,2,1,0:T(8,128)(2,1)}), bf16[8,2,32,32,128]{4,3,2,1,0:T(8,128)(2,1)}, u32[]{:S(2)}, u32[]{:S(2)}) async-start(bf16[8,2,32,32,128]{4,3,2,1,0:T(8,128)(2,1)} %shard_map.83), calls=%async_computation | async-start | bytes 8388608 | tf_op jit(solution)/shard_map/all_to_all | solution.py:354
  174.2 2.2 copy-start.32
  178.3 41.2 %copy-start.16 = (f32[256,256]{1,0:T(8,128)S(1)}, f32[256,256]{1,0:T(8,128)}, u32[]{:S(2)}) copy-start(f32[256,256]{1,0:T(8,128)} %s_ref.7) | copy-start | bytes 786436
  178.3 37.0 %collective-permute-start.3 = (bf16[768,1024]{1,0:T(8,128)(2,1)}, bf16[768,1024]{1,0:T(8,128)(2,1)}, u32[]{:S(2)}, u32[]{:S(2)}) collective-permute-start(bf16[768,1024]{1,0:T(8,128)(2,1)} %bitcast.6), channel_id=1, source_target_pairs={{0,1},{1,0},{2,3},{3,2},{4,5},{5,4},{6,7},{7,6},{8,9},{9,8},{10,11... | collective-permute-start | bytes 4718600 | tf_op jit(solution)/shard_map/ppermute | solution.py:299
  181.4 37.6 %collective-permute-start.8 = (bf16[1024,768]{1,0:T(8,128)(2,1)}, bf16[1024,768]{1,0:T(8,128)(2,1)}, u32[]{:S(2)}, u32[]{:S(2)}) collective-permute-start(bf16[1024,768]{1,0:T(8,128)(2,1)} %bitcast.11), channel_id=1, source_target_pairs={{0,2},{1,3},{2,0},{3,1},{4,6},{5,7},{6,4},{7,5},{8,10},{9,11},{10,... | collective-permute-start | bytes 4718600 | tf_op jit(solution)/shard_map/ppermute | solution.py:299
  182.9 89.0 %collective-permute-start.4 = (bf16[768,1024]{1,0:T(8,128)(2,1)}, bf16[768,1024]{1,0:T(8,128)(2,1)}, u32[]{:S(2)}, u32[]{:S(2)}) collective-permute-start(bf16[768,1024]{1,0:T(8,128)(2,1)} %bitcast.6), channel_id=1, source_target_pairs={{0,2},{1,3},{2,0},{3,1},{4,6},{5,7},{6,4},{7,5},{8,10},{9,11},{10,... | collective-permute-start | bytes 4718600 | tf_op jit(solution)/shard_map/ppermute | solution.py:299
  215.3 70.2 %collective-permute-start.5 = (bf16[768,1024]{1,0:T(8,128)(2,1)}, bf16[768,1024]{1,0:T(8,128)(2,1)}, u32[]{:S(2)}, u32[]{:S(2)}) collective-permute-start(bf16[768,1024]{1,0:T(8,128)(2,1)} %collective-permute-done.3.rest_0_), channel_id=1, source_target_pairs={{0,2},{1,3},{2,0},{3,1},{4,6},{5,7},{6,4},{7,5},{8,10},{9,11},{10,... | collective-permute-start | bytes 4718600 | tf_op jit(solution)/shard_map/ppermute | solution.py:299
  216.8 75.2 %collective-permute-start.7 = (bf16[1024,768]{1,0:T(8,128)(2,1)}, bf16[1024,768]{1,0:T(8,128)(2,1)}, u32[]{:S(2)}, u32[]{:S(2)}) collective-permute-start(bf16[1024,768]{1,0:T(8,128)(2,1)} %bitcast.11), channel_id=1, source_target_pairs={{0,1},{1,0},{2,3},{3,2},{4,5},{5,4},{6,7},{7,6},{8,9},{9,8},{10,11... | collective-permute-start | bytes 4718600 | tf_op jit(solution)/shard_map/ppermute | solution.py:299
  218.9 73.0 %collective-permute-start.9 = (bf16[1024,768]{1,0:T(8,128)(2,1)}, bf16[1024,768]{1,0:T(8,128)(2,1)}, u32[]{:S(2)}, u32[]{:S(2)}) collective-permute-start(bf16[1024,768]{1,0:T(8,128)(2,1)} %collective-permute-done.8.rest_1_), channel_id=1, source_target_pairs={{0,1},{1,0},{2,3},{3,2},{4,5},{5,4},{6,7},{7,6},{8,9},{9,8},{10,11... | collective-permute-start | bytes 4718600 | tf_op jit(solution)/shard_map/ppermute | solution.py:299
  268.2 52.6 %all-to-all-start.2 = ((bf16[8,32,32,128]{3,2,1,0:T(8,128)(2,1)}), bf16[8,32,32,128]{3,2,1,0:T(8,128)(2,1)S(1)}, u32[]{:S(2)}, u32[]{:S(2)}) async-start(bf16[8,32,32,128]{3,2,1,0:T(8,128)(2,1)} %copy-done.15), calls=%async_computation.2 | async-start | bytes 4194304 | tf_op jit(solution)/shard_map/all_to_all | solution.py:354
  291.9 100.4 %collective-permute-start.6 = (bf16[4,768,1024]{2,1,0:T(8,128)(2,1)}, bf16[4,768,1024]{2,1,0:T(8,128)(2,1)}, u32[]{:S(2)}, u32[]{:S(2)}) collective-permute-start(bf16[4,768,1024]{2,1,0:T(8,128)(2,1)} %pad_maximum_fusion.rest_4_.rest_0_), channel_id=1, source_target_pairs={{0,4},{4,0},{8,12},{12,8},{16,20},{20,16},{24,28},{28,24},{1,5},{5... | collective-permute-start | bytes 18874376 | tf_op jit(solution)/shard_map/ppermute | solution.py:299
  298.6 93.7 %collective-permute-start.10 = (bf16[4,1024,768]{2,1,0:T(8,128)(2,1)}, bf16[4,1024,768]{2,1,0:T(8,128)(2,1)}, u32[]{:S(2)}, u32[]{:S(2)}) collective-permute-start(bf16[4,1024,768]{2,1,0:T(8,128)(2,1)} %pad_maximum_fusion.1.rest_6_.rest_1_), channel_id=1, source_target_pairs={{0,4},{4,0},{8,12},{12,8},{16,20},{20,16},{24,28},{28,24},{1,5},{5... | collective-permute-start | bytes 18874376 | tf_op jit(solution)/shard_map/ppermute | solution.py:299
  322.1 52.6 %all-to-all-start.3 = ((bf16[8,32,32,128]{3,2,1,0:T(8,128)(2,1)}), bf16[8,32,32,128]{3,2,1,0:T(8,128)(2,1)S(1)}, u32[]{:S(2)}, u32[]{:S(2)}) async-start(bf16[8,32,32,128]{3,2,1,0:T(8,128)(2,1)} %copy-done.18), calls=%async_computation.3 | async-start | bytes 4194304 | tf_op jit(solution)/shard_map/all_to_all | solution.py:354
  327.6 3.4 copy-start.2
  331.0 1.6 copy-start.10
  337.3 14.8 %collective-permute-start.11 = (bf16[256,1024]{1,0:T(8,128)(2,1)S(1)}, bf16[256,1024]{1,0:T(8,128)(2,1)S(1)}, u32[]{:S(2)}, u32[]{:S(2)}) collective-permute-start(bf16[256,1024]{1,0:T(8,128)(2,1)S(1)} %get-tuple-element.38), channel_id=1, source_target_pairs={{0,1},{1,0},{2,3},{3,2},{4,5},{5,4},{6,7},{7,6},{8,9},{9,8},{10,11... | collective-permute-start | bytes 1572872 | tf_op jit(solution)/shard_map/ppermute | solution.py:284
  338.8 25.3 %collective-permute-start.12 = (bf16[256,1024]{1,0:T(8,128)(2,1)S(1)}, bf16[256,1024]{1,0:T(8,128)(2,1)}, u32[]{:S(2)}, u32[]{:S(2)}) collective-permute-start(bf16[256,1024]{1,0:T(8,128)(2,1)S(1)} %get-tuple-element.39), channel_id=1, source_target_pairs={{0,2},{1,3},{2,0},{3,1},{4,6},{5,7},{6,4},{7,5},{8,10},{9,11},{10,... | collective-permute-start | bytes 1572872 | tf_op jit(solution)/shard_map/ppermute | solution.py:284
  340.3 23.7 %collective-permute-start.13 = (bf16[256,1024]{1,0:T(8,128)(2,1)S(1)}, bf16[256,1024]{1,0:T(8,128)(2,1)}, u32[]{:S(2)}, u32[]{:S(2)}) collective-permute-start(bf16[256,1024]{1,0:T(8,128)(2,1)S(1)} %get-tuple-element.40), channel_id=1, source_target_pairs={{0,3},{1,2},{2,1},{3,0},{4,7},{5,6},{6,5},{7,4},{8,11},{9,10},{10,... | collective-permute-start | bytes 1572872 | tf_op jit(solution)/shard_map/ppermute | solution.py:284
  352.0 12.0 %copy-start.23 = (bf16[256,1024]{1,0:T(8,128)(2,1)}, bf16[256,1024]{1,0:T(8,128)(2,1)S(1)}, u32[]{:S(2)}) copy-start(bf16[256,1024]{1,0:T(8,128)(2,1)S(1)} %collective-permute-done.11.rest_1_.refs_1_) | copy-start | bytes 1572868
  376.1 57.0 %all-to-all-start.5 = ((bf16[8,32,32,128]{3,2,1,0:T(8,128)(2,1)}), bf16[8,32,32,128]{3,2,1,0:T(8,128)(2,1)S(1)}, u32[]{:S(2)}, u32[]{:S(2)}) async-start(bf16[8,32,32,128]{3,2,1,0:T(8,128)(2,1)} %shard_map.94), calls=%async_computation.5 | async-start | bytes 4194304 | tf_op jit(solution)/shard_map/all_to_all | solution.py:354
  379.9 3.4 copy-start.3
  383.2 1.6 copy-start.8
  388.7 9.9 %copy-start.25 = (bf16[256,1024]{1,0:T(8,128)(2,1)}, bf16[256,1024]{1,0:T(8,128)(2,1)S(1)}, u32[]{:S(2)}) copy-start(bf16[256,1024]{1,0:T(8,128)(2,1)S(1)} %get-tuple-element.41.rest_8_.rest_0_) | copy-start | bytes 1572868
  388.8 43.5 %collective-permute-start.14 = (bf16[256,1024]{1,0:T(8,128)(2,1)S(1)}, bf16[256,1024]{1,0:T(8,128)(2,1)S(1)}, u32[]{:S(2)}, u32[]{:S(2)}) collective-permute-start(bf16[256,1024]{1,0:T(8,128)(2,1)S(1)} %get-tuple-element.43), channel_id=1, source_target_pairs={{0,1},{1,0},{2,3},{3,2},{4,5},{5,4},{6,7},{7,6},{8,9},{9,8},{10,11... | collective-permute-start | bytes 1572872 | tf_op jit(solution)/shard_map/ppermute | solution.py:284
  390.3 41.9 %collective-permute-start.15 = (bf16[256,1024]{1,0:T(8,128)(2,1)S(1)}, bf16[256,1024]{1,0:T(8,128)(2,1)}, u32[]{:S(2)}, u32[]{:S(2)}) collective-permute-start(bf16[256,1024]{1,0:T(8,128)(2,1)S(1)} %get-tuple-element.44), channel_id=1, source_target_pairs={{0,2},{1,3},{2,0},{3,1},{4,6},{5,7},{6,4},{7,5},{8,10},{9,11},{10,... | collective-permute-start | bytes 1572872 | tf_op jit(solution)/shard_map/ppermute | solution.py:284
  391.8 6.8 %copy-start.24 = (bf16[256,1024]{1,0:T(8,128)(2,1)S(1)}, bf16[256,1024]{1,0:T(8,128)(2,1)}, u32[]{:S(2)}) copy-start(bf16[256,1024]{1,0:T(8,128)(2,1)} %copy-done.23) | copy-start | bytes 1572868
  391.8 6.8 %copy-start.28 = (bf16[256,1024]{1,0:T(8,128)(2,1)S(1)}, bf16[256,1024]{1,0:T(8,128)(2,1)}, u32[]{:S(2)}) copy-start(bf16[256,1024]{1,0:T(8,128)(2,1)} %copy-done.27) | copy-start | bytes 1572868
  391.8 40.4 %collective-permute-start.16 = (bf16[256,1024]{1,0:T(8,128)(2,1)S(1)}, bf16[256,1024]{1,0:T(8,128)(2,1)}, u32[]{:S(2)}, u32[]{:S(2)}) collective-permute-start(bf16[256,1024]{1,0:T(8,128)(2,1)S(1)} %get-tuple-element.45), channel_id=1, source_target_pairs={{0,3},{1,2},{2,1},{3,0},{4,7},{5,6},{6,5},{7,4},{8,11},{9,10},{10,... | collective-permute-start | bytes 1572872 | tf_op jit(solution)/shard_map/ppermute | solution.py:284
  397.2 1.4 copy-start.13
  433.0 57.9 %all-to-all-start.4 = ((bf16[8,32,32,128]{3,2,1,0:T(8,128)(2,1)}), bf16[8,32,32,128]{3,2,1,0:T(8,128)(2,1)}, u32[]{:S(2)}, u32[]{:S(2)}) async-start(bf16[8,32,32,128]{3,2,1,0:T(8,128)(2,1)} %shard_map.92), calls=%async_computation.4 | async-start | bytes 4194304 | tf_op jit(solution)/shard_map/all_to_all | solution.py:354
  438.1 47.1 %collective-permute-start.18 = (bf16[256,1024]{1,0:T(8,128)(2,1)}, bf16[256,1024]{1,0:T(8,128)(2,1)S(1)}, u32[]{:S(2)}, u32[]{:S(2)}) collective-permute-start(bf16[256,1024]{1,0:T(8,128)(2,1)} %get-tuple-element.49), channel_id=1, source_target_pairs={{0,1},{1,0},{2,3},{3,2},{4,5},{5,4},{6,7},{7,6},{8,9},{9,8},{10,11... | collective-permute-start | bytes 1572872 | tf_op jit(solution)/shard_map/ppermute | solution.py:284
  439.6 46.2 %collective-permute-start.19 = (bf16[256,1024]{1,0:T(8,128)(2,1)}, bf16[256,1024]{1,0:T(8,128)(2,1)S(1)}, u32[]{:S(2)}, u32[]{:S(2)}) collective-permute-start(bf16[256,1024]{1,0:T(8,128)(2,1)} %get-tuple-element.50), channel_id=1, source_target_pairs={{0,2},{1,3},{2,0},{3,1},{4,6},{5,7},{6,4},{7,5},{8,10},{9,11},{10,... | collective-permute-start | bytes 1572872 | tf_op jit(solution)/shard_map/ppermute | solution.py:284
  441.1 46.2 %collective-permute-start.20 = (bf16[256,1024]{1,0:T(8,128)(2,1)}, bf16[256,1024]{1,0:T(8,128)(2,1)S(1)}, u32[]{:S(2)}, u32[]{:S(2)}) collective-permute-start(bf16[256,1024]{1,0:T(8,128)(2,1)} %get-tuple-element.51), channel_id=1, source_target_pairs={{0,3},{1,2},{2,1},{3,0},{4,7},{5,6},{6,5},{7,4},{8,11},{9,10},{10,... | collective-permute-start | bytes 1572872 | tf_op jit(solution)/shard_map/ppermute | solution.py:284
  441.6 3.4 copy-start.4
  444.9 7.5 %copy-start.22 = (bf16[256,1024]{1,0:T(8,128)(2,1)S(1)}, bf16[256,1024]{1,0:T(8,128)(2,1)}, u32[]{:S(2)}) copy-start(bf16[256,1024]{1,0:T(8,128)(2,1)} %copy-done.21) | copy-start | bytes 1572868
  444.9 7.5 %copy-start.26 = (bf16[256,1024]{1,0:T(8,128)(2,1)S(1)}, bf16[256,1024]{1,0:T(8,128)(2,1)}, u32[]{:S(2)}) copy-start(bf16[256,1024]{1,0:T(8,128)(2,1)} %copy-done.25) | copy-start | bytes 1572868
  449.4 41.0 %collective-permute-start.17 = (bf16[256,1024]{1,0:T(8,128)(2,1)S(1)}, bf16[256,1024]{1,0:T(8,128)(2,1)S(1)}, u32[]{:S(2)}, u32[]{:S(2)}) collective-permute-start(bf16[256,1024]{1,0:T(8,128)(2,1)S(1)} %get-tuple-element.48), channel_id=1, source_target_pairs={{0,1},{1,0},{2,3},{3,2},{4,5},{5,4},{6,7},{7,6},{8,9},{9,8},{10,11... | collective-permute-start | bytes 1572872 | tf_op jit(solution)/shard_map/ppermute | solution.py:284
  450.9 51.8 %collective-permute-start.24 = (bf16[256,1024]{1,0:T(8,128)(2,1)}, bf16[256,1024]{1,0:T(8,128)(2,1)}, u32[]{:S(2)}, u32[]{:S(2)}) collective-permute-start(bf16[256,1024]{1,0:T(8,128)(2,1)} %get-tuple-element.56), channel_id=1, source_target_pairs={{0,2},{1,3},{2,0},{3,1},{4,6},{5,7},{6,4},{7,5},{8,10},{9,11},{10,... | collective-permute-start | bytes 1572872 | tf_op jit(solution)/shard_map/ppermute | solution.py:284
  452.4 34.8 %copy-start.20 = (bf16[256,1024]{1,0:T(8,128)(2,1)S(1)}, bf16[256,1024]{1,0:T(8,128)(2,1)}, u32[]{:S(2)}) copy-start(bf16[256,1024]{1,0:T(8,128)(2,1)} %copy-done.19) | copy-start | bytes 1572868
  485.2 19.0 %collective-permute-start.25 = (bf16[256,1024]{1,0:T(8,128)(2,1)}, bf16[256,1024]{1,0:T(8,128)(2,1)}, u32[]{:S(2)}, u32[]{:S(2)}) collective-permute-start(bf16[256,1024]{1,0:T(8,128)(2,1)} %get-tuple-element.57), channel_id=1, source_target_pairs={{0,3},{1,2},{2,1},{3,0},{4,7},{5,6},{6,5},{7,4},{8,11},{9,10},{10,... | collective-permute-start | bytes 1572872 | tf_op jit(solution)/shard_map/ppermute | solution.py:284
  485.8 25.8 %collective-permute-start.26 = (bf16[256,1024]{1,0:T(8,128)(2,1)}, bf16[256,1024]{1,0:T(8,128)(2,1)S(1)}, u32[]{:S(2)}, u32[]{:S(2)}) collective-permute-start(bf16[256,1024]{1,0:T(8,128)(2,1)} %get-tuple-element.59), channel_id=1, source_target_pairs={{0,1},{1,0},{2,3},{3,2},{4,5},{5,4},{6,7},{7,6},{8,9},{9,8},{10,11... | collective-permute-start | bytes 1572872 | tf_op jit(solution)/shard_map/ppermute | solution.py:284
  488.8 55.7 %collective-permute-start.27 = (bf16[256,1024]{1,0:T(8,128)(2,1)}, bf16[256,1024]{1,0:T(8,128)(2,1)S(1)}, u32[]{:S(2)}, u32[]{:S(2)}) collective-permute-start(bf16[256,1024]{1,0:T(8,128)(2,1)} %get-tuple-element.60), channel_id=1, source_target_pairs={{0,2},{1,3},{2,0},{3,1},{4,6},{5,7},{6,4},{7,5},{8,10},{9,11},{10,... | collective-permute-start | bytes 1572872 | tf_op jit(solution)/shard_map/ppermute | solution.py:284
  490.4 55.7 %collective-permute-start.28 = (bf16[256,1024]{1,0:T(8,128)(2,1)}, bf16[256,1024]{1,0:T(8,128)(2,1)S(1)}, u32[]{:S(2)}, u32[]{:S(2)}) collective-permute-start(bf16[256,1024]{1,0:T(8,128)(2,1)} %get-tuple-element.61), channel_id=1, source_target_pairs={{0,3},{1,2},{2,1},{3,0},{4,7},{5,6},{6,5},{7,4},{8,11},{9,10},{10,... | collective-permute-start | bytes 1572872 | tf_op jit(solution)/shard_map/ppermute | solution.py:284
  490.9 3.4 copy-start.5
  494.3 3.4 copy-start.6
  502.7 45.5 %collective-permute-start.21 = (bf16[256,1024]{1,0:T(8,128)(2,1)S(1)}, bf16[256,1024]{1,0:T(8,128)(2,1)S(1)}, u32[]{:S(2)}, u32[]{:S(2)}) collective-permute-start(bf16[256,1024]{1,0:T(8,128)(2,1)S(1)} %get-tuple-element.53), channel_id=1, source_target_pairs={{0,1},{1,0},{2,3},{3,2},{4,5},{5,4},{6,7},{7,6},{8,9},{9,8},{10,11... | collective-permute-start | bytes 1572872 | tf_op jit(solution)/shard_map/ppermute | solution.py:284
  504.3 45.5 %collective-permute-start.22 = (bf16[256,1024]{1,0:T(8,128)(2,1)S(1)}, bf16[256,1024]{1,0:T(8,128)(2,1)S(1)}, u32[]{:S(2)}, u32[]{:S(2)}) collective-permute-start(bf16[256,1024]{1,0:T(8,128)(2,1)S(1)} %get-tuple-element.54), channel_id=1, source_target_pairs={{0,2},{1,3},{2,0},{3,1},{4,6},{5,7},{6,4},{7,5},{8,10},{9,11},{10,... | collective-permute-start | bytes 1572872 | tf_op jit(solution)/shard_map/ppermute | solution.py:284
  511.6 38.2 %collective-permute-start.23 = (bf16[256,1024]{1,0:T(8,128)(2,1)S(1)}, bf16[256,1024]{1,0:T(8,128)(2,1)S(1)}, u32[]{:S(2)}, u32[]{:S(2)}) collective-permute-start(bf16[256,1024]{1,0:T(8,128)(2,1)S(1)} %get-tuple-element.55), channel_id=1, source_target_pairs={{0,3},{1,2},{2,1},{3,0},{4,7},{5,6},{6,5},{7,4},{8,11},{9,10},{10,... | collective-permute-start | bytes 1572872 | tf_op jit(solution)/shard_map/ppermute | solution.py:284
  544.6 37.7 %collective-permute-start.32 = (bf16[256,1024]{1,0:T(8,128)(2,1)S(1)}, bf16[256,1024]{1,0:T(8,128)(2,1)S(1)}, u32[]{:S(2)}, u32[]{:S(2)}) collective-permute-start(bf16[256,1024]{1,0:T(8,128)(2,1)S(1)} %get-tuple-element.66), channel_id=1, source_target_pairs={{0,1},{1,0},{2,3},{3,2},{4,5},{5,4},{6,7},{7,6},{8,9},{9,8},{10,11... | collective-permute-start | bytes 1572872 | tf_op jit(solution)/shard_map/ppermute | solution.py:284
  546.1 37.7 %collective-permute-start.33 = (bf16[256,1024]{1,0:T(8,128)(2,1)S(1)}, bf16[256,1024]{1,0:T(8,128)(2,1)S(1)}, u32[]{:S(2)}, u32[]{:S(2)}) collective-permute-start(bf16[256,1024]{1,0:T(8,128)(2,1)S(1)} %get-tuple-element.67), channel_id=1, source_target_pairs={{0,2},{1,3},{2,0},{3,1},{4,6},{5,7},{6,4},{7,5},{8,10},{9,11},{10,... | collective-permute-start | bytes 1572872 | tf_op jit(solution)/shard_map/ppermute | solution.py:284
  548.2 35.6 %collective-permute-start.34 = (bf16[256,1024]{1,0:T(8,128)(2,1)S(1)}, bf16[256,1024]{1,0:T(8,128)(2,1)S(1)}, u32[]{:S(2)}, u32[]{:S(2)}) collective-permute-start(bf16[256,1024]{1,0:T(8,128)(2,1)S(1)} %get-tuple-element.68), channel_id=1, source_target_pairs={{0,3},{1,2},{2,1},{3,0},{4,7},{5,6},{6,5},{7,4},{8,11},{9,10},{10,... | collective-permute-start | bytes 1572872 | tf_op jit(solution)/shard_map/ppermute | solution.py:284
  580.2 14.6 %collective-permute-start.29 = (bf16[256,1024]{1,0:T(8,128)(2,1)S(1)}, bf16[256,1024]{1,0:T(8,128)(2,1)S(1)}, u32[]{:S(2)}, u32[]{:S(2)}) collective-permute-start(bf16[256,1024]{1,0:T(8,128)(2,1)S(1)} %get-tuple-element.63), channel_id=1, source_target_pairs={{0,1},{1,0},{2,3},{3,2},{4,5},{5,4},{6,7},{7,6},{8,9},{9,8},{10,11... | collective-permute-start | bytes 1572872 | tf_op jit(solution)/shard_map/ppermute | solution.py:284
  581.8 19.9 %collective-permute-start.30 = (bf16[256,1024]{1,0:T(8,128)(2,1)S(1)}, bf16[256,1024]{1,0:T(8,128)(2,1)S(1)}, u32[]{:S(2)}, u32[]{:S(2)}) collective-permute-start(bf16[256,1024]{1,0:T(8,128)(2,1)S(1)} %get-tuple-element.64), channel_id=1, source_target_pairs={{0,2},{1,3},{2,0},{3,1},{4,6},{5,7},{6,4},{7,5},{8,10},{9,11},{10,... | collective-permute-start | bytes 1572872 | tf_op jit(solution)/shard_map/ppermute | solution.py:284
  582.3 19.4 %collective-permute-start.31 = (bf16[256,1024]{1,0:T(8,128)(2,1)S(1)}, bf16[256,1024]{1,0:T(8,128)(2,1)S(1)}, u32[]{:S(2)}, u32[]{:S(2)}) collective-permute-start(bf16[256,1024]{1,0:T(8,128)(2,1)S(1)} %get-tuple-element.65), channel_id=1, source_target_pairs={{0,3},{1,2},{2,1},{3,0},{4,7},{5,6},{6,5},{7,4},{8,11},{9,10},{10,... | collective-permute-start | bytes 1572872 | tf_op jit(solution)/shard_map/ppermute | solution.py:284
  (10 other events, 11.0 us)

commit v7 on v6

--- a/solution.py
+++ b/solution.py
@@ -1,4 +1,5 @@
 import functools
+import math
 
 import jax
 import jax.numpy as jnp
@@ -10,6 +11,8 @@
 B = 512
 J = 128
 epsilon = 1e-06
+inside = (2 / math.pi) ** 0.5
+cubic = 0.044715 * inside
 f32 = jnp.float32
 bf16 = jnp.bfloat16
 ANY = pl.BlockSpec(memory_space=pl.ANY)
@@ -139,7 +142,7 @@
             out_specs=[pl.BlockSpec((c, step * J), lambda i, me: (0, i))] * nt,
         ),
         out_shape=[jax.ShapeDtypeStruct((c, mine * J), bf16)] * nt,
-        compiler_params=params(32),
+        compiler_params=params(56),
         cost_estimate=pl.CostEstimate(
             flops=8 * c * blocks * J,
             bytes_accessed=2 * c * tokens + 4 * c * blocks * J,
@@ -202,14 +205,14 @@
             x = ahead
             if t + tile < tokens:
                 ahead = expand(t + tile)
-            h = jax.nn.gelu(x).astype(bf16)
+            h = (x + x * jnp.tanh(x * (inside + cubic * (x * x)))).astype(bf16)
             total[:, t : t + tile] += jnp.dot(w2[slot], h, preferred_element_type=f32)
 
         @pl.when(step == n - 1)
         def _():
             for s in range(nt):
                 at = pl.multiple_of((me_ref[0] ^ s) * c, c)
-                outs[s][...] = (xs[s][...].astype(f32) + total[pl.ds(at, c), :]).astype(bf16)
+                outs[s][...] = (xs[s][...].astype(f32) + 0.5 * total[pl.ds(at, c), :]).astype(bf16)
 
     whole = pl.BlockSpec((c, tokens), lambda i, me: (0, 0))
     return pl.pallas_call(
@@ -228,7 +231,7 @@
             ],
         ),
         out_shape=[jax.ShapeDtypeStruct((c, tokens), bf16)] * nt,
-        compiler_params=params(40),
+        compiler_params=params(56),
         cost_estimate=pl.CostEstimate(
             flops=4 * full * hb * n * tokens,
             bytes_accessed=4 * full * hb * n + 4 * full * tokens,
@@ -300,20 +303,24 @@
 
 
 def gather_along(ns, both):
-    got = [flip(both, "seq", ns, 2)]
-    both = jnp.concatenate([both, got[0]])
-    bit = 4
-    if ns % 8 == 0:
+    if ns % 8:
+        bit, marks = 2, [both, both]
+    else:
         middle = [i for i in range(ns) if ((i >> 1) ^ (i >> 2)) & 1]
-        got.append(lax.ppermute(both, "seq", [(i, i ^ 6) for i in middle]))
-        got.append(lax.ppermute(got[1], "seq", [(i, i ^ 2) for i in middle]))
-        both = jnp.concatenate([both, got[1] + got[2]])
-        bit = 8
+        across = [(i, i ^ 6) for i in middle]
+        inner = lax.ppermute(both, "seq", across)
+        outer = lax.ppermute(both, "seq", [(i ^ 2, i) for i in middle])
+        beyond = lax.ppermute(outer, "seq", across)
+        out = lax.ppermute(
+            jnp.concatenate([both, inner, beyond]), "seq", [(i, i ^ 2) for i in middle]
+        )
+        both = jnp.concatenate([both, jnp.concatenate([outer, inner, beyond]) + out])
+        bit, marks = 8, [beyond, out]
     while bit < ns:
-        got.append(flip(both, "seq", ns, bit))
-        both = jnp.concatenate([both, got[-1]])
+        marks[1] = flip(both, "seq", ns, bit)
+        both = jnp.concatenate([both, marks[1]])
         bit *= 2
-    return both, got
+    return both, marks
 
 
 def gather_across(nt, start, order):
@@ -368,8 +375,8 @@
     def put(k, done, result, group=0):
         return place(k, group, me, done, result, activations.shape)
 
-    front01 = exchange(after(first(0, 2), got[1]))
-    front23 = exchange(after(first(1, 2), got[-1]))
+    front01 = exchange(after(first(0, 2), got[0]))
+    front23 = exchange(after(first(1, 2), got[1]))
     (mixed0,) = second(front01, 0, [near_in[bits[0]], near_out[bits[-1]]])
     (mixed1,) = second(front01, 1)
     back0 = exchange(mixed0)
@@ -388,9 +395,9 @@
     out1 = layer(in1, [gate2[0]])
     done1 = swap(out1)
     result = put(0, done0, None)
-    gate3 = gated(3, back3, [out1[0], in2[1], result])
+    gate3 = gated(3, back3, [out1[0], in2[1]])
     in3 = swap(gate3)
-    out2 = layer(in2, [gate3[0]])
+    out2 = layer(in2, [gate3[0], result])
     done2 = swap(out2)
     result = put(1, done1, result)
     out3 = layer(in3, [out2[0], result])

time: 605 us -> 654 us (1.081)
  waiting for transfers between devices: 262 us -> 330 us
  local copies, waits for them, and re-layouts: 48.1 us -> 26.9 us
  Pallas kernels: 186 us -> 203 us
  starting transfers between devices: 89.8 us -> 75.3 us
    ppermute x2 -> x4, waiting for transfers between devices: 89.8 us -> 165 us  [the longest x1 148 us: gather_along(): lax.ppermute(jnp.concatenate([both, inner, beyond]), 'seq', [(i, i ^ 2) f...]
    unnamed x66 -> x68, local copies, waits for them, and re-layouts: 43.2 us -> 22.2 us
    ppermute x9 -> x8, waiting for transfers between devices: 63.7 us -> 44.6 us  [flip(): return lax.ppermute(x, axis, [(i, i ^ bit) for i in range(n)])]
    all_to_all x6, starting transfers between devices: 47.7 us -> 31.5 us  [exchange(): return lax.all_to_all(x, 'seq', split_axis=0, concat_axis=0, tiled=True)]
    pallas_call x4, Pallas kernels: 17.3 us -> 26.8 us  [gate(): pl.pallas_call(kernel, grid_spec=pltpu.PrefetchScalarGridSpec(num_scalar_...]
  transfers between devices with their start and end apart: 41 -> 42, of which waited for: 13 -> 14; matrix products, arithmetic and copies ran while one was open for 3% -> 3% of each run, Pallas kernels for 31% -> 31%
where the time goes in v7:
time: 654 us; the launch traced here: 652 us
  waiting for transfers between devices  330 us (50%)
  Pallas kernels  203 us (31%)
  starting transfers between devices  75.3 us (12%)
  local copies, waits for them, and re-layouts  26.9 us (4%)
  other arithmetic  16 us (2%)
    ppermute x1, waiting for transfers between devices, gather_along(): lax.ppermute(jnp.concatenate([both, inner, beyond]), 'seq', [(i, i ^ 2) f...  148 us
    pallas_call x4, Pallas kernels, mlp(): pl.pallas_call(kernel, grid_spec=pltpu.PrefetchScalarGridSpec(num_scalar_...  133 us
    all_to_all x6, waiting for transfers between devices, exchange(): return lax.all_to_all(x, 'seq', split_axis=0, concat_axis=0, tiled=True)  74.8 us
    ppermute x24, waiting for transfers between devices, swap(): lax.ppermute(slots[s], 'tensor', [(i, i ^ s) for i in range(n)])  45.6 us
    ppermute x8, waiting for transfers between devices, flip(): return lax.ppermute(x, axis, [(i, i ^ bit) for i in range(n)])  44.6 us
    all_to_all x6, starting transfers between devices, exchange(): return lax.all_to_all(x, 'seq', split_axis=0, concat_axis=0, tiled=True)  31.5 us
    ppermute x24, starting transfers between devices, swap(): lax.ppermute(slots[s], 'tensor', [(i, i ^ s) for i in range(n)])  28.4 us
    pallas_call x4, Pallas kernels, gate(): pl.pallas_call(kernel, grid_spec=pltpu.PrefetchScalarGridSpec(num_scalar_...  26.8 us
  transfers between devices with their start and end apart: 42, of which 14 were waited for; matrix products, arithmetic and copies ran while one was open for 3% of the time, Pallas kernels for 31%

profile of v7, /device:TPU:0, one launch (start us, length us, event | category | flops | bytes accessed | tf_op | source)
XLA Modules:
  0.0 651.8 jit_solution(3495649289587012094)
XLA Ops:
  1.2 5.0 collective-permute-start.1
  6.2 16.7 %collective-permute-done.1 = bf16[1,2,192,1024]{3,2,1,0:T(8,128)(2,1)S(1)} collective-permute-done((bf16[1,2,192,1024]{3,2,1,0:T(8,128)(2,1)S(1)}, bf16[1,2,192,1024]{3,2,1,0:T(8,128)(2,1)S(1)}, u32[]{:S(2)}, u32[]{:S(2)}) %collective-permute-start.1) | collective-permute-done | bytes 786464 | tf_op jit(solution)/shard_map/ppermute | solution.py:312
  23.6 3.4 copy-done
  28.0 7.9 %shard_map.85.refs_0_ = bf16[8,2,32,32,128]{4,3,2,1,0:T(8,128)(2,1)S(1)} custom-call(bf16[256,16384]{1,0:T(8,128)(2,1)S(1)} %copy-done, bf16[512,512]{1,0:T(8,128)(2,1)S(1)} %copy-done.7, f32[256,16384]{1,0:T(8,128)} %rest_3_.7, f32[256,16384]{1,0:T(8,128)} %rest_3_.7, f32[256,16384]{1,0:T(8,128)} %rest_3_.7, f32[256,16384]{1,0:T(8,128)} %rest_3_.7), custom_call_target="tpu_custom_call" | custom-call | flops 2147483648 | bytes 20971520 | tf_op jit(solution)/shard_map/pallas_call | solution.py:43
  36.0 2.0 copy-done.2
  39.0 10.1 %all-to-all-start.1 = ((bf16[8,2,32,32,128]{4,3,2,1,0:T(8,128)(2,1)}), bf16[8,2,32,32,128]{4,3,2,1,0:T(8,128)(2,1)}, u32[]{:S(2)}, u32[]{:S(2)}) async-start(bf16[8,2,32,32,128]{4,3,2,1,0:T(8,128)(2,1)} %shard_map.86), calls=%async_computation.1 | async-start | bytes 8388608 | tf_op jit(solution)/shard_map/all_to_all | solution.py:361
  52.4 3.4 copy-done.1
  55.8 8.0 %shard_map.82.refs_0_ = bf16[8,2,32,32,128]{4,3,2,1,0:T(8,128)(2,1)S(1)} custom-call(bf16[256,16384]{1,0:T(8,128)(2,1)S(1)} %copy-done.1, bf16[512,512]{1,0:T(8,128)(2,1)S(1)} %copy-done.8, f32[256,16384]{1,0:T(8,128)} %rest_3_.7, f32[256,16384]{1,0:T(8,128)} %rest_3_.7, f32[256,16384]{1,0:T(8,128)} %rest_3_.7, f32[256,16384]{1,0:T(8,128)} %rest_3_.7), custom_call_target="tpu_custom_call" | custom-call | flops 2147483648 | bytes 20971520 | tf_op jit(solution)/shard_map/pallas_call | solution.py:43
  63.8 2.0 copy-done.3
  65.8 147.9 %collective-permute-done.3.refs_1_ = bf16[3,2,192,1024]{3,2,1,0:T(8,128)(2,1)S(1)} collective-permute-done((bf16[3,2,192,1024]{3,2,1,0:T(8,128)(2,1)S(1)}, bf16[3,2,192,1024]{3,2,1,0:T(8,128)(2,1)S(1)}, u32[]{:S(2)}, u32[]{:S(2)}) %collective-permute-start.3) | collective-permute-done | bytes 2359328 | tf_op jit(solution)/shard_map/ppermute | solution.py:314
  215.1 4.7 all-to-all-start
  219.8 1.9 fusion
  223.2 1.5 collective-permute-start.4
  224.7 1.6 copy.17
  226.3 1.5 collective-permute-start.9
  228.3 31.8 %collective-permute-done.4.rest_0_ = bf16[768,1024]{1,0:T(8,128)(2,1)S(1)} collective-permute-done((bf16[768,1024]{1,0:T(8,128)(2,1)}, bf16[768,1024]{1,0:T(8,128)(2,1)S(1)}, u32[]{:S(2)}, u32[]{:S(2)}) %collective-permute-start.4) | collective-permute-done | bytes 1572896 | tf_op jit(solution)/shard_map/ppermute | solution.py:302
  260.1 1.5 collective-permute-start.6
  261.6 1.5 collective-permute-start.8
  264.3 5.7 shard_map.87
  270.0 43.8 %all-to-all-done.x_ref = bf16[8,2,32,32,128]{4,3,2,1,0:T(8,128)(2,1)} async-done(((bf16[8,2,32,32,128]{4,3,2,1,0:T(8,128)(2,1)}), bf16[8,2,32,32,128]{4,3,2,1,0:T(8,128)(2,1)}, u32[]{:S(2)}, u32[]{:S(2)}) %all-to-all-start) | async-done | bytes 4194336 | tf_op jit(solution)/shard_map/all_to_all | solution.py:361
  313.8 4.4 all-to-all-start.2
  318.2 12.2 %collective-permute-done.6 = bf16[768,1024]{1,0:T(8,128)(2,1)} collective-permute-done((bf16[768,1024]{1,0:T(8,128)(2,1)S(1)}, bf16[768,1024]{1,0:T(8,128)(2,1)}, u32[]{:S(2)}, u32[]{:S(2)}) %collective-permute-start.6) | collective-permute-done | bytes 1572896 | tf_op jit(solution)/shard_map/ppermute | solution.py:302
  330.4 5.9 pad_maximum_fusion.rest_4_.rest_0_
  336.3 5.3 pad_maximum_fusion.1.rest_6_.rest_1_
  342.1 5.6 shard_map.89
  347.7 19.5 %all-to-all-done.2.rest_4_.rest_5_.rest_6_.rest_7_ = bf16[8,32,32,128]{3,2,1,0:T(8,128)(2,1)} async-done(((bf16[8,32,32,128]{3,2,1,0:T(8,128)(2,1)}), bf16[8,32,32,128]{3,2,1,0:T(8,128)(2,1)}, u32[]{:S(2)}, u32[]{:S(2)}) %all-to-all-start.2) | async-done | bytes 2097184 | tf_op jit(solution)/shard_map/all_to_all | solution.py:361
  367.2 3.6 all-to-all-start.3
  374.0 6.7 %shard_map.88 = (bf16[256,1024]{1,0:T(8,128)(2,1)}, bf16[256,1024]{1,0:T(8,128)(2,1)}, bf16[256,1024]{1,0:T(8,128)(2,1)}, bf16[256,1024]{1,0:T(8,128)(2,1)}) custom-call(s32[1]{0:T(128)} %bitcast.me_ref, bf16[256,16384]{1,0:T(8,128)(2,1)} %rest_3_.11, bf16[256,16384]{1,0:T(8,128)(2,1)} %rest_3_.11, bf16[256,16384]{1,0:T(8,128)(2,1)} %rest_3_.11, ...), custom_call_target="tpu_custom_call" | custom-call | flops 8388608 | bytes 12582912 | tf_op jit(solution)/shard_map/pallas_call | solution.py:133
  380.7 1.6 collective-permute-start.12
  382.2 1.5 collective-permute-start.13
  384.2 4.8 shard_map.93.refs_0_
  390.4 5.3 collective-permute-done.12.rest_1_.refs_1_
  395.7 11.9 %collective-permute-done.13.rest_2_.refs_2_ = bf16[256,1024]{1,0:T(8,128)(2,1)S(1)} collective-permute-done((bf16[256,1024]{1,0:T(8,128)(2,1)}, bf16[256,1024]{1,0:T(8,128)(2,1)S(1)}, u32[]{:S(2)}, u32[]{:S(2)}) %collective-permute-start.13) | collective-permute-done | bytes 524320 | tf_op jit(solution)/shard_map/ppermute | solution.py:287
  408.4 11.4 %all-to-all-done.3.rest_4_.rest_5_.rest_6_.rest_7_ = bf16[8,32,32,128]{3,2,1,0:T(8,128)(2,1)S(1)} async-done(((bf16[8,32,32,128]{3,2,1,0:T(8,128)(2,1)}), bf16[8,32,32,128]{3,2,1,0:T(8,128)(2,1)S(1)}, u32[]{:S(2)}, u32[]{:S(2)}) %all-to-all-start.3) | async-done | bytes 2097184 | tf_op jit(solution)/shard_map/all_to_all | solution.py:361
  421.2 3.8 all-to-all-start.5
  425.0 6.7 %shard_map.90 = (bf16[256,1024]{1,0:T(8,128)(2,1)}, bf16[256,1024]{1,0:T(8,128)(2,1)}, bf16[256,1024]{1,0:T(8,128)(2,1)}, bf16[256,1024]{1,0:T(8,128)(2,1)}) custom-call(s32[1]{0:T(128)} %bitcast.me_ref, bf16[256,16384]{1,0:T(8,128)(2,1)} %rest_3_.11, bf16[256,16384]{1,0:T(8,128)(2,1)} %rest_3_.11, bf16[256,16384]{1,0:T(8,128)(2,1)} %rest_3_.11, ...), custom_call_target="tpu_custom_call" | custom-call | flops 8388608 | bytes 12582912 | tf_op jit(solution)/shard_map/pallas_call | solution.py:133
  431.7 1.6 collective-permute-start.15
  433.2 1.5 collective-permute-start.16
  435.2 33.3 %shard_map.91 = (bf16[256,1024]{1,0:T(8,128)(2,1)}, bf16[256,1024]{1,0:T(8,128)(2,1)}, bf16[256,1024]{1,0:T(8,128)(2,1)}, bf16[256,1024]{1,0:T(8,128)(2,1)}) custom-call(s32[1]{0:T(128)} %bitcast.me_ref, bf16[256,1024]{1,0:T(8,128)(2,1)} %get-tuple-element.37.rest_0_, bf16[256,1024]{1,0:T(8,128)(2,1)} %copy-done.25, bf16[256,1024]{1,0:T(8,128)(2,1)} %copy-done.26, ...), custom_call_target="tpu_custom_call" | custom-call | flops 25769803776 | bytes 29360128 | tf_op jit(solution)/shard_map/pallas_call | solution.py:218
  468.5 4.8 shard_map.84.refs_0_
  475.8 5.0 all-to-all-start.4
  480.8 1.5 collective-permute-start.24
  482.3 1.5 collective-permute-start.25
  484.3 6.7 %shard_map.95 = (bf16[256,1024]{1,0:T(8,128)(2,1)}, bf16[256,1024]{1,0:T(8,128)(2,1)}, bf16[256,1024]{1,0:T(8,128)(2,1)}, bf16[256,1024]{1,0:T(8,128)(2,1)}) custom-call(s32[1]{0:T(128)} %bitcast.me_ref, bf16[256,16384]{1,0:T(8,128)(2,1)} %rest_3_.11, bf16[256,16384]{1,0:T(8,128)(2,1)} %rest_3_.11, bf16[256,16384]{1,0:T(8,128)(2,1)} %rest_3_.11, ...), custom_call_target="tpu_custom_call" | custom-call | flops 8388608 | bytes 12582912 | tf_op jit(solution)/shard_map/pallas_call | solution.py:133
  491.0 1.6 collective-permute-start.18
  492.6 1.5 collective-permute-start.22
  494.1 33.3 %shard_map.96 = (bf16[256,1024]{1,0:T(8,128)(2,1)}, bf16[256,1024]{1,0:T(8,128)(2,1)}, bf16[256,1024]{1,0:T(8,128)(2,1)}, bf16[256,1024]{1,0:T(8,128)(2,1)}) custom-call(s32[1]{0:T(128)} %bitcast.me_ref, bf16[256,1024]{1,0:T(8,128)(2,1)} %get-tuple-element.41.rest_8_.rest_0_, bf16[256,1024]{1,0:T(8,128)(2,1)} %copy-done.23, bf16[256,1024]{1,0:T(8,128)(2,1)} %copy-done.24, ...), custom_call_target="tpu_custom_call" | custom-call | flops 25769803776 | bytes 29360128 | tf_op jit(solution)/shard_map/pallas_call | solution.py:218
  528.0 1.5 collective-permute-start.27
  529.5 1.6 shard_map.98.rest_9_.rest_4_
  531.1 1.5 collective-permute-start.28
  533.4 6.7 %shard_map.97 = (bf16[256,1024]{1,0:T(8,128)(2,1)}, bf16[256,1024]{1,0:T(8,128)(2,1)}, bf16[256,1024]{1,0:T(8,128)(2,1)}, bf16[256,1024]{1,0:T(8,128)(2,1)}) custom-call(s32[1]{0:T(128)} %bitcast.me_ref, bf16[256,16384]{1,0:T(8,128)(2,1)} %rest_3_.11, bf16[256,16384]{1,0:T(8,128)(2,1)} %rest_3_.11, bf16[256,16384]{1,0:T(8,128)(2,1)} %rest_3_.11, ...), custom_call_target="tpu_custom_call" | custom-call | flops 8388608 | bytes 12582912 | tf_op jit(solution)/shard_map/pallas_call | solution.py:133
  541.5 2.1 collective-permute-done.23.rest_3_
  544.1 9.7 %collective-permute-done.27.rest_1_ = bf16[256,1024]{1,0:T(8,128)(2,1)S(1)} collective-permute-done((bf16[256,1024]{1,0:T(8,128)(2,1)}, bf16[256,1024]{1,0:T(8,128)(2,1)S(1)}, u32[]{:S(2)}, u32[]{:S(2)}) %collective-permute-start.27) | collective-permute-done | bytes 524320 | tf_op jit(solution)/shard_map/ppermute | solution.py:287
  555.3 33.4 %shard_map.99 = (bf16[256,1024]{1,0:T(8,128)(2,1)}, bf16[256,1024]{1,0:T(8,128)(2,1)}, bf16[256,1024]{1,0:T(8,128)(2,1)}, bf16[256,1024]{1,0:T(8,128)(2,1)}) custom-call(s32[1]{0:T(128)} %bitcast.me_ref, bf16[256,1024]{1,0:T(8,128)(2,1)} %get-tuple-element.46.rest_8_.rest_0_, bf16[256,1024]{1,0:T(8,128)(2,1)} %copy-done.22, bf16[256,1024]{1,0:T(8,128)(2,1)} %copy-done.28, ...), custom_call_target="tpu_custom_call" | custom-call | flops 25769803776 | bytes 29360128 | tf_op jit(solution)/shard_map/pallas_call | solution.py:218
  588.7 1.5 collective-permute-start.33
  590.7 1.6 shard_map.100.rest_9_.rest_4_
  592.3 1.5 collective-permute-start.35
  594.9 33.4 %shard_map.101 = (bf16[256,1024]{1,0:T(8,128)(2,1)}, bf16[256,1024]{1,0:T(8,128)(2,1)}, bf16[256,1024]{1,0:T(8,128)(2,1)}, bf16[256,1024]{1,0:T(8,128)(2,1)}) custom-call(s32[1]{0:T(128)} %bitcast.me_ref, bf16[256,1024]{1,0:T(8,128)(2,1)} %get-tuple-element.49.rest_8_.rest_0_, bf16[256,1024]{1,0:T(8,128)(2,1)} %copy-done.31, bf16[256,1024]{1,0:T(8,128)(2,1)} %copy-done.32, ...), custom_call_target="tpu_custom_call" | custom-call | flops 25769803776 | bytes 29360128 | tf_op jit(solution)/shard_map/pallas_call | solution.py:218
  628.3 1.5 collective-permute-start.30
  630.4 1.5 collective-permute-start.32
  631.8 1.6 shard_map.102.rest_4_
  633.4 9.7 %collective-permute-done.30.rest_1_ = bf16[256,1024]{1,0:T(8,128)(2,1)S(1)} collective-permute-done((bf16[256,1024]{1,0:T(8,128)(2,1)}, bf16[256,1024]{1,0:T(8,128)(2,1)S(1)}, u32[]{:S(2)}, u32[]{:S(2)}) %collective-permute-start.30) | collective-permute-done | bytes 524320 | tf_op jit(solution)/shard_map/ppermute | solution.py:287
  643.1 6.9 %collective-permute-done.31.rest_2_ = bf16[256,1024]{1,0:T(8,128)(2,1)S(1)} collective-permute-done((bf16[256,1024]{1,0:T(8,128)(2,1)}, bf16[256,1024]{1,0:T(8,128)(2,1)S(1)}, u32[]{:S(2)}, u32[]{:S(2)}) %collective-permute-start.31) | collective-permute-done | bytes 524320 | tf_op jit(solution)/shard_map/ppermute | solution.py:287
  650.0 1.6 shard_map.103
  (121 shorter events, 29.5 us)
Async XLA Ops:
  1.2 21.7 %collective-permute-start.1 = (bf16[1,2,192,1024]{3,2,1,0:T(8,128)(2,1)S(1)}, bf16[1,2,192,1024]{3,2,1,0:T(8,128)(2,1)S(1)}, u32[]{:S(2)}, u32[]{:S(2)}) collective-permute-start(bf16[1,2,192,1024]{3,2,1,0:T(8,128)(2,1)S(1)} %maximum_bitcast_fusion), channel_id=1, source_target_pairs={{0,8},{4,12},{24,16},{28,20},{1,9},{5,13},{25,17},{29,21},{2,10},{... | collective-permute-start | bytes 2359304 | tf_op jit(solution)/shard_map/ppermute | solution.py:312
  22.9 13.1 %copy-start.21 = (bf16[1,2,192,1024]{3,2,1,0:T(8,128)(2,1)}, bf16[1,2,192,1024]{3,2,1,0:T(8,128)(2,1)S(1)}, u32[]{:S(2)}) copy-start(bf16[1,2,192,1024]{3,2,1,0:T(8,128)(2,1)S(1)} %collective-permute-done.1) | copy-start | bytes 2359300
  22.9 15.1 %collective-permute-start.2 = (bf16[1,2,192,1024]{3,2,1,0:T(8,128)(2,1)S(1)}, bf16[1,2,192,1024]{3,2,1,0:T(8,128)(2,1)S(1)}, u32[]{:S(2)}, u32[]{:S(2)}) collective-permute-start(bf16[1,2,192,1024]{3,2,1,0:T(8,128)(2,1)S(1)} %collective-permute-done.1), channel_id=1, source_target_pairs={{8,16},{12,20},{16,8},{20,12},{9,17},{13,21},{17,9},{21,13},{10,18... | collective-permute-start | bytes 2359304 | tf_op jit(solution)/shard_map/ppermute | solution.py:313
  23.6 3.4 copy-start
  36.0 2.0 copy-start.2
  39.0 11.8 %copy-start.18 = (bf16[1,2,192,1024]{3,2,1,0:T(8,128)(2,1)S(1)}, bf16[1,2,192,1024]{3,2,1,0:T(8,128)(2,1)}, u32[]{:S(2)}) copy-start(bf16[1,2,192,1024]{3,2,1,0:T(8,128)(2,1)} %copy-done.17) | copy-start | bytes 2359300
  39.0 176.1 %all-to-all-start.1 = ((bf16[8,2,32,32,128]{4,3,2,1,0:T(8,128)(2,1)}), bf16[8,2,32,32,128]{4,3,2,1,0:T(8,128)(2,1)}, u32[]{:S(2)}, u32[]{:S(2)}) async-start(bf16[8,2,32,32,128]{4,3,2,1,0:T(8,128)(2,1)} %shard_map.86), calls=%async_computation.1 | async-start | bytes 8388608 | tf_op jit(solution)/shard_map/all_to_all | solution.py:361
  49.1 3.3 copy-start.8
  49.1 0.9 collective-permute-start
  51.1 162.6 %collective-permute-start.3 = (bf16[3,2,192,1024]{3,2,1,0:T(8,128)(2,1)S(1)}, bf16[3,2,192,1024]{3,2,1,0:T(8,128)(2,1)S(1)}, u32[]{:S(2)}, u32[]{:S(2)}) collective-permute-start(bf16[3,2,192,1024]{3,2,1,0:T(8,128)(2,1)S(1)} %pad_maximum_fusion.3), channel_id=1, source_target_pairs={{8,0},{12,4},{16,24},{20,28},{9,1},{13,5},{17,25},{21,29},{10,2},{... | collective-permute-start | bytes 7077896 | tf_op jit(solution)/shard_map/ppermute | solution.py:314
  52.4 3.4 copy-start.1
  63.8 2.0 copy-start.3
  215.1 4.7 copy-start.16
  215.1 98.7 %all-to-all-start = ((bf16[8,2,32,32,128]{4,3,2,1,0:T(8,128)(2,1)}), bf16[8,2,32,32,128]{4,3,2,1,0:T(8,128)(2,1)}, u32[]{:S(2)}, u32[]{:S(2)}) async-start(bf16[8,2,32,32,128]{4,3,2,1,0:T(8,128)(2,1)} %shard_map.83), calls=%async_computation | async-start | bytes 8388608 | tf_op jit(solution)/shard_map/all_to_all | solution.py:361
  223.2 41.1 %copy-start.6 = (f32[256,256]{1,0:T(8,128)S(1)}, f32[256,256]{1,0:T(8,128)}, u32[]{:S(2)}) copy-start(f32[256,256]{1,0:T(8,128)} %s_ref.7) | copy-start | bytes 786436
  223.2 36.9 %collective-permute-start.4 = (bf16[768,1024]{1,0:T(8,128)(2,1)}, bf16[768,1024]{1,0:T(8,128)(2,1)S(1)}, u32[]{:S(2)}, u32[]{:S(2)}) collective-permute-start(bf16[768,1024]{1,0:T(8,128)(2,1)} %bitcast.6), channel_id=1, source_target_pairs={{0,1},{1,0},{2,3},{3,2},{4,5},{5,4},{6,7},{7,6},{8,9},{9,8},{10,11... | collective-permute-start | bytes 4718600 | tf_op jit(solution)/shard_map/ppermute | solution.py:302
  226.3 37.5 %collective-permute-start.9 = (bf16[1024,768]{1,0:T(8,128)(2,1)}, bf16[1024,768]{1,0:T(8,128)(2,1)S(1)}, u32[]{:S(2)}, u32[]{:S(2)}) collective-permute-start(bf16[1024,768]{1,0:T(8,128)(2,1)} %bitcast.23), channel_id=1, source_target_pairs={{0,2},{1,3},{2,0},{3,1},{4,6},{5,7},{6,4},{7,5},{8,10},{9,11},{10,... | collective-permute-start | bytes 4718600 | tf_op jit(solution)/shard_map/ppermute | solution.py:302
  227.8 90.4 %collective-permute-start.5 = (bf16[768,1024]{1,0:T(8,128)(2,1)}, bf16[768,1024]{1,0:T(8,128)(2,1)}, u32[]{:S(2)}, u32[]{:S(2)}) collective-permute-start(bf16[768,1024]{1,0:T(8,128)(2,1)} %bitcast.6), channel_id=1, source_target_pairs={{0,2},{1,3},{2,0},{3,1},{4,6},{5,7},{6,4},{7,5},{8,10},{9,11},{10,... | collective-permute-start | bytes 4718600 | tf_op jit(solution)/shard_map/ppermute | solution.py:302
  260.1 70.3 %collective-permute-start.6 = (bf16[768,1024]{1,0:T(8,128)(2,1)S(1)}, bf16[768,1024]{1,0:T(8,128)(2,1)}, u32[]{:S(2)}, u32[]{:S(2)}) collective-permute-start(bf16[768,1024]{1,0:T(8,128)(2,1)S(1)} %collective-permute-done.4.rest_0_), channel_id=1, source_target_pairs={{0,2},{1,3},{2,0},{3,1},{4,6},{5,7},{6,4},{7,5},{8,10},{9,11},{10,... | collective-permute-start | bytes 4718600 | tf_op jit(solution)/shard_map/ppermute | solution.py:302
  261.6 74.7 %collective-permute-start.8 = (bf16[1024,768]{1,0:T(8,128)(2,1)}, bf16[1024,768]{1,0:T(8,128)(2,1)}, u32[]{:S(2)}, u32[]{:S(2)}) collective-permute-start(bf16[1024,768]{1,0:T(8,128)(2,1)} %bitcast.24), channel_id=1, source_target_pairs={{0,1},{1,0},{2,3},{3,2},{4,5},{5,4},{6,7},{7,6},{8,9},{9,8},{10,11... | collective-permute-start | bytes 4718600 | tf_op jit(solution)/shard_map/ppermute | solution.py:302
  263.7 72.6 %collective-permute-start.10 = (bf16[1024,768]{1,0:T(8,128)(2,1)S(1)}, bf16[1024,768]{1,0:T(8,128)(2,1)}, u32[]{:S(2)}, u32[]{:S(2)}) collective-permute-start(bf16[1024,768]{1,0:T(8,128)(2,1)S(1)} %collective-permute-done.9.rest_1_), channel_id=1, source_target_pairs={{0,1},{1,0},{2,3},{3,2},{4,5},{5,4},{6,7},{7,6},{8,9},{9,8},{10,11... | collective-permute-start | bytes 4718600 | tf_op jit(solution)/shard_map/ppermute | solution.py:302
  313.8 53.4 %all-to-all-start.2 = ((bf16[8,32,32,128]{3,2,1,0:T(8,128)(2,1)}), bf16[8,32,32,128]{3,2,1,0:T(8,128)(2,1)}, u32[]{:S(2)}, u32[]{:S(2)}) async-start(bf16[8,32,32,128]{3,2,1,0:T(8,128)(2,1)} %shard_map.87), calls=%async_computation.2 | async-start | bytes 4194304 | tf_op jit(solution)/shard_map/all_to_all | solution.py:361
  330.4 5.9 copy-start.19
  336.3 98.9 %collective-permute-start.7 = (bf16[4,768,1024]{2,1,0:T(8,128)(2,1)}, bf16[4,768,1024]{2,1,0:T(8,128)(2,1)}, u32[]{:S(2)}, u32[]{:S(2)}) collective-permute-start(bf16[4,768,1024]{2,1,0:T(8,128)(2,1)} %pad_maximum_fusion.rest_4_.rest_0_), channel_id=1, source_target_pairs={{0,4},{4,0},{8,12},{12,8},{16,20},{20,16},{24,28},{28,24},{1,5},{5... | collective-permute-start | bytes 18874376 | tf_op jit(solution)/shard_map/ppermute | solution.py:302
  341.6 93.6 %collective-permute-start.11 = (bf16[4,1024,768]{2,1,0:T(8,128)(2,1)}, bf16[4,1024,768]{2,1,0:T(8,128)(2,1)}, u32[]{:S(2)}, u32[]{:S(2)}) collective-permute-start(bf16[4,1024,768]{2,1,0:T(8,128)(2,1)} %pad_maximum_fusion.1.rest_6_.rest_1_), channel_id=1, source_target_pairs={{0,4},{4,0},{8,12},{12,8},{16,20},{20,16},{24,28},{28,24},{1,5},{5... | collective-permute-start | bytes 18874376 | tf_op jit(solution)/shard_map/ppermute | solution.py:302
  367.2 52.6 %all-to-all-start.3 = ((bf16[8,32,32,128]{3,2,1,0:T(8,128)(2,1)}), bf16[8,32,32,128]{3,2,1,0:T(8,128)(2,1)S(1)}, u32[]{:S(2)}, u32[]{:S(2)}) async-start(bf16[8,32,32,128]{3,2,1,0:T(8,128)(2,1)} %shard_map.89), calls=%async_computation.3 | async-start | bytes 4194304 | tf_op jit(solution)/shard_map/all_to_all | solution.py:361
  380.7 15.0 %collective-permute-start.12 = (bf16[256,1024]{1,0:T(8,128)(2,1)}, bf16[256,1024]{1,0:T(8,128)(2,1)S(1)}, u32[]{:S(2)}, u32[]{:S(2)}) collective-permute-start(bf16[256,1024]{1,0:T(8,128)(2,1)} %get-tuple-element.38), channel_id=1, source_target_pairs={{0,1},{1,0},{2,3},{3,2},{4,5},{5,4},{6,7},{7,6},{8,9},{9,8},{10,11... | collective-permute-start | bytes 1572872 | tf_op jit(solution)/shard_map/ppermute | solution.py:287
  382.2 25.4 %collective-permute-start.13 = (bf16[256,1024]{1,0:T(8,128)(2,1)}, bf16[256,1024]{1,0:T(8,128)(2,1)S(1)}, u32[]{:S(2)}, u32[]{:S(2)}) collective-permute-start(bf16[256,1024]{1,0:T(8,128)(2,1)} %get-tuple-element.39), channel_id=1, source_target_pairs={{0,2},{1,3},{2,0},{3,1},{4,6},{5,7},{6,4},{7,5},{8,10},{9,11},{10,... | collective-permute-start | bytes 1572872 | tf_op jit(solution)/shard_map/ppermute | solution.py:287
  383.8 23.8 %collective-permute-start.14 = (bf16[256,1024]{1,0:T(8,128)(2,1)}, bf16[256,1024]{1,0:T(8,128)(2,1)}, u32[]{:S(2)}, u32[]{:S(2)}) collective-permute-start(bf16[256,1024]{1,0:T(8,128)(2,1)} %get-tuple-element.40), channel_id=1, source_target_pairs={{0,3},{1,2},{2,1},{3,0},{4,7},{5,6},{6,5},{7,4},{8,11},{9,10},{10,... | collective-permute-start | bytes 1572872 | tf_op jit(solution)/shard_map/ppermute | solution.py:287
  395.7 11.9 %copy-start.25 = (bf16[256,1024]{1,0:T(8,128)(2,1)}, bf16[256,1024]{1,0:T(8,128)(2,1)S(1)}, u32[]{:S(2)}) copy-start(bf16[256,1024]{1,0:T(8,128)(2,1)S(1)} %collective-permute-done.12.rest_1_.refs_1_) | copy-start | bytes 1572868
  421.2 54.6 %all-to-all-start.5 = ((bf16[8,32,32,128]{3,2,1,0:T(8,128)(2,1)}), bf16[8,32,32,128]{3,2,1,0:T(8,128)(2,1)S(1)}, u32[]{:S(2)}, u32[]{:S(2)}) async-start(bf16[8,32,32,128]{3,2,1,0:T(8,128)(2,1)} %shard_map.94), calls=%async_computation.5 | async-start | bytes 4194304 | tf_op jit(solution)/shard_map/all_to_all | solution.py:361
  431.7 43.1 %collective-permute-start.15 = (bf16[256,1024]{1,0:T(8,128)(2,1)}, bf16[256,1024]{1,0:T(8,128)(2,1)S(1)}, u32[]{:S(2)}, u32[]{:S(2)}) collective-permute-start(bf16[256,1024]{1,0:T(8,128)(2,1)} %get-tuple-element.43), channel_id=1, source_target_pairs={{0,1},{1,0},{2,3},{3,2},{4,5},{5,4},{6,7},{7,6},{8,9},{9,8},{10,11... | collective-permute-start | bytes 1572872 | tf_op jit(solution)/shard_map/ppermute | solution.py:287
  433.2 41.6 %collective-permute-start.16 = (bf16[256,1024]{1,0:T(8,128)(2,1)}, bf16[256,1024]{1,0:T(8,128)(2,1)S(1)}, u32[]{:S(2)}, u32[]{:S(2)}) collective-permute-start(bf16[256,1024]{1,0:T(8,128)(2,1)} %get-tuple-element.44), channel_id=1, source_target_pairs={{0,2},{1,3},{2,0},{3,1},{4,6},{5,7},{6,4},{7,5},{8,10},{9,11},{10,... | collective-permute-start | bytes 1572872 | tf_op jit(solution)/shard_map/ppermute | solution.py:287
  434.7 40.1 %collective-permute-start.17 = (bf16[256,1024]{1,0:T(8,128)(2,1)}, bf16[256,1024]{1,0:T(8,128)(2,1)}, u32[]{:S(2)}, u32[]{:S(2)}) collective-permute-start(bf16[256,1024]{1,0:T(8,128)(2,1)} %get-tuple-element.45), channel_id=1, source_target_pairs={{0,3},{1,2},{2,1},{3,0},{4,7},{5,6},{6,5},{7,4},{8,11},{9,10},{10,... | collective-permute-start | bytes 1572872 | tf_op jit(solution)/shard_map/ppermute | solution.py:287
  473.3 1.4 copy-start.4
  475.8 6.5 copy-start.29
  475.8 8.5 %copy-start.13 = (bf16[8,32,32,128]{3,2,1,0:T(8,128)(2,1)}, bf16[8,32,32,128]{3,2,1,0:T(8,128)(2,1)S(1)}, u32[]{:S(2)}) copy-start(bf16[8,32,32,128]{3,2,1,0:T(8,128)(2,1)S(1)} %all-to-all-done.5.rest_4_.rest_5_.rest_6_.rest_7_) | copy-start | bytes 6291460
  475.8 57.4 %all-to-all-start.4 = ((bf16[8,32,32,128]{3,2,1,0:T(8,128)(2,1)}), bf16[8,32,32,128]{3,2,1,0:T(8,128)(2,1)}, u32[]{:S(2)}, u32[]{:S(2)}) async-start(bf16[8,32,32,128]{3,2,1,0:T(8,128)(2,1)} %shard_map.92), calls=%async_computation.4 | async-start | bytes 4194304 | tf_op jit(solution)/shard_map/all_to_all | solution.py:361
  480.8 46.6 %collective-permute-start.24 = (bf16[256,1024]{1,0:T(8,128)(2,1)}, bf16[256,1024]{1,0:T(8,128)(2,1)S(1)}, u32[]{:S(2)}, u32[]{:S(2)}) collective-permute-start(bf16[256,1024]{1,0:T(8,128)(2,1)} %get-tuple-element.55), channel_id=1, source_target_pairs={{0,1},{1,0},{2,3},{3,2},{4,5},{5,4},{6,7},{7,6},{8,9},{9,8},{10,11... | collective-permute-start | bytes 1572872 | tf_op jit(solution)/shard_map/ppermute | solution.py:287
  482.3 45.7 %collective-permute-start.25 = (bf16[256,1024]{1,0:T(8,128)(2,1)S(1)}, bf16[256,1024]{1,0:T(8,128)(2,1)S(1)}, u32[]{:S(2)}, u32[]{:S(2)}) collective-permute-start(bf16[256,1024]{1,0:T(8,128)(2,1)S(1)} %copy-done.29), channel_id=1, source_target_pairs={{0,2},{1,3},{2,0},{3,1},{4,6},{5,7},{6,4},{7,5},{8,10},{9,11},{10,... | collective-permute-start | bytes 1572872 | tf_op jit(solution)/shard_map/ppermute | solution.py:287
  483.8 45.7 %collective-permute-start.26 = (bf16[256,1024]{1,0:T(8,128)(2,1)}, bf16[256,1024]{1,0:T(8,128)(2,1)S(1)}, u32[]{:S(2)}, u32[]{:S(2)}) collective-permute-start(bf16[256,1024]{1,0:T(8,128)(2,1)} %get-tuple-element.57), channel_id=1, source_target_pairs={{0,3},{1,2},{2,1},{3,0},{4,7},{5,6},{6,5},{7,4},{8,11},{9,10},{10,... | collective-permute-start | bytes 1572872 | tf_op jit(solution)/shard_map/ppermute | solution.py:287
  491.0 41.6 %collective-permute-start.18 = (bf16[256,1024]{1,0:T(8,128)(2,1)}, bf16[256,1024]{1,0:T(8,128)(2,1)S(1)}, u32[]{:S(2)}, u32[]{:S(2)}) collective-permute-start(bf16[256,1024]{1,0:T(8,128)(2,1)} %get-tuple-element.48), channel_id=1, source_target_pairs={{0,1},{1,0},{2,3},{3,2},{4,5},{5,4},{6,7},{7,6},{8,9},{9,8},{10,11... | collective-permute-start | bytes 1572872 | tf_op jit(solution)/shard_map/ppermute | solution.py:287
  492.6 47.5 %collective-permute-start.22 = (bf16[256,1024]{1,0:T(8,128)(2,1)}, bf16[256,1024]{1,0:T(8,128)(2,1)S(1)}, u32[]{:S(2)}, u32[]{:S(2)}) collective-permute-start(bf16[256,1024]{1,0:T(8,128)(2,1)} %get-tuple-element.53), channel_id=1, source_target_pairs={{0,2},{1,3},{2,0},{3,1},{4,6},{5,7},{6,4},{7,5},{8,10},{9,11},{10,... | collective-permute-start | bytes 1572872 | tf_op jit(solution)/shard_map/ppermute | solution.py:287
  494.1 35.4 %copy-start.10 = (bf16[256,1024]{1,0:T(8,128)(2,1)S(1)}, bf16[256,1024]{1,0:T(8,128)(2,1)}, u32[]{:S(2)}) copy-start(bf16[256,1024]{1,0:T(8,128)(2,1)} %get-tuple-element.42.refs_1_.rest_0_) | copy-start | bytes 1572868
  527.4 16.2 %collective-permute-start.23 = (bf16[256,1024]{1,0:T(8,128)(2,1)}, bf16[256,1024]{1,0:T(8,128)(2,1)}, u32[]{:S(2)}, u32[]{:S(2)}) collective-permute-start(bf16[256,1024]{1,0:T(8,128)(2,1)} %get-tuple-element.54), channel_id=1, source_target_pairs={{0,3},{1,2},{2,1},{3,0},{4,7},{5,6},{6,5},{7,4},{8,11},{9,10},{10,... | collective-permute-start | bytes 1572872 | tf_op jit(solution)/shard_map/ppermute | solution.py:287
  528.0 4.6 copy-start.27
  528.0 25.8 %collective-permute-start.27 = (bf16[256,1024]{1,0:T(8,128)(2,1)}, bf16[256,1024]{1,0:T(8,128)(2,1)S(1)}, u32[]{:S(2)}, u32[]{:S(2)}) collective-permute-start(bf16[256,1024]{1,0:T(8,128)(2,1)} %get-tuple-element.59), channel_id=1, source_target_pairs={{0,1},{1,0},{2,3},{3,2},{4,5},{5,4},{6,7},{7,6},{8,9},{9,8},{10,11... | collective-permute-start | bytes 1572872 | tf_op jit(solution)/shard_map/ppermute | solution.py:287
  531.1 57.6 %collective-permute-start.28 = (bf16[256,1024]{1,0:T(8,128)(2,1)}, bf16[256,1024]{1,0:T(8,128)(2,1)S(1)}, u32[]{:S(2)}, u32[]{:S(2)}) collective-permute-start(bf16[256,1024]{1,0:T(8,128)(2,1)} %get-tuple-element.60), channel_id=1, source_target_pairs={{0,2},{1,3},{2,0},{3,1},{4,6},{5,7},{6,4},{7,5},{8,10},{9,11},{10,... | collective-permute-start | bytes 1572872 | tf_op jit(solution)/shard_map/ppermute | solution.py:287
  532.6 57.6 %collective-permute-start.29 = (bf16[256,1024]{1,0:T(8,128)(2,1)S(1)}, bf16[256,1024]{1,0:T(8,128)(2,1)S(1)}, u32[]{:S(2)}, u32[]{:S(2)}) collective-permute-start(bf16[256,1024]{1,0:T(8,128)(2,1)S(1)} %copy-done.27), channel_id=1, source_target_pairs={{0,3},{1,2},{2,1},{3,0},{4,7},{5,6},{6,5},{7,4},{8,11},{9,10},{10,... | collective-permute-start | bytes 1572872 | tf_op jit(solution)/shard_map/ppermute | solution.py:287
  540.1 15.2 %copy-start.28 = (bf16[256,1024]{1,0:T(8,128)(2,1)}, bf16[256,1024]{1,0:T(8,128)(2,1)S(1)}, u32[]{:S(2)}) copy-start(bf16[256,1024]{1,0:T(8,128)(2,1)S(1)} %collective-permute-done.22.rest_2_) | copy-start | bytes 1572868
  540.1 52.2 %collective-permute-start.19 = (bf16[256,1024]{1,0:T(8,128)(2,1)}, bf16[256,1024]{1,0:T(8,128)(2,1)S(1)}, u32[]{:S(2)}, u32[]{:S(2)}) collective-permute-start(bf16[256,1024]{1,0:T(8,128)(2,1)} %get-tuple-element.50), channel_id=1, source_target_pairs={{0,1},{1,0},{2,3},{3,2},{4,5},{5,4},{6,7},{7,6},{8,9},{9,8},{10,11... | collective-permute-start | bytes 1572872 | tf_op jit(solution)/shard_map/ppermute | solution.py:287
  543.6 50.3 %collective-permute-start.20 = (bf16[256,1024]{1,0:T(8,128)(2,1)}, bf16[256,1024]{1,0:T(8,128)(2,1)S(1)}, u32[]{:S(2)}, u32[]{:S(2)}) collective-permute-start(bf16[256,1024]{1,0:T(8,128)(2,1)} %get-tuple-element.51), channel_id=1, source_target_pairs={{0,2},{1,3},{2,0},{3,1},{4,6},{5,7},{6,4},{7,5},{8,10},{9,11},{10,... | collective-permute-start | bytes 1572872 | tf_op jit(solution)/shard_map/ppermute | solution.py:287
  553.8 40.1 %collective-permute-start.21 = (bf16[256,1024]{1,0:T(8,128)(2,1)}, bf16[256,1024]{1,0:T(8,128)(2,1)S(1)}, u32[]{:S(2)}, u32[]{:S(2)}) collective-permute-start(bf16[256,1024]{1,0:T(8,128)(2,1)} %get-tuple-element.52), channel_id=1, source_target_pairs={{0,3},{1,2},{2,1},{3,0},{4,7},{5,6},{6,5},{7,4},{8,11},{9,10},{10,... | collective-permute-start | bytes 1572872 | tf_op jit(solution)/shard_map/ppermute | solution.py:287
  555.3 35.5 %copy-start.9 = (bf16[256,1024]{1,0:T(8,128)(2,1)S(1)}, bf16[256,1024]{1,0:T(8,128)(2,1)}, u32[]{:S(2)}) copy-start(bf16[256,1024]{1,0:T(8,128)(2,1)} %get-tuple-element.47.rest_10_.rest_0_) | copy-start | bytes 1572868
  588.7 41.7 %collective-permute-start.33 = (bf16[256,1024]{1,0:T(8,128)(2,1)}, bf16[256,1024]{1,0:T(8,128)(2,1)S(1)}, u32[]{:S(2)}, u32[]{:S(2)}) collective-permute-start(bf16[256,1024]{1,0:T(8,128)(2,1)} %get-tuple-element.66), channel_id=1, source_target_pairs={{0,1},{1,0},{2,3},{3,2},{4,5},{5,4},{6,7},{7,6},{8,9},{9,8},{10,11... | collective-permute-start | bytes 1572872 | tf_op jit(solution)/shard_map/ppermute | solution.py:287
  590.2 2.1 copy-start.30
  590.2 41.7 %collective-permute-start.34 = (bf16[256,1024]{1,0:T(8,128)(2,1)}, bf16[256,1024]{1,0:T(8,128)(2,1)S(1)}, u32[]{:S(2)}, u32[]{:S(2)}) collective-permute-start(bf16[256,1024]{1,0:T(8,128)(2,1)} %get-tuple-element.67), channel_id=1, source_target_pairs={{0,2},{1,3},{2,0},{3,1},{4,6},{5,7},{6,4},{7,5},{8,10},{9,11},{10,... | collective-permute-start | bytes 1572872 | tf_op jit(solution)/shard_map/ppermute | solution.py:287
  592.3 1.6 copy-start.31
  592.3 39.5 %collective-permute-start.35 = (bf16[256,1024]{1,0:T(8,128)(2,1)S(1)}, bf16[256,1024]{1,0:T(8,128)(2,1)S(1)}, u32[]{:S(2)}, u32[]{:S(2)}) collective-permute-start(bf16[256,1024]{1,0:T(8,128)(2,1)S(1)} %copy-done.30), channel_id=1, source_target_pairs={{0,3},{1,2},{2,1},{3,0},{4,7},{5,6},{6,5},{7,4},{8,11},{9,10},{10,... | collective-permute-start | bytes 1572872 | tf_op jit(solution)/shard_map/ppermute | solution.py:287
  594.9 37.0 %copy-start.11 = (bf16[256,1024]{1,0:T(8,128)(2,1)S(1)}, bf16[256,1024]{1,0:T(8,128)(2,1)}, u32[]{:S(2)}) copy-start(bf16[256,1024]{1,0:T(8,128)(2,1)} %get-tuple-element.58.rest_8_.rest_0_) | copy-start | bytes 1572868
  628.3 14.8 %collective-permute-start.30 = (bf16[256,1024]{1,0:T(8,128)(2,1)}, bf16[256,1024]{1,0:T(8,128)(2,1)S(1)}, u32[]{:S(2)}, u32[]{:S(2)}) collective-permute-start(bf16[256,1024]{1,0:T(8,128)(2,1)} %get-tuple-element.63), channel_id=1, source_target_pairs={{0,1},{1,0},{2,3},{3,2},{4,5},{5,4},{6,7},{7,6},{8,9},{9,8},{10,11... | collective-permute-start | bytes 1572872 | tf_op jit(solution)/shard_map/ppermute | solution.py:287
  629.8 20.2 %collective-permute-start.31 = (bf16[256,1024]{1,0:T(8,128)(2,1)}, bf16[256,1024]{1,0:T(8,128)(2,1)S(1)}, u32[]{:S(2)}, u32[]{:S(2)}) collective-permute-start(bf16[256,1024]{1,0:T(8,128)(2,1)} %get-tuple-element.64), channel_id=1, source_target_pairs={{0,2},{1,3},{2,0},{3,1},{4,6},{5,7},{6,4},{7,5},{8,10},{9,11},{10,... | collective-permute-start | bytes 1572872 | tf_op jit(solution)/shard_map/ppermute | solution.py:287
  630.4 19.7 %copy-start.12 = (bf16[256,1024]{1,0:T(8,128)(2,1)S(1)}, bf16[256,1024]{1,0:T(8,128)(2,1)}, u32[]{:S(2)}) copy-start(bf16[256,1024]{1,0:T(8,128)(2,1)} %get-tuple-element.62.rest_0_) | copy-start | bytes 1572868
  630.4 19.7 %collective-permute-start.32 = (bf16[256,1024]{1,0:T(8,128)(2,1)}, bf16[256,1024]{1,0:T(8,128)(2,1)S(1)}, u32[]{:S(2)}, u32[]{:S(2)}) collective-permute-start(bf16[256,1024]{1,0:T(8,128)(2,1)} %get-tuple-element.65), channel_id=1, source_target_pairs={{0,3},{1,2},{2,1},{3,0},{4,7},{5,6},{6,5},{7,4},{8,11},{9,10},{10,... | collective-permute-start | bytes 1572872 | tf_op jit(solution)/shard_map/ppermute | solution.py:287
  (12 other events, 12.2 us)

commit v8 on v7

--- a/solution.py
+++ b/solution.py
@@ -164,18 +164,23 @@
         normed, total, w1, w2, sems = rest[-5:]
         step = pl.program_id(0)
 
-        def fetch(piece, slot):
-            return (
-                pltpu.make_async_copy(
-                    w1s[piece // half].at[piece % half], w1.at[slot], sems.at[0, slot]
-                ),
-                pltpu.make_async_copy(
-                    w2s[piece // half].at[piece % half], w2.at[slot], sems.at[1, slot]
-                ),
-            )
-
-        def start(piece):
-            for copy in fetch(piece, piece % 2):
+        def fetch(pair, slot):
+            copies = []
+            for h in range(2):
+                which, at = divmod(2 * pair + h, half)
+                rows = slice(h * hb, (h + 1) * hb)
+                copies += [
+                    pltpu.make_async_copy(
+                        w1s[which].at[at], w1.at[slot, rows], sems.at[0, h, slot]
+                    ),
+                    pltpu.make_async_copy(
+                        w2s[which].at[at], w2.at[slot, :, rows], sems.at[1, h, slot]
+                    ),
+                ]
+            return copies
+
+        def start(pair):
+            for copy in fetch(pair, pair % 2):
                 copy.start()
 
         @pl.when(step == 0)
@@ -191,8 +196,8 @@
                 normed[pl.ds(at, c), :] = (xs[s][...].astype(f32) * scale).astype(bf16)
             total[...] = jnp.zeros_like(total)
 
-        for piece in range(1, n):
-            pl.when(step == piece - 1)(functools.partial(start, piece))
+        for pair in range(1, half):
+            pl.when(step == pair - 1)(functools.partial(start, pair))
         slot = lax.rem(step, 2)
         for copy in fetch(0, slot):
             copy.wait()
@@ -208,7 +213,7 @@
             h = (x + x * jnp.tanh(x * (inside + cubic * (x * x)))).astype(bf16)
             total[:, t : t + tile] += jnp.dot(w2[slot], h, preferred_element_type=f32)
 
-        @pl.when(step == n - 1)
+        @pl.when(step == half - 1)
         def _():
             for s in range(nt):
                 at = pl.multiple_of((me_ref[0] ^ s) * c, c)
@@ -219,19 +224,19 @@
         kernel,
         grid_spec=pltpu.PrefetchScalarGridSpec(
             num_scalar_prefetch=1,
-            grid=(n,),
+            grid=(half,),
             in_specs=[whole] * nt + [ANY] * (4 + len(deps)),
             out_specs=[whole] * nt,
             scratch_shapes=[
                 pltpu.VMEM((full, tokens), bf16),
                 pltpu.VMEM((full, tokens), f32),
-                pltpu.VMEM((2, hb, full), bf16),
-                pltpu.VMEM((2, full, hb), bf16),
-                pltpu.SemaphoreType.DMA((2, 2)),
+                pltpu.VMEM((2, 2 * hb, full), bf16),
+                pltpu.VMEM((2, full, 2 * hb), bf16),
+                pltpu.SemaphoreType.DMA((2, 2, 2)),
             ],
         ),
         out_shape=[jax.ShapeDtypeStruct((c, tokens), bf16)] * nt,
-        compiler_params=params(56),
+        compiler_params=params(44),
         cost_estimate=pl.CostEstimate(
             flops=4 * full * hb * n * tokens,
             bytes_accessed=4 * full * hb * n + 4 * full * tokens,
@@ -304,7 +309,7 @@
 
 def gather_along(ns, both):
     if ns % 8:
-        bit, marks = 2, [both, both]
+        bit, marks = 2, [both, both, both]
     else:
         middle = [i for i in range(ns) if ((i >> 1) ^ (i >> 2)) & 1]
         across = [(i, i ^ 6) for i in middle]
@@ -315,7 +320,7 @@
             jnp.concatenate([both, inner, beyond]), "seq", [(i, i ^ 2) for i in middle]
         )
         both = jnp.concatenate([both, jnp.concatenate([outer, inner, beyond]) + out])
-        bit, marks = 8, [beyond, out]
+        bit, marks = 8, [beyond, out, inner]
     while bit < ns:
         marks[1] = flip(both, "seq", ns, bit)
         both = jnp.concatenate([both, marks[1]])
@@ -375,7 +380,7 @@
     def put(k, done, result, group=0):
         return place(k, group, me, done, result, activations.shape)
 
-    front01 = exchange(after(first(0, 2), got[0]))
+    front01 = exchange(after(first(0, 2), got[0], got[2]))
     front23 = exchange(after(first(1, 2), got[1]))
     (mixed0,) = second(front01, 0, [near_in[bits[0]], near_out[bits[-1]]])
     (mixed1,) = second(front01, 1)
@@ -400,7 +405,7 @@
     out2 = layer(in2, [gate3[0], result])
     done2 = swap(out2)
     result = put(1, done1, result)
-    out3 = layer(in3, [out2[0], result])
+    out3 = layer(in3, [out2[0]])
     done3 = swap(out3)
     result = put(2, done2, result)
     return put(3, done3, result)

time: 654 us -> 640 us (0.979); the launches traced: 652 us -> 630 us
  waiting for transfers between devices: 330 us -> 307 us
  Pallas kernels: 203 us -> 195 us
  local copies, waits for them, and re-layouts: 26.9 us -> 34.1 us
    ppermute x1, waiting for transfers between devices: 148 us -> 106 us  [gather_along(): lax.ppermute(jnp.concatenate([both, inner, beyond]), 'seq', [(i, i ^ 2) f...]
    ppermute x24, waiting for transfers between devices: 45.6 us -> 66.1 us  [swap(): lax.ppermute(slots[s], 'tensor', [(i, i ^ s) for i in range(n)])]
    pallas_call x4, Pallas kernels: 133 us -> 125 us  [mlp(): pl.pallas_call(kernel, grid_spec=pltpu.PrefetchScalarGridSpec(num_scalar_...]
    unnamed x68 -> x94, local copies, waits for them, and re-layouts: 22.2 us -> 29.4 us
  transfers between devices with their start and end apart: 42 -> 42, of which waited for: 14 -> 16; matrix products, arithmetic and copies ran while one was open for 3% -> 3% of each run, Pallas kernels for 31% -> 31%
where the time goes in v8:
time: 640 us; the launch traced here: 630 us
  waiting for transfers between devices  307 us (48%)
  Pallas kernels  195 us (30%)
  starting transfers between devices  76.4 us (12%)
  local copies, waits for them, and re-layouts  34.1 us (5%)
  other arithmetic  15.9 us (2%)
    pallas_call x4, Pallas kernels, mlp(): pl.pallas_call(kernel, grid_spec=pltpu.PrefetchScalarGridSpec(num_scalar_...  125 us
    ppermute x1, waiting for transfers between devices, gather_along(): lax.ppermute(jnp.concatenate([both, inner, beyond]), 'seq', [(i, i ^ 2) f...  106 us
    all_to_all x6, waiting for transfers between devices, exchange(): return lax.all_to_all(x, 'seq', split_axis=0, concat_axis=0, tiled=True)  74.1 us
    ppermute x24, waiting for transfers between devices, swap(): lax.ppermute(slots[s], 'tensor', [(i, i ^ s) for i in range(n)])  66.1 us
    ppermute x8, waiting for transfers between devices, flip(): return lax.ppermute(x, axis, [(i, i ^ bit) for i in range(n)])  44.7 us
    all_to_all x6, starting transfers between devices, exchange(): return lax.all_to_all(x, 'seq', split_axis=0, concat_axis=0, tiled=True)  32.8 us
    unnamed x94, local copies, waits for them, and re-layouts  29.4 us
    ppermute x24, starting transfers between devices, swap(): lax.ppermute(slots[s], 'tensor', [(i, i ^ s) for i in range(n)])  28.4 us
  transfers between devices with their start and end apart: 42, of which 16 were waited for; matrix products, arithmetic and copies ran while one was open for 3% of the time, Pallas kernels for 31%

profile of v8, /device:TPU:0, one launch (start us, length us, event | category | flops | bytes accessed | tf_op | source)
XLA Modules:
  0.0 629.9 jit_solution(3494211512286842786)
XLA Ops:
  1.2 5.0 collective-permute-start.1
  6.9 16.0 %collective-permute-done.1 = bf16[1,2,192,1024]{3,2,1,0:T(8,128)(2,1)S(1)} collective-permute-done((bf16[1,2,192,1024]{3,2,1,0:T(8,128)(2,1)S(1)}, bf16[1,2,192,1024]{3,2,1,0:T(8,128)(2,1)S(1)}, u32[]{:S(2)}, u32[]{:S(2)}) %collective-permute-start.1) | collective-permute-done | bytes 786464 | tf_op jit(solution)/shard_map/ppermute | solution.py:317
  23.6 3.4 copy-done
  28.0 7.9 %shard_map.85.refs_0_ = bf16[8,2,32,32,128]{4,3,2,1,0:T(8,128)(2,1)S(1)} custom-call(bf16[256,16384]{1,0:T(8,128)(2,1)S(1)} %copy-done, bf16[512,512]{1,0:T(8,128)(2,1)S(1)} %copy-done.7, f32[256,16384]{1,0:T(8,128)} %rest_3_.7, f32[256,16384]{1,0:T(8,128)} %rest_3_.7, f32[256,16384]{1,0:T(8,128)} %rest_3_.7, f32[256,16384]{1,0:T(8,128)} %rest_3_.7), custom_call_target="tpu_custom_call" | custom-call | flops 2147483648 | bytes 20971520 | tf_op jit(solution)/shard_map/pallas_call | solution.py:43
  36.0 2.0 copy-done.2
  39.8 9.2 %all-to-all-start.1 = ((bf16[8,2,32,32,128]{4,3,2,1,0:T(8,128)(2,1)}), bf16[8,2,32,32,128]{4,3,2,1,0:T(8,128)(2,1)}, u32[]{:S(2)}, u32[]{:S(2)}) async-start(bf16[8,2,32,32,128]{4,3,2,1,0:T(8,128)(2,1)} %shard_map.86), calls=%async_computation.1 | async-start | bytes 8388608 | tf_op jit(solution)/shard_map/all_to_all | solution.py:366
  50.7 3.4 copy-done.1
  54.0 8.0 %shard_map.82.refs_0_ = bf16[8,2,32,32,128]{4,3,2,1,0:T(8,128)(2,1)S(1)} custom-call(bf16[256,16384]{1,0:T(8,128)(2,1)S(1)} %copy-done.1, bf16[512,512]{1,0:T(8,128)(2,1)S(1)} %copy-done.8, f32[256,16384]{1,0:T(8,128)} %rest_3_.7, f32[256,16384]{1,0:T(8,128)} %rest_3_.7, f32[256,16384]{1,0:T(8,128)} %rest_3_.7, f32[256,16384]{1,0:T(8,128)} %rest_3_.7), custom_call_target="tpu_custom_call" | custom-call | flops 2147483648 | bytes 20971520 | tf_op jit(solution)/shard_map/pallas_call | solution.py:43
  62.0 2.0 copy-done.3
  64.0 106.2 %collective-permute-done.3.refs_1_ = bf16[3,2,192,1024]{3,2,1,0:T(8,128)(2,1)S(1)} collective-permute-done((bf16[3,2,192,1024]{3,2,1,0:T(8,128)(2,1)S(1)}, bf16[3,2,192,1024]{3,2,1,0:T(8,128)(2,1)S(1)}, u32[]{:S(2)}, u32[]{:S(2)}) %collective-permute-start.3) | collective-permute-done | bytes 2359328 | tf_op jit(solution)/shard_map/ppermute | solution.py:319
  171.6 4.7 all-to-all-start
  176.3 1.9 fusion
  178.3 1.4 pad_maximum_fusion.6
  179.7 1.5 collective-permute-start.4
  181.2 1.6 copy.17
  182.8 1.5 collective-permute-start.9
  184.8 31.8 %collective-permute-done.4.rest_0_ = bf16[768,1024]{1,0:T(8,128)(2,1)S(1)} collective-permute-done((bf16[768,1024]{1,0:T(8,128)(2,1)}, bf16[768,1024]{1,0:T(8,128)(2,1)S(1)}, u32[]{:S(2)}, u32[]{:S(2)}) %collective-permute-start.4) | collective-permute-done | bytes 1572896 | tf_op jit(solution)/shard_map/ppermute | solution.py:307
  216.6 1.5 collective-permute-start.6
  218.1 1.5 collective-permute-start.8
  220.8 5.7 shard_map.87
  226.5 43.9 %all-to-all-done.x_ref = bf16[8,2,32,32,128]{4,3,2,1,0:T(8,128)(2,1)} async-done(((bf16[8,2,32,32,128]{4,3,2,1,0:T(8,128)(2,1)}), bf16[8,2,32,32,128]{4,3,2,1,0:T(8,128)(2,1)}, u32[]{:S(2)}, u32[]{:S(2)}) %all-to-all-start) | async-done | bytes 4194336 | tf_op jit(solution)/shard_map/all_to_all | solution.py:366
  270.3 4.3 all-to-all-start.2
  274.7 12.2 %collective-permute-done.6 = bf16[768,1024]{1,0:T(8,128)(2,1)} collective-permute-done((bf16[768,1024]{1,0:T(8,128)(2,1)S(1)}, bf16[768,1024]{1,0:T(8,128)(2,1)}, u32[]{:S(2)}, u32[]{:S(2)}) %collective-permute-start.6) | collective-permute-done | bytes 1572896 | tf_op jit(solution)/shard_map/ppermute | solution.py:307
  286.9 5.9 pad_maximum_fusion.rest_4_.rest_0_
  292.8 5.2 pad_maximum_fusion.1.rest_6_.rest_1_
  298.6 5.6 shard_map.89
  304.2 19.6 %all-to-all-done.2.rest_4_.rest_5_.rest_6_.rest_7_ = bf16[8,32,32,128]{3,2,1,0:T(8,128)(2,1)} async-done(((bf16[8,32,32,128]{3,2,1,0:T(8,128)(2,1)}), bf16[8,32,32,128]{3,2,1,0:T(8,128)(2,1)}, u32[]{:S(2)}, u32[]{:S(2)}) %all-to-all-start.2) | async-done | bytes 2097184 | tf_op jit(solution)/shard_map/all_to_all | solution.py:366
  323.7 4.3 all-to-all-start.3
  331.2 6.7 %shard_map.88 = (bf16[256,1024]{1,0:T(8,128)(2,1)}, bf16[256,1024]{1,0:T(8,128)(2,1)}, bf16[256,1024]{1,0:T(8,128)(2,1)}, bf16[256,1024]{1,0:T(8,128)(2,1)}) custom-call(s32[1]{0:T(128)} %bitcast.me_ref, bf16[256,16384]{1,0:T(8,128)(2,1)} %rest_3_.11, bf16[256,16384]{1,0:T(8,128)(2,1)} %rest_3_.11, bf16[256,16384]{1,0:T(8,128)(2,1)} %rest_3_.11, ...), custom_call_target="tpu_custom_call" | custom-call | flops 8388608 | bytes 12582912 | tf_op jit(solution)/shard_map/pallas_call | solution.py:133
  337.9 1.6 collective-permute-start.12
  339.5 1.5 collective-permute-start.13
  341.5 4.8 shard_map.93.refs_0_
  347.6 5.3 collective-permute-done.12.rest_1_.refs_1_
  352.9 11.9 %collective-permute-done.13.rest_2_.refs_2_ = bf16[256,1024]{1,0:T(8,128)(2,1)S(1)} collective-permute-done((bf16[256,1024]{1,0:T(8,128)(2,1)}, bf16[256,1024]{1,0:T(8,128)(2,1)S(1)}, u32[]{:S(2)}, u32[]{:S(2)}) %collective-permute-start.13) | collective-permute-done | bytes 524320 | tf_op jit(solution)/shard_map/ppermute | solution.py:292
  366.4 10.7 %all-to-all-done.3.rest_4_.rest_5_.rest_6_.rest_7_ = bf16[8,32,32,128]{3,2,1,0:T(8,128)(2,1)} async-done(((bf16[8,32,32,128]{3,2,1,0:T(8,128)(2,1)}), bf16[8,32,32,128]{3,2,1,0:T(8,128)(2,1)}, u32[]{:S(2)}, u32[]{:S(2)}) %all-to-all-start.3) | async-done | bytes 2097184 | tf_op jit(solution)/shard_map/all_to_all | solution.py:366
  377.1 4.5 all-to-all-start.5
  381.7 6.8 %shard_map.90 = (bf16[256,1024]{1,0:T(8,128)(2,1)}, bf16[256,1024]{1,0:T(8,128)(2,1)}, bf16[256,1024]{1,0:T(8,128)(2,1)}, bf16[256,1024]{1,0:T(8,128)(2,1)}) custom-call(s32[1]{0:T(128)} %bitcast.me_ref, bf16[256,16384]{1,0:T(8,128)(2,1)} %rest_3_.11, bf16[256,16384]{1,0:T(8,128)(2,1)} %rest_3_.11, bf16[256,16384]{1,0:T(8,128)(2,1)} %rest_3_.11, ...), custom_call_target="tpu_custom_call" | custom-call | flops 8388608 | bytes 12582912 | tf_op jit(solution)/shard_map/pallas_call | solution.py:133
  388.5 1.6 collective-permute-start.15
  390.1 1.5 collective-permute-start.16
  393.2 30.9 %shard_map.91 = (bf16[256,1024]{1,0:T(8,128)(2,1)S(1)}, bf16[256,1024]{1,0:T(8,128)(2,1)S(1)}, bf16[256,1024]{1,0:T(8,128)(2,1)S(1)}, bf16[256,1024]{1,0:T(8,128)(2,1)S(1)}) custom-call(s32[1]{0:T(128)} %bitcast.me_ref, bf16[256,1024]{1,0:T(8,128)(2,1)S(1)} %copy-done.31, bf16[256,1024]{1,0:T(8,128)(2,1)S(1)} %copy-done.22, ...), custom_call_target="tpu_custom_call" | custom-call | flops 25769803776 | bytes 29360128 | tf_op jit(solution)/shard_map/pallas_call | solution.py:223
  427.3 4.8 shard_map.84.refs_0_
  434.7 5.7 all-to-all-start.4
  440.4 1.5 collective-permute-start.24
  441.9 1.5 collective-permute-start.25
  443.9 11.2 %collective-permute-done.24.rest_1_ = bf16[256,1024]{1,0:T(8,128)(2,1)S(1)} collective-permute-done((bf16[256,1024]{1,0:T(8,128)(2,1)S(1)}, bf16[256,1024]{1,0:T(8,128)(2,1)S(1)}, u32[]{:S(2)}, u32[]{:S(2)}) %collective-permute-start.24) | collective-permute-done | bytes 524320 | tf_op jit(solution)/shard_map/ppermute | solution.py:292
  455.2 12.1 %collective-permute-done.25.rest_2_ = bf16[256,1024]{1,0:T(8,128)(2,1)S(1)} collective-permute-done((bf16[256,1024]{1,0:T(8,128)(2,1)S(1)}, bf16[256,1024]{1,0:T(8,128)(2,1)S(1)}, u32[]{:S(2)}, u32[]{:S(2)}) %collective-permute-start.25) | collective-permute-done | bytes 524320 | tf_op jit(solution)/shard_map/ppermute | solution.py:292
  467.2 1.6 shard_map.98.rest_9_.rest_4_
  468.8 6.8 %shard_map.95 = (bf16[256,1024]{1,0:T(8,128)(2,1)}, bf16[256,1024]{1,0:T(8,128)(2,1)}, bf16[256,1024]{1,0:T(8,128)(2,1)}, bf16[256,1024]{1,0:T(8,128)(2,1)}) custom-call(s32[1]{0:T(128)} %bitcast.me_ref, bf16[256,16384]{1,0:T(8,128)(2,1)} %rest_3_.11, bf16[256,16384]{1,0:T(8,128)(2,1)} %rest_3_.11, bf16[256,16384]{1,0:T(8,128)(2,1)} %rest_3_.11, ...), custom_call_target="tpu_custom_call" | custom-call | flops 8388608 | bytes 12582912 | tf_op jit(solution)/shard_map/pallas_call | solution.py:133
  477.8 1.4 collective-permute-start.23
  480.3 30.9 %shard_map.96 = (bf16[256,1024]{1,0:T(8,128)(2,1)S(1)}, bf16[256,1024]{1,0:T(8,128)(2,1)S(1)}, bf16[256,1024]{1,0:T(8,128)(2,1)S(1)}, bf16[256,1024]{1,0:T(8,128)(2,1)S(1)}) custom-call(s32[1]{0:T(128)} %bitcast.me_ref, bf16[256,1024]{1,0:T(8,128)(2,1)S(1)} %copy-done.28, bf16[256,1024]{1,0:T(8,128)(2,1)S(1)} %copy-done.16, ...), custom_call_target="tpu_custom_call" | custom-call | flops 25769803776 | bytes 29360128 | tf_op jit(solution)/shard_map/pallas_call | solution.py:223
  514.9 6.7 %shard_map.97 = (bf16[256,1024]{1,0:T(8,128)(2,1)}, bf16[256,1024]{1,0:T(8,128)(2,1)}, bf16[256,1024]{1,0:T(8,128)(2,1)}, bf16[256,1024]{1,0:T(8,128)(2,1)}) custom-call(s32[1]{0:T(128)} %bitcast.me_ref, bf16[256,16384]{1,0:T(8,128)(2,1)} %rest_3_.11, bf16[256,16384]{1,0:T(8,128)(2,1)} %rest_3_.11, bf16[256,16384]{1,0:T(8,128)(2,1)} %rest_3_.11, ...), custom_call_target="tpu_custom_call" | custom-call | flops 8388608 | bytes 12582912 | tf_op jit(solution)/shard_map/pallas_call | solution.py:133
  521.6 1.6 collective-permute-start.19
  523.7 1.5 collective-permute-start.21
  527.2 32.3 %shard_map.99 = (bf16[256,1024]{1,0:T(8,128)(2,1)S(1)}, bf16[256,1024]{1,0:T(8,128)(2,1)S(1)}, bf16[256,1024]{1,0:T(8,128)(2,1)S(1)}, bf16[256,1024]{1,0:T(8,128)(2,1)S(1)}) custom-call(s32[1]{0:T(128)} %bitcast.me_ref, bf16[256,1024]{1,0:T(8,128)(2,1)S(1)} %copy-done.30, bf16[256,1024]{1,0:T(8,128)(2,1)S(1)} %copy-done.14, ...), custom_call_target="tpu_custom_call" | custom-call | flops 25769803776 | bytes 29360128 | tf_op jit(solution)/shard_map/pallas_call | solution.py:223
  559.6 1.5 collective-permute-start.35
  563.2 31.2 %shard_map.100 = (bf16[256,1024]{1,0:T(8,128)(2,1)S(1)}, bf16[256,1024]{1,0:T(8,128)(2,1)S(1)}, bf16[256,1024]{1,0:T(8,128)(2,1)S(1)}, bf16[256,1024]{1,0:T(8,128)(2,1)S(1)}) custom-call(s32[1]{0:T(128)} %bitcast.me_ref, bf16[256,1024]{1,0:T(8,128)(2,1)S(1)} %copy-done.32, bf16[256,1024]{1,0:T(8,128)(2,1)S(1)} %collective-permute-done.19.rest_1_, ...), custom_call_target="tpu_custom_call" | custom-call | flops 25769803776 | bytes 29360128 | tf_op jit(solution)/shard_map/pallas_call | solution.py:223
  594.3 1.5 collective-permute-start.32
  597.9 1.5 collective-permute-start.29
  599.4 1.6 shard_map.101.rest_4_
  600.9 9.2 %collective-permute-done.32.rest_3_ = bf16[256,1024]{1,0:T(8,128)(2,1)S(1)} collective-permute-done((bf16[256,1024]{1,0:T(8,128)(2,1)S(1)}, bf16[256,1024]{1,0:T(8,128)(2,1)S(1)}, u32[]{:S(2)}, u32[]{:S(2)}) %collective-permute-start.32) | collective-permute-done | bytes 524320 | tf_op jit(solution)/shard_map/ppermute | solution.py:292
  610.2 1.6 shard_map.102.rest_4_
  611.7 9.4 %collective-permute-done.27.rest_1_ = bf16[256,1024]{1,0:T(8,128)(2,1)S(1)} collective-permute-done((bf16[256,1024]{1,0:T(8,128)(2,1)S(1)}, bf16[256,1024]{1,0:T(8,128)(2,1)S(1)}, u32[]{:S(2)}, u32[]{:S(2)}) %collective-permute-start.27) | collective-permute-done | bytes 524320 | tf_op jit(solution)/shard_map/ppermute | solution.py:292
  621.3 6.8 %collective-permute-done.29.rest_3_ = bf16[256,1024]{1,0:T(8,128)(2,1)S(1)} collective-permute-done((bf16[256,1024]{1,0:T(8,128)(2,1)S(1)}, bf16[256,1024]{1,0:T(8,128)(2,1)S(1)}, u32[]{:S(2)}, u32[]{:S(2)}) %collective-permute-start.29) | collective-permute-done | bytes 524320 | tf_op jit(solution)/shard_map/ppermute | solution.py:292
  628.1 1.6 shard_map.103
  (147 shorter events, 38.6 us)
Async XLA Ops:
  1.2 21.7 %collective-permute-start.1 = (bf16[1,2,192,1024]{3,2,1,0:T(8,128)(2,1)S(1)}, bf16[1,2,192,1024]{3,2,1,0:T(8,128)(2,1)S(1)}, u32[]{:S(2)}, u32[]{:S(2)}) collective-permute-start(bf16[1,2,192,1024]{3,2,1,0:T(8,128)(2,1)S(1)} %maximum_bitcast_fusion), channel_id=1, source_target_pairs={{0,8},{4,12},{24,16},{28,20},{1,9},{5,13},{25,17},{29,21},{2,10},{... | collective-permute-start | bytes 2359304 | tf_op jit(solution)/shard_map/ppermute | solution.py:317
  6.2 31.8 %collective-permute-start = (bf16[1,2,192,1024]{3,2,1,0:T(8,128)(2,1)S(1)}, bf16[1,2,192,1024]{3,2,1,0:T(8,128)(2,1)S(1)}, u32[]{:S(2)}, u32[]{:S(2)}) collective-permute-start(bf16[1,2,192,1024]{3,2,1,0:T(8,128)(2,1)S(1)} %maximum_bitcast_fusion), channel_id=1, source_target_pairs={{8,16},{12,20},{16,8},{20,12},{9,17},{13,21},{17,9},{21,13},{10,18... | collective-permute-start | bytes 2359304 | tf_op jit(solution)/shard_map/ppermute | solution.py:316
  22.9 13.1 %copy-start.46 = (bf16[1,2,192,1024]{3,2,1,0:T(8,128)(2,1)}, bf16[1,2,192,1024]{3,2,1,0:T(8,128)(2,1)S(1)}, u32[]{:S(2)}) copy-start(bf16[1,2,192,1024]{3,2,1,0:T(8,128)(2,1)S(1)} %collective-permute-done.1) | copy-start | bytes 2359300
  22.9 15.1 %collective-permute-start.2 = (bf16[1,2,192,1024]{3,2,1,0:T(8,128)(2,1)S(1)}, bf16[1,2,192,1024]{3,2,1,0:T(8,128)(2,1)S(1)}, u32[]{:S(2)}, u32[]{:S(2)}) collective-permute-start(bf16[1,2,192,1024]{3,2,1,0:T(8,128)(2,1)S(1)} %collective-permute-done.1), channel_id=1, source_target_pairs={{8,16},{12,20},{16,8},{20,12},{9,17},{13,21},{17,9},{21,13},{10,18... | collective-permute-start | bytes 2359304 | tf_op jit(solution)/shard_map/ppermute | solution.py:318
  23.6 3.4 copy-start
  39.8 9.2 %copy-start.42 = (bf16[1,2,192,1024]{3,2,1,0:T(8,128)(2,1)S(1)}, bf16[1,2,192,1024]{3,2,1,0:T(8,128)(2,1)}, u32[]{:S(2)}) copy-start(bf16[1,2,192,1024]{3,2,1,0:T(8,128)(2,1)} %copy-done.41) | copy-start | bytes 2359300
  39.8 9.2 %copy-start.44 = (bf16[1,2,192,1024]{3,2,1,0:T(8,128)(2,1)S(1)}, bf16[1,2,192,1024]{3,2,1,0:T(8,128)(2,1)}, u32[]{:S(2)}) copy-start(bf16[1,2,192,1024]{3,2,1,0:T(8,128)(2,1)} %copy-done.43) | copy-start | bytes 2359300
  39.8 131.8 %all-to-all-start.1 = ((bf16[8,2,32,32,128]{4,3,2,1,0:T(8,128)(2,1)}), bf16[8,2,32,32,128]{4,3,2,1,0:T(8,128)(2,1)}, u32[]{:S(2)}, u32[]{:S(2)}) async-start(bf16[8,2,32,32,128]{4,3,2,1,0:T(8,128)(2,1)} %shard_map.86), calls=%async_computation.1 | async-start | bytes 8388608 | tf_op jit(solution)/shard_map/all_to_all | solution.py:366
  49.3 120.9 %collective-permute-start.3 = (bf16[3,2,192,1024]{3,2,1,0:T(8,128)(2,1)S(1)}, bf16[3,2,192,1024]{3,2,1,0:T(8,128)(2,1)S(1)}, u32[]{:S(2)}, u32[]{:S(2)}) collective-permute-start(bf16[3,2,192,1024]{3,2,1,0:T(8,128)(2,1)S(1)} %pad_maximum_fusion.3), channel_id=1, source_target_pairs={{8,0},{12,4},{16,24},{20,28},{9,1},{13,5},{17,25},{21,29},{10,2},{... | collective-permute-start | bytes 7077896 | tf_op jit(solution)/shard_map/ppermute | solution.py:319
  171.6 4.7 copy-start.40
  171.6 98.7 %all-to-all-start = ((bf16[8,2,32,32,128]{4,3,2,1,0:T(8,128)(2,1)}), bf16[8,2,32,32,128]{4,3,2,1,0:T(8,128)(2,1)}, u32[]{:S(2)}, u32[]{:S(2)}) async-start(bf16[8,2,32,32,128]{4,3,2,1,0:T(8,128)(2,1)} %shard_map.83), calls=%async_computation | async-start | bytes 8388608 | tf_op jit(solution)/shard_map/all_to_all | solution.py:366
  179.7 41.1 %copy-start.6 = (f32[256,256]{1,0:T(8,128)S(1)}, f32[256,256]{1,0:T(8,128)}, u32[]{:S(2)}) copy-start(f32[256,256]{1,0:T(8,128)} %s_ref.7) | copy-start | bytes 786436
  179.7 36.9 %collective-permute-start.4 = (bf16[768,1024]{1,0:T(8,128)(2,1)}, bf16[768,1024]{1,0:T(8,128)(2,1)S(1)}, u32[]{:S(2)}, u32[]{:S(2)}) collective-permute-start(bf16[768,1024]{1,0:T(8,128)(2,1)} %bitcast.6), channel_id=1, source_target_pairs={{0,1},{1,0},{2,3},{3,2},{4,5},{5,4},{6,7},{7,6},{8,9},{9,8},{10,11... | collective-permute-start | bytes 4718600 | tf_op jit(solution)/shard_map/ppermute | solution.py:307
  182.8 37.5 %collective-permute-start.9 = (bf16[1024,768]{1,0:T(8,128)(2,1)}, bf16[1024,768]{1,0:T(8,128)(2,1)S(1)}, u32[]{:S(2)}, u32[]{:S(2)}) collective-permute-start(bf16[1024,768]{1,0:T(8,128)(2,1)} %bitcast.23), channel_id=1, source_target_pairs={{0,2},{1,3},{2,0},{3,1},{4,6},{5,7},{6,4},{7,5},{8,10},{9,11},{10,... | collective-permute-start | bytes 4718600 | tf_op jit(solution)/shard_map/ppermute | solution.py:307
  184.3 90.3 %collective-permute-start.5 = (bf16[768,1024]{1,0:T(8,128)(2,1)}, bf16[768,1024]{1,0:T(8,128)(2,1)}, u32[]{:S(2)}, u32[]{:S(2)}) collective-permute-start(bf16[768,1024]{1,0:T(8,128)(2,1)} %bitcast.6), channel_id=1, source_target_pairs={{0,2},{1,3},{2,0},{3,1},{4,6},{5,7},{6,4},{7,5},{8,10},{9,11},{10,... | collective-permute-start | bytes 4718600 | tf_op jit(solution)/shard_map/ppermute | solution.py:307
  216.6 70.3 %collective-permute-start.6 = (bf16[768,1024]{1,0:T(8,128)(2,1)S(1)}, bf16[768,1024]{1,0:T(8,128)(2,1)}, u32[]{:S(2)}, u32[]{:S(2)}) collective-permute-start(bf16[768,1024]{1,0:T(8,128)(2,1)S(1)} %collective-permute-done.4.rest_0_), channel_id=1, source_target_pairs={{0,2},{1,3},{2,0},{3,1},{4,6},{5,7},{6,4},{7,5},{8,10},{9,11},{10,... | collective-permute-start | bytes 4718600 | tf_op jit(solution)/shard_map/ppermute | solution.py:307
  218.1 74.7 %collective-permute-start.8 = (bf16[1024,768]{1,0:T(8,128)(2,1)}, bf16[1024,768]{1,0:T(8,128)(2,1)}, u32[]{:S(2)}, u32[]{:S(2)}) collective-permute-start(bf16[1024,768]{1,0:T(8,128)(2,1)} %bitcast.24), channel_id=1, source_target_pairs={{0,1},{1,0},{2,3},{3,2},{4,5},{5,4},{6,7},{7,6},{8,9},{9,8},{10,11... | collective-permute-start | bytes 4718600 | tf_op jit(solution)/shard_map/ppermute | solution.py:307
  220.3 72.5 %collective-permute-start.10 = (bf16[1024,768]{1,0:T(8,128)(2,1)S(1)}, bf16[1024,768]{1,0:T(8,128)(2,1)}, u32[]{:S(2)}, u32[]{:S(2)}) collective-permute-start(bf16[1024,768]{1,0:T(8,128)(2,1)S(1)} %collective-permute-done.9.rest_1_), channel_id=1, source_target_pairs={{0,1},{1,0},{2,3},{3,2},{4,5},{5,4},{6,7},{7,6},{8,9},{9,8},{10,11... | collective-permute-start | bytes 4718600 | tf_op jit(solution)/shard_map/ppermute | solution.py:307
  270.3 53.4 %all-to-all-start.2 = ((bf16[8,32,32,128]{3,2,1,0:T(8,128)(2,1)}), bf16[8,32,32,128]{3,2,1,0:T(8,128)(2,1)}, u32[]{:S(2)}, u32[]{:S(2)}) async-start(bf16[8,32,32,128]{3,2,1,0:T(8,128)(2,1)} %shard_map.87), calls=%async_computation.2 | async-start | bytes 4194304 | tf_op jit(solution)/shard_map/all_to_all | solution.py:366
  286.9 5.9 copy-start.45
  292.8 99.3 %collective-permute-start.7 = (bf16[4,768,1024]{2,1,0:T(8,128)(2,1)}, bf16[4,768,1024]{2,1,0:T(8,128)(2,1)}, u32[]{:S(2)}, u32[]{:S(2)}) collective-permute-start(bf16[4,768,1024]{2,1,0:T(8,128)(2,1)} %pad_maximum_fusion.rest_4_.rest_0_), channel_id=1, source_target_pairs={{0,4},{4,0},{8,12},{12,8},{16,20},{20,16},{24,28},{28,24},{1,5},{5... | collective-permute-start | bytes 18874376 | tf_op jit(solution)/shard_map/ppermute | solution.py:307
  298.1 94.0 %collective-permute-start.11 = (bf16[4,1024,768]{2,1,0:T(8,128)(2,1)}, bf16[4,1024,768]{2,1,0:T(8,128)(2,1)}, u32[]{:S(2)}, u32[]{:S(2)}) collective-permute-start(bf16[4,1024,768]{2,1,0:T(8,128)(2,1)} %pad_maximum_fusion.1.rest_6_.rest_1_), channel_id=1, source_target_pairs={{0,4},{4,0},{8,12},{12,8},{16,20},{20,16},{24,28},{28,24},{1,5},{5... | collective-permute-start | bytes 18874376 | tf_op jit(solution)/shard_map/ppermute | solution.py:307
  323.7 53.4 %all-to-all-start.3 = ((bf16[8,32,32,128]{3,2,1,0:T(8,128)(2,1)}), bf16[8,32,32,128]{3,2,1,0:T(8,128)(2,1)}, u32[]{:S(2)}, u32[]{:S(2)}) async-start(bf16[8,32,32,128]{3,2,1,0:T(8,128)(2,1)} %shard_map.89), calls=%async_computation.3 | async-start | bytes 4194304 | tf_op jit(solution)/shard_map/all_to_all | solution.py:366
  337.9 15.0 %collective-permute-start.12 = (bf16[256,1024]{1,0:T(8,128)(2,1)}, bf16[256,1024]{1,0:T(8,128)(2,1)S(1)}, u32[]{:S(2)}, u32[]{:S(2)}) collective-permute-start(bf16[256,1024]{1,0:T(8,128)(2,1)} %get-tuple-element.38), channel_id=1, source_target_pairs={{0,1},{1,0},{2,3},{3,2},{4,5},{5,4},{6,7},{7,6},{8,9},{9,8},{10,11... | collective-permute-start | bytes 1572872 | tf_op jit(solution)/shard_map/ppermute | solution.py:292
  339.5 25.3 %collective-permute-start.13 = (bf16[256,1024]{1,0:T(8,128)(2,1)}, bf16[256,1024]{1,0:T(8,128)(2,1)S(1)}, u32[]{:S(2)}, u32[]{:S(2)}) collective-permute-start(bf16[256,1024]{1,0:T(8,128)(2,1)} %get-tuple-element.39), channel_id=1, source_target_pairs={{0,2},{1,3},{2,0},{3,1},{4,6},{5,7},{6,4},{7,5},{8,10},{9,11},{10,... | collective-permute-start | bytes 1572872 | tf_op jit(solution)/shard_map/ppermute | solution.py:292
  341.0 23.8 %collective-permute-start.14 = (bf16[256,1024]{1,0:T(8,128)(2,1)}, bf16[256,1024]{1,0:T(8,128)(2,1)S(1)}, u32[]{:S(2)}, u32[]{:S(2)}) collective-permute-start(bf16[256,1024]{1,0:T(8,128)(2,1)} %get-tuple-element.40), channel_id=1, source_target_pairs={{0,3},{1,2},{2,1},{3,0},{4,7},{5,6},{6,5},{7,4},{8,11},{9,10},{10,... | collective-permute-start | bytes 1572872 | tf_op jit(solution)/shard_map/ppermute | solution.py:292
  352.9 11.9 %copy-start.21 = (bf16[256,1024]{1,0:T(8,128)(2,1)}, bf16[256,1024]{1,0:T(8,128)(2,1)S(1)}, u32[]{:S(2)}) copy-start(bf16[256,1024]{1,0:T(8,128)(2,1)S(1)} %collective-permute-done.12.rest_1_.refs_1_) | copy-start | bytes 1572868
  377.1 57.5 %all-to-all-start.5 = ((bf16[8,32,32,128]{3,2,1,0:T(8,128)(2,1)}), bf16[8,32,32,128]{3,2,1,0:T(8,128)(2,1)}, u32[]{:S(2)}, u32[]{:S(2)}) async-start(bf16[8,32,32,128]{3,2,1,0:T(8,128)(2,1)} %shard_map.94), calls=%async_computation.5 | async-start | bytes 4194304 | tf_op jit(solution)/shard_map/all_to_all | solution.py:366
  381.7 10.4 %copy-start.22 = (bf16[256,1024]{1,0:T(8,128)(2,1)S(1)}, bf16[256,1024]{1,0:T(8,128)(2,1)}, u32[]{:S(2)}) copy-start(bf16[256,1024]{1,0:T(8,128)(2,1)} %copy-done.21) | copy-start | bytes 1572868
  381.7 10.4 %copy-start.24 = (bf16[256,1024]{1,0:T(8,128)(2,1)S(1)}, bf16[256,1024]{1,0:T(8,128)(2,1)}, u32[]{:S(2)}) copy-start(bf16[256,1024]{1,0:T(8,128)(2,1)} %copy-done.23) | copy-start | bytes 1572868
  381.7 10.4 %copy-start.26 = (bf16[256,1024]{1,0:T(8,128)(2,1)S(1)}, bf16[256,1024]{1,0:T(8,128)(2,1)}, u32[]{:S(2)}) copy-start(bf16[256,1024]{1,0:T(8,128)(2,1)} %copy-done.25) | copy-start | bytes 1572868
  381.7 10.4 %copy-start.31 = (bf16[256,1024]{1,0:T(8,128)(2,1)S(1)}, bf16[256,1024]{1,0:T(8,128)(2,1)}, u32[]{:S(2)}) copy-start(bf16[256,1024]{1,0:T(8,128)(2,1)} %get-tuple-element.37.rest_0_) | copy-start | bytes 1572868
  388.5 45.0 %collective-permute-start.15 = (bf16[256,1024]{1,0:T(8,128)(2,1)}, bf16[256,1024]{1,0:T(8,128)(2,1)S(1)}, u32[]{:S(2)}, u32[]{:S(2)}) collective-permute-start(bf16[256,1024]{1,0:T(8,128)(2,1)} %get-tuple-element.43), channel_id=1, source_target_pairs={{0,1},{1,0},{2,3},{3,2},{4,5},{5,4},{6,7},{7,6},{8,9},{9,8},{10,11... | collective-permute-start | bytes 1572872 | tf_op jit(solution)/shard_map/ppermute | solution.py:292
  390.1 43.5 %collective-permute-start.16 = (bf16[256,1024]{1,0:T(8,128)(2,1)}, bf16[256,1024]{1,0:T(8,128)(2,1)S(1)}, u32[]{:S(2)}, u32[]{:S(2)}) collective-permute-start(bf16[256,1024]{1,0:T(8,128)(2,1)} %get-tuple-element.44), channel_id=1, source_target_pairs={{0,2},{1,3},{2,0},{3,1},{4,6},{5,7},{6,4},{7,5},{8,10},{9,11},{10,... | collective-permute-start | bytes 1572872 | tf_op jit(solution)/shard_map/ppermute | solution.py:292
  391.6 41.9 %collective-permute-start.17 = (bf16[256,1024]{1,0:T(8,128)(2,1)}, bf16[256,1024]{1,0:T(8,128)(2,1)S(1)}, u32[]{:S(2)}, u32[]{:S(2)}) collective-permute-start(bf16[256,1024]{1,0:T(8,128)(2,1)} %get-tuple-element.45), channel_id=1, source_target_pairs={{0,3},{1,2},{2,1},{3,0},{4,7},{5,6},{6,5},{7,4},{8,11},{9,10},{10,... | collective-permute-start | bytes 1572872 | tf_op jit(solution)/shard_map/ppermute | solution.py:292
  434.7 5.7 copy-start.38
  434.7 7.3 %copy-start.36 = (bf16[256,1024]{1,0:T(8,128)(2,1)S(1)}, bf16[256,1024]{1,0:T(8,128)(2,1)}, u32[]{:S(2)}) copy-start(bf16[256,1024]{1,0:T(8,128)(2,1)} %copy-done.35) | copy-start | bytes 1572868
  434.7 8.8 %copy-start.34 = (bf16[256,1024]{1,0:T(8,128)(2,1)S(1)}, bf16[256,1024]{1,0:T(8,128)(2,1)}, u32[]{:S(2)}) copy-start(bf16[256,1024]{1,0:T(8,128)(2,1)} %copy-done.33) | copy-start | bytes 1572868
  434.7 32.5 %copy-start.12 = (bf16[256,1024]{1,0:T(8,128)(2,1)S(1)}, bf16[256,1024]{1,0:T(8,128)(2,1)}, u32[]{:S(2)}) copy-start(bf16[256,1024]{1,0:T(8,128)(2,1)} %copy-done.11) | copy-start | bytes 1572868
  434.7 79.4 %all-to-all-start.4 = ((bf16[8,32,32,128]{3,2,1,0:T(8,128)(2,1)}), bf16[8,32,32,128]{3,2,1,0:T(8,128)(2,1)}, u32[]{:S(2)}, u32[]{:S(2)}) async-start(bf16[8,32,32,128]{3,2,1,0:T(8,128)(2,1)} %shard_map.92), calls=%async_computation.4 | async-start | bytes 4194304 | tf_op jit(solution)/shard_map/all_to_all | solution.py:366
  440.4 14.8 %collective-permute-start.24 = (bf16[256,1024]{1,0:T(8,128)(2,1)S(1)}, bf16[256,1024]{1,0:T(8,128)(2,1)S(1)}, u32[]{:S(2)}, u32[]{:S(2)}) collective-permute-start(bf16[256,1024]{1,0:T(8,128)(2,1)S(1)} %copy-done.38), channel_id=1, source_target_pairs={{0,1},{1,0},{2,3},{3,2},{4,5},{5,4},{6,7},{7,6},{8,9},{9,8},{10,11... | collective-permute-start | bytes 1572872 | tf_op jit(solution)/shard_map/ppermute | solution.py:292
  441.9 25.3 %collective-permute-start.25 = (bf16[256,1024]{1,0:T(8,128)(2,1)S(1)}, bf16[256,1024]{1,0:T(8,128)(2,1)S(1)}, u32[]{:S(2)}, u32[]{:S(2)}) collective-permute-start(bf16[256,1024]{1,0:T(8,128)(2,1)S(1)} %copy-done.36), channel_id=1, source_target_pairs={{0,2},{1,3},{2,0},{3,1},{4,6},{5,7},{6,4},{7,5},{8,10},{9,11},{10,... | collective-permute-start | bytes 1572872 | tf_op jit(solution)/shard_map/ppermute | solution.py:292
  443.5 23.8 %collective-permute-start.26 = (bf16[256,1024]{1,0:T(8,128)(2,1)S(1)}, bf16[256,1024]{1,0:T(8,128)(2,1)S(1)}, u32[]{:S(2)}, u32[]{:S(2)}) collective-permute-start(bf16[256,1024]{1,0:T(8,128)(2,1)S(1)} %copy-done.34), channel_id=1, source_target_pairs={{0,3},{1,2},{2,1},{3,0},{4,7},{5,6},{6,5},{7,4},{8,11},{9,10},{10,... | collective-permute-start | bytes 1572872 | tf_op jit(solution)/shard_map/ppermute | solution.py:292
  468.8 10.4 %copy-start.16 = (bf16[256,1024]{1,0:T(8,128)(2,1)S(1)}, bf16[256,1024]{1,0:T(8,128)(2,1)}, u32[]{:S(2)}) copy-start(bf16[256,1024]{1,0:T(8,128)(2,1)} %copy-done.15) | copy-start | bytes 1572868
  468.8 10.4 %copy-start.18 = (bf16[256,1024]{1,0:T(8,128)(2,1)S(1)}, bf16[256,1024]{1,0:T(8,128)(2,1)}, u32[]{:S(2)}) copy-start(bf16[256,1024]{1,0:T(8,128)(2,1)} %copy-done.17) | copy-start | bytes 1572868
  468.8 10.4 %copy-start.20 = (bf16[256,1024]{1,0:T(8,128)(2,1)S(1)}, bf16[256,1024]{1,0:T(8,128)(2,1)}, u32[]{:S(2)}) copy-start(bf16[256,1024]{1,0:T(8,128)(2,1)} %copy-done.19) | copy-start | bytes 1572868
  468.8 10.4 %copy-start.28 = (bf16[256,1024]{1,0:T(8,128)(2,1)S(1)}, bf16[256,1024]{1,0:T(8,128)(2,1)}, u32[]{:S(2)}) copy-start(bf16[256,1024]{1,0:T(8,128)(2,1)} %get-tuple-element.41.rest_8_.rest_0_) | copy-start | bytes 1572868
  475.7 38.4 %collective-permute-start.18 = (bf16[256,1024]{1,0:T(8,128)(2,1)}, bf16[256,1024]{1,0:T(8,128)(2,1)S(1)}, u32[]{:S(2)}, u32[]{:S(2)}) collective-permute-start(bf16[256,1024]{1,0:T(8,128)(2,1)} %get-tuple-element.48), channel_id=1, source_target_pairs={{0,1},{1,0},{2,3},{3,2},{4,5},{5,4},{6,7},{7,6},{8,9},{9,8},{10,11... | collective-permute-start | bytes 1572872 | tf_op jit(solution)/shard_map/ppermute | solution.py:292
  477.0 46.2 %collective-permute-start.22 = (bf16[256,1024]{1,0:T(8,128)(2,1)}, bf16[256,1024]{1,0:T(8,128)(2,1)}, u32[]{:S(2)}, u32[]{:S(2)}) collective-permute-start(bf16[256,1024]{1,0:T(8,128)(2,1)} %get-tuple-element.53), channel_id=1, source_target_pairs={{0,2},{1,3},{2,0},{3,1},{4,6},{5,7},{6,4},{7,5},{8,10},{9,11},{10,... | collective-permute-start | bytes 1572872 | tf_op jit(solution)/shard_map/ppermute | solution.py:292
  477.8 45.9 %collective-permute-start.23 = (bf16[256,1024]{1,0:T(8,128)(2,1)}, bf16[256,1024]{1,0:T(8,128)(2,1)}, u32[]{:S(2)}, u32[]{:S(2)}) collective-permute-start(bf16[256,1024]{1,0:T(8,128)(2,1)} %get-tuple-element.54), channel_id=1, source_target_pairs={{0,3},{1,2},{2,1},{3,0},{4,7},{5,6},{6,5},{7,4},{8,11},{9,10},{10,... | collective-permute-start | bytes 1572872 | tf_op jit(solution)/shard_map/ppermute | solution.py:292
  512.0 82.3 %collective-permute-start.33 = (bf16[256,1024]{1,0:T(8,128)(2,1)S(1)}, bf16[256,1024]{1,0:T(8,128)(2,1)S(1)}, u32[]{:S(2)}, u32[]{:S(2)}) collective-permute-start(bf16[256,1024]{1,0:T(8,128)(2,1)S(1)} %get-tuple-element.66), channel_id=1, source_target_pairs={{0,1},{1,0},{2,3},{3,2},{4,5},{5,4},{6,7},{7,6},{8,9},{9,8},{10,11... | collective-permute-start | bytes 1572872 | tf_op jit(solution)/shard_map/ppermute | solution.py:292
  513.2 82.6 %collective-permute-start.34 = (bf16[256,1024]{1,0:T(8,128)(2,1)S(1)}, bf16[256,1024]{1,0:T(8,128)(2,1)S(1)}, u32[]{:S(2)}, u32[]{:S(2)}) collective-permute-start(bf16[256,1024]{1,0:T(8,128)(2,1)S(1)} %get-tuple-element.67), channel_id=1, source_target_pairs={{0,2},{1,3},{2,0},{3,1},{4,6},{5,7},{6,4},{7,5},{8,10},{9,11},{10,... | collective-permute-start | bytes 1572872 | tf_op jit(solution)/shard_map/ppermute | solution.py:292
  514.9 10.3 %copy-start.30 = (bf16[256,1024]{1,0:T(8,128)(2,1)S(1)}, bf16[256,1024]{1,0:T(8,128)(2,1)}, u32[]{:S(2)}) copy-start(bf16[256,1024]{1,0:T(8,128)(2,1)} %get-tuple-element.46.rest_8_.rest_0_) | copy-start | bytes 1572868
  521.6 38.0 %collective-permute-start.19 = (bf16[256,1024]{1,0:T(8,128)(2,1)}, bf16[256,1024]{1,0:T(8,128)(2,1)S(1)}, u32[]{:S(2)}, u32[]{:S(2)}) collective-permute-start(bf16[256,1024]{1,0:T(8,128)(2,1)} %get-tuple-element.50), channel_id=1, source_target_pairs={{0,1},{1,0},{2,3},{3,2},{4,5},{5,4},{6,7},{7,6},{8,9},{9,8},{10,11... | collective-permute-start | bytes 1572872 | tf_op jit(solution)/shard_map/ppermute | solution.py:292
  523.2 37.9 %collective-permute-start.20 = (bf16[256,1024]{1,0:T(8,128)(2,1)}, bf16[256,1024]{1,0:T(8,128)(2,1)S(1)}, u32[]{:S(2)}, u32[]{:S(2)}) collective-permute-start(bf16[256,1024]{1,0:T(8,128)(2,1)} %get-tuple-element.51), channel_id=1, source_target_pairs={{0,2},{1,3},{2,0},{3,1},{4,6},{5,7},{6,4},{7,5},{8,10},{9,11},{10,... | collective-permute-start | bytes 1572872 | tf_op jit(solution)/shard_map/ppermute | solution.py:292
  523.7 38.7 %collective-permute-start.21 = (bf16[256,1024]{1,0:T(8,128)(2,1)}, bf16[256,1024]{1,0:T(8,128)(2,1)S(1)}, u32[]{:S(2)}, u32[]{:S(2)}) collective-permute-start(bf16[256,1024]{1,0:T(8,128)(2,1)} %get-tuple-element.52), channel_id=1, source_target_pairs={{0,3},{1,2},{2,1},{3,0},{4,7},{5,6},{6,5},{7,4},{8,11},{9,10},{10,... | collective-permute-start | bytes 1572872 | tf_op jit(solution)/shard_map/ppermute | solution.py:292
  559.6 37.5 %collective-permute-start.35 = (bf16[256,1024]{1,0:T(8,128)(2,1)S(1)}, bf16[256,1024]{1,0:T(8,128)(2,1)S(1)}, u32[]{:S(2)}, u32[]{:S(2)}) collective-permute-start(bf16[256,1024]{1,0:T(8,128)(2,1)S(1)} %get-tuple-element.68), channel_id=1, source_target_pairs={{0,3},{1,2},{2,1},{3,0},{4,7},{5,6},{6,5},{7,4},{8,11},{9,10},{10,... | collective-permute-start | bytes 1572872 | tf_op jit(solution)/shard_map/ppermute | solution.py:292
  561.1 36.8 %collective-permute-start.30 = (bf16[256,1024]{1,0:T(8,128)(2,1)S(1)}, bf16[256,1024]{1,0:T(8,128)(2,1)S(1)}, u32[]{:S(2)}, u32[]{:S(2)}) collective-permute-start(bf16[256,1024]{1,0:T(8,128)(2,1)S(1)} %get-tuple-element.63), channel_id=1, source_target_pairs={{0,1},{1,0},{2,3},{3,2},{4,5},{5,4},{6,7},{7,6},{8,9},{9,8},{10,11... | collective-permute-start | bytes 1572872 | tf_op jit(solution)/shard_map/ppermute | solution.py:292
  562.3 38.6 %collective-permute-start.31 = (bf16[256,1024]{1,0:T(8,128)(2,1)S(1)}, bf16[256,1024]{1,0:T(8,128)(2,1)S(1)}, u32[]{:S(2)}, u32[]{:S(2)}) collective-permute-start(bf16[256,1024]{1,0:T(8,128)(2,1)S(1)} %get-tuple-element.64), channel_id=1, source_target_pairs={{0,2},{1,3},{2,0},{3,1},{4,6},{5,7},{6,4},{7,5},{8,10},{9,11},{10,... | collective-permute-start | bytes 1572872 | tf_op jit(solution)/shard_map/ppermute | solution.py:292
  563.2 36.2 %copy-start.10 = (bf16[256,1024]{1,0:T(8,128)(2,1)S(1)}, bf16[256,1024]{1,0:T(8,128)(2,1)}, u32[]{:S(2)}) copy-start(bf16[256,1024]{1,0:T(8,128)(2,1)} %copy-done.9) | copy-start | bytes 1572868
  594.3 15.8 %collective-permute-start.32 = (bf16[256,1024]{1,0:T(8,128)(2,1)S(1)}, bf16[256,1024]{1,0:T(8,128)(2,1)S(1)}, u32[]{:S(2)}, u32[]{:S(2)}) collective-permute-start(bf16[256,1024]{1,0:T(8,128)(2,1)S(1)} %get-tuple-element.65), channel_id=1, source_target_pairs={{0,3},{1,2},{2,1},{3,0},{4,7},{5,6},{6,5},{7,4},{8,11},{9,10},{10,... | collective-permute-start | bytes 1572872 | tf_op jit(solution)/shard_map/ppermute | solution.py:292
  595.9 25.3 %collective-permute-start.27 = (bf16[256,1024]{1,0:T(8,128)(2,1)S(1)}, bf16[256,1024]{1,0:T(8,128)(2,1)S(1)}, u32[]{:S(2)}, u32[]{:S(2)}) collective-permute-start(bf16[256,1024]{1,0:T(8,128)(2,1)S(1)} %get-tuple-element.60), channel_id=1, source_target_pairs={{0,1},{1,0},{2,3},{3,2},{4,5},{5,4},{6,7},{7,6},{8,9},{9,8},{10,11... | collective-permute-start | bytes 1572872 | tf_op jit(solution)/shard_map/ppermute | solution.py:292
  597.1 24.2 %collective-permute-start.28 = (bf16[256,1024]{1,0:T(8,128)(2,1)S(1)}, bf16[256,1024]{1,0:T(8,128)(2,1)S(1)}, u32[]{:S(2)}, u32[]{:S(2)}) collective-permute-start(bf16[256,1024]{1,0:T(8,128)(2,1)S(1)} %get-tuple-element.61), channel_id=1, source_target_pairs={{0,2},{1,3},{2,0},{3,1},{4,6},{5,7},{6,4},{7,5},{8,10},{9,11},{10,... | collective-permute-start | bytes 1572872 | tf_op jit(solution)/shard_map/ppermute | solution.py:292
  597.9 30.2 %collective-permute-start.29 = (bf16[256,1024]{1,0:T(8,128)(2,1)S(1)}, bf16[256,1024]{1,0:T(8,128)(2,1)S(1)}, u32[]{:S(2)}, u32[]{:S(2)}) collective-permute-start(bf16[256,1024]{1,0:T(8,128)(2,1)S(1)} %get-tuple-element.62), channel_id=1, source_target_pairs={{0,3},{1,2},{2,1},{3,0},{4,7},{5,6},{6,5},{7,4},{8,11},{9,10},{10,... | collective-permute-start | bytes 1572872 | tf_op jit(solution)/shard_map/ppermute | solution.py:292
  (25 other events, 29.4 us)

commit v9 on v6

--- a/solution.py
+++ b/solution.py
@@ -139,7 +139,7 @@
             out_specs=[pl.BlockSpec((c, step * J), lambda i, me: (0, i))] * nt,
         ),
         out_shape=[jax.ShapeDtypeStruct((c, mine * J), bf16)] * nt,
-        compiler_params=params(32),
+        compiler_params=params(56),
         cost_estimate=pl.CostEstimate(
             flops=8 * c * blocks * J,
             bytes_accessed=2 * c * tokens + 4 * c * blocks * J,
@@ -392,9 +392,9 @@
     in3 = swap(gate3)
     out2 = layer(in2, [gate3[0]])
     done2 = swap(out2)
+    out3 = layer(in3, [out2[0], *done1[1:3]])
+    done3 = swap(out3)
     result = put(1, done1, result)
-    out3 = layer(in3, [out2[0], result])
-    done3 = swap(out3)
     result = put(2, done2, result)
     return put(3, done3, result)
 

time: 605 us -> 616 us (1.018)
  waiting for transfers between devices: 262 us -> 281 us
  local copies, waits for them, and re-layouts: 48.1 us -> 32.2 us
  Pallas kernels: 186 us -> 194 us
    unnamed x66 -> x88, local copies, waits for them, and re-layouts: 43.2 us -> 26 us
    ppermute x24, waiting for transfers between devices: 39.3 us -> 56 us  [swap(): lax.ppermute(slots[s], 'tensor', [(i, i ^ s) for i in range(n)])]
    pallas_call x4, Pallas kernels: 17.3 us -> 26.9 us  [gate(): pl.pallas_call(kernel, grid_spec=pltpu.PrefetchScalarGridSpec(num_scalar_...]
  transfers between devices with their start and end apart: 41 -> 41, of which waited for: 13 -> 14; matrix products, arithmetic and copies ran while one was open for 3% -> 3% of each run, Pallas kernels for 31% -> 31%
where the time goes in v9:
time: 616 us; the launch traced here: 614 us
  waiting for transfers between devices  281 us (46%)
  Pallas kernels  194 us (31%)
  starting transfers between devices  91 us (15%)
  local copies, waits for them, and re-layouts  32.2 us (5%)
  other arithmetic  15 us (2%)
    pallas_call x4, Pallas kernels, mlp(): pl.pallas_call(kernel, grid_spec=pltpu.PrefetchScalarGridSpec(num_scalar_...  123 us
    ppermute x1, waiting for transfers between devices, gather_along(): got.append(lax.ppermute(got[1], 'seq', [(i, i ^ 2) for i in middle]))  89.8 us
    all_to_all x6, waiting for transfers between devices, exchange(): return lax.all_to_all(x, 'seq', split_axis=0, concat_axis=0, tiled=True)  72.9 us
    ppermute x9, waiting for transfers between devices, flip(): return lax.ppermute(x, axis, [(i, i ^ bit) for i in range(n)])  62.8 us
    ppermute x24, waiting for transfers between devices, swap(): lax.ppermute(slots[s], 'tensor', [(i, i ^ s) for i in range(n)])  56 us
    all_to_all x6, starting transfers between devices, exchange(): return lax.all_to_all(x, 'seq', split_axis=0, concat_axis=0, tiled=True)  49.9 us
    ppermute x24, starting transfers between devices, swap(): lax.ppermute(slots[s], 'tensor', [(i, i ^ s) for i in range(n)])  28.4 us
    pallas_call x4, Pallas kernels, gate(): pl.pallas_call(kernel, grid_spec=pltpu.PrefetchScalarGridSpec(num_scalar_...  26.9 us
  transfers between devices with their start and end apart: 41, of which 14 were waited for; matrix products, arithmetic and copies ran while one was open for 3% of the time, Pallas kernels for 31%

profile of v9, /device:TPU:0, one launch (start us, length us, event | category | flops | bytes accessed | tf_op | source)
XLA Modules:
  0.0 614.0 jit_solution(8166746125363033765)
XLA Ops:
  1.3 3.1 collective-permute-start
  4.3 17.5 %collective-permute-done = bf16[1,2,192,1024]{3,2,1,0:T(8,128)(2,1)S(1)} collective-permute-done((bf16[1,2,192,1024]{3,2,1,0:T(8,128)(2,1)S(1)}, bf16[1,2,192,1024]{3,2,1,0:T(8,128)(2,1)S(1)}, u32[]{:S(2)}, u32[]{:S(2)}) %collective-permute-start) | collective-permute-done | bytes 786464 | tf_op jit(solution)/shard_map/ppermute | solution.py:299
  23.5 3.4 copy-done
  26.9 7.9 %shard_map.85.refs_0_ = bf16[8,2,32,32,128]{4,3,2,1,0:T(8,128)(2,1)S(1)} custom-call(bf16[256,16384]{1,0:T(8,128)(2,1)S(1)} %copy-done, bf16[512,512]{1,0:T(8,128)(2,1)S(1)} %copy-done.7, f32[256,16384]{1,0:T(8,128)} %rest_3_.7, f32[256,16384]{1,0:T(8,128)} %rest_3_.7, f32[256,16384]{1,0:T(8,128)} %rest_3_.7, f32[256,16384]{1,0:T(8,128)} %rest_3_.7), custom_call_target="tpu_custom_call" | custom-call | flops 2147483648 | bytes 20971520 | tf_op jit(solution)/shard_map/pallas_call | solution.py:40
  34.9 2.0 copy-done.2
  38.0 27.2 %all-to-all-start.1 = ((bf16[8,2,32,32,128]{4,3,2,1,0:T(8,128)(2,1)}), bf16[8,2,32,32,128]{4,3,2,1,0:T(8,128)(2,1)}, u32[]{:S(2)}, u32[]{:S(2)}) async-start(bf16[8,2,32,32,128]{4,3,2,1,0:T(8,128)(2,1)} %shard_map.86), calls=%async_computation.1 | async-start | bytes 8388608 | tf_op jit(solution)/shard_map/all_to_all | solution.py:354
  66.5 3.4 copy-done.1
  69.9 8.0 %shard_map.82.refs_0_ = bf16[8,2,32,32,128]{4,3,2,1,0:T(8,128)(2,1)S(1)} custom-call(bf16[256,16384]{1,0:T(8,128)(2,1)S(1)} %copy-done.1, bf16[512,512]{1,0:T(8,128)(2,1)S(1)} %copy-done.7, f32[256,16384]{1,0:T(8,128)} %rest_3_.7, f32[256,16384]{1,0:T(8,128)} %rest_3_.7, f32[256,16384]{1,0:T(8,128)} %rest_3_.7, f32[256,16384]{1,0:T(8,128)} %rest_3_.7), custom_call_target="tpu_custom_call" | custom-call | flops 2147483648 | bytes 20971520 | tf_op jit(solution)/shard_map/pallas_call | solution.py:40
  77.9 2.0 copy-done.3
  79.9 89.8 %collective-permute-done.2.refs_1_ = bf16[2,2,192,1024]{3,2,1,0:T(8,128)(2,1)} collective-permute-done((bf16[2,2,192,1024]{3,2,1,0:T(8,128)(2,1)S(1)}, bf16[2,2,192,1024]{3,2,1,0:T(8,128)(2,1)}, u32[]{:S(2)}, u32[]{:S(2)}) %collective-permute-start.2) | collective-permute-done | bytes 1572896 | tf_op jit(solution)/shard_map/ppermute | solution.py:309
  169.7 4.5 all-to-all-start
  174.2 2.1 add.7
  176.7 1.5 fusion
  178.2 1.5 collective-permute-start.3
  179.7 1.6 copy.17
  181.3 1.5 collective-permute-start.8
  183.3 31.8 %collective-permute-done.3.rest_0_ = bf16[768,1024]{1,0:T(8,128)(2,1)S(1)} collective-permute-done((bf16[768,1024]{1,0:T(8,128)(2,1)}, bf16[768,1024]{1,0:T(8,128)(2,1)S(1)}, u32[]{:S(2)}, u32[]{:S(2)}) %collective-permute-start.3) | collective-permute-done | bytes 1572896 | tf_op jit(solution)/shard_map/ppermute | solution.py:299
  215.1 1.5 collective-permute-start.5
  216.6 1.5 collective-permute-start.7
  219.3 5.7 shard_map.87
  225.0 43.2 %all-to-all-done.x_ref = bf16[8,2,32,32,128]{4,3,2,1,0:T(8,128)(2,1)} async-done(((bf16[8,2,32,32,128]{4,3,2,1,0:T(8,128)(2,1)}), bf16[8,2,32,32,128]{4,3,2,1,0:T(8,128)(2,1)}, u32[]{:S(2)}, u32[]{:S(2)}) %all-to-all-start) | async-done | bytes 4194336 | tf_op jit(solution)/shard_map/all_to_all | solution.py:354
  268.2 4.3 all-to-all-start.2
  272.6 12.8 %collective-permute-done.5 = bf16[768,1024]{1,0:T(8,128)(2,1)} collective-permute-done((bf16[768,1024]{1,0:T(8,128)(2,1)S(1)}, bf16[768,1024]{1,0:T(8,128)(2,1)}, u32[]{:S(2)}, u32[]{:S(2)}) %collective-permute-start.5) | collective-permute-done | bytes 1572896 | tf_op jit(solution)/shard_map/ppermute | solution.py:299
  285.4 5.9 pad_maximum_fusion.rest_4_.rest_0_
  291.4 5.3 pad_maximum_fusion.1.rest_6_.rest_1_
  297.1 5.6 shard_map.89
  302.7 18.9 %all-to-all-done.2.rest_4_.rest_5_.rest_6_.rest_7_ = bf16[8,32,32,128]{3,2,1,0:T(8,128)(2,1)} async-done(((bf16[8,32,32,128]{3,2,1,0:T(8,128)(2,1)}), bf16[8,32,32,128]{3,2,1,0:T(8,128)(2,1)}, u32[]{:S(2)}, u32[]{:S(2)}) %all-to-all-start.2) | async-done | bytes 2097184 | tf_op jit(solution)/shard_map/all_to_all | solution.py:354
  321.6 4.3 all-to-all-start.3
  329.1 6.7 %shard_map.88 = (bf16[256,1024]{1,0:T(8,128)(2,1)}, bf16[256,1024]{1,0:T(8,128)(2,1)}, bf16[256,1024]{1,0:T(8,128)(2,1)}, bf16[256,1024]{1,0:T(8,128)(2,1)}) custom-call(s32[1]{0:T(128)} %bitcast.me_ref, bf16[256,16384]{1,0:T(8,128)(2,1)} %rest_3_.11, bf16[256,16384]{1,0:T(8,128)(2,1)} %rest_3_.11, bf16[256,16384]{1,0:T(8,128)(2,1)} %rest_3_.11, ...), custom_call_target="tpu_custom_call" | custom-call | flops 8388608 | bytes 12582912 | tf_op jit(solution)/shard_map/pallas_call | solution.py:130
  335.8 1.6 collective-permute-start.11
  337.3 1.5 collective-permute-start.12
  339.3 4.8 shard_map.93.refs_0_
  345.5 5.3 collective-permute-done.11.rest_1_.refs_1_
  350.8 11.9 %collective-permute-done.12.rest_2_.refs_2_ = bf16[256,1024]{1,0:T(8,128)(2,1)S(1)} collective-permute-done((bf16[256,1024]{1,0:T(8,128)(2,1)}, bf16[256,1024]{1,0:T(8,128)(2,1)S(1)}, u32[]{:S(2)}, u32[]{:S(2)}) %collective-permute-start.12) | collective-permute-done | bytes 524320 | tf_op jit(solution)/shard_map/ppermute | solution.py:284
  364.3 10.7 %all-to-all-done.3.rest_4_.rest_5_.rest_6_.rest_7_ = bf16[8,32,32,128]{3,2,1,0:T(8,128)(2,1)} async-done(((bf16[8,32,32,128]{3,2,1,0:T(8,128)(2,1)}), bf16[8,32,32,128]{3,2,1,0:T(8,128)(2,1)}, u32[]{:S(2)}, u32[]{:S(2)}) %all-to-all-start.3) | async-done | bytes 2097184 | tf_op jit(solution)/shard_map/all_to_all | solution.py:354
  375.0 4.5 all-to-all-start.5
  379.6 6.7 %shard_map.90 = (bf16[256,1024]{1,0:T(8,128)(2,1)}, bf16[256,1024]{1,0:T(8,128)(2,1)}, bf16[256,1024]{1,0:T(8,128)(2,1)}, bf16[256,1024]{1,0:T(8,128)(2,1)}) custom-call(s32[1]{0:T(128)} %bitcast.me_ref, bf16[256,16384]{1,0:T(8,128)(2,1)} %rest_3_.11, bf16[256,16384]{1,0:T(8,128)(2,1)} %rest_3_.11, bf16[256,16384]{1,0:T(8,128)(2,1)} %rest_3_.11, ...), custom_call_target="tpu_custom_call" | custom-call | flops 8388608 | bytes 12582912 | tf_op jit(solution)/shard_map/pallas_call | solution.py:130
  386.3 1.6 collective-permute-start.14
  387.8 1.5 collective-permute-start.15
  389.9 5.0 shard_map.84.refs_0_
  395.0 1.4 copy-done.4
  396.4 30.3 %shard_map.91 = (bf16[256,1024]{1,0:T(8,128)(2,1)S(1)}, bf16[256,1024]{1,0:T(8,128)(2,1)S(1)}, bf16[256,1024]{1,0:T(8,128)(2,1)S(1)}, bf16[256,1024]{1,0:T(8,128)(2,1)S(1)}) custom-call(s32[1]{0:T(128)} %bitcast.me_ref, bf16[256,1024]{1,0:T(8,128)(2,1)S(1)} %copy-done.32, bf16[256,1024]{1,0:T(8,128)(2,1)S(1)} %copy-done.19, ...), custom_call_target="tpu_custom_call" | custom-call | flops 25769803776 | bytes 29360128 | tf_op jit(solution)/shard_map/pallas_call | solution.py:215
  431.1 5.0 all-to-all-start.4
  436.1 1.3 collective-permute-start.18
  437.4 1.5 collective-permute-start.19
  439.6 11.2 %collective-permute-done.18.rest_1_ = bf16[256,1024]{1,0:T(8,128)(2,1)S(1)} collective-permute-done((bf16[256,1024]{1,0:T(8,128)(2,1)S(1)}, bf16[256,1024]{1,0:T(8,128)(2,1)S(1)}, u32[]{:S(2)}, u32[]{:S(2)}) %collective-permute-start.18) | collective-permute-done | bytes 524320 | tf_op jit(solution)/shard_map/ppermute | solution.py:284
  450.9 11.8 %collective-permute-done.19.rest_2_ = bf16[256,1024]{1,0:T(8,128)(2,1)S(1)} collective-permute-done((bf16[256,1024]{1,0:T(8,128)(2,1)S(1)}, bf16[256,1024]{1,0:T(8,128)(2,1)S(1)}, u32[]{:S(2)}, u32[]{:S(2)}) %collective-permute-start.19) | collective-permute-done | bytes 524320 | tf_op jit(solution)/shard_map/ppermute | solution.py:284
  462.6 1.6 shard_map.97.rest_12_.rest_4_
  464.3 6.8 %shard_map.95 = (bf16[256,1024]{1,0:T(8,128)(2,1)}, bf16[256,1024]{1,0:T(8,128)(2,1)}, bf16[256,1024]{1,0:T(8,128)(2,1)}, bf16[256,1024]{1,0:T(8,128)(2,1)}) custom-call(s32[1]{0:T(128)} %bitcast.me_ref, bf16[256,16384]{1,0:T(8,128)(2,1)} %rest_3_.11, bf16[256,16384]{1,0:T(8,128)(2,1)} %rest_3_.11, bf16[256,16384]{1,0:T(8,128)(2,1)} %rest_3_.11, ...), custom_call_target="tpu_custom_call" | custom-call | flops 8388608 | bytes 12582912 | tf_op jit(solution)/shard_map/pallas_call | solution.py:130
  473.2 1.4 collective-permute-start.25
  475.7 31.1 %shard_map.96 = (bf16[256,1024]{1,0:T(8,128)(2,1)S(1)}, bf16[256,1024]{1,0:T(8,128)(2,1)}, bf16[256,1024]{1,0:T(8,128)(2,1)S(1)}, bf16[256,1024]{1,0:T(8,128)(2,1)S(1)}) custom-call(s32[1]{0:T(128)} %bitcast.me_ref, bf16[256,1024]{1,0:T(8,128)(2,1)S(1)} %copy-done.27, bf16[256,1024]{1,0:T(8,128)(2,1)S(1)} %copy-done.13, bf16[256,1024]{1,0:T(8,128)(2,1)S(1)} %copy-done.15, ...), custom_call_target="tpu_custom_call" | custom-call | flops 25769803776 | bytes 29360128 | tf_op jit(solution)/shard_map/pallas_call | solution.py:215
  510.4 6.7 %shard_map.98 = (bf16[256,1024]{1,0:T(8,128)(2,1)}, bf16[256,1024]{1,0:T(8,128)(2,1)}, bf16[256,1024]{1,0:T(8,128)(2,1)}, bf16[256,1024]{1,0:T(8,128)(2,1)}) custom-call(s32[1]{0:T(128)} %bitcast.me_ref, bf16[256,16384]{1,0:T(8,128)(2,1)} %rest_3_.11, bf16[256,16384]{1,0:T(8,128)(2,1)} %rest_3_.11, bf16[256,16384]{1,0:T(8,128)(2,1)} %rest_3_.11, ...), custom_call_target="tpu_custom_call" | custom-call | flops 8388608 | bytes 12582912 | tf_op jit(solution)/shard_map/pallas_call | solution.py:130
  517.1 1.6 collective-permute-start.21
  519.2 1.5 collective-permute-start.23
  522.8 31.3 %shard_map.99 = (bf16[256,1024]{1,0:T(8,128)(2,1)S(1)}, bf16[256,1024]{1,0:T(8,128)(2,1)S(1)}, bf16[256,1024]{1,0:T(8,128)(2,1)S(1)}, bf16[256,1024]{1,0:T(8,128)(2,1)S(1)}) custom-call(s32[1]{0:T(128)} %bitcast.me_ref, bf16[256,1024]{1,0:T(8,128)(2,1)S(1)} %copy-done.31, bf16[256,1024]{1,0:T(8,128)(2,1)S(1)} %copy-done.25, ...), custom_call_target="tpu_custom_call" | custom-call | flops 25769803776 | bytes 29360128 | tf_op jit(solution)/shard_map/pallas_call | solution.py:215
  554.1 1.5 collective-permute-start.34
  557.7 1.4 collective-permute-start.33
  559.2 30.6 %shard_map.100 = (bf16[256,1024]{1,0:T(8,128)(2,1)S(1)}, bf16[256,1024]{1,0:T(8,128)(2,1)S(1)}, bf16[256,1024]{1,0:T(8,128)(2,1)S(1)}, bf16[256,1024]{1,0:T(8,128)(2,1)S(1)}) custom-call(s32[1]{0:T(128)} %bitcast.me_ref, bf16[256,1024]{1,0:T(8,128)(2,1)S(1)} %copy-done.29, bf16[256,1024]{1,0:T(8,128)(2,1)S(1)} %collective-permute-done.21.rest_1_, ...), custom_call_target="tpu_custom_call" | custom-call | flops 25769803776 | bytes 29360128 | tf_op jit(solution)/shard_map/pallas_call | solution.py:215
  591.9 1.4 collective-permute-start.30
  593.3 1.6 shard_map.101.rest_4_
  594.9 1.6 shard_map.102.rest_4_
  596.5 8.2 %collective-permute-done.28.rest_1_ = bf16[256,1024]{1,0:T(8,128)(2,1)S(1)} collective-permute-done((bf16[256,1024]{1,0:T(8,128)(2,1)S(1)}, bf16[256,1024]{1,0:T(8,128)(2,1)S(1)}, u32[]{:S(2)}, u32[]{:S(2)}) %collective-permute-start.28) | collective-permute-done | bytes 524320 | tf_op jit(solution)/shard_map/ppermute | solution.py:284
  604.7 7.6 %collective-permute-done.29.rest_2_ = bf16[256,1024]{1,0:T(8,128)(2,1)S(1)} collective-permute-done((bf16[256,1024]{1,0:T(8,128)(2,1)S(1)}, bf16[256,1024]{1,0:T(8,128)(2,1)S(1)}, u32[]{:S(2)}, u32[]{:S(2)}) %collective-permute-start.29) | collective-permute-done | bytes 524320 | tf_op jit(solution)/shard_map/ppermute | solution.py:284
  612.2 1.6 shard_map.103
  (140 shorter events, 33.6 us)
Async XLA Ops:
  0.0 23.5 %copy-start.7 = (bf16[512,512]{1,0:T(8,128)(2,1)S(1)}, bf16[512,512]{1,0:T(8,128)(2,1)}, u32[]{:S(2)}) copy-start(bf16[512,512]{1,0:T(8,128)(2,1)} %factor.3) | copy-start | bytes 1572868
  1.3 20.6 %collective-permute-start = (bf16[1,2,192,1024]{3,2,1,0:T(8,128)(2,1)S(1)}, bf16[1,2,192,1024]{3,2,1,0:T(8,128)(2,1)S(1)}, u32[]{:S(2)}, u32[]{:S(2)}) collective-permute-start(bf16[1,2,192,1024]{3,2,1,0:T(8,128)(2,1)S(1)} %maximum_bitcast_fusion), channel_id=1, source_target_pairs={{0,8},{4,12},{8,0},{12,4},{16,24},{20,28},{24,16},{28,20},{1,9},{5... | collective-permute-start | bytes 2359304 | tf_op jit(solution)/shard_map/ppermute | solution.py:299
  22.8 14.1 %collective-permute-start.1 = (bf16[2,2,192,1024]{3,2,1,0:T(8,128)(2,1)S(1)}, bf16[2,2,192,1024]{3,2,1,0:T(8,128)(2,1)S(1)}, u32[]{:S(2)}, u32[]{:S(2)}) collective-permute-start(bf16[2,2,192,1024]{3,2,1,0:T(8,128)(2,1)S(1)} %pad_maximum_fusion.3), channel_id=1, source_target_pairs={{8,16},{12,20},{16,8},{20,12},{9,17},{13,21},{17,9},{21,13},{10,18... | collective-permute-start | bytes 4718600 | tf_op jit(solution)/shard_map/ppermute | solution.py:308
  23.5 3.4 copy-start
  38.0 27.2 %copy-start.41 = (bf16[2,2,192,1024]{3,2,1,0:T(8,128)(2,1)S(1)}, bf16[2,2,192,1024]{3,2,1,0:T(8,128)(2,1)}, u32[]{:S(2)}) copy-start(bf16[2,2,192,1024]{3,2,1,0:T(8,128)(2,1)} %copy-done.40) | copy-start | bytes 4718596
  38.0 131.6 %all-to-all-start.1 = ((bf16[8,2,32,32,128]{4,3,2,1,0:T(8,128)(2,1)}), bf16[8,2,32,32,128]{4,3,2,1,0:T(8,128)(2,1)}, u32[]{:S(2)}, u32[]{:S(2)}) async-start(bf16[8,2,32,32,128]{4,3,2,1,0:T(8,128)(2,1)} %shard_map.86), calls=%async_computation.1 | async-start | bytes 8388608 | tf_op jit(solution)/shard_map/all_to_all | solution.py:354
  65.2 104.4 %collective-permute-start.2 = (bf16[2,2,192,1024]{3,2,1,0:T(8,128)(2,1)S(1)}, bf16[2,2,192,1024]{3,2,1,0:T(8,128)(2,1)}, u32[]{:S(2)}, u32[]{:S(2)}) collective-permute-start(bf16[2,2,192,1024]{3,2,1,0:T(8,128)(2,1)S(1)} %copy-done.41), channel_id=1, source_target_pairs={{8,0},{12,4},{16,24},{20,28},{9,1},{13,5},{17,25},{21,29},{10,2},{... | collective-permute-start | bytes 4718600 | tf_op jit(solution)/shard_map/ppermute | solution.py:309
  66.5 3.4 copy-start.1
  169.7 98.6 %all-to-all-start = ((bf16[8,2,32,32,128]{4,3,2,1,0:T(8,128)(2,1)}), bf16[8,2,32,32,128]{4,3,2,1,0:T(8,128)(2,1)}, u32[]{:S(2)}, u32[]{:S(2)}) async-start(bf16[8,2,32,32,128]{4,3,2,1,0:T(8,128)(2,1)} %shard_map.83), calls=%async_computation | async-start | bytes 8388608 | tf_op jit(solution)/shard_map/all_to_all | solution.py:354
  178.2 41.1 %copy-start.6 = (f32[256,256]{1,0:T(8,128)S(1)}, f32[256,256]{1,0:T(8,128)}, u32[]{:S(2)}) copy-start(f32[256,256]{1,0:T(8,128)} %s_ref.7) | copy-start | bytes 786436
  178.2 36.9 %collective-permute-start.3 = (bf16[768,1024]{1,0:T(8,128)(2,1)}, bf16[768,1024]{1,0:T(8,128)(2,1)S(1)}, u32[]{:S(2)}, u32[]{:S(2)}) collective-permute-start(bf16[768,1024]{1,0:T(8,128)(2,1)} %bitcast.6), channel_id=1, source_target_pairs={{0,1},{1,0},{2,3},{3,2},{4,5},{5,4},{6,7},{7,6},{8,9},{9,8},{10,11... | collective-permute-start | bytes 4718600 | tf_op jit(solution)/shard_map/ppermute | solution.py:299
  181.3 37.5 %collective-permute-start.8 = (bf16[1024,768]{1,0:T(8,128)(2,1)}, bf16[1024,768]{1,0:T(8,128)(2,1)S(1)}, u32[]{:S(2)}, u32[]{:S(2)}) collective-permute-start(bf16[1024,768]{1,0:T(8,128)(2,1)} %bitcast.23), channel_id=1, source_target_pairs={{0,2},{1,3},{2,0},{3,1},{4,6},{5,7},{6,4},{7,5},{8,10},{9,11},{10,... | collective-permute-start | bytes 4718600 | tf_op jit(solution)/shard_map/ppermute | solution.py:299
  182.8 89.7 %collective-permute-start.4 = (bf16[768,1024]{1,0:T(8,128)(2,1)}, bf16[768,1024]{1,0:T(8,128)(2,1)}, u32[]{:S(2)}, u32[]{:S(2)}) collective-permute-start(bf16[768,1024]{1,0:T(8,128)(2,1)} %bitcast.6), channel_id=1, source_target_pairs={{0,2},{1,3},{2,0},{3,1},{4,6},{5,7},{6,4},{7,5},{8,10},{9,11},{10,... | collective-permute-start | bytes 4718600 | tf_op jit(solution)/shard_map/ppermute | solution.py:299
  215.1 70.3 %collective-permute-start.5 = (bf16[768,1024]{1,0:T(8,128)(2,1)S(1)}, bf16[768,1024]{1,0:T(8,128)(2,1)}, u32[]{:S(2)}, u32[]{:S(2)}) collective-permute-start(bf16[768,1024]{1,0:T(8,128)(2,1)S(1)} %collective-permute-done.3.rest_0_), channel_id=1, source_target_pairs={{0,2},{1,3},{2,0},{3,1},{4,6},{5,7},{6,4},{7,5},{8,10},{9,11},{10,... | collective-permute-start | bytes 4718600 | tf_op jit(solution)/shard_map/ppermute | solution.py:299
  216.6 74.7 %collective-permute-start.7 = (bf16[1024,768]{1,0:T(8,128)(2,1)}, bf16[1024,768]{1,0:T(8,128)(2,1)}, u32[]{:S(2)}, u32[]{:S(2)}) collective-permute-start(bf16[1024,768]{1,0:T(8,128)(2,1)} %bitcast.24), channel_id=1, source_target_pairs={{0,1},{1,0},{2,3},{3,2},{4,5},{5,4},{6,7},{7,6},{8,9},{9,8},{10,11... | collective-permute-start | bytes 4718600 | tf_op jit(solution)/shard_map/ppermute | solution.py:299
  218.8 72.6 %collective-permute-start.9 = (bf16[1024,768]{1,0:T(8,128)(2,1)S(1)}, bf16[1024,768]{1,0:T(8,128)(2,1)}, u32[]{:S(2)}, u32[]{:S(2)}) collective-permute-start(bf16[1024,768]{1,0:T(8,128)(2,1)S(1)} %collective-permute-done.8.rest_1_), channel_id=1, source_target_pairs={{0,1},{1,0},{2,3},{3,2},{4,5},{5,4},{6,7},{7,6},{8,9},{9,8},{10,11... | collective-permute-start | bytes 4718600 | tf_op jit(solution)/shard_map/ppermute | solution.py:299
  268.2 53.4 %all-to-all-start.2 = ((bf16[8,32,32,128]{3,2,1,0:T(8,128)(2,1)}), bf16[8,32,32,128]{3,2,1,0:T(8,128)(2,1)}, u32[]{:S(2)}, u32[]{:S(2)}) async-start(bf16[8,32,32,128]{3,2,1,0:T(8,128)(2,1)} %shard_map.87), calls=%async_computation.2 | async-start | bytes 4194304 | tf_op jit(solution)/shard_map/all_to_all | solution.py:354
  285.4 5.9 copy-start.39
  291.3 98.6 %collective-permute-start.6 = (bf16[4,768,1024]{2,1,0:T(8,128)(2,1)}, bf16[4,768,1024]{2,1,0:T(8,128)(2,1)}, u32[]{:S(2)}, u32[]{:S(2)}) collective-permute-start(bf16[4,768,1024]{2,1,0:T(8,128)(2,1)} %pad_maximum_fusion.rest_4_.rest_0_), channel_id=1, source_target_pairs={{0,4},{4,0},{8,12},{12,8},{16,20},{20,16},{24,28},{28,24},{1,5},{5... | collective-permute-start | bytes 18874376 | tf_op jit(solution)/shard_map/ppermute | solution.py:299
  296.6 93.3 %collective-permute-start.10 = (bf16[4,1024,768]{2,1,0:T(8,128)(2,1)}, bf16[4,1024,768]{2,1,0:T(8,128)(2,1)}, u32[]{:S(2)}, u32[]{:S(2)}) collective-permute-start(bf16[4,1024,768]{2,1,0:T(8,128)(2,1)} %pad_maximum_fusion.1.rest_6_.rest_1_), channel_id=1, source_target_pairs={{0,4},{4,0},{8,12},{12,8},{16,20},{20,16},{24,28},{28,24},{1,5},{5... | collective-permute-start | bytes 18874376 | tf_op jit(solution)/shard_map/ppermute | solution.py:299
  321.6 53.4 %all-to-all-start.3 = ((bf16[8,32,32,128]{3,2,1,0:T(8,128)(2,1)}), bf16[8,32,32,128]{3,2,1,0:T(8,128)(2,1)}, u32[]{:S(2)}, u32[]{:S(2)}) async-start(bf16[8,32,32,128]{3,2,1,0:T(8,128)(2,1)} %shard_map.89), calls=%async_computation.3 | async-start | bytes 4194304 | tf_op jit(solution)/shard_map/all_to_all | solution.py:354
  335.8 15.0 %collective-permute-start.11 = (bf16[256,1024]{1,0:T(8,128)(2,1)}, bf16[256,1024]{1,0:T(8,128)(2,1)S(1)}, u32[]{:S(2)}, u32[]{:S(2)}) collective-permute-start(bf16[256,1024]{1,0:T(8,128)(2,1)} %get-tuple-element.38), channel_id=1, source_target_pairs={{0,1},{1,0},{2,3},{3,2},{4,5},{5,4},{6,7},{7,6},{8,9},{9,8},{10,11... | collective-permute-start | bytes 1572872 | tf_op jit(solution)/shard_map/ppermute | solution.py:284
  337.3 25.3 %collective-permute-start.12 = (bf16[256,1024]{1,0:T(8,128)(2,1)}, bf16[256,1024]{1,0:T(8,128)(2,1)S(1)}, u32[]{:S(2)}, u32[]{:S(2)}) collective-permute-start(bf16[256,1024]{1,0:T(8,128)(2,1)} %get-tuple-element.39), channel_id=1, source_target_pairs={{0,2},{1,3},{2,0},{3,1},{4,6},{5,7},{6,4},{7,5},{8,10},{9,11},{10,... | collective-permute-start | bytes 1572872 | tf_op jit(solution)/shard_map/ppermute | solution.py:284
  338.9 23.8 %collective-permute-start.13 = (bf16[256,1024]{1,0:T(8,128)(2,1)}, bf16[256,1024]{1,0:T(8,128)(2,1)S(1)}, u32[]{:S(2)}, u32[]{:S(2)}) collective-permute-start(bf16[256,1024]{1,0:T(8,128)(2,1)} %get-tuple-element.40), channel_id=1, source_target_pairs={{0,3},{1,2},{2,1},{3,0},{4,7},{5,6},{6,5},{7,4},{8,11},{9,10},{10,... | collective-permute-start | bytes 1572872 | tf_op jit(solution)/shard_map/ppermute | solution.py:284
  350.8 11.9 %copy-start.18 = (bf16[256,1024]{1,0:T(8,128)(2,1)}, bf16[256,1024]{1,0:T(8,128)(2,1)S(1)}, u32[]{:S(2)}) copy-start(bf16[256,1024]{1,0:T(8,128)(2,1)S(1)} %collective-permute-done.11.rest_1_.refs_1_) | copy-start | bytes 1572868
  375.0 56.1 %all-to-all-start.5 = ((bf16[8,32,32,128]{3,2,1,0:T(8,128)(2,1)}), bf16[8,32,32,128]{3,2,1,0:T(8,128)(2,1)}, u32[]{:S(2)}, u32[]{:S(2)}) async-start(bf16[8,32,32,128]{3,2,1,0:T(8,128)(2,1)} %shard_map.94), calls=%async_computation.5 | async-start | bytes 4194304 | tf_op jit(solution)/shard_map/all_to_all | solution.py:354
  386.3 43.7 %collective-permute-start.14 = (bf16[256,1024]{1,0:T(8,128)(2,1)}, bf16[256,1024]{1,0:T(8,128)(2,1)S(1)}, u32[]{:S(2)}, u32[]{:S(2)}) collective-permute-start(bf16[256,1024]{1,0:T(8,128)(2,1)} %get-tuple-element.43), channel_id=1, source_target_pairs={{0,1},{1,0},{2,3},{3,2},{4,5},{5,4},{6,7},{7,6},{8,9},{9,8},{10,11... | collective-permute-start | bytes 1572872 | tf_op jit(solution)/shard_map/ppermute | solution.py:284
  387.8 42.1 %collective-permute-start.15 = (bf16[256,1024]{1,0:T(8,128)(2,1)}, bf16[256,1024]{1,0:T(8,128)(2,1)S(1)}, u32[]{:S(2)}, u32[]{:S(2)}) collective-permute-start(bf16[256,1024]{1,0:T(8,128)(2,1)} %get-tuple-element.44), channel_id=1, source_target_pairs={{0,2},{1,3},{2,0},{3,1},{4,6},{5,7},{6,4},{7,5},{8,10},{9,11},{10,... | collective-permute-start | bytes 1572872 | tf_op jit(solution)/shard_map/ppermute | solution.py:284
  389.4 7.0 %copy-start.19 = (bf16[256,1024]{1,0:T(8,128)(2,1)S(1)}, bf16[256,1024]{1,0:T(8,128)(2,1)}, u32[]{:S(2)}) copy-start(bf16[256,1024]{1,0:T(8,128)(2,1)} %copy-done.18) | copy-start | bytes 1572868
  389.4 7.0 %copy-start.21 = (bf16[256,1024]{1,0:T(8,128)(2,1)S(1)}, bf16[256,1024]{1,0:T(8,128)(2,1)}, u32[]{:S(2)}) copy-start(bf16[256,1024]{1,0:T(8,128)(2,1)} %copy-done.20) | copy-start | bytes 1572868
  389.4 7.0 %copy-start.23 = (bf16[256,1024]{1,0:T(8,128)(2,1)S(1)}, bf16[256,1024]{1,0:T(8,128)(2,1)}, u32[]{:S(2)}) copy-start(bf16[256,1024]{1,0:T(8,128)(2,1)} %copy-done.22) | copy-start | bytes 1572868
  389.4 7.0 %copy-start.26 = (bf16[256,1024]{1,0:T(8,128)(2,1)S(1)}, bf16[256,1024]{1,0:T(8,128)(2,1)}, u32[]{:S(2)}) copy-start(bf16[256,1024]{1,0:T(8,128)(2,1)} %get-tuple-element.41.rest_8_.rest_0_) | copy-start | bytes 1572868
  389.4 7.0 %copy-start.32 = (bf16[256,1024]{1,0:T(8,128)(2,1)S(1)}, bf16[256,1024]{1,0:T(8,128)(2,1)}, u32[]{:S(2)}) copy-start(bf16[256,1024]{1,0:T(8,128)(2,1)} %get-tuple-element.37.rest_0_) | copy-start | bytes 1572868
  389.4 40.6 %collective-permute-start.16 = (bf16[256,1024]{1,0:T(8,128)(2,1)}, bf16[256,1024]{1,0:T(8,128)(2,1)S(1)}, u32[]{:S(2)}, u32[]{:S(2)}) collective-permute-start(bf16[256,1024]{1,0:T(8,128)(2,1)} %get-tuple-element.45), channel_id=1, source_target_pairs={{0,3},{1,2},{2,1},{3,0},{4,7},{5,6},{6,5},{7,4},{8,11},{9,10},{10,... | collective-permute-start | bytes 1572872 | tf_op jit(solution)/shard_map/ppermute | solution.py:284
  431.1 5.0 copy-start.38
  431.1 6.3 %copy-start.36 = (bf16[256,1024]{1,0:T(8,128)(2,1)S(1)}, bf16[256,1024]{1,0:T(8,128)(2,1)}, u32[]{:S(2)}) copy-start(bf16[256,1024]{1,0:T(8,128)(2,1)} %copy-done.35) | copy-start | bytes 1572868
  431.1 7.8 %copy-start.34 = (bf16[256,1024]{1,0:T(8,128)(2,1)S(1)}, bf16[256,1024]{1,0:T(8,128)(2,1)}, u32[]{:S(2)}) copy-start(bf16[256,1024]{1,0:T(8,128)(2,1)} %copy-done.33) | copy-start | bytes 1572868
  431.1 31.5 %copy-start.9 = (bf16[256,1024]{1,0:T(8,128)(2,1)S(1)}, bf16[256,1024]{1,0:T(8,128)(2,1)}, u32[]{:S(2)}) copy-start(bf16[256,1024]{1,0:T(8,128)(2,1)} %copy-done.8) | copy-start | bytes 1572868
  431.1 78.5 %all-to-all-start.4 = ((bf16[8,32,32,128]{3,2,1,0:T(8,128)(2,1)}), bf16[8,32,32,128]{3,2,1,0:T(8,128)(2,1)}, u32[]{:S(2)}, u32[]{:S(2)}) async-start(bf16[8,32,32,128]{3,2,1,0:T(8,128)(2,1)} %shard_map.92), calls=%async_computation.4 | async-start | bytes 4194304 | tf_op jit(solution)/shard_map/all_to_all | solution.py:354
  436.1 14.8 %collective-permute-start.18 = (bf16[256,1024]{1,0:T(8,128)(2,1)S(1)}, bf16[256,1024]{1,0:T(8,128)(2,1)S(1)}, u32[]{:S(2)}, u32[]{:S(2)}) collective-permute-start(bf16[256,1024]{1,0:T(8,128)(2,1)S(1)} %copy-done.38), channel_id=1, source_target_pairs={{0,1},{1,0},{2,3},{3,2},{4,5},{5,4},{6,7},{7,6},{8,9},{9,8},{10,11... | collective-permute-start | bytes 1572872 | tf_op jit(solution)/shard_map/ppermute | solution.py:284
  437.4 25.2 %collective-permute-start.19 = (bf16[256,1024]{1,0:T(8,128)(2,1)S(1)}, bf16[256,1024]{1,0:T(8,128)(2,1)S(1)}, u32[]{:S(2)}, u32[]{:S(2)}) collective-permute-start(bf16[256,1024]{1,0:T(8,128)(2,1)S(1)} %copy-done.36), channel_id=1, source_target_pairs={{0,2},{1,3},{2,0},{3,1},{4,6},{5,7},{6,4},{7,5},{8,10},{9,11},{10,... | collective-permute-start | bytes 1572872 | tf_op jit(solution)/shard_map/ppermute | solution.py:284
  438.9 23.7 %collective-permute-start.20 = (bf16[256,1024]{1,0:T(8,128)(2,1)S(1)}, bf16[256,1024]{1,0:T(8,128)(2,1)S(1)}, u32[]{:S(2)}, u32[]{:S(2)}) collective-permute-start(bf16[256,1024]{1,0:T(8,128)(2,1)S(1)} %copy-done.34), channel_id=1, source_target_pairs={{0,3},{1,2},{2,1},{3,0},{4,7},{5,6},{6,5},{7,4},{8,11},{9,10},{10,... | collective-permute-start | bytes 1572872 | tf_op jit(solution)/shard_map/ppermute | solution.py:284
  464.2 10.4 %copy-start.13 = (bf16[256,1024]{1,0:T(8,128)(2,1)S(1)}, bf16[256,1024]{1,0:T(8,128)(2,1)}, u32[]{:S(2)}) copy-start(bf16[256,1024]{1,0:T(8,128)(2,1)} %copy-done.12) | copy-start | bytes 1572868
  464.2 10.4 %copy-start.15 = (bf16[256,1024]{1,0:T(8,128)(2,1)S(1)}, bf16[256,1024]{1,0:T(8,128)(2,1)}, u32[]{:S(2)}) copy-start(bf16[256,1024]{1,0:T(8,128)(2,1)} %copy-done.14) | copy-start | bytes 1572868
  464.2 10.4 %copy-start.17 = (bf16[256,1024]{1,0:T(8,128)(2,1)S(1)}, bf16[256,1024]{1,0:T(8,128)(2,1)}, u32[]{:S(2)}) copy-start(bf16[256,1024]{1,0:T(8,128)(2,1)} %copy-done.16) | copy-start | bytes 1572868
  464.2 10.4 %copy-start.27 = (bf16[256,1024]{1,0:T(8,128)(2,1)S(1)}, bf16[256,1024]{1,0:T(8,128)(2,1)}, u32[]{:S(2)}) copy-start(bf16[256,1024]{1,0:T(8,128)(2,1)} %get-tuple-element.41.rest_8_.rest_0_) | copy-start | bytes 1572868
  471.1 38.5 %collective-permute-start.17 = (bf16[256,1024]{1,0:T(8,128)(2,1)}, bf16[256,1024]{1,0:T(8,128)(2,1)S(1)}, u32[]{:S(2)}, u32[]{:S(2)}) collective-permute-start(bf16[256,1024]{1,0:T(8,128)(2,1)} %get-tuple-element.48), channel_id=1, source_target_pairs={{0,1},{1,0},{2,3},{3,2},{4,5},{5,4},{6,7},{7,6},{8,9},{9,8},{10,11... | collective-permute-start | bytes 1572872 | tf_op jit(solution)/shard_map/ppermute | solution.py:284
  472.4 46.3 %collective-permute-start.24 = (bf16[256,1024]{1,0:T(8,128)(2,1)}, bf16[256,1024]{1,0:T(8,128)(2,1)S(1)}, u32[]{:S(2)}, u32[]{:S(2)}) collective-permute-start(bf16[256,1024]{1,0:T(8,128)(2,1)} %get-tuple-element.56), channel_id=1, source_target_pairs={{0,2},{1,3},{2,0},{3,1},{4,6},{5,7},{6,4},{7,5},{8,10},{9,11},{10,... | collective-permute-start | bytes 1572872 | tf_op jit(solution)/shard_map/ppermute | solution.py:284
  473.2 46.0 %collective-permute-start.25 = (bf16[256,1024]{1,0:T(8,128)(2,1)}, bf16[256,1024]{1,0:T(8,128)(2,1)}, u32[]{:S(2)}, u32[]{:S(2)}) collective-permute-start(bf16[256,1024]{1,0:T(8,128)(2,1)} %get-tuple-element.57), channel_id=1, source_target_pairs={{0,3},{1,2},{2,1},{3,0},{4,7},{5,6},{6,5},{7,4},{8,11},{9,10},{10,... | collective-permute-start | bytes 1572872 | tf_op jit(solution)/shard_map/ppermute | solution.py:284
  507.5 46.6 %collective-permute-start.26 = (bf16[256,1024]{1,0:T(8,128)(2,1)}, bf16[256,1024]{1,0:T(8,128)(2,1)S(1)}, u32[]{:S(2)}, u32[]{:S(2)}) collective-permute-start(bf16[256,1024]{1,0:T(8,128)(2,1)} %get-tuple-element.59), channel_id=1, source_target_pairs={{0,1},{1,0},{2,3},{3,2},{4,5},{5,4},{6,7},{7,6},{8,9},{9,8},{10,11... | collective-permute-start | bytes 1572872 | tf_op jit(solution)/shard_map/ppermute | solution.py:284
  508.8 46.9 %collective-permute-start.27 = (bf16[256,1024]{1,0:T(8,128)(2,1)S(1)}, bf16[256,1024]{1,0:T(8,128)(2,1)S(1)}, u32[]{:S(2)}, u32[]{:S(2)}) collective-permute-start(bf16[256,1024]{1,0:T(8,128)(2,1)S(1)} %get-tuple-element.60), channel_id=1, source_target_pairs={{0,2},{1,3},{2,0},{3,1},{4,6},{5,7},{6,4},{7,5},{8,10},{9,11},{10,... | collective-permute-start | bytes 1572872 | tf_op jit(solution)/shard_map/ppermute | solution.py:284
  510.4 10.3 %copy-start.31 = (bf16[256,1024]{1,0:T(8,128)(2,1)S(1)}, bf16[256,1024]{1,0:T(8,128)(2,1)}, u32[]{:S(2)}) copy-start(bf16[256,1024]{1,0:T(8,128)(2,1)} %get-tuple-element.46.rest_8_.rest_0_) | copy-start | bytes 1572868
  517.1 39.8 %collective-permute-start.21 = (bf16[256,1024]{1,0:T(8,128)(2,1)}, bf16[256,1024]{1,0:T(8,128)(2,1)S(1)}, u32[]{:S(2)}, u32[]{:S(2)}) collective-permute-start(bf16[256,1024]{1,0:T(8,128)(2,1)} %get-tuple-element.53), channel_id=1, source_target_pairs={{0,1},{1,0},{2,3},{3,2},{4,5},{5,4},{6,7},{7,6},{8,9},{9,8},{10,11... | collective-permute-start | bytes 1572872 | tf_op jit(solution)/shard_map/ppermute | solution.py:284
  518.7 39.0 %collective-permute-start.22 = (bf16[256,1024]{1,0:T(8,128)(2,1)}, bf16[256,1024]{1,0:T(8,128)(2,1)S(1)}, u32[]{:S(2)}, u32[]{:S(2)}) collective-permute-start(bf16[256,1024]{1,0:T(8,128)(2,1)} %get-tuple-element.54), channel_id=1, source_target_pairs={{0,2},{1,3},{2,0},{3,1},{4,6},{5,7},{6,4},{7,5},{8,10},{9,11},{10,... | collective-permute-start | bytes 1572872 | tf_op jit(solution)/shard_map/ppermute | solution.py:284
  519.2 40.0 %collective-permute-start.23 = (bf16[256,1024]{1,0:T(8,128)(2,1)}, bf16[256,1024]{1,0:T(8,128)(2,1)S(1)}, u32[]{:S(2)}, u32[]{:S(2)}) collective-permute-start(bf16[256,1024]{1,0:T(8,128)(2,1)} %get-tuple-element.55), channel_id=1, source_target_pairs={{0,3},{1,2},{2,1},{3,0},{4,7},{5,6},{6,5},{7,4},{8,11},{9,10},{10,... | collective-permute-start | bytes 1572872 | tf_op jit(solution)/shard_map/ppermute | solution.py:284
  522.8 36.4 %copy-start.29 = (bf16[256,1024]{1,0:T(8,128)(2,1)S(1)}, bf16[256,1024]{1,0:T(8,128)(2,1)}, u32[]{:S(2)}) copy-start(bf16[256,1024]{1,0:T(8,128)(2,1)} %get-tuple-element.52.rest_8_.rest_0_) | copy-start | bytes 1572868
  554.1 36.9 %collective-permute-start.34 = (bf16[256,1024]{1,0:T(8,128)(2,1)S(1)}, bf16[256,1024]{1,0:T(8,128)(2,1)S(1)}, u32[]{:S(2)}, u32[]{:S(2)}) collective-permute-start(bf16[256,1024]{1,0:T(8,128)(2,1)S(1)} %get-tuple-element.68), channel_id=1, source_target_pairs={{0,3},{1,2},{2,1},{3,0},{4,7},{5,6},{6,5},{7,4},{8,11},{9,10},{10,... | collective-permute-start | bytes 1572872 | tf_op jit(solution)/shard_map/ppermute | solution.py:284
  555.6 36.2 %collective-permute-start.31 = (bf16[256,1024]{1,0:T(8,128)(2,1)S(1)}, bf16[256,1024]{1,0:T(8,128)(2,1)S(1)}, u32[]{:S(2)}, u32[]{:S(2)}) collective-permute-start(bf16[256,1024]{1,0:T(8,128)(2,1)S(1)} %get-tuple-element.65), channel_id=1, source_target_pairs={{0,1},{1,0},{2,3},{3,2},{4,5},{5,4},{6,7},{7,6},{8,9},{9,8},{10,11... | collective-permute-start | bytes 1572872 | tf_op jit(solution)/shard_map/ppermute | solution.py:284
  556.9 38.0 %collective-permute-start.32 = (bf16[256,1024]{1,0:T(8,128)(2,1)S(1)}, bf16[256,1024]{1,0:T(8,128)(2,1)S(1)}, u32[]{:S(2)}, u32[]{:S(2)}) collective-permute-start(bf16[256,1024]{1,0:T(8,128)(2,1)S(1)} %get-tuple-element.66), channel_id=1, source_target_pairs={{0,2},{1,3},{2,0},{3,1},{4,6},{5,7},{6,4},{7,5},{8,10},{9,11},{10,... | collective-permute-start | bytes 1572872 | tf_op jit(solution)/shard_map/ppermute | solution.py:284
  557.7 37.2 %collective-permute-start.33 = (bf16[256,1024]{1,0:T(8,128)(2,1)S(1)}, bf16[256,1024]{1,0:T(8,128)(2,1)S(1)}, u32[]{:S(2)}, u32[]{:S(2)}) collective-permute-start(bf16[256,1024]{1,0:T(8,128)(2,1)S(1)} %get-tuple-element.67), channel_id=1, source_target_pairs={{0,3},{1,2},{2,1},{3,0},{4,7},{5,6},{6,5},{7,4},{8,11},{9,10},{10,... | collective-permute-start | bytes 1572872 | tf_op jit(solution)/shard_map/ppermute | solution.py:284
  559.1 34.2 %copy-start.11 = (bf16[256,1024]{1,0:T(8,128)(2,1)S(1)}, bf16[256,1024]{1,0:T(8,128)(2,1)}, u32[]{:S(2)}) copy-start(bf16[256,1024]{1,0:T(8,128)(2,1)} %copy-done.10) | copy-start | bytes 1572868
  589.7 14.9 %collective-permute-start.28 = (bf16[256,1024]{1,0:T(8,128)(2,1)S(1)}, bf16[256,1024]{1,0:T(8,128)(2,1)S(1)}, u32[]{:S(2)}, u32[]{:S(2)}) collective-permute-start(bf16[256,1024]{1,0:T(8,128)(2,1)S(1)} %get-tuple-element.62), channel_id=1, source_target_pairs={{0,1},{1,0},{2,3},{3,2},{4,5},{5,4},{6,7},{7,6},{8,9},{9,8},{10,11... | collective-permute-start | bytes 1572872 | tf_op jit(solution)/shard_map/ppermute | solution.py:284
  591.1 21.2 %collective-permute-start.29 = (bf16[256,1024]{1,0:T(8,128)(2,1)S(1)}, bf16[256,1024]{1,0:T(8,128)(2,1)S(1)}, u32[]{:S(2)}, u32[]{:S(2)}) collective-permute-start(bf16[256,1024]{1,0:T(8,128)(2,1)S(1)} %get-tuple-element.63), channel_id=1, source_target_pairs={{0,2},{1,3},{2,0},{3,1},{4,6},{5,7},{6,4},{7,5},{8,10},{9,11},{10,... | collective-permute-start | bytes 1572872 | tf_op jit(solution)/shard_map/ppermute | solution.py:284
  591.9 20.4 %collective-permute-start.30 = (bf16[256,1024]{1,0:T(8,128)(2,1)S(1)}, bf16[256,1024]{1,0:T(8,128)(2,1)S(1)}, u32[]{:S(2)}, u32[]{:S(2)}) collective-permute-start(bf16[256,1024]{1,0:T(8,128)(2,1)S(1)} %get-tuple-element.64), channel_id=1, source_target_pairs={{0,3},{1,2},{2,1},{3,0},{4,7},{5,6},{6,5},{7,4},{8,11},{9,10},{10,... | collective-permute-start | bytes 1572872 | tf_op jit(solution)/shard_map/ppermute | solution.py:284
  (21 other events, 23.4 us)

commit v10 on v9

--- a/solution.py
+++ b/solution.py
@@ -387,7 +387,7 @@
     in2 = swap(gate2)
     out1 = layer(in1, [gate2[0]])
     done1 = swap(out1)
-    result = put(0, done0, None)
+    result = put(0, [after(done0[0], out1[0]), *done0[1:]], None)
     gate3 = gated(3, back3, [out1[0], in2[1], result])
     in3 = swap(gate3)
     out2 = layer(in2, [gate3[0]])

time: 616 us -> 598 us (0.971)
  waiting for transfers between devices: 281 us -> 260 us
    ppermute x24, waiting for transfers between devices: 56 us -> 34.4 us  [swap(): lax.ppermute(slots[s], 'tensor', [(i, i ^ s) for i in range(n)])]
    unnamed x88 -> x90, local copies, waits for them, and re-layouts: 26 us -> 28.7 us
  transfers between devices with their start and end apart: 41 -> 41, of which waited for: 14 -> 13; matrix products, arithmetic and copies ran while one was open for 3% -> 3% of each run, Pallas kernels for 31% -> 32%
where the time goes in v10:
time: 598 us; the launch traced here: 596 us
  waiting for transfers between devices  260 us (43%)
  Pallas kernels  193 us (32%)
  starting transfers between devices  92.6 us (15%)
  local copies, waits for them, and re-layouts  35 us (6%)
  other arithmetic  15 us (3%)
    pallas_call x4, Pallas kernels, mlp(): pl.pallas_call(kernel, grid_spec=pltpu.PrefetchScalarGridSpec(num_scalar_...  123 us
    ppermute x1, waiting for transfers between devices, gather_along(): got.append(lax.ppermute(got[1], 'seq', [(i, i ^ 2) for i in middle]))  89.8 us
    all_to_all x6, waiting for transfers between devices, exchange(): return lax.all_to_all(x, 'seq', split_axis=0, concat_axis=0, tiled=True)  72.9 us
    ppermute x9, waiting for transfers between devices, flip(): return lax.ppermute(x, axis, [(i, i ^ bit) for i in range(n)])  62.8 us
    all_to_all x6, starting transfers between devices, exchange(): return lax.all_to_all(x, 'seq', split_axis=0, concat_axis=0, tiled=True)  49.9 us
    ppermute x24, waiting for transfers between devices, swap(): lax.ppermute(slots[s], 'tensor', [(i, i ^ s) for i in range(n)])  34.4 us
    ppermute x24, starting transfers between devices, swap(): lax.ppermute(slots[s], 'tensor', [(i, i ^ s) for i in range(n)])  30 us
    unnamed x90, local copies, waits for them, and re-layouts  28.7 us
  transfers between devices with their start and end apart: 41, of which 13 were waited for; matrix products, arithmetic and copies ran while one was open for 3% of the time, Pallas kernels for 32%

profile of v10, /device:TPU:0, one launch (start us, length us, event | category | flops | bytes accessed | tf_op | source)
XLA Modules:
  0.0 596.4 jit_solution(391796405753178770)
XLA Ops:
  1.3 3.1 collective-permute-start
  4.3 17.5 %collective-permute-done = bf16[1,2,192,1024]{3,2,1,0:T(8,128)(2,1)S(1)} collective-permute-done((bf16[1,2,192,1024]{3,2,1,0:T(8,128)(2,1)S(1)}, bf16[1,2,192,1024]{3,2,1,0:T(8,128)(2,1)S(1)}, u32[]{:S(2)}, u32[]{:S(2)}) %collective-permute-start) | collective-permute-done | bytes 786464 | tf_op jit(solution)/shard_map/ppermute | solution.py:299
  23.6 3.4 copy-done
  26.9 7.9 %shard_map.85.refs_0_ = bf16[8,2,32,32,128]{4,3,2,1,0:T(8,128)(2,1)S(1)} custom-call(bf16[256,16384]{1,0:T(8,128)(2,1)S(1)} %copy-done, bf16[512,512]{1,0:T(8,128)(2,1)S(1)} %copy-done.11, f32[256,16384]{1,0:T(8,128)} %rest_3_.7, f32[256,16384]{1,0:T(8,128)} %rest_3_.7, f32[256,16384]{1,0:T(8,128)} %rest_3_.7, f32[256,16384]{1,0:T(8,128)} %rest_3_.7), custom_call_target="tpu_custom_call" | custom-call | flops 2147483648 | bytes 20971520 | tf_op jit(solution)/shard_map/pallas_call | solution.py:40
  34.9 2.0 copy-done.2
  38.0 27.2 %all-to-all-start.1 = ((bf16[8,2,32,32,128]{4,3,2,1,0:T(8,128)(2,1)}), bf16[8,2,32,32,128]{4,3,2,1,0:T(8,128)(2,1)}, u32[]{:S(2)}, u32[]{:S(2)}) async-start(bf16[8,2,32,32,128]{4,3,2,1,0:T(8,128)(2,1)} %shard_map.86), calls=%async_computation.1 | async-start | bytes 8388608 | tf_op jit(solution)/shard_map/all_to_all | solution.py:354
  66.5 3.4 copy-done.1
  69.9 7.9 %shard_map.82.refs_0_ = bf16[8,2,32,32,128]{4,3,2,1,0:T(8,128)(2,1)S(1)} custom-call(bf16[256,16384]{1,0:T(8,128)(2,1)S(1)} %copy-done.1, bf16[512,512]{1,0:T(8,128)(2,1)S(1)} %copy-done.11, f32[256,16384]{1,0:T(8,128)} %rest_3_.7, f32[256,16384]{1,0:T(8,128)} %rest_3_.7, f32[256,16384]{1,0:T(8,128)} %rest_3_.7, f32[256,16384]{1,0:T(8,128)} %rest_3_.7), custom_call_target="tpu_custom_call" | custom-call | flops 2147483648 | bytes 20971520 | tf_op jit(solution)/shard_map/pallas_call | solution.py:40
  77.9 2.0 copy-done.3
  79.9 89.8 %collective-permute-done.2.refs_1_ = bf16[2,2,192,1024]{3,2,1,0:T(8,128)(2,1)} collective-permute-done((bf16[2,2,192,1024]{3,2,1,0:T(8,128)(2,1)S(1)}, bf16[2,2,192,1024]{3,2,1,0:T(8,128)(2,1)}, u32[]{:S(2)}, u32[]{:S(2)}) %collective-permute-start.2) | collective-permute-done | bytes 1572896 | tf_op jit(solution)/shard_map/ppermute | solution.py:309
  169.7 4.5 all-to-all-start
  174.2 2.1 add.7
  176.7 1.5 fusion
  178.2 1.5 collective-permute-start.3
  179.7 1.6 copy.18
  181.3 1.5 collective-permute-start.8
  183.4 31.8 %collective-permute-done.3.rest_0_ = bf16[768,1024]{1,0:T(8,128)(2,1)S(1)} collective-permute-done((bf16[768,1024]{1,0:T(8,128)(2,1)}, bf16[768,1024]{1,0:T(8,128)(2,1)S(1)}, u32[]{:S(2)}, u32[]{:S(2)}) %collective-permute-start.3) | collective-permute-done | bytes 1572896 | tf_op jit(solution)/shard_map/ppermute | solution.py:299
  215.1 1.5 collective-permute-start.5
  216.6 1.5 collective-permute-start.7
  219.3 5.7 shard_map.87
  225.0 43.2 %all-to-all-done.x_ref = bf16[8,2,32,32,128]{4,3,2,1,0:T(8,128)(2,1)} async-done(((bf16[8,2,32,32,128]{4,3,2,1,0:T(8,128)(2,1)}), bf16[8,2,32,32,128]{4,3,2,1,0:T(8,128)(2,1)}, u32[]{:S(2)}, u32[]{:S(2)}) %all-to-all-start) | async-done | bytes 4194336 | tf_op jit(solution)/shard_map/all_to_all | solution.py:354
  268.2 4.3 all-to-all-start.2
  272.6 12.8 %collective-permute-done.5 = bf16[768,1024]{1,0:T(8,128)(2,1)} collective-permute-done((bf16[768,1024]{1,0:T(8,128)(2,1)S(1)}, bf16[768,1024]{1,0:T(8,128)(2,1)}, u32[]{:S(2)}, u32[]{:S(2)}) %collective-permute-start.5) | collective-permute-done | bytes 1572896 | tf_op jit(solution)/shard_map/ppermute | solution.py:299
  285.4 5.9 pad_maximum_fusion.rest_4_.rest_0_
  291.4 5.2 pad_maximum_fusion.1.rest_6_.rest_1_
  297.1 5.6 shard_map.89
  302.7 18.9 %all-to-all-done.2.rest_4_.rest_5_.rest_6_.rest_7_ = bf16[8,32,32,128]{3,2,1,0:T(8,128)(2,1)} async-done(((bf16[8,32,32,128]{3,2,1,0:T(8,128)(2,1)}), bf16[8,32,32,128]{3,2,1,0:T(8,128)(2,1)}, u32[]{:S(2)}, u32[]{:S(2)}) %all-to-all-start.2) | async-done | bytes 2097184 | tf_op jit(solution)/shard_map/all_to_all | solution.py:354
  321.6 4.3 all-to-all-start.3
  329.1 6.7 %shard_map.88 = (bf16[256,1024]{1,0:T(8,128)(2,1)}, bf16[256,1024]{1,0:T(8,128)(2,1)}, bf16[256,1024]{1,0:T(8,128)(2,1)}, bf16[256,1024]{1,0:T(8,128)(2,1)}) custom-call(s32[1]{0:T(128)} %bitcast.me_ref, bf16[256,16384]{1,0:T(8,128)(2,1)} %rest_3_.11, bf16[256,16384]{1,0:T(8,128)(2,1)} %rest_3_.11, bf16[256,16384]{1,0:T(8,128)(2,1)} %rest_3_.11, ...), custom_call_target="tpu_custom_call" | custom-call | flops 8388608 | bytes 12582912 | tf_op jit(solution)/shard_map/pallas_call | solution.py:130
  335.8 1.6 collective-permute-start.11
  337.4 1.5 collective-permute-start.12
  339.4 4.8 shard_map.93.refs_0_
  345.5 5.3 collective-permute-done.11.rest_1_.refs_1_
  350.8 11.9 %collective-permute-done.12.rest_2_.refs_2_ = bf16[256,1024]{1,0:T(8,128)(2,1)S(1)} collective-permute-done((bf16[256,1024]{1,0:T(8,128)(2,1)}, bf16[256,1024]{1,0:T(8,128)(2,1)S(1)}, u32[]{:S(2)}, u32[]{:S(2)}) %collective-permute-start.12) | collective-permute-done | bytes 524320 | tf_op jit(solution)/shard_map/ppermute | solution.py:284
  364.3 10.7 %all-to-all-done.3.rest_4_.rest_5_.rest_6_.rest_7_ = bf16[8,32,32,128]{3,2,1,0:T(8,128)(2,1)} async-done(((bf16[8,32,32,128]{3,2,1,0:T(8,128)(2,1)}), bf16[8,32,32,128]{3,2,1,0:T(8,128)(2,1)}, u32[]{:S(2)}, u32[]{:S(2)}) %all-to-all-start.3) | async-done | bytes 2097184 | tf_op jit(solution)/shard_map/all_to_all | solution.py:354
  375.1 4.5 all-to-all-start.5
  379.6 6.7 %shard_map.90 = (bf16[256,1024]{1,0:T(8,128)(2,1)}, bf16[256,1024]{1,0:T(8,128)(2,1)}, bf16[256,1024]{1,0:T(8,128)(2,1)}, bf16[256,1024]{1,0:T(8,128)(2,1)}) custom-call(s32[1]{0:T(128)} %bitcast.me_ref, bf16[256,16384]{1,0:T(8,128)(2,1)} %rest_3_.11, bf16[256,16384]{1,0:T(8,128)(2,1)} %rest_3_.11, bf16[256,16384]{1,0:T(8,128)(2,1)} %rest_3_.11, ...), custom_call_target="tpu_custom_call" | custom-call | flops 8388608 | bytes 12582912 | tf_op jit(solution)/shard_map/pallas_call | solution.py:130
  386.3 1.6 collective-permute-start.14
  387.8 1.5 collective-permute-start.15
  389.9 5.0 shard_map.84.refs_0_
  395.0 1.4 copy-done.4
  396.4 31.1 %shard_map.91 = (bf16[256,1024]{1,0:T(8,128)(2,1)S(1)}, bf16[256,1024]{1,0:T(8,128)(2,1)}, bf16[256,1024]{1,0:T(8,128)(2,1)S(1)}, bf16[256,1024]{1,0:T(8,128)(2,1)S(1)}) custom-call(s32[1]{0:T(128)} %bitcast.me_ref, bf16[256,1024]{1,0:T(8,128)(2,1)S(1)} %copy-done.39, bf16[256,1024]{1,0:T(8,128)(2,1)S(1)} %copy-done.19, bf16[256,1024]{1,0:T(8,128)(2,1)S(1)} %copy-done.21, ...), custom_call_target="tpu_custom_call" | custom-call | flops 25769803776 | bytes 29360128 | tf_op jit(solution)/shard_map/pallas_call | solution.py:215
  431.1 4.9 all-to-all-start.4
  437.3 1.5 collective-permute-start.19
  439.6 6.7 %shard_map.95 = (bf16[256,1024]{1,0:T(8,128)(2,1)}, bf16[256,1024]{1,0:T(8,128)(2,1)}, bf16[256,1024]{1,0:T(8,128)(2,1)}, bf16[256,1024]{1,0:T(8,128)(2,1)}) custom-call(s32[1]{0:T(128)} %bitcast.me_ref, bf16[256,16384]{1,0:T(8,128)(2,1)} %rest_3_.11, bf16[256,16384]{1,0:T(8,128)(2,1)} %rest_3_.11, bf16[256,16384]{1,0:T(8,128)(2,1)} %rest_3_.11, ...), custom_call_target="tpu_custom_call" | custom-call | flops 8388608 | bytes 12582912 | tf_op jit(solution)/shard_map/pallas_call | solution.py:130
  446.3 1.3 collective-permute-start.17
  447.6 1.5 collective-permute-start.24
  449.2 1.8 collective-permute-done.18.rest_1_
  451.0 2.2 collective-permute-start.25
  454.3 30.2 %shard_map.96 = (bf16[256,1024]{1,0:T(8,128)(2,1)S(1)}, bf16[256,1024]{1,0:T(8,128)(2,1)S(1)}, bf16[256,1024]{1,0:T(8,128)(2,1)S(1)}, bf16[256,1024]{1,0:T(8,128)(2,1)S(1)}) custom-call(s32[1]{0:T(128)} %bitcast.me_ref, bf16[256,1024]{1,0:T(8,128)(2,1)S(1)} %copy-done.29, bf16[256,1024]{1,0:T(8,128)(2,1)S(1)} %copy-done.13, ...), custom_call_target="tpu_custom_call" | custom-call | flops 25769803776 | bytes 29360128 | tf_op jit(solution)/shard_map/pallas_call | solution.py:215
  490.0 1.6 shard_map.98.rest_12_.rest_4_
  492.4 6.7 %shard_map.99 = (bf16[256,1024]{1,0:T(8,128)(2,1)}, bf16[256,1024]{1,0:T(8,128)(2,1)}, bf16[256,1024]{1,0:T(8,128)(2,1)}, bf16[256,1024]{1,0:T(8,128)(2,1)}) custom-call(s32[1]{0:T(128)} %bitcast.me_ref, bf16[256,16384]{1,0:T(8,128)(2,1)} %rest_3_.11, bf16[256,16384]{1,0:T(8,128)(2,1)} %rest_3_.11, bf16[256,16384]{1,0:T(8,128)(2,1)} %rest_3_.11, ...), custom_call_target="tpu_custom_call" | custom-call | flops 8388608 | bytes 12582912 | tf_op jit(solution)/shard_map/pallas_call | solution.py:130
  499.1 1.3 collective-permute-start.21
  500.4 1.5 collective-permute-start.22
  504.7 31.5 %shard_map.100 = (bf16[256,1024]{1,0:T(8,128)(2,1)S(1)}, bf16[256,1024]{1,0:T(8,128)(2,1)S(1)}, bf16[256,1024]{1,0:T(8,128)(2,1)S(1)}, bf16[256,1024]{1,0:T(8,128)(2,1)S(1)}) custom-call(s32[1]{0:T(128)} %bitcast.me_ref, bf16[256,1024]{1,0:T(8,128)(2,1)S(1)} %copy-done.31, bf16[256,1024]{1,0:T(8,128)(2,1)S(1)} %copy-done.25, ...), custom_call_target="tpu_custom_call" | custom-call | flops 25769803776 | bytes 29360128 | tf_op jit(solution)/shard_map/pallas_call | solution.py:215
  536.3 2.3 collective-permute-start.34
  539.9 2.2 collective-permute-start.33
  542.1 30.5 %shard_map.101 = (bf16[256,1024]{1,0:T(8,128)(2,1)S(1)}, bf16[256,1024]{1,0:T(8,128)(2,1)S(1)}, bf16[256,1024]{1,0:T(8,128)(2,1)S(1)}, bf16[256,1024]{1,0:T(8,128)(2,1)S(1)}) custom-call(s32[1]{0:T(128)} %bitcast.me_ref, bf16[256,1024]{1,0:T(8,128)(2,1)S(1)} %copy-done.35, bf16[256,1024]{1,0:T(8,128)(2,1)S(1)} %collective-permute-done.21.rest_1_, ...), custom_call_target="tpu_custom_call" | custom-call | flops 25769803776 | bytes 29360128 | tf_op jit(solution)/shard_map/pallas_call | solution.py:215
  573.9 2.2 collective-permute-start.30
  576.1 1.6 shard_map.102.rest_4_
  577.7 1.6 shard_map.103.rest_4_
  579.3 8.2 %collective-permute-done.28.rest_1_ = bf16[256,1024]{1,0:T(8,128)(2,1)S(1)} collective-permute-done((bf16[256,1024]{1,0:T(8,128)(2,1)S(1)}, bf16[256,1024]{1,0:T(8,128)(2,1)S(1)}, u32[]{:S(2)}, u32[]{:S(2)}) %collective-permute-start.28) | collective-permute-done | bytes 524320 | tf_op jit(solution)/shard_map/ppermute | solution.py:284
  587.5 7.1 %collective-permute-done.29.rest_2_ = bf16[256,1024]{1,0:T(8,128)(2,1)S(1)} collective-permute-done((bf16[256,1024]{1,0:T(8,128)(2,1)S(1)}, bf16[256,1024]{1,0:T(8,128)(2,1)S(1)}, u32[]{:S(2)}, u32[]{:S(2)}) %collective-permute-start.29) | collective-permute-done | bytes 524320 | tf_op jit(solution)/shard_map/ppermute | solution.py:284
  594.6 1.6 shard_map.104
  (143 shorter events, 33.3 us)
Async XLA Ops:
  0.0 23.5 %copy-start.11 = (bf16[512,512]{1,0:T(8,128)(2,1)S(1)}, bf16[512,512]{1,0:T(8,128)(2,1)}, u32[]{:S(2)}) copy-start(bf16[512,512]{1,0:T(8,128)(2,1)} %factor.3) | copy-start | bytes 1572868
  1.3 20.6 %collective-permute-start = (bf16[1,2,192,1024]{3,2,1,0:T(8,128)(2,1)S(1)}, bf16[1,2,192,1024]{3,2,1,0:T(8,128)(2,1)S(1)}, u32[]{:S(2)}, u32[]{:S(2)}) collective-permute-start(bf16[1,2,192,1024]{3,2,1,0:T(8,128)(2,1)S(1)} %maximum_bitcast_fusion), channel_id=1, source_target_pairs={{0,8},{4,12},{8,0},{12,4},{16,24},{20,28},{24,16},{28,20},{1,9},{5... | collective-permute-start | bytes 2359304 | tf_op jit(solution)/shard_map/ppermute | solution.py:299
  22.8 14.1 %collective-permute-start.1 = (bf16[2,2,192,1024]{3,2,1,0:T(8,128)(2,1)S(1)}, bf16[2,2,192,1024]{3,2,1,0:T(8,128)(2,1)S(1)}, u32[]{:S(2)}, u32[]{:S(2)}) collective-permute-start(bf16[2,2,192,1024]{3,2,1,0:T(8,128)(2,1)S(1)} %pad_maximum_fusion.3), channel_id=1, source_target_pairs={{8,16},{12,20},{16,8},{20,12},{9,17},{13,21},{17,9},{21,13},{10,18... | collective-permute-start | bytes 4718600 | tf_op jit(solution)/shard_map/ppermute | solution.py:308
  23.5 3.4 copy-start
  34.9 2.0 copy-start.2
  38.0 27.2 %copy-start.42 = (bf16[2,2,192,1024]{3,2,1,0:T(8,128)(2,1)S(1)}, bf16[2,2,192,1024]{3,2,1,0:T(8,128)(2,1)}, u32[]{:S(2)}) copy-start(bf16[2,2,192,1024]{3,2,1,0:T(8,128)(2,1)} %copy-done.41) | copy-start | bytes 4718596
  38.0 131.6 %all-to-all-start.1 = ((bf16[8,2,32,32,128]{4,3,2,1,0:T(8,128)(2,1)}), bf16[8,2,32,32,128]{4,3,2,1,0:T(8,128)(2,1)}, u32[]{:S(2)}, u32[]{:S(2)}) async-start(bf16[8,2,32,32,128]{4,3,2,1,0:T(8,128)(2,1)} %shard_map.86), calls=%async_computation.1 | async-start | bytes 8388608 | tf_op jit(solution)/shard_map/all_to_all | solution.py:354
  65.2 104.4 %collective-permute-start.2 = (bf16[2,2,192,1024]{3,2,1,0:T(8,128)(2,1)S(1)}, bf16[2,2,192,1024]{3,2,1,0:T(8,128)(2,1)}, u32[]{:S(2)}, u32[]{:S(2)}) collective-permute-start(bf16[2,2,192,1024]{3,2,1,0:T(8,128)(2,1)S(1)} %copy-done.42), channel_id=1, source_target_pairs={{8,0},{12,4},{16,24},{20,28},{9,1},{13,5},{17,25},{21,29},{10,2},{... | collective-permute-start | bytes 4718600 | tf_op jit(solution)/shard_map/ppermute | solution.py:309
  66.5 3.4 copy-start.1
  169.7 98.5 %all-to-all-start = ((bf16[8,2,32,32,128]{4,3,2,1,0:T(8,128)(2,1)}), bf16[8,2,32,32,128]{4,3,2,1,0:T(8,128)(2,1)}, u32[]{:S(2)}, u32[]{:S(2)}) async-start(bf16[8,2,32,32,128]{4,3,2,1,0:T(8,128)(2,1)} %shard_map.83), calls=%async_computation | async-start | bytes 8388608 | tf_op jit(solution)/shard_map/all_to_all | solution.py:354
  174.2 2.2 copy-start.44
  178.2 41.1 %copy-start.10 = (f32[256,256]{1,0:T(8,128)S(1)}, f32[256,256]{1,0:T(8,128)}, u32[]{:S(2)}) copy-start(f32[256,256]{1,0:T(8,128)} %s_ref.7) | copy-start | bytes 786436
  178.2 36.9 %collective-permute-start.3 = (bf16[768,1024]{1,0:T(8,128)(2,1)}, bf16[768,1024]{1,0:T(8,128)(2,1)S(1)}, u32[]{:S(2)}, u32[]{:S(2)}) collective-permute-start(bf16[768,1024]{1,0:T(8,128)(2,1)} %bitcast.6), channel_id=1, source_target_pairs={{0,1},{1,0},{2,3},{3,2},{4,5},{5,4},{6,7},{7,6},{8,9},{9,8},{10,11... | collective-permute-start | bytes 4718600 | tf_op jit(solution)/shard_map/ppermute | solution.py:299
  181.3 37.5 %collective-permute-start.8 = (bf16[1024,768]{1,0:T(8,128)(2,1)}, bf16[1024,768]{1,0:T(8,128)(2,1)S(1)}, u32[]{:S(2)}, u32[]{:S(2)}) collective-permute-start(bf16[1024,768]{1,0:T(8,128)(2,1)} %bitcast.23), channel_id=1, source_target_pairs={{0,2},{1,3},{2,0},{3,1},{4,6},{5,7},{6,4},{7,5},{8,10},{9,11},{10,... | collective-permute-start | bytes 4718600 | tf_op jit(solution)/shard_map/ppermute | solution.py:299
  182.8 89.7 %collective-permute-start.4 = (bf16[768,1024]{1,0:T(8,128)(2,1)}, bf16[768,1024]{1,0:T(8,128)(2,1)}, u32[]{:S(2)}, u32[]{:S(2)}) collective-permute-start(bf16[768,1024]{1,0:T(8,128)(2,1)} %bitcast.6), channel_id=1, source_target_pairs={{0,2},{1,3},{2,0},{3,1},{4,6},{5,7},{6,4},{7,5},{8,10},{9,11},{10,... | collective-permute-start | bytes 4718600 | tf_op jit(solution)/shard_map/ppermute | solution.py:299
  215.1 70.3 %collective-permute-start.5 = (bf16[768,1024]{1,0:T(8,128)(2,1)S(1)}, bf16[768,1024]{1,0:T(8,128)(2,1)}, u32[]{:S(2)}, u32[]{:S(2)}) collective-permute-start(bf16[768,1024]{1,0:T(8,128)(2,1)S(1)} %collective-permute-done.3.rest_0_), channel_id=1, source_target_pairs={{0,2},{1,3},{2,0},{3,1},{4,6},{5,7},{6,4},{7,5},{8,10},{9,11},{10,... | collective-permute-start | bytes 4718600 | tf_op jit(solution)/shard_map/ppermute | solution.py:299
  216.6 74.7 %collective-permute-start.7 = (bf16[1024,768]{1,0:T(8,128)(2,1)}, bf16[1024,768]{1,0:T(8,128)(2,1)}, u32[]{:S(2)}, u32[]{:S(2)}) collective-permute-start(bf16[1024,768]{1,0:T(8,128)(2,1)} %bitcast.24), channel_id=1, source_target_pairs={{0,1},{1,0},{2,3},{3,2},{4,5},{5,4},{6,7},{7,6},{8,9},{9,8},{10,11... | collective-permute-start | bytes 4718600 | tf_op jit(solution)/shard_map/ppermute | solution.py:299
  218.8 72.6 %collective-permute-start.9 = (bf16[1024,768]{1,0:T(8,128)(2,1)S(1)}, bf16[1024,768]{1,0:T(8,128)(2,1)}, u32[]{:S(2)}, u32[]{:S(2)}) collective-permute-start(bf16[1024,768]{1,0:T(8,128)(2,1)S(1)} %collective-permute-done.8.rest_1_), channel_id=1, source_target_pairs={{0,1},{1,0},{2,3},{3,2},{4,5},{5,4},{6,7},{7,6},{8,9},{9,8},{10,11... | collective-permute-start | bytes 4718600 | tf_op jit(solution)/shard_map/ppermute | solution.py:299
  268.2 53.4 %all-to-all-start.2 = ((bf16[8,32,32,128]{3,2,1,0:T(8,128)(2,1)}), bf16[8,32,32,128]{3,2,1,0:T(8,128)(2,1)}, u32[]{:S(2)}, u32[]{:S(2)}) async-start(bf16[8,32,32,128]{3,2,1,0:T(8,128)(2,1)} %shard_map.87), calls=%async_computation.2 | async-start | bytes 4194304 | tf_op jit(solution)/shard_map/all_to_all | solution.py:354
  285.4 5.9 copy-start.40
  291.3 98.6 %collective-permute-start.6 = (bf16[4,768,1024]{2,1,0:T(8,128)(2,1)}, bf16[4,768,1024]{2,1,0:T(8,128)(2,1)}, u32[]{:S(2)}, u32[]{:S(2)}) collective-permute-start(bf16[4,768,1024]{2,1,0:T(8,128)(2,1)} %pad_maximum_fusion.rest_4_.rest_0_), channel_id=1, source_target_pairs={{0,4},{4,0},{8,12},{12,8},{16,20},{20,16},{24,28},{28,24},{1,5},{5... | collective-permute-start | bytes 18874376 | tf_op jit(solution)/shard_map/ppermute | solution.py:299
  296.6 93.3 %collective-permute-start.10 = (bf16[4,1024,768]{2,1,0:T(8,128)(2,1)}, bf16[4,1024,768]{2,1,0:T(8,128)(2,1)}, u32[]{:S(2)}, u32[]{:S(2)}) collective-permute-start(bf16[4,1024,768]{2,1,0:T(8,128)(2,1)} %pad_maximum_fusion.1.rest_6_.rest_1_), channel_id=1, source_target_pairs={{0,4},{4,0},{8,12},{12,8},{16,20},{20,16},{24,28},{28,24},{1,5},{5... | collective-permute-start | bytes 18874376 | tf_op jit(solution)/shard_map/ppermute | solution.py:299
  321.6 53.4 %all-to-all-start.3 = ((bf16[8,32,32,128]{3,2,1,0:T(8,128)(2,1)}), bf16[8,32,32,128]{3,2,1,0:T(8,128)(2,1)}, u32[]{:S(2)}, u32[]{:S(2)}) async-start(bf16[8,32,32,128]{3,2,1,0:T(8,128)(2,1)} %shard_map.89), calls=%async_computation.3 | async-start | bytes 4194304 | tf_op jit(solution)/shard_map/all_to_all | solution.py:354
  335.8 15.0 %collective-permute-start.11 = (bf16[256,1024]{1,0:T(8,128)(2,1)}, bf16[256,1024]{1,0:T(8,128)(2,1)S(1)}, u32[]{:S(2)}, u32[]{:S(2)}) collective-permute-start(bf16[256,1024]{1,0:T(8,128)(2,1)} %get-tuple-element.38), channel_id=1, source_target_pairs={{0,1},{1,0},{2,3},{3,2},{4,5},{5,4},{6,7},{7,6},{8,9},{9,8},{10,11... | collective-permute-start | bytes 1572872 | tf_op jit(solution)/shard_map/ppermute | solution.py:284
  337.4 25.3 %collective-permute-start.12 = (bf16[256,1024]{1,0:T(8,128)(2,1)}, bf16[256,1024]{1,0:T(8,128)(2,1)S(1)}, u32[]{:S(2)}, u32[]{:S(2)}) collective-permute-start(bf16[256,1024]{1,0:T(8,128)(2,1)} %get-tuple-element.39), channel_id=1, source_target_pairs={{0,2},{1,3},{2,0},{3,1},{4,6},{5,7},{6,4},{7,5},{8,10},{9,11},{10,... | collective-permute-start | bytes 1572872 | tf_op jit(solution)/shard_map/ppermute | solution.py:284
  338.9 23.8 %collective-permute-start.13 = (bf16[256,1024]{1,0:T(8,128)(2,1)}, bf16[256,1024]{1,0:T(8,128)(2,1)S(1)}, u32[]{:S(2)}, u32[]{:S(2)}) collective-permute-start(bf16[256,1024]{1,0:T(8,128)(2,1)} %get-tuple-element.40), channel_id=1, source_target_pairs={{0,3},{1,2},{2,1},{3,0},{4,7},{5,6},{6,5},{7,4},{8,11},{9,10},{10,... | collective-permute-start | bytes 1572872 | tf_op jit(solution)/shard_map/ppermute | solution.py:284
  350.8 11.9 %copy-start.18 = (bf16[256,1024]{1,0:T(8,128)(2,1)}, bf16[256,1024]{1,0:T(8,128)(2,1)S(1)}, u32[]{:S(2)}) copy-start(bf16[256,1024]{1,0:T(8,128)(2,1)S(1)} %collective-permute-done.11.rest_1_.refs_1_) | copy-start | bytes 1572868
  375.1 56.0 %all-to-all-start.5 = ((bf16[8,32,32,128]{3,2,1,0:T(8,128)(2,1)}), bf16[8,32,32,128]{3,2,1,0:T(8,128)(2,1)}, u32[]{:S(2)}, u32[]{:S(2)}) async-start(bf16[8,32,32,128]{3,2,1,0:T(8,128)(2,1)} %shard_map.94), calls=%async_computation.5 | async-start | bytes 4194304 | tf_op jit(solution)/shard_map/all_to_all | solution.py:354
  386.3 43.7 %collective-permute-start.14 = (bf16[256,1024]{1,0:T(8,128)(2,1)}, bf16[256,1024]{1,0:T(8,128)(2,1)S(1)}, u32[]{:S(2)}, u32[]{:S(2)}) collective-permute-start(bf16[256,1024]{1,0:T(8,128)(2,1)} %get-tuple-element.43), channel_id=1, source_target_pairs={{0,1},{1,0},{2,3},{3,2},{4,5},{5,4},{6,7},{7,6},{8,9},{9,8},{10,11... | collective-permute-start | bytes 1572872 | tf_op jit(solution)/shard_map/ppermute | solution.py:284
  387.8 42.1 %collective-permute-start.15 = (bf16[256,1024]{1,0:T(8,128)(2,1)}, bf16[256,1024]{1,0:T(8,128)(2,1)S(1)}, u32[]{:S(2)}, u32[]{:S(2)}) collective-permute-start(bf16[256,1024]{1,0:T(8,128)(2,1)} %get-tuple-element.44), channel_id=1, source_target_pairs={{0,2},{1,3},{2,0},{3,1},{4,6},{5,7},{6,4},{7,5},{8,10},{9,11},{10,... | collective-permute-start | bytes 1572872 | tf_op jit(solution)/shard_map/ppermute | solution.py:284
  389.3 7.0 %copy-start.19 = (bf16[256,1024]{1,0:T(8,128)(2,1)S(1)}, bf16[256,1024]{1,0:T(8,128)(2,1)}, u32[]{:S(2)}) copy-start(bf16[256,1024]{1,0:T(8,128)(2,1)} %copy-done.18) | copy-start | bytes 1572868
  389.3 7.0 %copy-start.21 = (bf16[256,1024]{1,0:T(8,128)(2,1)S(1)}, bf16[256,1024]{1,0:T(8,128)(2,1)}, u32[]{:S(2)}) copy-start(bf16[256,1024]{1,0:T(8,128)(2,1)} %copy-done.20) | copy-start | bytes 1572868
  389.3 7.0 %copy-start.23 = (bf16[256,1024]{1,0:T(8,128)(2,1)S(1)}, bf16[256,1024]{1,0:T(8,128)(2,1)}, u32[]{:S(2)}) copy-start(bf16[256,1024]{1,0:T(8,128)(2,1)} %copy-done.22) | copy-start | bytes 1572868
  389.3 7.0 %copy-start.28 = (bf16[256,1024]{1,0:T(8,128)(2,1)S(1)}, bf16[256,1024]{1,0:T(8,128)(2,1)}, u32[]{:S(2)}) copy-start(bf16[256,1024]{1,0:T(8,128)(2,1)} %get-tuple-element.41.rest_8_.rest_0_) | copy-start | bytes 1572868
  389.3 7.0 %copy-start.39 = (bf16[256,1024]{1,0:T(8,128)(2,1)S(1)}, bf16[256,1024]{1,0:T(8,128)(2,1)}, u32[]{:S(2)}) copy-start(bf16[256,1024]{1,0:T(8,128)(2,1)} %get-tuple-element.37.rest_0_) | copy-start | bytes 1572868
  389.4 40.6 %collective-permute-start.16 = (bf16[256,1024]{1,0:T(8,128)(2,1)}, bf16[256,1024]{1,0:T(8,128)(2,1)S(1)}, u32[]{:S(2)}, u32[]{:S(2)}) collective-permute-start(bf16[256,1024]{1,0:T(8,128)(2,1)} %get-tuple-element.45), channel_id=1, source_target_pairs={{0,3},{1,2},{2,1},{3,0},{4,7},{5,6},{6,5},{7,4},{8,11},{9,10},{10,... | collective-permute-start | bytes 1572872 | tf_op jit(solution)/shard_map/ppermute | solution.py:284
  431.1 6.2 %copy-start.38 = (bf16[256,1024]{1,0:T(8,128)(2,1)S(1)}, bf16[256,1024]{1,0:T(8,128)(2,1)}, u32[]{:S(2)}) copy-start(bf16[256,1024]{1,0:T(8,128)(2,1)} %copy-done.37) | copy-start | bytes 1572868
  431.1 7.8 %copy-start.34 = (bf16[256,1024]{1,0:T(8,128)(2,1)S(1)}, bf16[256,1024]{1,0:T(8,128)(2,1)}, u32[]{:S(2)}) copy-start(bf16[256,1024]{1,0:T(8,128)(2,1)} %copy-done.33) | copy-start | bytes 1572868
  431.1 60.5 %all-to-all-start.4 = ((bf16[8,32,32,128]{3,2,1,0:T(8,128)(2,1)}), bf16[8,32,32,128]{3,2,1,0:T(8,128)(2,1)}, u32[]{:S(2)}, u32[]{:S(2)}) async-start(bf16[8,32,32,128]{3,2,1,0:T(8,128)(2,1)} %shard_map.92), calls=%async_computation.4 | async-start | bytes 4194304 | tf_op jit(solution)/shard_map/all_to_all | solution.py:354
  436.1 14.9 %collective-permute-start.18 = (bf16[256,1024]{1,0:T(8,128)(2,1)}, bf16[256,1024]{1,0:T(8,128)(2,1)S(1)}, u32[]{:S(2)}, u32[]{:S(2)}) collective-permute-start(bf16[256,1024]{1,0:T(8,128)(2,1)} %get-tuple-element.49), channel_id=1, source_target_pairs={{0,1},{1,0},{2,3},{3,2},{4,5},{5,4},{6,7},{7,6},{8,9},{9,8},{10,11... | collective-permute-start | bytes 1572872 | tf_op jit(solution)/shard_map/ppermute | solution.py:284
  437.3 50.3 %collective-permute-start.19 = (bf16[256,1024]{1,0:T(8,128)(2,1)S(1)}, bf16[256,1024]{1,0:T(8,128)(2,1)S(1)}, u32[]{:S(2)}, u32[]{:S(2)}) collective-permute-start(bf16[256,1024]{1,0:T(8,128)(2,1)S(1)} %copy-done.38), channel_id=1, source_target_pairs={{0,2},{1,3},{2,0},{3,1},{4,6},{5,7},{6,4},{7,5},{8,10},{9,11},{10,... | collective-permute-start | bytes 1572872 | tf_op jit(solution)/shard_map/ppermute | solution.py:284
  438.9 14.4 %copy-start.13 = (bf16[256,1024]{1,0:T(8,128)(2,1)S(1)}, bf16[256,1024]{1,0:T(8,128)(2,1)}, u32[]{:S(2)}) copy-start(bf16[256,1024]{1,0:T(8,128)(2,1)} %copy-done.12) | copy-start | bytes 1572868
  438.9 14.4 %copy-start.15 = (bf16[256,1024]{1,0:T(8,128)(2,1)S(1)}, bf16[256,1024]{1,0:T(8,128)(2,1)}, u32[]{:S(2)}) copy-start(bf16[256,1024]{1,0:T(8,128)(2,1)} %copy-done.14) | copy-start | bytes 1572868
  438.9 14.4 %copy-start.17 = (bf16[256,1024]{1,0:T(8,128)(2,1)S(1)}, bf16[256,1024]{1,0:T(8,128)(2,1)}, u32[]{:S(2)}) copy-start(bf16[256,1024]{1,0:T(8,128)(2,1)} %copy-done.16) | copy-start | bytes 1572868
  438.9 14.4 %copy-start.29 = (bf16[256,1024]{1,0:T(8,128)(2,1)S(1)}, bf16[256,1024]{1,0:T(8,128)(2,1)}, u32[]{:S(2)}) copy-start(bf16[256,1024]{1,0:T(8,128)(2,1)} %get-tuple-element.41.rest_8_.rest_0_) | copy-start | bytes 1572868
  438.9 49.3 %collective-permute-start.20 = (bf16[256,1024]{1,0:T(8,128)(2,1)S(1)}, bf16[256,1024]{1,0:T(8,128)(2,1)S(1)}, u32[]{:S(2)}, u32[]{:S(2)}) collective-permute-start(bf16[256,1024]{1,0:T(8,128)(2,1)S(1)} %copy-done.34), channel_id=1, source_target_pairs={{0,3},{1,2},{2,1},{3,0},{4,7},{5,6},{6,5},{7,4},{8,11},{9,10},{10,... | collective-permute-start | bytes 1572872 | tf_op jit(solution)/shard_map/ppermute | solution.py:284
  446.3 45.3 %collective-permute-start.17 = (bf16[256,1024]{1,0:T(8,128)(2,1)}, bf16[256,1024]{1,0:T(8,128)(2,1)S(1)}, u32[]{:S(2)}, u32[]{:S(2)}) collective-permute-start(bf16[256,1024]{1,0:T(8,128)(2,1)} %get-tuple-element.48), channel_id=1, source_target_pairs={{0,1},{1,0},{2,3},{3,2},{4,5},{5,4},{6,7},{7,6},{8,9},{9,8},{10,11... | collective-permute-start | bytes 1572872 | tf_op jit(solution)/shard_map/ppermute | solution.py:284
  447.6 52.8 %collective-permute-start.24 = (bf16[256,1024]{1,0:T(8,128)(2,1)}, bf16[256,1024]{1,0:T(8,128)(2,1)}, u32[]{:S(2)}, u32[]{:S(2)}) collective-permute-start(bf16[256,1024]{1,0:T(8,128)(2,1)} %get-tuple-element.56), channel_id=1, source_target_pairs={{0,2},{1,3},{2,0},{3,1},{4,6},{5,7},{6,4},{7,5},{8,10},{9,11},{10,... | collective-permute-start | bytes 1572872 | tf_op jit(solution)/shard_map/ppermute | solution.py:284
  451.0 51.0 %collective-permute-start.25 = (bf16[256,1024]{1,0:T(8,128)(2,1)}, bf16[256,1024]{1,0:T(8,128)(2,1)}, u32[]{:S(2)}, u32[]{:S(2)}) collective-permute-start(bf16[256,1024]{1,0:T(8,128)(2,1)} %get-tuple-element.57), channel_id=1, source_target_pairs={{0,3},{1,2},{2,1},{3,0},{4,7},{5,6},{6,5},{7,4},{8,11},{9,10},{10,... | collective-permute-start | bytes 1572872 | tf_op jit(solution)/shard_map/ppermute | solution.py:284
  487.7 48.6 %collective-permute-start.26 = (bf16[256,1024]{1,0:T(8,128)(2,1)}, bf16[256,1024]{1,0:T(8,128)(2,1)S(1)}, u32[]{:S(2)}, u32[]{:S(2)}) collective-permute-start(bf16[256,1024]{1,0:T(8,128)(2,1)} %copy-done.36), channel_id=1, source_target_pairs={{0,1},{1,0},{2,3},{3,2},{4,5},{5,4},{6,7},{7,6},{8,9},{9,8},{10,11... | collective-permute-start | bytes 1572872 | tf_op jit(solution)/shard_map/ppermute | solution.py:284
  488.2 50.4 %collective-permute-start.27 = (bf16[256,1024]{1,0:T(8,128)(2,1)}, bf16[256,1024]{1,0:T(8,128)(2,1)S(1)}, u32[]{:S(2)}, u32[]{:S(2)}) collective-permute-start(bf16[256,1024]{1,0:T(8,128)(2,1)} %copy-done.32), channel_id=1, source_target_pairs={{0,2},{1,3},{2,0},{3,1},{4,6},{5,7},{6,4},{7,5},{8,10},{9,11},{10,... | collective-permute-start | bytes 1572872 | tf_op jit(solution)/shard_map/ppermute | solution.py:284
  491.6 11.1 %copy-start.31 = (bf16[256,1024]{1,0:T(8,128)(2,1)S(1)}, bf16[256,1024]{1,0:T(8,128)(2,1)}, u32[]{:S(2)}) copy-start(bf16[256,1024]{1,0:T(8,128)(2,1)} %get-tuple-element.46.rest_8_.rest_0_) | copy-start | bytes 1572868
  499.1 40.0 %collective-permute-start.21 = (bf16[256,1024]{1,0:T(8,128)(2,1)}, bf16[256,1024]{1,0:T(8,128)(2,1)S(1)}, u32[]{:S(2)}, u32[]{:S(2)}) collective-permute-start(bf16[256,1024]{1,0:T(8,128)(2,1)} %get-tuple-element.53), channel_id=1, source_target_pairs={{0,1},{1,0},{2,3},{3,2},{4,5},{5,4},{6,7},{7,6},{8,9},{9,8},{10,11... | collective-permute-start | bytes 1572872 | tf_op jit(solution)/shard_map/ppermute | solution.py:284
  500.4 39.4 %collective-permute-start.22 = (bf16[256,1024]{1,0:T(8,128)(2,1)}, bf16[256,1024]{1,0:T(8,128)(2,1)S(1)}, u32[]{:S(2)}, u32[]{:S(2)}) collective-permute-start(bf16[256,1024]{1,0:T(8,128)(2,1)} %get-tuple-element.54), channel_id=1, source_target_pairs={{0,2},{1,3},{2,0},{3,1},{4,6},{5,7},{6,4},{7,5},{8,10},{9,11},{10,... | collective-permute-start | bytes 1572872 | tf_op jit(solution)/shard_map/ppermute | solution.py:284
  502.0 40.1 %collective-permute-start.23 = (bf16[256,1024]{1,0:T(8,128)(2,1)}, bf16[256,1024]{1,0:T(8,128)(2,1)S(1)}, u32[]{:S(2)}, u32[]{:S(2)}) collective-permute-start(bf16[256,1024]{1,0:T(8,128)(2,1)} %get-tuple-element.55), channel_id=1, source_target_pairs={{0,3},{1,2},{2,1},{3,0},{4,7},{5,6},{6,5},{7,4},{8,11},{9,10},{10,... | collective-permute-start | bytes 1572872 | tf_op jit(solution)/shard_map/ppermute | solution.py:284
  504.7 31.5 %copy-start.27 = (bf16[256,1024]{1,0:T(8,128)(2,1)S(1)}, bf16[256,1024]{1,0:T(8,128)(2,1)}, u32[]{:S(2)}) copy-start(bf16[256,1024]{1,0:T(8,128)(2,1)} %copy-done.26) | copy-start | bytes 1572868
  536.3 36.9 %collective-permute-start.34 = (bf16[256,1024]{1,0:T(8,128)(2,1)S(1)}, bf16[256,1024]{1,0:T(8,128)(2,1)S(1)}, u32[]{:S(2)}, u32[]{:S(2)}) collective-permute-start(bf16[256,1024]{1,0:T(8,128)(2,1)S(1)} %copy-done.27), channel_id=1, source_target_pairs={{0,3},{1,2},{2,1},{3,0},{4,7},{5,6},{6,5},{7,4},{8,11},{9,10},{10,... | collective-permute-start | bytes 1572872 | tf_op jit(solution)/shard_map/ppermute | solution.py:284
  538.6 35.3 %collective-permute-start.31 = (bf16[256,1024]{1,0:T(8,128)(2,1)S(1)}, bf16[256,1024]{1,0:T(8,128)(2,1)S(1)}, u32[]{:S(2)}, u32[]{:S(2)}) collective-permute-start(bf16[256,1024]{1,0:T(8,128)(2,1)S(1)} %get-tuple-element.65), channel_id=1, source_target_pairs={{0,1},{1,0},{2,3},{3,2},{4,5},{5,4},{6,7},{7,6},{8,9},{9,8},{10,11... | collective-permute-start | bytes 1572872 | tf_op jit(solution)/shard_map/ppermute | solution.py:284
  539.1 38.6 %collective-permute-start.32 = (bf16[256,1024]{1,0:T(8,128)(2,1)S(1)}, bf16[256,1024]{1,0:T(8,128)(2,1)S(1)}, u32[]{:S(2)}, u32[]{:S(2)}) collective-permute-start(bf16[256,1024]{1,0:T(8,128)(2,1)S(1)} %get-tuple-element.66), channel_id=1, source_target_pairs={{0,2},{1,3},{2,0},{3,1},{4,6},{5,7},{6,4},{7,5},{8,10},{9,11},{10,... | collective-permute-start | bytes 1572872 | tf_op jit(solution)/shard_map/ppermute | solution.py:284
  539.9 37.9 %collective-permute-start.33 = (bf16[256,1024]{1,0:T(8,128)(2,1)S(1)}, bf16[256,1024]{1,0:T(8,128)(2,1)S(1)}, u32[]{:S(2)}, u32[]{:S(2)}) collective-permute-start(bf16[256,1024]{1,0:T(8,128)(2,1)S(1)} %get-tuple-element.67), channel_id=1, source_target_pairs={{0,3},{1,2},{2,1},{3,0},{4,7},{5,6},{6,5},{7,4},{8,11},{9,10},{10,... | collective-permute-start | bytes 1572872 | tf_op jit(solution)/shard_map/ppermute | solution.py:284
  542.1 34.0 %copy-start.9 = (bf16[256,1024]{1,0:T(8,128)(2,1)S(1)}, bf16[256,1024]{1,0:T(8,128)(2,1)}, u32[]{:S(2)}) copy-start(bf16[256,1024]{1,0:T(8,128)(2,1)} %copy-done.8) | copy-start | bytes 1572868
  572.6 14.9 %collective-permute-start.28 = (bf16[256,1024]{1,0:T(8,128)(2,1)S(1)}, bf16[256,1024]{1,0:T(8,128)(2,1)S(1)}, u32[]{:S(2)}, u32[]{:S(2)}) collective-permute-start(bf16[256,1024]{1,0:T(8,128)(2,1)S(1)} %get-tuple-element.62), channel_id=1, source_target_pairs={{0,1},{1,0},{2,3},{3,2},{4,5},{5,4},{6,7},{7,6},{8,9},{9,8},{10,11... | collective-permute-start | bytes 1572872 | tf_op jit(solution)/shard_map/ppermute | solution.py:284
  573.2 21.4 %collective-permute-start.29 = (bf16[256,1024]{1,0:T(8,128)(2,1)S(1)}, bf16[256,1024]{1,0:T(8,128)(2,1)S(1)}, u32[]{:S(2)}, u32[]{:S(2)}) collective-permute-start(bf16[256,1024]{1,0:T(8,128)(2,1)S(1)} %get-tuple-element.63), channel_id=1, source_target_pairs={{0,2},{1,3},{2,0},{3,1},{4,6},{5,7},{6,4},{7,5},{8,10},{9,11},{10,... | collective-permute-start | bytes 1572872 | tf_op jit(solution)/shard_map/ppermute | solution.py:284
  573.9 20.7 %collective-permute-start.30 = (bf16[256,1024]{1,0:T(8,128)(2,1)S(1)}, bf16[256,1024]{1,0:T(8,128)(2,1)S(1)}, u32[]{:S(2)}, u32[]{:S(2)}) collective-permute-start(bf16[256,1024]{1,0:T(8,128)(2,1)S(1)} %get-tuple-element.64), channel_id=1, source_target_pairs={{0,3},{1,2},{2,1},{3,0},{4,7},{5,6},{6,5},{7,4},{8,11},{9,10},{10,... | collective-permute-start | bytes 1572872 | tf_op jit(solution)/shard_map/ppermute | solution.py:284
  (22 other events, 21.9 us)

commit v11 on v10

--- a/solution.py
+++ b/solution.py
@@ -153,7 +153,7 @@
     c, tokens = slots[0].shape
     half, hb, full = halves_in[0].shape
     n = 2 * half
-    tile = min(256, tokens)
+    tile = min(512, tokens)
 
     def kernel(me_ref, *rest):
         xs, w1s, w2s = rest[:nt], rest[nt : nt + 2], rest[nt + 2 : nt + 4]

time: 598 us -> 598 us (level)
  no operation moved by 1% of the time
where the time goes in v11:
time: 598 us; the launch traced here: 597 us
  waiting for transfers between devices  260 us (43%)
  Pallas kernels  193 us (32%)
  starting transfers between devices  92.6 us (15%)
  local copies, waits for them, and re-layouts  35 us (6%)
  other arithmetic  15 us (3%)
    pallas_call x4, Pallas kernels, mlp(): pl.pallas_call(kernel, grid_spec=pltpu.PrefetchScalarGridSpec(num_scalar_...  123 us
    ppermute x1, waiting for transfers between devices, gather_along(): got.append(lax.ppermute(got[1], 'seq', [(i, i ^ 2) for i in middle]))  89.8 us
    all_to_all x6, waiting for transfers between devices, exchange(): return lax.all_to_all(x, 'seq', split_axis=0, concat_axis=0, tiled=True)  72.9 us
    ppermute x9, waiting for transfers between devices, flip(): return lax.ppermute(x, axis, [(i, i ^ bit) for i in range(n)])  62.8 us
    all_to_all x6, starting transfers between devices, exchange(): return lax.all_to_all(x, 'seq', split_axis=0, concat_axis=0, tiled=True)  49.9 us
    ppermute x24, waiting for transfers between devices, swap(): lax.ppermute(slots[s], 'tensor', [(i, i ^ s) for i in range(n)])  34.4 us
    ppermute x24, starting transfers between devices, swap(): lax.ppermute(slots[s], 'tensor', [(i, i ^ s) for i in range(n)])  30 us
    unnamed x90, local copies, waits for them, and re-layouts  28.7 us
  transfers between devices with their start and end apart: 41, of which 13 were waited for; matrix products, arithmetic and copies ran while one was open for 3% of the time, Pallas kernels for 32%

profile of v11, /device:TPU:0, one launch (start us, length us, event | category | flops | bytes accessed | tf_op | source)
XLA Modules:
  0.0 596.5 jit_solution(10124970344748735642)
XLA Ops:
  1.3 3.1 collective-permute-start
  4.3 17.5 %collective-permute-done = bf16[1,2,192,1024]{3,2,1,0:T(8,128)(2,1)S(1)} collective-permute-done((bf16[1,2,192,1024]{3,2,1,0:T(8,128)(2,1)S(1)}, bf16[1,2,192,1024]{3,2,1,0:T(8,128)(2,1)S(1)}, u32[]{:S(2)}, u32[]{:S(2)}) %collective-permute-start) | collective-permute-done | bytes 786464 | tf_op jit(solution)/shard_map/ppermute | solution.py:299
  23.6 3.4 copy-done
  26.9 7.9 %shard_map.85.refs_0_ = bf16[8,2,32,32,128]{4,3,2,1,0:T(8,128)(2,1)S(1)} custom-call(bf16[256,16384]{1,0:T(8,128)(2,1)S(1)} %copy-done, bf16[512,512]{1,0:T(8,128)(2,1)S(1)} %copy-done.11, f32[256,16384]{1,0:T(8,128)} %rest_3_.7, f32[256,16384]{1,0:T(8,128)} %rest_3_.7, f32[256,16384]{1,0:T(8,128)} %rest_3_.7, f32[256,16384]{1,0:T(8,128)} %rest_3_.7), custom_call_target="tpu_custom_call" | custom-call | flops 2147483648 | bytes 20971520 | tf_op jit(solution)/shard_map/pallas_call | solution.py:40
  34.9 2.0 copy-done.2
  38.0 27.2 %all-to-all-start.1 = ((bf16[8,2,32,32,128]{4,3,2,1,0:T(8,128)(2,1)}), bf16[8,2,32,32,128]{4,3,2,1,0:T(8,128)(2,1)}, u32[]{:S(2)}, u32[]{:S(2)}) async-start(bf16[8,2,32,32,128]{4,3,2,1,0:T(8,128)(2,1)} %shard_map.86), calls=%async_computation.1 | async-start | bytes 8388608 | tf_op jit(solution)/shard_map/all_to_all | solution.py:354
  66.5 3.4 copy-done.1
  69.9 7.9 %shard_map.82.refs_0_ = bf16[8,2,32,32,128]{4,3,2,1,0:T(8,128)(2,1)S(1)} custom-call(bf16[256,16384]{1,0:T(8,128)(2,1)S(1)} %copy-done.1, bf16[512,512]{1,0:T(8,128)(2,1)S(1)} %copy-done.11, f32[256,16384]{1,0:T(8,128)} %rest_3_.7, f32[256,16384]{1,0:T(8,128)} %rest_3_.7, f32[256,16384]{1,0:T(8,128)} %rest_3_.7, f32[256,16384]{1,0:T(8,128)} %rest_3_.7), custom_call_target="tpu_custom_call" | custom-call | flops 2147483648 | bytes 20971520 | tf_op jit(solution)/shard_map/pallas_call | solution.py:40
  77.9 2.0 copy-done.3
  79.9 89.8 %collective-permute-done.2.refs_1_ = bf16[2,2,192,1024]{3,2,1,0:T(8,128)(2,1)} collective-permute-done((bf16[2,2,192,1024]{3,2,1,0:T(8,128)(2,1)S(1)}, bf16[2,2,192,1024]{3,2,1,0:T(8,128)(2,1)}, u32[]{:S(2)}, u32[]{:S(2)}) %collective-permute-start.2) | collective-permute-done | bytes 1572896 | tf_op jit(solution)/shard_map/ppermute | solution.py:309
  169.7 4.5 all-to-all-start
  174.2 2.1 add.7
  176.7 1.5 fusion
  178.2 1.5 collective-permute-start.3
  179.7 1.6 copy.18
  181.3 1.5 collective-permute-start.8
  183.4 31.8 %collective-permute-done.3.rest_0_ = bf16[768,1024]{1,0:T(8,128)(2,1)S(1)} collective-permute-done((bf16[768,1024]{1,0:T(8,128)(2,1)}, bf16[768,1024]{1,0:T(8,128)(2,1)S(1)}, u32[]{:S(2)}, u32[]{:S(2)}) %collective-permute-start.3) | collective-permute-done | bytes 1572896 | tf_op jit(solution)/shard_map/ppermute | solution.py:299
  215.1 1.5 collective-permute-start.5
  216.6 1.5 collective-permute-start.7
  219.3 5.7 shard_map.87
  225.0 43.2 %all-to-all-done.x_ref = bf16[8,2,32,32,128]{4,3,2,1,0:T(8,128)(2,1)} async-done(((bf16[8,2,32,32,128]{4,3,2,1,0:T(8,128)(2,1)}), bf16[8,2,32,32,128]{4,3,2,1,0:T(8,128)(2,1)}, u32[]{:S(2)}, u32[]{:S(2)}) %all-to-all-start) | async-done | bytes 4194336 | tf_op jit(solution)/shard_map/all_to_all | solution.py:354
  268.2 4.3 all-to-all-start.2
  272.6 12.8 %collective-permute-done.5 = bf16[768,1024]{1,0:T(8,128)(2,1)} collective-permute-done((bf16[768,1024]{1,0:T(8,128)(2,1)S(1)}, bf16[768,1024]{1,0:T(8,128)(2,1)}, u32[]{:S(2)}, u32[]{:S(2)}) %collective-permute-start.5) | collective-permute-done | bytes 1572896 | tf_op jit(solution)/shard_map/ppermute | solution.py:299
  285.4 5.9 pad_maximum_fusion.rest_4_.rest_0_
  291.4 5.2 pad_maximum_fusion.1.rest_6_.rest_1_
  297.1 5.6 shard_map.89
  302.7 18.9 %all-to-all-done.2.rest_4_.rest_5_.rest_6_.rest_7_ = bf16[8,32,32,128]{3,2,1,0:T(8,128)(2,1)} async-done(((bf16[8,32,32,128]{3,2,1,0:T(8,128)(2,1)}), bf16[8,32,32,128]{3,2,1,0:T(8,128)(2,1)}, u32[]{:S(2)}, u32[]{:S(2)}) %all-to-all-start.2) | async-done | bytes 2097184 | tf_op jit(solution)/shard_map/all_to_all | solution.py:354
  321.6 4.3 all-to-all-start.3
  329.1 6.7 %shard_map.88 = (bf16[256,1024]{1,0:T(8,128)(2,1)}, bf16[256,1024]{1,0:T(8,128)(2,1)}, bf16[256,1024]{1,0:T(8,128)(2,1)}, bf16[256,1024]{1,0:T(8,128)(2,1)}) custom-call(s32[1]{0:T(128)} %bitcast.me_ref, bf16[256,16384]{1,0:T(8,128)(2,1)} %rest_3_.11, bf16[256,16384]{1,0:T(8,128)(2,1)} %rest_3_.11, bf16[256,16384]{1,0:T(8,128)(2,1)} %rest_3_.11, ...), custom_call_target="tpu_custom_call" | custom-call | flops 8388608 | bytes 12582912 | tf_op jit(solution)/shard_map/pallas_call | solution.py:130
  335.8 1.6 collective-permute-start.11
  337.4 1.5 collective-permute-start.12
  339.4 4.8 shard_map.93.refs_0_
  345.5 5.3 collective-permute-done.11.rest_1_.refs_1_
  350.8 11.9 %collective-permute-done.12.rest_2_.refs_2_ = bf16[256,1024]{1,0:T(8,128)(2,1)S(1)} collective-permute-done((bf16[256,1024]{1,0:T(8,128)(2,1)}, bf16[256,1024]{1,0:T(8,128)(2,1)S(1)}, u32[]{:S(2)}, u32[]{:S(2)}) %collective-permute-start.12) | collective-permute-done | bytes 524320 | tf_op jit(solution)/shard_map/ppermute | solution.py:284
  364.3 10.7 %all-to-all-done.3.rest_4_.rest_5_.rest_6_.rest_7_ = bf16[8,32,32,128]{3,2,1,0:T(8,128)(2,1)} async-done(((bf16[8,32,32,128]{3,2,1,0:T(8,128)(2,1)}), bf16[8,32,32,128]{3,2,1,0:T(8,128)(2,1)}, u32[]{:S(2)}, u32[]{:S(2)}) %all-to-all-start.3) | async-done | bytes 2097184 | tf_op jit(solution)/shard_map/all_to_all | solution.py:354
  375.1 4.5 all-to-all-start.5
  379.6 6.7 %shard_map.90 = (bf16[256,1024]{1,0:T(8,128)(2,1)}, bf16[256,1024]{1,0:T(8,128)(2,1)}, bf16[256,1024]{1,0:T(8,128)(2,1)}, bf16[256,1024]{1,0:T(8,128)(2,1)}) custom-call(s32[1]{0:T(128)} %bitcast.me_ref, bf16[256,16384]{1,0:T(8,128)(2,1)} %rest_3_.11, bf16[256,16384]{1,0:T(8,128)(2,1)} %rest_3_.11, bf16[256,16384]{1,0:T(8,128)(2,1)} %rest_3_.11, ...), custom_call_target="tpu_custom_call" | custom-call | flops 8388608 | bytes 12582912 | tf_op jit(solution)/shard_map/pallas_call | solution.py:130
  386.3 1.6 collective-permute-start.14
  387.8 1.5 collective-permute-start.15
  389.9 5.0 shard_map.84.refs_0_
  395.0 1.4 copy-done.4
  396.4 31.2 %shard_map.91 = (bf16[256,1024]{1,0:T(8,128)(2,1)S(1)}, bf16[256,1024]{1,0:T(8,128)(2,1)}, bf16[256,1024]{1,0:T(8,128)(2,1)S(1)}, bf16[256,1024]{1,0:T(8,128)(2,1)S(1)}) custom-call(s32[1]{0:T(128)} %bitcast.me_ref, bf16[256,1024]{1,0:T(8,128)(2,1)S(1)} %copy-done.39, bf16[256,1024]{1,0:T(8,128)(2,1)S(1)} %copy-done.19, bf16[256,1024]{1,0:T(8,128)(2,1)S(1)} %copy-done.21, ...), custom_call_target="tpu_custom_call" | custom-call | flops 25769803776 | bytes 29360128 | tf_op jit(solution)/shard_map/pallas_call | solution.py:215
  431.1 4.9 all-to-all-start.4
  437.4 1.5 collective-permute-start.19
  439.7 6.7 %shard_map.95 = (bf16[256,1024]{1,0:T(8,128)(2,1)}, bf16[256,1024]{1,0:T(8,128)(2,1)}, bf16[256,1024]{1,0:T(8,128)(2,1)}, bf16[256,1024]{1,0:T(8,128)(2,1)}) custom-call(s32[1]{0:T(128)} %bitcast.me_ref, bf16[256,16384]{1,0:T(8,128)(2,1)} %rest_3_.11, bf16[256,16384]{1,0:T(8,128)(2,1)} %rest_3_.11, bf16[256,16384]{1,0:T(8,128)(2,1)} %rest_3_.11, ...), custom_call_target="tpu_custom_call" | custom-call | flops 8388608 | bytes 12582912 | tf_op jit(solution)/shard_map/pallas_call | solution.py:130
  446.3 1.3 collective-permute-start.17
  447.7 1.5 collective-permute-start.24
  449.2 1.8 collective-permute-done.18.rest_1_
  451.0 2.2 collective-permute-start.25
  454.3 30.3 %shard_map.96 = (bf16[256,1024]{1,0:T(8,128)(2,1)S(1)}, bf16[256,1024]{1,0:T(8,128)(2,1)S(1)}, bf16[256,1024]{1,0:T(8,128)(2,1)S(1)}, bf16[256,1024]{1,0:T(8,128)(2,1)S(1)}) custom-call(s32[1]{0:T(128)} %bitcast.me_ref, bf16[256,1024]{1,0:T(8,128)(2,1)S(1)} %copy-done.29, bf16[256,1024]{1,0:T(8,128)(2,1)S(1)} %copy-done.13, ...), custom_call_target="tpu_custom_call" | custom-call | flops 25769803776 | bytes 29360128 | tf_op jit(solution)/shard_map/pallas_call | solution.py:215
  490.1 1.6 shard_map.98.rest_12_.rest_4_
  492.5 6.7 %shard_map.99 = (bf16[256,1024]{1,0:T(8,128)(2,1)}, bf16[256,1024]{1,0:T(8,128)(2,1)}, bf16[256,1024]{1,0:T(8,128)(2,1)}, bf16[256,1024]{1,0:T(8,128)(2,1)}) custom-call(s32[1]{0:T(128)} %bitcast.me_ref, bf16[256,16384]{1,0:T(8,128)(2,1)} %rest_3_.11, bf16[256,16384]{1,0:T(8,128)(2,1)} %rest_3_.11, bf16[256,16384]{1,0:T(8,128)(2,1)} %rest_3_.11, ...), custom_call_target="tpu_custom_call" | custom-call | flops 8388608 | bytes 12582912 | tf_op jit(solution)/shard_map/pallas_call | solution.py:130
  499.2 1.3 collective-permute-start.21
  500.5 1.5 collective-permute-start.22
  504.8 31.5 %shard_map.100 = (bf16[256,1024]{1,0:T(8,128)(2,1)S(1)}, bf16[256,1024]{1,0:T(8,128)(2,1)S(1)}, bf16[256,1024]{1,0:T(8,128)(2,1)S(1)}, bf16[256,1024]{1,0:T(8,128)(2,1)S(1)}) custom-call(s32[1]{0:T(128)} %bitcast.me_ref, bf16[256,1024]{1,0:T(8,128)(2,1)S(1)} %copy-done.31, bf16[256,1024]{1,0:T(8,128)(2,1)S(1)} %copy-done.25, ...), custom_call_target="tpu_custom_call" | custom-call | flops 25769803776 | bytes 29360128 | tf_op jit(solution)/shard_map/pallas_call | solution.py:215
  536.4 2.3 collective-permute-start.34
  540.0 2.2 collective-permute-start.33
  542.2 30.5 %shard_map.101 = (bf16[256,1024]{1,0:T(8,128)(2,1)S(1)}, bf16[256,1024]{1,0:T(8,128)(2,1)S(1)}, bf16[256,1024]{1,0:T(8,128)(2,1)S(1)}, bf16[256,1024]{1,0:T(8,128)(2,1)S(1)}) custom-call(s32[1]{0:T(128)} %bitcast.me_ref, bf16[256,1024]{1,0:T(8,128)(2,1)S(1)} %copy-done.35, bf16[256,1024]{1,0:T(8,128)(2,1)S(1)} %collective-permute-done.21.rest_1_, ...), custom_call_target="tpu_custom_call" | custom-call | flops 25769803776 | bytes 29360128 | tf_op jit(solution)/shard_map/pallas_call | solution.py:215
  574.1 2.2 collective-permute-start.30
  576.3 1.6 shard_map.102.rest_4_
  577.9 1.6 shard_map.103.rest_4_
  579.5 8.2 %collective-permute-done.28.rest_1_ = bf16[256,1024]{1,0:T(8,128)(2,1)S(1)} collective-permute-done((bf16[256,1024]{1,0:T(8,128)(2,1)S(1)}, bf16[256,1024]{1,0:T(8,128)(2,1)S(1)}, u32[]{:S(2)}, u32[]{:S(2)}) %collective-permute-start.28) | collective-permute-done | bytes 524320 | tf_op jit(solution)/shard_map/ppermute | solution.py:284
  587.7 7.1 %collective-permute-done.29.rest_2_ = bf16[256,1024]{1,0:T(8,128)(2,1)S(1)} collective-permute-done((bf16[256,1024]{1,0:T(8,128)(2,1)S(1)}, bf16[256,1024]{1,0:T(8,128)(2,1)S(1)}, u32[]{:S(2)}, u32[]{:S(2)}) %collective-permute-start.29) | collective-permute-done | bytes 524320 | tf_op jit(solution)/shard_map/ppermute | solution.py:284
  594.8 1.6 shard_map.104
  (143 shorter events, 33.3 us)
Async XLA Ops:
  0.0 23.5 %copy-start.11 = (bf16[512,512]{1,0:T(8,128)(2,1)S(1)}, bf16[512,512]{1,0:T(8,128)(2,1)}, u32[]{:S(2)}) copy-start(bf16[512,512]{1,0:T(8,128)(2,1)} %factor.3) | copy-start | bytes 1572868
  1.3 20.6 %collective-permute-start = (bf16[1,2,192,1024]{3,2,1,0:T(8,128)(2,1)S(1)}, bf16[1,2,192,1024]{3,2,1,0:T(8,128)(2,1)S(1)}, u32[]{:S(2)}, u32[]{:S(2)}) collective-permute-start(bf16[1,2,192,1024]{3,2,1,0:T(8,128)(2,1)S(1)} %maximum_bitcast_fusion), channel_id=1, source_target_pairs={{0,8},{4,12},{8,0},{12,4},{16,24},{20,28},{24,16},{28,20},{1,9},{5... | collective-permute-start | bytes 2359304 | tf_op jit(solution)/shard_map/ppermute | solution.py:299
  22.8 14.1 %collective-permute-start.1 = (bf16[2,2,192,1024]{3,2,1,0:T(8,128)(2,1)S(1)}, bf16[2,2,192,1024]{3,2,1,0:T(8,128)(2,1)S(1)}, u32[]{:S(2)}, u32[]{:S(2)}) collective-permute-start(bf16[2,2,192,1024]{3,2,1,0:T(8,128)(2,1)S(1)} %pad_maximum_fusion.3), channel_id=1, source_target_pairs={{8,16},{12,20},{16,8},{20,12},{9,17},{13,21},{17,9},{21,13},{10,18... | collective-permute-start | bytes 4718600 | tf_op jit(solution)/shard_map/ppermute | solution.py:308
  23.5 3.4 copy-start
  34.9 2.0 copy-start.2
  38.0 27.2 %copy-start.42 = (bf16[2,2,192,1024]{3,2,1,0:T(8,128)(2,1)S(1)}, bf16[2,2,192,1024]{3,2,1,0:T(8,128)(2,1)}, u32[]{:S(2)}) copy-start(bf16[2,2,192,1024]{3,2,1,0:T(8,128)(2,1)} %copy-done.41) | copy-start | bytes 4718596
  38.0 131.6 %all-to-all-start.1 = ((bf16[8,2,32,32,128]{4,3,2,1,0:T(8,128)(2,1)}), bf16[8,2,32,32,128]{4,3,2,1,0:T(8,128)(2,1)}, u32[]{:S(2)}, u32[]{:S(2)}) async-start(bf16[8,2,32,32,128]{4,3,2,1,0:T(8,128)(2,1)} %shard_map.86), calls=%async_computation.1 | async-start | bytes 8388608 | tf_op jit(solution)/shard_map/all_to_all | solution.py:354
  65.2 104.4 %collective-permute-start.2 = (bf16[2,2,192,1024]{3,2,1,0:T(8,128)(2,1)S(1)}, bf16[2,2,192,1024]{3,2,1,0:T(8,128)(2,1)}, u32[]{:S(2)}, u32[]{:S(2)}) collective-permute-start(bf16[2,2,192,1024]{3,2,1,0:T(8,128)(2,1)S(1)} %copy-done.42), channel_id=1, source_target_pairs={{8,0},{12,4},{16,24},{20,28},{9,1},{13,5},{17,25},{21,29},{10,2},{... | collective-permute-start | bytes 4718600 | tf_op jit(solution)/shard_map/ppermute | solution.py:309
  66.5 3.4 copy-start.1
  169.7 98.5 %all-to-all-start = ((bf16[8,2,32,32,128]{4,3,2,1,0:T(8,128)(2,1)}), bf16[8,2,32,32,128]{4,3,2,1,0:T(8,128)(2,1)}, u32[]{:S(2)}, u32[]{:S(2)}) async-start(bf16[8,2,32,32,128]{4,3,2,1,0:T(8,128)(2,1)} %shard_map.83), calls=%async_computation | async-start | bytes 8388608 | tf_op jit(solution)/shard_map/all_to_all | solution.py:354
  174.2 2.2 copy-start.44
  178.2 41.1 %copy-start.10 = (f32[256,256]{1,0:T(8,128)S(1)}, f32[256,256]{1,0:T(8,128)}, u32[]{:S(2)}) copy-start(f32[256,256]{1,0:T(8,128)} %s_ref.7) | copy-start | bytes 786436
  178.2 36.9 %collective-permute-start.3 = (bf16[768,1024]{1,0:T(8,128)(2,1)}, bf16[768,1024]{1,0:T(8,128)(2,1)S(1)}, u32[]{:S(2)}, u32[]{:S(2)}) collective-permute-start(bf16[768,1024]{1,0:T(8,128)(2,1)} %bitcast.6), channel_id=1, source_target_pairs={{0,1},{1,0},{2,3},{3,2},{4,5},{5,4},{6,7},{7,6},{8,9},{9,8},{10,11... | collective-permute-start | bytes 4718600 | tf_op jit(solution)/shard_map/ppermute | solution.py:299
  181.3 37.5 %collective-permute-start.8 = (bf16[1024,768]{1,0:T(8,128)(2,1)}, bf16[1024,768]{1,0:T(8,128)(2,1)S(1)}, u32[]{:S(2)}, u32[]{:S(2)}) collective-permute-start(bf16[1024,768]{1,0:T(8,128)(2,1)} %bitcast.23), channel_id=1, source_target_pairs={{0,2},{1,3},{2,0},{3,1},{4,6},{5,7},{6,4},{7,5},{8,10},{9,11},{10,... | collective-permute-start | bytes 4718600 | tf_op jit(solution)/shard_map/ppermute | solution.py:299
  182.8 89.7 %collective-permute-start.4 = (bf16[768,1024]{1,0:T(8,128)(2,1)}, bf16[768,1024]{1,0:T(8,128)(2,1)}, u32[]{:S(2)}, u32[]{:S(2)}) collective-permute-start(bf16[768,1024]{1,0:T(8,128)(2,1)} %bitcast.6), channel_id=1, source_target_pairs={{0,2},{1,3},{2,0},{3,1},{4,6},{5,7},{6,4},{7,5},{8,10},{9,11},{10,... | collective-permute-start | bytes 4718600 | tf_op jit(solution)/shard_map/ppermute | solution.py:299
  215.1 70.3 %collective-permute-start.5 = (bf16[768,1024]{1,0:T(8,128)(2,1)S(1)}, bf16[768,1024]{1,0:T(8,128)(2,1)}, u32[]{:S(2)}, u32[]{:S(2)}) collective-permute-start(bf16[768,1024]{1,0:T(8,128)(2,1)S(1)} %collective-permute-done.3.rest_0_), channel_id=1, source_target_pairs={{0,2},{1,3},{2,0},{3,1},{4,6},{5,7},{6,4},{7,5},{8,10},{9,11},{10,... | collective-permute-start | bytes 4718600 | tf_op jit(solution)/shard_map/ppermute | solution.py:299
  216.6 74.7 %collective-permute-start.7 = (bf16[1024,768]{1,0:T(8,128)(2,1)}, bf16[1024,768]{1,0:T(8,128)(2,1)}, u32[]{:S(2)}, u32[]{:S(2)}) collective-permute-start(bf16[1024,768]{1,0:T(8,128)(2,1)} %bitcast.24), channel_id=1, source_target_pairs={{0,1},{1,0},{2,3},{3,2},{4,5},{5,4},{6,7},{7,6},{8,9},{9,8},{10,11... | collective-permute-start | bytes 4718600 | tf_op jit(solution)/shard_map/ppermute | solution.py:299
  218.8 72.6 %collective-permute-start.9 = (bf16[1024,768]{1,0:T(8,128)(2,1)S(1)}, bf16[1024,768]{1,0:T(8,128)(2,1)}, u32[]{:S(2)}, u32[]{:S(2)}) collective-permute-start(bf16[1024,768]{1,0:T(8,128)(2,1)S(1)} %collective-permute-done.8.rest_1_), channel_id=1, source_target_pairs={{0,1},{1,0},{2,3},{3,2},{4,5},{5,4},{6,7},{7,6},{8,9},{9,8},{10,11... | collective-permute-start | bytes 4718600 | tf_op jit(solution)/shard_map/ppermute | solution.py:299
  268.2 53.4 %all-to-all-start.2 = ((bf16[8,32,32,128]{3,2,1,0:T(8,128)(2,1)}), bf16[8,32,32,128]{3,2,1,0:T(8,128)(2,1)}, u32[]{:S(2)}, u32[]{:S(2)}) async-start(bf16[8,32,32,128]{3,2,1,0:T(8,128)(2,1)} %shard_map.87), calls=%async_computation.2 | async-start | bytes 4194304 | tf_op jit(solution)/shard_map/all_to_all | solution.py:354
  285.4 5.9 copy-start.40
  291.3 98.6 %collective-permute-start.6 = (bf16[4,768,1024]{2,1,0:T(8,128)(2,1)}, bf16[4,768,1024]{2,1,0:T(8,128)(2,1)}, u32[]{:S(2)}, u32[]{:S(2)}) collective-permute-start(bf16[4,768,1024]{2,1,0:T(8,128)(2,1)} %pad_maximum_fusion.rest_4_.rest_0_), channel_id=1, source_target_pairs={{0,4},{4,0},{8,12},{12,8},{16,20},{20,16},{24,28},{28,24},{1,5},{5... | collective-permute-start | bytes 18874376 | tf_op jit(solution)/shard_map/ppermute | solution.py:299
  296.6 93.3 %collective-permute-start.10 = (bf16[4,1024,768]{2,1,0:T(8,128)(2,1)}, bf16[4,1024,768]{2,1,0:T(8,128)(2,1)}, u32[]{:S(2)}, u32[]{:S(2)}) collective-permute-start(bf16[4,1024,768]{2,1,0:T(8,128)(2,1)} %pad_maximum_fusion.1.rest_6_.rest_1_), channel_id=1, source_target_pairs={{0,4},{4,0},{8,12},{12,8},{16,20},{20,16},{24,28},{28,24},{1,5},{5... | collective-permute-start | bytes 18874376 | tf_op jit(solution)/shard_map/ppermute | solution.py:299
  321.6 53.4 %all-to-all-start.3 = ((bf16[8,32,32,128]{3,2,1,0:T(8,128)(2,1)}), bf16[8,32,32,128]{3,2,1,0:T(8,128)(2,1)}, u32[]{:S(2)}, u32[]{:S(2)}) async-start(bf16[8,32,32,128]{3,2,1,0:T(8,128)(2,1)} %shard_map.89), calls=%async_computation.3 | async-start | bytes 4194304 | tf_op jit(solution)/shard_map/all_to_all | solution.py:354
  335.8 15.0 %collective-permute-start.11 = (bf16[256,1024]{1,0:T(8,128)(2,1)}, bf16[256,1024]{1,0:T(8,128)(2,1)S(1)}, u32[]{:S(2)}, u32[]{:S(2)}) collective-permute-start(bf16[256,1024]{1,0:T(8,128)(2,1)} %get-tuple-element.38), channel_id=1, source_target_pairs={{0,1},{1,0},{2,3},{3,2},{4,5},{5,4},{6,7},{7,6},{8,9},{9,8},{10,11... | collective-permute-start | bytes 1572872 | tf_op jit(solution)/shard_map/ppermute | solution.py:284
  337.4 25.3 %collective-permute-start.12 = (bf16[256,1024]{1,0:T(8,128)(2,1)}, bf16[256,1024]{1,0:T(8,128)(2,1)S(1)}, u32[]{:S(2)}, u32[]{:S(2)}) collective-permute-start(bf16[256,1024]{1,0:T(8,128)(2,1)} %get-tuple-element.39), channel_id=1, source_target_pairs={{0,2},{1,3},{2,0},{3,1},{4,6},{5,7},{6,4},{7,5},{8,10},{9,11},{10,... | collective-permute-start | bytes 1572872 | tf_op jit(solution)/shard_map/ppermute | solution.py:284
  338.9 23.8 %collective-permute-start.13 = (bf16[256,1024]{1,0:T(8,128)(2,1)}, bf16[256,1024]{1,0:T(8,128)(2,1)S(1)}, u32[]{:S(2)}, u32[]{:S(2)}) collective-permute-start(bf16[256,1024]{1,0:T(8,128)(2,1)} %get-tuple-element.40), channel_id=1, source_target_pairs={{0,3},{1,2},{2,1},{3,0},{4,7},{5,6},{6,5},{7,4},{8,11},{9,10},{10,... | collective-permute-start | bytes 1572872 | tf_op jit(solution)/shard_map/ppermute | solution.py:284
  350.8 11.9 %copy-start.18 = (bf16[256,1024]{1,0:T(8,128)(2,1)}, bf16[256,1024]{1,0:T(8,128)(2,1)S(1)}, u32[]{:S(2)}) copy-start(bf16[256,1024]{1,0:T(8,128)(2,1)S(1)} %collective-permute-done.11.rest_1_.refs_1_) | copy-start | bytes 1572868
  375.1 56.1 %all-to-all-start.5 = ((bf16[8,32,32,128]{3,2,1,0:T(8,128)(2,1)}), bf16[8,32,32,128]{3,2,1,0:T(8,128)(2,1)}, u32[]{:S(2)}, u32[]{:S(2)}) async-start(bf16[8,32,32,128]{3,2,1,0:T(8,128)(2,1)} %shard_map.94), calls=%async_computation.5 | async-start | bytes 4194304 | tf_op jit(solution)/shard_map/all_to_all | solution.py:354
  386.3 43.7 %collective-permute-start.14 = (bf16[256,1024]{1,0:T(8,128)(2,1)}, bf16[256,1024]{1,0:T(8,128)(2,1)S(1)}, u32[]{:S(2)}, u32[]{:S(2)}) collective-permute-start(bf16[256,1024]{1,0:T(8,128)(2,1)} %get-tuple-element.43), channel_id=1, source_target_pairs={{0,1},{1,0},{2,3},{3,2},{4,5},{5,4},{6,7},{7,6},{8,9},{9,8},{10,11... | collective-permute-start | bytes 1572872 | tf_op jit(solution)/shard_map/ppermute | solution.py:284
  387.8 42.2 %collective-permute-start.15 = (bf16[256,1024]{1,0:T(8,128)(2,1)}, bf16[256,1024]{1,0:T(8,128)(2,1)S(1)}, u32[]{:S(2)}, u32[]{:S(2)}) collective-permute-start(bf16[256,1024]{1,0:T(8,128)(2,1)} %get-tuple-element.44), channel_id=1, source_target_pairs={{0,2},{1,3},{2,0},{3,1},{4,6},{5,7},{6,4},{7,5},{8,10},{9,11},{10,... | collective-permute-start | bytes 1572872 | tf_op jit(solution)/shard_map/ppermute | solution.py:284
  389.3 7.0 %copy-start.19 = (bf16[256,1024]{1,0:T(8,128)(2,1)S(1)}, bf16[256,1024]{1,0:T(8,128)(2,1)}, u32[]{:S(2)}) copy-start(bf16[256,1024]{1,0:T(8,128)(2,1)} %copy-done.18) | copy-start | bytes 1572868
  389.3 7.0 %copy-start.21 = (bf16[256,1024]{1,0:T(8,128)(2,1)S(1)}, bf16[256,1024]{1,0:T(8,128)(2,1)}, u32[]{:S(2)}) copy-start(bf16[256,1024]{1,0:T(8,128)(2,1)} %copy-done.20) | copy-start | bytes 1572868
  389.3 7.0 %copy-start.23 = (bf16[256,1024]{1,0:T(8,128)(2,1)S(1)}, bf16[256,1024]{1,0:T(8,128)(2,1)}, u32[]{:S(2)}) copy-start(bf16[256,1024]{1,0:T(8,128)(2,1)} %copy-done.22) | copy-start | bytes 1572868
  389.3 7.0 %copy-start.28 = (bf16[256,1024]{1,0:T(8,128)(2,1)S(1)}, bf16[256,1024]{1,0:T(8,128)(2,1)}, u32[]{:S(2)}) copy-start(bf16[256,1024]{1,0:T(8,128)(2,1)} %get-tuple-element.41.rest_8_.rest_0_) | copy-start | bytes 1572868
  389.3 7.0 %copy-start.39 = (bf16[256,1024]{1,0:T(8,128)(2,1)S(1)}, bf16[256,1024]{1,0:T(8,128)(2,1)}, u32[]{:S(2)}) copy-start(bf16[256,1024]{1,0:T(8,128)(2,1)} %get-tuple-element.37.rest_0_) | copy-start | bytes 1572868
  389.4 40.6 %collective-permute-start.16 = (bf16[256,1024]{1,0:T(8,128)(2,1)}, bf16[256,1024]{1,0:T(8,128)(2,1)S(1)}, u32[]{:S(2)}, u32[]{:S(2)}) collective-permute-start(bf16[256,1024]{1,0:T(8,128)(2,1)} %get-tuple-element.45), channel_id=1, source_target_pairs={{0,3},{1,2},{2,1},{3,0},{4,7},{5,6},{6,5},{7,4},{8,11},{9,10},{10,... | collective-permute-start | bytes 1572872 | tf_op jit(solution)/shard_map/ppermute | solution.py:284
  431.1 6.2 %copy-start.38 = (bf16[256,1024]{1,0:T(8,128)(2,1)S(1)}, bf16[256,1024]{1,0:T(8,128)(2,1)}, u32[]{:S(2)}) copy-start(bf16[256,1024]{1,0:T(8,128)(2,1)} %copy-done.37) | copy-start | bytes 1572868
  431.1 7.8 %copy-start.34 = (bf16[256,1024]{1,0:T(8,128)(2,1)S(1)}, bf16[256,1024]{1,0:T(8,128)(2,1)}, u32[]{:S(2)}) copy-start(bf16[256,1024]{1,0:T(8,128)(2,1)} %copy-done.33) | copy-start | bytes 1572868
  431.1 60.5 %all-to-all-start.4 = ((bf16[8,32,32,128]{3,2,1,0:T(8,128)(2,1)}), bf16[8,32,32,128]{3,2,1,0:T(8,128)(2,1)}, u32[]{:S(2)}, u32[]{:S(2)}) async-start(bf16[8,32,32,128]{3,2,1,0:T(8,128)(2,1)} %shard_map.92), calls=%async_computation.4 | async-start | bytes 4194304 | tf_op jit(solution)/shard_map/all_to_all | solution.py:354
  436.1 14.9 %collective-permute-start.18 = (bf16[256,1024]{1,0:T(8,128)(2,1)}, bf16[256,1024]{1,0:T(8,128)(2,1)S(1)}, u32[]{:S(2)}, u32[]{:S(2)}) collective-permute-start(bf16[256,1024]{1,0:T(8,128)(2,1)} %get-tuple-element.49), channel_id=1, source_target_pairs={{0,1},{1,0},{2,3},{3,2},{4,5},{5,4},{6,7},{7,6},{8,9},{9,8},{10,11... | collective-permute-start | bytes 1572872 | tf_op jit(solution)/shard_map/ppermute | solution.py:284
  437.4 50.4 %collective-permute-start.19 = (bf16[256,1024]{1,0:T(8,128)(2,1)S(1)}, bf16[256,1024]{1,0:T(8,128)(2,1)S(1)}, u32[]{:S(2)}, u32[]{:S(2)}) collective-permute-start(bf16[256,1024]{1,0:T(8,128)(2,1)S(1)} %copy-done.38), channel_id=1, source_target_pairs={{0,2},{1,3},{2,0},{3,1},{4,6},{5,7},{6,4},{7,5},{8,10},{9,11},{10,... | collective-permute-start | bytes 1572872 | tf_op jit(solution)/shard_map/ppermute | solution.py:284
  438.9 14.4 %copy-start.13 = (bf16[256,1024]{1,0:T(8,128)(2,1)S(1)}, bf16[256,1024]{1,0:T(8,128)(2,1)}, u32[]{:S(2)}) copy-start(bf16[256,1024]{1,0:T(8,128)(2,1)} %copy-done.12) | copy-start | bytes 1572868
  438.9 14.4 %copy-start.15 = (bf16[256,1024]{1,0:T(8,128)(2,1)S(1)}, bf16[256,1024]{1,0:T(8,128)(2,1)}, u32[]{:S(2)}) copy-start(bf16[256,1024]{1,0:T(8,128)(2,1)} %copy-done.14) | copy-start | bytes 1572868
  438.9 14.4 %copy-start.17 = (bf16[256,1024]{1,0:T(8,128)(2,1)S(1)}, bf16[256,1024]{1,0:T(8,128)(2,1)}, u32[]{:S(2)}) copy-start(bf16[256,1024]{1,0:T(8,128)(2,1)} %copy-done.16) | copy-start | bytes 1572868
  438.9 14.4 %copy-start.29 = (bf16[256,1024]{1,0:T(8,128)(2,1)S(1)}, bf16[256,1024]{1,0:T(8,128)(2,1)}, u32[]{:S(2)}) copy-start(bf16[256,1024]{1,0:T(8,128)(2,1)} %get-tuple-element.41.rest_8_.rest_0_) | copy-start | bytes 1572868
  438.9 49.4 %collective-permute-start.20 = (bf16[256,1024]{1,0:T(8,128)(2,1)S(1)}, bf16[256,1024]{1,0:T(8,128)(2,1)S(1)}, u32[]{:S(2)}, u32[]{:S(2)}) collective-permute-start(bf16[256,1024]{1,0:T(8,128)(2,1)S(1)} %copy-done.34), channel_id=1, source_target_pairs={{0,3},{1,2},{2,1},{3,0},{4,7},{5,6},{6,5},{7,4},{8,11},{9,10},{10,... | collective-permute-start | bytes 1572872 | tf_op jit(solution)/shard_map/ppermute | solution.py:284
  446.3 45.3 %collective-permute-start.17 = (bf16[256,1024]{1,0:T(8,128)(2,1)}, bf16[256,1024]{1,0:T(8,128)(2,1)S(1)}, u32[]{:S(2)}, u32[]{:S(2)}) collective-permute-start(bf16[256,1024]{1,0:T(8,128)(2,1)} %get-tuple-element.48), channel_id=1, source_target_pairs={{0,1},{1,0},{2,3},{3,2},{4,5},{5,4},{6,7},{7,6},{8,9},{9,8},{10,11... | collective-permute-start | bytes 1572872 | tf_op jit(solution)/shard_map/ppermute | solution.py:284
  447.7 52.9 %collective-permute-start.24 = (bf16[256,1024]{1,0:T(8,128)(2,1)}, bf16[256,1024]{1,0:T(8,128)(2,1)}, u32[]{:S(2)}, u32[]{:S(2)}) collective-permute-start(bf16[256,1024]{1,0:T(8,128)(2,1)} %get-tuple-element.56), channel_id=1, source_target_pairs={{0,2},{1,3},{2,0},{3,1},{4,6},{5,7},{6,4},{7,5},{8,10},{9,11},{10,... | collective-permute-start | bytes 1572872 | tf_op jit(solution)/shard_map/ppermute | solution.py:284
  451.0 51.0 %collective-permute-start.25 = (bf16[256,1024]{1,0:T(8,128)(2,1)}, bf16[256,1024]{1,0:T(8,128)(2,1)}, u32[]{:S(2)}, u32[]{:S(2)}) collective-permute-start(bf16[256,1024]{1,0:T(8,128)(2,1)} %get-tuple-element.57), channel_id=1, source_target_pairs={{0,3},{1,2},{2,1},{3,0},{4,7},{5,6},{6,5},{7,4},{8,11},{9,10},{10,... | collective-permute-start | bytes 1572872 | tf_op jit(solution)/shard_map/ppermute | solution.py:284
  487.8 48.6 %collective-permute-start.26 = (bf16[256,1024]{1,0:T(8,128)(2,1)}, bf16[256,1024]{1,0:T(8,128)(2,1)S(1)}, u32[]{:S(2)}, u32[]{:S(2)}) collective-permute-start(bf16[256,1024]{1,0:T(8,128)(2,1)} %copy-done.36), channel_id=1, source_target_pairs={{0,1},{1,0},{2,3},{3,2},{4,5},{5,4},{6,7},{7,6},{8,9},{9,8},{10,11... | collective-permute-start | bytes 1572872 | tf_op jit(solution)/shard_map/ppermute | solution.py:284
  488.3 50.4 %collective-permute-start.27 = (bf16[256,1024]{1,0:T(8,128)(2,1)}, bf16[256,1024]{1,0:T(8,128)(2,1)S(1)}, u32[]{:S(2)}, u32[]{:S(2)}) collective-permute-start(bf16[256,1024]{1,0:T(8,128)(2,1)} %copy-done.32), channel_id=1, source_target_pairs={{0,2},{1,3},{2,0},{3,1},{4,6},{5,7},{6,4},{7,5},{8,10},{9,11},{10,... | collective-permute-start | bytes 1572872 | tf_op jit(solution)/shard_map/ppermute | solution.py:284
  491.6 11.1 %copy-start.31 = (bf16[256,1024]{1,0:T(8,128)(2,1)S(1)}, bf16[256,1024]{1,0:T(8,128)(2,1)}, u32[]{:S(2)}) copy-start(bf16[256,1024]{1,0:T(8,128)(2,1)} %get-tuple-element.46.rest_8_.rest_0_) | copy-start | bytes 1572868
  499.2 40.1 %collective-permute-start.21 = (bf16[256,1024]{1,0:T(8,128)(2,1)}, bf16[256,1024]{1,0:T(8,128)(2,1)S(1)}, u32[]{:S(2)}, u32[]{:S(2)}) collective-permute-start(bf16[256,1024]{1,0:T(8,128)(2,1)} %get-tuple-element.53), channel_id=1, source_target_pairs={{0,1},{1,0},{2,3},{3,2},{4,5},{5,4},{6,7},{7,6},{8,9},{9,8},{10,11... | collective-permute-start | bytes 1572872 | tf_op jit(solution)/shard_map/ppermute | solution.py:284
  500.5 39.4 %collective-permute-start.22 = (bf16[256,1024]{1,0:T(8,128)(2,1)}, bf16[256,1024]{1,0:T(8,128)(2,1)S(1)}, u32[]{:S(2)}, u32[]{:S(2)}) collective-permute-start(bf16[256,1024]{1,0:T(8,128)(2,1)} %get-tuple-element.54), channel_id=1, source_target_pairs={{0,2},{1,3},{2,0},{3,1},{4,6},{5,7},{6,4},{7,5},{8,10},{9,11},{10,... | collective-permute-start | bytes 1572872 | tf_op jit(solution)/shard_map/ppermute | solution.py:284
  502.1 40.1 %collective-permute-start.23 = (bf16[256,1024]{1,0:T(8,128)(2,1)}, bf16[256,1024]{1,0:T(8,128)(2,1)S(1)}, u32[]{:S(2)}, u32[]{:S(2)}) collective-permute-start(bf16[256,1024]{1,0:T(8,128)(2,1)} %get-tuple-element.55), channel_id=1, source_target_pairs={{0,3},{1,2},{2,1},{3,0},{4,7},{5,6},{6,5},{7,4},{8,11},{9,10},{10,... | collective-permute-start | bytes 1572872 | tf_op jit(solution)/shard_map/ppermute | solution.py:284
  504.8 31.6 %copy-start.27 = (bf16[256,1024]{1,0:T(8,128)(2,1)S(1)}, bf16[256,1024]{1,0:T(8,128)(2,1)}, u32[]{:S(2)}) copy-start(bf16[256,1024]{1,0:T(8,128)(2,1)} %copy-done.26) | copy-start | bytes 1572868
  536.4 36.9 %collective-permute-start.34 = (bf16[256,1024]{1,0:T(8,128)(2,1)S(1)}, bf16[256,1024]{1,0:T(8,128)(2,1)S(1)}, u32[]{:S(2)}, u32[]{:S(2)}) collective-permute-start(bf16[256,1024]{1,0:T(8,128)(2,1)S(1)} %copy-done.27), channel_id=1, source_target_pairs={{0,3},{1,2},{2,1},{3,0},{4,7},{5,6},{6,5},{7,4},{8,11},{9,10},{10,... | collective-permute-start | bytes 1572872 | tf_op jit(solution)/shard_map/ppermute | solution.py:284
  538.7 35.4 %collective-permute-start.31 = (bf16[256,1024]{1,0:T(8,128)(2,1)S(1)}, bf16[256,1024]{1,0:T(8,128)(2,1)S(1)}, u32[]{:S(2)}, u32[]{:S(2)}) collective-permute-start(bf16[256,1024]{1,0:T(8,128)(2,1)S(1)} %get-tuple-element.65), channel_id=1, source_target_pairs={{0,1},{1,0},{2,3},{3,2},{4,5},{5,4},{6,7},{7,6},{8,9},{9,8},{10,11... | collective-permute-start | bytes 1572872 | tf_op jit(solution)/shard_map/ppermute | solution.py:284
  539.2 38.6 %collective-permute-start.32 = (bf16[256,1024]{1,0:T(8,128)(2,1)S(1)}, bf16[256,1024]{1,0:T(8,128)(2,1)S(1)}, u32[]{:S(2)}, u32[]{:S(2)}) collective-permute-start(bf16[256,1024]{1,0:T(8,128)(2,1)S(1)} %get-tuple-element.66), channel_id=1, source_target_pairs={{0,2},{1,3},{2,0},{3,1},{4,6},{5,7},{6,4},{7,5},{8,10},{9,11},{10,... | collective-permute-start | bytes 1572872 | tf_op jit(solution)/shard_map/ppermute | solution.py:284
  540.0 37.9 %collective-permute-start.33 = (bf16[256,1024]{1,0:T(8,128)(2,1)S(1)}, bf16[256,1024]{1,0:T(8,128)(2,1)S(1)}, u32[]{:S(2)}, u32[]{:S(2)}) collective-permute-start(bf16[256,1024]{1,0:T(8,128)(2,1)S(1)} %get-tuple-element.67), channel_id=1, source_target_pairs={{0,3},{1,2},{2,1},{3,0},{4,7},{5,6},{6,5},{7,4},{8,11},{9,10},{10,... | collective-permute-start | bytes 1572872 | tf_op jit(solution)/shard_map/ppermute | solution.py:284
  542.2 34.1 %copy-start.9 = (bf16[256,1024]{1,0:T(8,128)(2,1)S(1)}, bf16[256,1024]{1,0:T(8,128)(2,1)}, u32[]{:S(2)}) copy-start(bf16[256,1024]{1,0:T(8,128)(2,1)} %copy-done.8) | copy-start | bytes 1572868
  572.7 14.9 %collective-permute-start.28 = (bf16[256,1024]{1,0:T(8,128)(2,1)S(1)}, bf16[256,1024]{1,0:T(8,128)(2,1)S(1)}, u32[]{:S(2)}, u32[]{:S(2)}) collective-permute-start(bf16[256,1024]{1,0:T(8,128)(2,1)S(1)} %get-tuple-element.62), channel_id=1, source_target_pairs={{0,1},{1,0},{2,3},{3,2},{4,5},{5,4},{6,7},{7,6},{8,9},{9,8},{10,11... | collective-permute-start | bytes 1572872 | tf_op jit(solution)/shard_map/ppermute | solution.py:284
  573.3 21.4 %collective-permute-start.29 = (bf16[256,1024]{1,0:T(8,128)(2,1)S(1)}, bf16[256,1024]{1,0:T(8,128)(2,1)S(1)}, u32[]{:S(2)}, u32[]{:S(2)}) collective-permute-start(bf16[256,1024]{1,0:T(8,128)(2,1)S(1)} %get-tuple-element.63), channel_id=1, source_target_pairs={{0,2},{1,3},{2,0},{3,1},{4,6},{5,7},{6,4},{7,5},{8,10},{9,11},{10,... | collective-permute-start | bytes 1572872 | tf_op jit(solution)/shard_map/ppermute | solution.py:284
  574.1 20.7 %collective-permute-start.30 = (bf16[256,1024]{1,0:T(8,128)(2,1)S(1)}, bf16[256,1024]{1,0:T(8,128)(2,1)S(1)}, u32[]{:S(2)}, u32[]{:S(2)}) collective-permute-start(bf16[256,1024]{1,0:T(8,128)(2,1)S(1)} %get-tuple-element.64), channel_id=1, source_target_pairs={{0,3},{1,2},{2,1},{3,0},{4,7},{5,6},{6,5},{7,4},{8,11},{9,10},{10,... | collective-permute-start | bytes 1572872 | tf_op jit(solution)/shard_map/ppermute | solution.py:284
  (22 other events, 21.9 us)
